TPU v7x, 32 devices: a whole 2x2x4 slice. The times are simulated.
32 devices in a mesh: tile: 8 (over y, x, core), rad: 4 (over z).
Axes of the slice: x: 2, y: 2, z: 4, core: 2. Of those that a mesh axis runs over, the one named last changes fastest.
Arguments:
- fields: float32 [3072, 1, 512], P('tile', None, 'rad'), may hold values from -6 to 6
- velocity: float32 [3072, 2, 512], P('tile', None, 'rad'), may hold values from -6 to 6
- operators: bfloat16 [24, 3, 128, 896], P('tile'), may hold values from -0.1875 to 0.1875
- neighbours: int32 [24, 7], P('tile'), may hold values from 0 to 23, as said below
- kappa_ref: float32 [512], replicated, may hold values from 0.3 to 3
- quad_weight: float32 [3072], P('tile'), may hold values from 0.5 to 2
- basis: float32 [3072, 512], P('tile'), may hold values from -0.375 to 0.375
- degree: int32 [512], replicated, may hold values from 0 to 22
Outputs:
- filtered: float32 [3072, 1, 512], P('tile', None, 'rad')
Inputs may be any that keep to these rules, and one draw needn't show every extreme that they name: `neighbours`: row b lists seven different blocks; the first is b itself, and each lies in the tile of b (block // 3) or in one of the two tiles beside it, counted cyclically over the 8 tiles; every row names at least one block of each of the two tiles beside its own.
All inputs are finite; a program needn't handle non-finite values.
Results may differ from a plain program's by a relative error of at most 0.0011.
Values may be sent and summed in bfloat16 or wider, within the bound.
No kernel may reach another device: no remote copies, remote signals or barrier semaphores. Data moves between devices by JAX's collectives and lax.ppermute only.
A program may use at most 64 MiB of HBM per device.

v0:
```python
import jax
import jax.numpy as jnp
from jax import lax
from jax.sharding import PartitionSpec as P

DEGMAX = 22


advect_step = 0.25
hyper_rate = 0.1
radial_step = 0.25


def padded(block, sides, width):
    for axis, dim in sides:
        count = lax.axis_size(axis)
        forward = [(i, i + 1) for i in range(count - 1)]
        forward.append((count - 1, 0))
        backward = [(target, source) for source, target in forward]
        low = lax.ppermute(
            lax.slice_in_dim(block, block.shape[dim] - width, None, axis=dim), axis, forward
        )
        high = lax.ppermute(lax.slice_in_dim(block, 0, width, axis=dim), axis, backward)
        block = jnp.concatenate([low, block, high], axis=dim)
    return block


def cheb_matrix(count):
    points = jnp.arange(count, dtype=jnp.int32)
    angles = jnp.pi * points.astype(jnp.float32) / (count - 1)
    upper = angles[:, None]
    lower = angles[None, :]
    spacing = -2.0 * jnp.sin((upper + lower) / 2.0) * jnp.sin((upper - lower) / 2.0)
    on_diag = points[:, None] == points[None, :]
    spacing = jnp.where(on_diag, jnp.float32(1.0), spacing)
    weights = jnp.where((points == 0) | (points == count - 1), jnp.float32(2.0), jnp.float32(1.0))
    parity = jnp.where(
        (points[:, None] + points[None, :]) % 2 == 0, jnp.float32(1.0), jnp.float32(-1.0)
    )
    entries = weights[:, None] / weights[None, :] * parity / spacing
    entries = jnp.where(on_diag, jnp.float32(0.0), entries)
    diagonal = -jnp.sum(entries, axis=1)
    matrix = entries + jnp.diag(diagonal)
    return jnp.sin(angles)[:, None] * matrix / count


def stencil(window, block_ops, local_ids, blocks, block_size, columns):
    cell_rows = window.reshape(3 * blocks, block_size, columns)
    nearby = jnp.take(cell_rows, local_ids, axis=0).reshape(blocks, 7 * block_size, columns)
    return jnp.einsum("bkij,bjc->bkic", block_ops, nearby, preferred_element_type=jnp.float32)


def diffuse(stepped, derivative, kappa_ref):
    slopes = jnp.einsum("nfj,ij->nfi", stepped, derivative, precision=lax.Precision.HIGHEST)
    fluxes = kappa_ref[None, None, :] * (1.0 + 0.5 * jnp.tanh(stepped)) * slopes
    return stepped + radial_step * jnp.einsum(
        "nfj,ij->nfi", fluxes, derivative, precision=lax.Precision.HIGHEST
    )


def body(fields, velocity, operators, neighbours, kappa_ref, quad_weight, basis, degree):
    nodes_dev, nfield, levels = fields.shape
    blocks = operators.shape[0]
    block_size = operators.shape[2]
    columns = nfield * levels
    tile_count = lax.axis_size("tile")
    total_blocks = blocks * tile_count
    offset = (lax.axis_index("tile") - 1) * blocks
    local_ids = jnp.mod(neighbours - offset + total_blocks, total_blocks)
    rounded = fields.astype(jnp.bfloat16).reshape(nodes_dev, columns)
    window = padded(rounded, (("tile", 0),), nodes_dev)
    first_pass = stencil(window, operators, local_ids, blocks, block_size, columns)
    products = first_pass.reshape(blocks, 3, block_size, nfield, levels)
    vel_blocks = velocity.reshape(blocks, block_size, 2, 1, levels)
    advect = vel_blocks[:, :, 0] * products[:, 0] + vel_blocks[:, :, 1] * products[:, 1]
    lap_round = products[:, 2].astype(jnp.bfloat16).reshape(nodes_dev, columns)
    window_two = padded(lap_round, (("tile", 0),), nodes_dev)
    lap_two = stencil(window_two, operators[:, 2:3], local_ids, blocks, block_size, columns)[:, 0]
    stepped = (
        fields
        - advect_step * advect.reshape(nodes_dev, nfield, levels)
        - hyper_rate * lap_two.reshape(nodes_dev, nfield, levels)
    )
    full_levels = levels * lax.axis_size("rad")
    derivative = cheb_matrix(full_levels)
    done = diffuse(
        lax.all_to_all(stepped, "rad", split_axis=0, concat_axis=2, tiled=True),
        derivative,
        kappa_ref,
    )
    diffused = lax.all_to_all(done, "rad", split_axis=2, concat_axis=0, tiled=True)
    flattened = diffused.reshape(nodes_dev, columns)
    weighted = quad_weight[:, None] * flattened
    modes = basis.shape[1]
    ratio = degree.astype(jnp.float32) / DEGMAX
    gain = (
        0.5
        * jnp.sqrt(jnp.float32(modes) / (nodes_dev * tile_count))
        * (1.0 - jnp.exp(-4.0 * ratio * ratio))
    )
    share = modes // tile_count
    chosen = basis
    owned = lax.psum_scatter(
        jnp.dot(chosen.T, weighted, precision=lax.Precision.HIGHEST),
        "tile",
        scatter_dimension=0,
        tiled=True,
    )
    my_gain = lax.dynamic_slice_in_dim(gain, lax.axis_index("tile") * share, share, 0)
    scaled = my_gain[:, None] * owned
    chosen = basis
    removed = jnp.dot(
        chosen, lax.all_gather(scaled, "tile", axis=0, tiled=True), precision=lax.Precision.HIGHEST
    )
    return (flattened - removed).reshape(nodes_dev, nfield, levels)


def solution(mesh):
    return jax.shard_map(
        body,
        mesh=mesh,
        in_specs=(
            P("tile", None, "rad"),
            P("tile", None, "rad"),
            P("tile", None, None, None),
            P("tile", None),
            P(),
            P("tile"),
            P("tile", None),
            P(),
        ),
        out_specs=P("tile", None, "rad"),
        check_vma=False,
    )
```

profile of v0, /device:TPU:0, one launch (start us, length us, event | category | flops | bytes accessed | tf_op | source)
XLA Modules:
  0.0 124.6 jit_solution(8102643564752901848)
XLA Ops:
  6.5 1.1 convert_element_type.31
  7.7 3.4 %collective-permute-start.1 = (bf16[384,128]{1,0:T(8,128)(2,1)S(1)}, bf16[384,128]{1,0:T(8,128)(2,1)S(1)}, u32[]{:S(2)}, u32[]{:S(2)}) collective-permute-start(bf16[384,128]{1,0:T(8,128)(2,1)S(1)} %bitcast.106), channel_id=1, source_target_pairs={{4,0},{8,4},{12,8},{16,12},{20,16},{24,20},{28,24},{0,28},{5,1},{9... | collective-permute-start | bytes 294920 | tf_op jit(solution)/shard_map/ppermute | solution.py:23
  11.1 0.7 compare_and_fusion
  11.9 1.5 %fusion.62 = (f32[3,128,1,1,128]{4,2,1,0,3:T(1,128)S(1)}, f32[3,128,1,1,128]{4,2,1,0,3:T(1,128)S(1)}) fusion(f32[3,128,2,1,128]{4,2,1,0,3:T(2,128)} %bitcast.105), kind=kLoop, calls=%fused_computation.91 | loop fusion | bytes 786432 | tf_op jit(solution)/shard_map/slice | solution.py:75
  13.4 2.6 %collective-permute-done = bf16[384,128]{1,0:T(8,128)(2,1)S(1)} collective-permute-done((bf16[384,128]{1,0:T(8,128)(2,1)S(1)}, bf16[384,128]{1,0:T(8,128)(2,1)S(1)}, u32[]{:S(2)}, u32[]{:S(2)}) %collective-permute-start) | collective-permute-done | bytes 98336 | tf_op jit(solution)/shard_map/ppermute | solution.py:20
  16.1 0.7 gather_fusion
  16.9 2.3 %convolution_bitcast_fusion = f32[3,3,128,1,128]{4,2,1,0,3:T(8,128)S(1)} fusion(bf16[3,896,128,1]{2,1,3,0:T(8,128)(2,1)S(1)} %bitcast.95, bf16[3,3,128,896]{3,2,1,0:T(8,128)(2,1)} %param.12), kind=kOutput, calls=%fused_computation.11 | convolution fusion | flops 264241152 | bytes 3342336 | tf_op jit(solution)/shard_map/bkij,bjc->bkic/dot_general | solution.py:50
  19.8 2.5 %collective-permute-done.3 = bf16[384,128]{1,0:T(8,128)(2,1)S(1)} collective-permute-done((bf16[384,128]{1,0:T(8,128)(2,1)S(1)}, bf16[384,128]{1,0:T(8,128)(2,1)S(1)}, u32[]{:S(2)}, u32[]{:S(2)}) %collective-permute-start.3) | collective-permute-done | bytes 98336 | tf_op jit(solution)/shard_map/ppermute | solution.py:23
  22.2 2.1 %collective-permute-done.2 = bf16[384,128]{1,0:T(8,128)(2,1)S(1)} collective-permute-done((bf16[384,128]{1,0:T(8,128)(2,1)S(1)}, bf16[384,128]{1,0:T(8,128)(2,1)S(1)}, u32[]{:S(2)}, u32[]{:S(2)}) %collective-permute-start.2) | collective-permute-done | bytes 98336 | tf_op jit(solution)/shard_map/ppermute | solution.py:20
  24.4 0.7 gather_fusion.1
  25.2 1.4 %convolution_multiply_fusion = f32[3,128,128]{1,2,0:T(8,128)S(1)} fusion(bf16[3,896,128]{2,1,0:T(8,128)(2,1)S(1)} %bitcast.104, bf16[3,3,128,896]{3,2,1,0:T(8,128)(2,1)} %param.12), kind=kOutput, calls=%fused_computation.13 | convolution fusion | flops 88129536 | bytes 1572864 | tf_op jit(solution)/shard_map/bkij,bjc->bkic/dot_general | solution.py:50
  26.6 1.2 %fusion.37 = f32[384,1,128]{2,1,0:T(1,128)} fusion(f32[384,1,128]{2,1,0:T(1,128)S(1)} %bitcast.114, f32[384,1,128]{2,1,0:T(1,128)S(1)} %copy-done.1, f32[384,1,128]{2,1,0:T(1,128)S(1)} %bitcast.103, f32[3,128,1,1,128]{4,2,1,0,3:T(1,128)S(1)} %get-tuple-element.11, f32[384,1,128]{2,1,0:T(1,128)S(1)} %bitcast.102, f32[3,128,1,1,128]{4,2,1,0,3:T(1,128)S(1)} %get-tuple-element.10), kind=kLoop, calls=%fused_computation.55 | loop fusion | flops 294912 | bytes 1376256 | tf_op jit(solution)/shard_map/sub | solution.py:80
  27.9 4.9 %all-to-all-start = ((f32[384,1,128]{2,1,0:T(1,128)}), f32[384,1,128]{2,1,0:T(1,128)S(1)}, u32[]{:S(2)}, u32[]{:S(2)}) async-start(f32[384,1,128]{2,1,0:T(1,128)} %fusion.37), calls=%async_computation | async-start | bytes 393216 | tf_op jit(solution)/shard_map/all_to_all | solution.py:87
  32.8 8.5 %fusion.26 = f32[512]{0:T(512)S(1)} fusion(f32[512]{0:T(512)S(1)} %get-tuple-element.12, f32[512]{0:T(512)S(1)} %fusion.41), kind=kLoop, calls=%fused_computation.38 | loop fusion | flops 7077376 | bytes 6144 | tf_op jit(solution)/shard_map/reduce_sum | solution.py:42
  41.4 8.5 %convolution_multiply_fusion.2 = f32[96,512]{1,0:T(8,128)S(1)} fusion(f32[512]{0:T(512)S(1)} %neg.7, f32[512]{0:T(512)S(1)} %get-tuple-element.12, f32[512]{0:T(512)S(1)} %fusion.41, f32[512]{0:T(512)S(1)} %get-tuple-element.13, f32[12,8,4,128]{3,2,1,0:T(4,128)S(1)} %bitcast.112, f32[512]{0:T(512)S(1)} %copy-done.4), kind=kOutput, calls=%fused_computation.20 | convolution fusion | flops 310050816 | bytes 403456 | tf_op jit(solution)/shard_map/nfj,ij->nfi/dot_general | solution.py:54
  50.0 8.7 %fusion.7 = f32[96,1,512]{2,0,1:T(8,128)S(1)} fusion(f32[96,512]{1,0:T(8,128)S(1)} %convolution_multiply_fusion.2, f32[512]{0:T(512)S(1)} %neg.7, f32[512]{0:T(512)S(1)} %get-tuple-element.12, f32[512]{0:T(512)S(1)} %fusion.41, f32[512]{0:T(512)S(1)} %get-tuple-element.13, f32[12,8,4,128]{3,2,1,0:T(4,128)S(1)} %bitcast.113), kind=kOutput, calls=%fused_computation.19 | convolution fusion | flops 309952512 | bytes 598016 | tf_op jit(solution)/shard_map/nfj,ij->nfi/dot_general | solution.py:56
  58.8 12.0 %all_to_all.33 = f32[96,1,512]{0,1,2:T(1,128)S(1)} all-to-all(f32[96,1,512]{0,1,2:T(1,128)S(1)} %copy.69), channel_id=1, replica_groups=mesh['tile'=8,'rad'=4] {'rad'}, dimensions={2} | all-to-all | bytes 393216 | tf_op jit(solution)/shard_map/all_to_all | solution.py:91
  71.2 0.7 convolution_bitcast_fusion.1
  71.9 0.8 copy.76
  73.0 32.7 %reduce-scatter.4.cloned.1.call-done = f32[64,128]{1,0:T(8,128)} async-done(((f32[512,128]{1,0:T(8,128)}), f32[64,128]{1,0:T(8,128)}) %reduce-scatter.4.cloned.1.call-update) | async-done | bytes 32784 | tf_op jit(solution)/shard_map/reduce_scatter | solution.py:103
  105.7 0.8 broadcast_multiply_fusion
  106.6 9.3 %all_gather.3 = f32[512,128]{1,0:T(8,128)S(1)} all-gather(f32[64,128]{1,0:T(8,128)S(1)} %broadcast_multiply_fusion), channel_id=1, replica_groups=mesh['tile'=8,'rad'=4] {'tile'}, dimensions={0}, use_global_device_ids=true | all-gather | bytes 294912 | tf_op jit(solution)/shard_map/all_gather | solution.py:113
  115.8 1.1 fusion.5
  116.9 0.8 copy.74
  (36 shorter events, 1.9 us)
Async XLA Ops:
  6.5 64.6 %copy-start = (f32[384,512]{1,0:T(8,128)S(1)}, f32[384,512]{1,0:T(8,128)}, u32[]{:S(2)}) copy-start(f32[384,512]{1,0:T(8,128)} %param.16) | copy-start | bytes 2359300
  7.7 5.7 %collective-permute-start.1 = (bf16[384,128]{1,0:T(8,128)(2,1)S(1)}, bf16[384,128]{1,0:T(8,128)(2,1)S(1)}, u32[]{:S(2)}, u32[]{:S(2)}) collective-permute-start(bf16[384,128]{1,0:T(8,128)(2,1)S(1)} %bitcast.106), channel_id=1, source_target_pairs={{4,0},{8,4},{12,8},{16,12},{20,16},{24,20},{28,24},{0,28},{5,1},{9... | collective-permute-start | bytes 294920 | tf_op jit(solution)/shard_map/ppermute | solution.py:23
  11.1 4.9 %collective-permute-start = (bf16[384,128]{1,0:T(8,128)(2,1)S(1)}, bf16[384,128]{1,0:T(8,128)(2,1)S(1)}, u32[]{:S(2)}, u32[]{:S(2)}) collective-permute-start(bf16[384,128]{1,0:T(8,128)(2,1)S(1)} %bitcast.107), channel_id=1, source_target_pairs={{0,4},{4,8},{8,12},{12,16},{16,20},{20,24},{24,28},{28,0},{1,5},{5... | collective-permute-start | bytes 294920 | tf_op jit(solution)/shard_map/ppermute | solution.py:20
  19.2 3.1 %collective-permute-start.3 = (bf16[384,128]{1,0:T(8,128)(2,1)S(1)}, bf16[384,128]{1,0:T(8,128)(2,1)S(1)}, u32[]{:S(2)}, u32[]{:S(2)}) collective-permute-start(bf16[384,128]{1,0:T(8,128)(2,1)S(1)} %bitcast.109), channel_id=1, source_target_pairs={{4,0},{8,4},{12,8},{16,12},{20,16},{24,20},{28,24},{0,28},{5,1},{9... | collective-permute-start | bytes 294920 | tf_op jit(solution)/shard_map/ppermute | solution.py:23
  19.4 4.9 %collective-permute-start.2 = (bf16[384,128]{1,0:T(8,128)(2,1)S(1)}, bf16[384,128]{1,0:T(8,128)(2,1)S(1)}, u32[]{:S(2)}, u32[]{:S(2)}) collective-permute-start(bf16[384,128]{1,0:T(8,128)(2,1)S(1)} %bitcast.110), channel_id=1, source_target_pairs={{0,4},{4,8},{8,12},{12,16},{16,20},{20,24},{24,28},{28,0},{1,5},{5... | collective-permute-start | bytes 294920 | tf_op jit(solution)/shard_map/ppermute | solution.py:20
  24.3 2.3 %copy-start.1 = (f32[384,1,128]{2,1,0:T(1,128)S(1)}, f32[384,1,128]{2,1,0:T(1,128)}, u32[]{:S(2)}) copy-start(f32[384,1,128]{2,1,0:T(1,128)} %param.10) | copy-start | bytes 589828
  25.2 16.3 %copy-start.4 = (f32[512]{0:T(512)S(1)}, f32[512]{0:T(512)}, u32[]{:S(2)}) copy-start(f32[512]{0:T(512)} %param.14) | copy-start | bytes 6148
  27.9 13.4 %all-to-all-start = ((f32[384,1,128]{2,1,0:T(1,128)}), f32[384,1,128]{2,1,0:T(1,128)S(1)}, u32[]{:S(2)}, u32[]{:S(2)}) async-start(f32[384,1,128]{2,1,0:T(1,128)} %fusion.37), calls=%async_computation | async-start | bytes 393216 | tf_op jit(solution)/shard_map/all_to_all | solution.py:87
  32.8 73.0 %reduce-scatter.4.cloned.1.call-start = ((), (), s32[]{:S(2)}) async-start(), calls=%async_computation.3 | async-start | bytes 294912 | tf_op jit(solution)/shard_map/reduce_scatter | solution.py:103
  50.0 21.2 %copy-start.2 = (f32[384]{0:T(512)S(1)}, f32[384]{0:T(512)}, u32[]{:S(2)}) copy-start(f32[384]{0:T(512)} %param.15) | copy-start | bytes 4612
  58.7 14.1 %copy-start.3 = (s32[512]{0:T(512)S(1)}, s32[512]{0:T(512)}, u32[]{:S(2)}) copy-start(s32[512]{0:T(512)} %param.17) | copy-start | bytes 6148
Sparse Core Ops, SparseCore 0:
  72.9 32.7 reduce-scatter.3
where the time goes:
time: 125 us
  waiting for transfers between devices  39.9 us (32%)
  matrix products  22.7 us (18%)
  blocking collectives  21.3 us (17%)
  between operations  13.7 us (11%)
  other arithmetic  12.8 us (10%)
  starting transfers between devices  8.82 us (7%)
  local copies, waits for them, and re-layouts  5.4 us (4%)
    reduce_scatter x1, waiting for transfers between devices, body(): lax.psum_scatter(jnp.dot(chosen.T, weighted, precision=lax.Precision.HIGH...  32.7 us
    all_to_all x1, blocking collectives, body(): lax.all_to_all(done, 'rad', split_axis=2, concat_axis=0, tiled=True)  12 us
    all_gather x1, blocking collectives, body(): lax.all_gather(scaled, 'tile', axis=0, tiled=True)  9.26 us
    dot_general x1, matrix products, diffuse(): jnp.einsum('nfj,ij->nfi', fluxes, derivative, precision=lax.Precision.HIG...  8.72 us
    dot_general x1, matrix products, diffuse(): jnp.einsum('nfj,ij->nfi', stepped, derivative, precision=lax.Precision.HI...  8.5 us
    reduce_sum x1, other arithmetic, cheb_matrix(): diagonal = -jnp.sum(entries, axis=1)  8.5 us
    all_to_all x1, starting transfers between devices, body(): lax.all_to_all(stepped, 'rad', split_axis=0, concat_axis=2, tiled=True)  4.87 us
    ppermute x2, waiting for transfers between devices, padded(): lax.ppermute(lax.slice_in_dim(block, block.shape[dim] - width, None, axis...  4.7 us
  transfers between devices with their start and end apart: 6, of which 4 were waited for; matrix products, arithmetic and copies ran while one was open for 9% of the time, Pallas kernels for 0%

commit v1 on v0

v1 whole, which is shorter than its diff:
```python
import jax
import jax.numpy as jnp
import numpy as np
from jax import lax
from jax.experimental import pallas as pl
from jax.experimental.pallas import tpu as pltpu
from jax.sharding import PartitionSpec as P

DEGMAX = 22

advect_step = 0.25
hyper_rate = 0.1
radial_step = 0.25

BF = jnp.bfloat16
F32 = jnp.float32
VMEM = pl.BlockSpec(memory_space=pltpu.VMEM)
SMEM = pl.BlockSpec(memory_space=pltpu.SMEM)
PARAMS = pltpu.CompilerParams(vmem_limit_bytes=32 * 1024 * 1024)


def cheb_matrix(count):
    points = np.arange(count)
    angles = np.pi * points / (count - 1)
    upper, lower = angles[:, None], angles[None, :]
    spacing = -2.0 * np.sin((upper + lower) / 2.0) * np.sin((upper - lower) / 2.0)
    np.fill_diagonal(spacing, 1.0)
    weights = np.where((points == 0) | (points == count - 1), 2.0, 1.0)
    parity = np.where((upper * 0 + points[:, None] + points[None, :]) % 2 == 0, 1.0, -1.0)
    entries = weights[:, None] / weights[None, :] * parity / spacing
    np.fill_diagonal(entries, 0.0)
    matrix = entries - np.diag(entries.sum(axis=1))
    return (np.sin(angles)[:, None] * matrix / count).T.astype(np.float32)


def split(value):
    high = value.astype(BF)
    return high, (value - high.astype(F32)).astype(BF)


def dot(left, right):
    return jnp.dot(left, right, preferred_element_type=F32)


def dot3(left, right):
    return dot(left[0], right[0]) + (dot(left[0], right[1]) + dot(left[1], right[0]))


def call(kernel, outs, args, smem=0, scratch=()):
    return pl.pallas_call(
        kernel,
        out_shape=outs,
        in_specs=[SMEM] * smem + [VMEM] * (len(args) - smem),
        out_specs=jax.tree.map(lambda _: VMEM, outs),
        scratch_shapes=list(scratch),
        compiler_params=PARAMS,
    )(*args)


def shape(dims, kind):
    return jax.ShapeDtypeStruct(dims, kind)


def fill_window(window, low, own, high):
    rows = own.shape[0]
    window[0:rows] = low[...]
    window[rows : 2 * rows] = own[...]
    window[2 * rows : 3 * rows] = high[...]


def nearby(window, ids, b, block_size, near):
    parts = []
    for k in range(near):
        start = pl.multiple_of(ids[b, k] * block_size, block_size)
        parts.append(window[pl.ds(start, block_size), :])
    return jnp.concatenate(parts, axis=0)


def first_lap_kernel(ids, low, own, high, ops, lap, window):
    blocks, _, size, wide = ops.shape
    fill_window(window, low, own, high)
    for b in range(blocks):
        around = nearby(window, ids, b, size, wide // size)
        lap[b * size : (b + 1) * size] = dot(ops[b, 2], around).astype(BF)


def advect_kernel(ids, low, own, high, ops, fields, velocity, out, window):
    blocks, _, size, wide = ops.shape
    fill_window(window, low, own, high)
    for b in range(blocks):
        around = nearby(window, ids, b, size, wide // size)
        grad = dot(ops[b, 0:2].reshape(2 * size, wide), around)
        vel_x = velocity[pl.ds(2 * b * size, size, stride=2), :]
        vel_y = velocity[pl.ds(2 * b * size + 1, size, stride=2), :]
        rows = slice(b * size, (b + 1) * size)
        out[rows] = fields[rows] - advect_step * (vel_x * grad[:size] + vel_y * grad[size:])


def second_lap_kernel(ids, low, own, high, ops, part, stepped, narrow, window):
    blocks, _, size, wide = ops.shape
    fill_window(window, low, own, high)
    for b in range(blocks):
        around = nearby(window, ids, b, size, wide // size)
        rows = slice(b * size, (b + 1) * size)
        value = part[rows] - hyper_rate * dot(ops[b, 2], around)
        stepped[rows] = value
        narrow[rows] = value.astype(BF)


def prepare_kernel(basis, weight, gain, wbt_high, wbt_low, bg_high, bg_low):
    half = basis.shape[1] // 2
    high, low = split((basis[...] * weight[...]).T)
    wbt_high[...] = high
    wbt_low[...] = low
    for c in range(2):
        cols = slice(c * half, (c + 1) * half)
        high, low = split(basis[:, cols] * gain[:, cols])
        bg_high[c] = high
        bg_low[c] = low


def diffuse_kernel(count, place, *refs):
    shards = refs[:count]
    stepped, dh_high, dh_low, kappa, wbt_high, wbt_low, diffused, keep, send, levels = refs[count:]
    rad, core = place[0], place[1]
    nodes = stepped.shape[0]
    for d in range(count):
        levels[lax.rem(rad + count - d, count)] = shards[d][...]
    full_high = jnp.concatenate([dh_high[c] for c in range(count)], axis=1)
    full_low = jnp.concatenate([dh_low[c] for c in range(count)], axis=1)
    own = (dh_high[rad], dh_low[rad])
    step = nodes // 3
    for start in range(0, nodes, step):
        rows = slice(start, start + step)
        value = jnp.concatenate([levels[c, rows] for c in range(count)], axis=1)
        slopes = dot(value, full_high) + dot(value, full_low)
        fluxes = kappa[...] * (1.0 + 0.5 * jnp.tanh(value.astype(F32))) * slopes
        diffused[rows] = stepped[rows] + radial_step * dot3(split(fluxes), own)
    parts = split(diffused[...])
    half = keep.shape[0]
    for out, which in ((send, 1 - core), (keep, core)):
        rows = pl.ds(pl.multiple_of(which * half, half), half)
        out[...] = dot3((wbt_high[rows, :], wbt_low[rows, :]), parts)


def filter_kernel(place, diffused, mine, other, bg_high, bg_low, out):
    core = place[1]
    removed = dot3((bg_high[core], bg_low[core]), split(mine[...]))
    removed += dot3((bg_high[1 - core], bg_low[1 - core]), split(other[...]))
    out[...] = diffused[...] - removed


def shift(axis, by):
    count = lax.axis_size(axis)
    return [(i, (i + by) % count) for i in range(count)]


def halo(block):
    return lax.ppermute(block, "tile", shift("tile", 1)), lax.ppermute(block, "tile", shift("tile", -1))


def tile_sum(keep, send):
    count = lax.axis_size("tile")
    swap = [(i, i ^ 1) for i in range(count)]
    bits = [1 << k for k in range(1, count.bit_length() - 1)]
    mine = keep + lax.ppermute(send, "tile", swap)
    for k in range(len(bits)):
        pairs = [(i, i ^ bits[(k + i % 2) % len(bits)]) for i in range(count)]
        mine = mine + lax.ppermute(mine, "tile", pairs)
    return mine, lax.ppermute(mine, "tile", swap)


def body(fields, velocity, operators, neighbours, kappa_ref, quad_weight, basis, degree):
    nodes, nfield, levels = fields.shape
    blocks, _, size, _ = operators.shape
    modes = basis.shape[1]
    tiles, rads = lax.axis_size("tile"), lax.axis_size("rad")
    tile, rad = lax.axis_index("tile"), lax.axis_index("rad")
    fields = fields.reshape(nodes, levels)
    velocity = velocity.reshape(2 * nodes, levels)
    total = blocks * tiles
    ids = jnp.mod(neighbours - (tile - 1) * blocks + total, total)
    place = jnp.stack([rad, tile % 2])
    window = pltpu.VMEM((3 * nodes, levels), BF)

    ratio = degree.astype(F32) / DEGMAX
    gain = 0.5 * jnp.sqrt(F32(modes) / (nodes * tiles)) * (1.0 - jnp.exp(-4.0 * ratio * ratio))
    wbt_high, wbt_low, bg_high, bg_low = call(
        prepare_kernel,
        (shape((modes, nodes), BF),) * 2 + (shape((2, nodes, modes // 2), BF),) * 2,
        (basis, quad_weight[:, None], gain[None, :]),
    )
    dhat = cheb_matrix(rads * levels)
    dhat = np.stack([dhat[:, c * levels : (c + 1) * levels] for c in range(rads)])
    dh_high = dhat.astype(BF)
    dh_low = (dhat - dh_high.astype(np.float32)).astype(BF)

    rounded = fields.astype(BF)
    low, high = halo(rounded)
    lap = call(first_lap_kernel, shape((nodes, levels), BF), (ids, low, rounded, high, operators), 1, (window,))
    low_two, high_two = halo(lap)
    part = call(
        advect_kernel, shape((nodes, levels), F32), (ids, low, rounded, high, operators, fields, velocity), 1, (window,)
    )
    stepped, narrow = call(
        second_lap_kernel,
        (shape((nodes, levels), F32), shape((nodes, levels), BF)),
        (ids, low_two, lap, high_two, operators, part),
        1,
        (window,),
    )
    shards = [narrow] + [lax.ppermute(narrow, "rad", shift("rad", d)) for d in range(1, rads)]
    diffused, keep, send = call(
        lambda *refs: diffuse_kernel(rads, *refs),
        (shape((nodes, levels), F32),) + (shape((modes // 2, levels), F32),) * 2,
        (place, *shards, stepped, jnp.asarray(dh_high), jnp.asarray(dh_low), kappa_ref[None, :], wbt_high, wbt_low),
        1,
        (pltpu.VMEM((rads, nodes, levels), BF),),
    )
    mine, other = tile_sum(keep, send)
    filtered = call(
        filter_kernel, shape((nodes, levels), F32), (place, diffused, mine, other, bg_high, bg_low), 1
    )
    return filtered.reshape(nodes, nfield, levels)


def solution(mesh):
    return jax.shard_map(
        body,
        mesh=mesh,
        in_specs=(
            P("tile", None, "rad"),
            P("tile", None, "rad"),
            P("tile", None, None, None),
            P("tile", None),
            P(),
            P("tile"),
            P("tile", None),
            P(),
        ),
        out_specs=P("tile", None, "rad"),
        check_vma=False,
    )
```

time: 125 us -> 47.2 us (0.38)
  matrix products: 22.7 us -> 0 us
  blocking collectives: 21.3 us -> 0 us
  waiting for transfers between devices: 39.9 us -> 22.6 us
  between operations: 13.7 us -> 0.18 us
  other arithmetic: 12.8 us -> 1.83 us
  Pallas kernels: 0 us -> 7.46 us
  starting transfers between devices: 8.82 us -> 12 us
  local copies, waits for them, and re-layouts: 5.4 us -> 2.85 us
    reduce_scatter x1 -> x0, waiting for transfers between devices: 32.7 us -> none  [body(): lax.psum_scatter(jnp.dot(chosen.T, weighted, precision=lax.Precision.HIGH...]
    dot_general x6 -> x0, matrix products: 22.7 us -> none  [the longest x1 8.72 us: diffuse(): jnp.einsum('nfj,ij->nfi', fluxes, derivative, precision=lax.Precision.HIG...]
    ppermute x4 -> x11, waiting for transfers between devices: 7.17 us -> 22.6 us  [the longest x2 7.29 us: tile_sum(): mine = mine + lax.ppermute(mine, 'tile', pairs)]
    all_to_all x1 -> x0, blocking collectives: 12 us -> none  [body(): lax.all_to_all(done, 'rad', split_axis=2, concat_axis=0, tiled=True)]
    all_gather x1 -> x0, blocking collectives: 9.26 us -> none  [body(): lax.all_gather(scaled, 'tile', axis=0, tiled=True)]
    reduce_sum x1 -> x0, other arithmetic: 8.5 us -> none  [cheb_matrix(): diagonal = -jnp.sum(entries, axis=1)]
    ppermute x4 -> x11, starting transfers between devices: 3.95 us -> 12 us  [the longest x3 4.67 us: body(): lax.ppermute(narrow, 'rad', shift('rad', d))]
    pallas_call x0 -> x6, Pallas kernels: none -> 7.46 us  [call(): pl.pallas_call(kernel, out_shape=outs, in_specs=[SMEM] * smem + [VMEM] *...]
  transfers between devices with their start and end apart: 6 -> 11, of which waited for: 4 -> 9; matrix products, arithmetic and copies ran while one was open for 9% -> 2% of each run, Pallas kernels for 0% -> 3%
where the time goes in v1:
time: 47.2 us; the launch traced here: 46.9 us
  waiting for transfers between devices  22.6 us (48%)
  starting transfers between devices  12 us (25%)
  Pallas kernels  7.46 us (16%)
  local copies, waits for them, and re-layouts  2.85 us (6%)
  other arithmetic  1.83 us (4%)
    pallas_call x6, Pallas kernels, call(): pl.pallas_call(kernel, out_shape=outs, in_specs=[SMEM] * smem + [VMEM] *...  7.46 us
    ppermute x2, waiting for transfers between devices, tile_sum(): mine = mine + lax.ppermute(mine, 'tile', pairs)  7.29 us
    ppermute x3, waiting for transfers between devices, body(): lax.ppermute(narrow, 'rad', shift('rad', d))  6.8 us
    ppermute x3, starting transfers between devices, body(): lax.ppermute(narrow, 'rad', shift('rad', d))  4.67 us
    ppermute x2, waiting for transfers between devices, halo(): lax.ppermute(block, 'tile', shift('tile', 1))  4.23 us
    ppermute x2, starting transfers between devices, halo(): lax.ppermute(block, 'tile', shift('tile', -1))  3.59 us
    ppermute x2, starting transfers between devices, tile_sum(): mine = mine + lax.ppermute(mine, 'tile', pairs)  3.27 us
    unnamed x20, local copies, waits for them, and re-layouts  2.75 us
  transfers between devices with their start and end apart: 11, of which 9 were waited for; matrix products, arithmetic and copies ran while one was open for 2% of the time, Pallas kernels for 3%

profile of v1, /device:TPU:0, one launch (start us, length us, event | category | flops | bytes accessed | tf_op | source)
XLA Modules:
  0.0 46.9 jit_solution(12626468257861982916)
XLA Ops:
  0.0 1.0 %convert_element_type.6.own = bf16[384,128]{1,0:T(8,128)(2,1)S(1)} convert(f32[384,128]{1,0:T(8,128)} %bitcast.9) | non-fusion elementwise | flops 49152 | bytes 294912 | tf_op jit(solution)/shard_map/convert_element_type | solution.py:198
  1.0 3.4 %collective-permute-start.1 = (bf16[384,128]{1,0:T(8,128)(2,1)S(1)}, bf16[384,128]{1,0:T(8,128)(2,1)S(1)}, u32[]{:S(2)}, u32[]{:S(2)}) collective-permute-start(bf16[384,128]{1,0:T(8,128)(2,1)S(1)} %convert_element_type.6.own), channel_id=1, source_target_pairs={{0,28},{4,0},{8,4},{12,8},{16,12},{20,16},{24,20},{28,24},{1,29},{... | collective-permute-start | bytes 294920 | tf_op jit(solution)/shard_map/ppermute | solution.py:159
  4.4 0.7 %add_select_fusion.ids = s32[3,7]{1,0:T(4,128)S(1)} fusion(s32[3,7]{1,0:T(4,128)} %param.13, s32[]{:T(128)S(6)} %mul.18), kind=kLoop, calls=%fused_computation | loop fusion | flops 168 | bytes 172 | tf_op jit(solution)/shard_map/jit(remainder)/select_n | solution.py:182
  5.1 1.6 %collective-permute-done.1.high = bf16[384,128]{1,0:T(8,128)(2,1)S(1)} collective-permute-done((bf16[384,128]{1,0:T(8,128)(2,1)S(1)}, bf16[384,128]{1,0:T(8,128)(2,1)S(1)}, u32[]{:S(2)}, u32[]{:S(2)}) %collective-permute-start.1) | collective-permute-done | bytes 98336 | tf_op jit(solution)/shard_map/ppermute | solution.py:159
  6.7 2.7 %collective-permute-done.low = bf16[384,128]{1,0:T(8,128)(2,1)S(1)} collective-permute-done((bf16[384,128]{1,0:T(8,128)(2,1)S(1)}, bf16[384,128]{1,0:T(8,128)(2,1)S(1)}, u32[]{:S(2)}, u32[]{:S(2)}) %collective-permute-start) | collective-permute-done | bytes 98336 | tf_op jit(solution)/shard_map/ppermute | solution.py:159
  9.3 1.6 %copy-done = bf16[3,3,128,896]{3,2,1,0:T(8,128)(2,1)S(1)} copy-done((bf16[3,3,128,896]{3,2,1,0:T(8,128)(2,1)S(1)}, bf16[3,3,128,896]{3,2,1,0:T(8,128)(2,1)}, u32[]{:S(2)}) %copy-start) | copy-done | bytes 2064408
  10.9 0.9 %shard_map.100.own = bf16[384,128]{1,0:T(8,128)(2,1)S(1)} custom-call(s32[3,7]{1,0:T(4,128)S(1)} %add_select_fusion.ids, bf16[384,128]{1,0:T(8,128)(2,1)S(1)} %collective-permute-done.low, bf16[384,128]{1,0:T(8,128)(2,1)S(1)} %convert_element_type.6.own, bf16[384,128]{1,0:T(8,128)(2,1)S(1)} %collective-permute-done.1.high, bf16[3,3,128,896]{3,2,1,0:T(8,128)(2,1)S(1)} %copy-done), custom_call_target="tpu_custom_call" | custom-call | tf_op jit(solution)/shard_map/pallas_call | solution.py:50
  12.6 1.1 %copy-done.2 = f32[384,512]{1,0:T(8,128)S(1)} copy-done((f32[384,512]{1,0:T(8,128)S(1)}, f32[384,512]{1,0:T(8,128)}, u32[]{:S(2)}) %copy-start.2) | copy-done | bytes 786456
  13.7 0.5 %shard_map.103 = (bf16[512,384]{1,0:T(8,128)(2,1)S(1)}, bf16[512,384]{1,0:T(8,128)(2,1)S(1)}, bf16[2,384,256]{2,1,0:T(8,128)(2,1)S(1)}, bf16[2,384,256]{2,1,0:T(8,128)(2,1)S(1)}) custom-call(f32[384,512]{1,0:T(8,128)S(1)} %copy-done.2, f32[384,1]{1,0:T(8,128)S(1)} %broadcast_in_dim.12.weight, f32[1,512]{1,0:T(1,128)S(1)} %bitcast.12), custom_call_target="tpu_custom_call" | custom-call | tf_op jit(solution)/shard_map/pallas_call | solution.py:50
  14.3 1.1 %shard_map.101.part = f32[384,128]{1,0:T(8,128)S(1)} custom-call(s32[3,7]{1,0:T(4,128)S(1)} %add_select_fusion.ids, bf16[384,128]{1,0:T(8,128)(2,1)S(1)} %collective-permute-done.low, bf16[384,128]{1,0:T(8,128)(2,1)S(1)} %convert_element_type.6.own, bf16[384,128]{1,0:T(8,128)(2,1)S(1)} %collective-permute-done.1.high, ...), custom_call_target="tpu_custom_call" | custom-call | tf_op jit(solution)/shard_map/pallas_call | solution.py:50
  15.4 1.6 %collective-permute-done.2.low = bf16[384,128]{1,0:T(8,128)(2,1)S(1)} collective-permute-done((bf16[384,128]{1,0:T(8,128)(2,1)S(1)}, bf16[384,128]{1,0:T(8,128)(2,1)S(1)}, u32[]{:S(2)}, u32[]{:S(2)}) %collective-permute-start.2) | collective-permute-done | bytes 98336 | tf_op jit(solution)/shard_map/ppermute | solution.py:159
  17.0 0.9 %shard_map.102 = (f32[384,128]{1,0:T(8,128)S(1)}, bf16[384,128]{1,0:T(8,128)(2,1)S(1)}) custom-call(s32[3,7]{1,0:T(4,128)S(1)} %add_select_fusion.ids, bf16[384,128]{1,0:T(8,128)(2,1)S(1)} %collective-permute-done.2.low, bf16[384,128]{1,0:T(8,128)(2,1)S(1)} %shard_map.100.own, bf16[384,128]{1,0:T(8,128)(2,1)S(1)} %collective-permute-done.3.high, ...), custom_call_target="tpu_custom_call" | custom-call | tf_op jit(solution)/shard_map/pallas_call | solution.py:50
  17.9 3.7 %collective-permute-start.6 = (bf16[384,128]{1,0:T(8,128)(2,1)S(1)}, bf16[384,128]{1,0:T(8,128)(2,1)S(1)}, u32[]{:S(2)}, u32[]{:S(2)}) collective-permute-start(bf16[384,128]{1,0:T(8,128)(2,1)S(1)} %get-tuple-element.14.refs_1_), channel_id=1, source_target_pairs={{0,3},{1,0},{2,1},{3,2},{4,7},{5,4},{6,5},{7,6},{8,11},{9,8},{10,9... | collective-permute-start | bytes 294920 | tf_op jit(solution)/shard_map/ppermute | solution.py:212
  21.6 1.0 %collective-permute-start.4 = (bf16[384,128]{1,0:T(8,128)(2,1)S(1)}, bf16[384,128]{1,0:T(8,128)(2,1)S(1)}, u32[]{:S(2)}, u32[]{:S(2)}) collective-permute-start(bf16[384,128]{1,0:T(8,128)(2,1)S(1)} %get-tuple-element.14.refs_1_), channel_id=1, source_target_pairs={{0,1},{1,2},{2,3},{3,0},{4,5},{5,6},{6,7},{7,4},{8,9},{9,10},{10,1... | collective-permute-start | bytes 294920 | tf_op jit(solution)/shard_map/ppermute | solution.py:212
  22.7 1.7 %collective-permute-done.6.refs_4_ = bf16[384,128]{1,0:T(8,128)(2,1)S(1)} collective-permute-done((bf16[384,128]{1,0:T(8,128)(2,1)S(1)}, bf16[384,128]{1,0:T(8,128)(2,1)S(1)}, u32[]{:S(2)}, u32[]{:S(2)}) %collective-permute-start.6) | collective-permute-done | bytes 98336 | tf_op jit(solution)/shard_map/ppermute | solution.py:212
  24.4 5.1 %collective-permute-done.5.refs_3_ = bf16[384,128]{1,0:T(8,128)(2,1)S(1)} collective-permute-done((bf16[384,128]{1,0:T(8,128)(2,1)S(1)}, bf16[384,128]{1,0:T(8,128)(2,1)S(1)}, u32[]{:S(2)}, u32[]{:S(2)}) %collective-permute-start.5) | collective-permute-done | bytes 98336 | tf_op jit(solution)/shard_map/ppermute | solution.py:212
  29.5 2.3 %shard_map.104 = (f32[384,128]{1,0:T(8,128)S(1)}, f32[256,128]{1,0:T(8,128)S(1)}, f32[256,128]{1,0:T(8,128)S(1)}) custom-call(s32[2]{0:T(128)S(1)} %pad_add_fusion.refs_0_.place, bf16[384,128]{1,0:T(8,128)(2,1)S(1)} %get-tuple-element.14.refs_1_, bf16[384,128]{1,0:T(8,128)(2,1)S(1)} %collective-permute-done.4.refs_2_, ...), custom_call_target="tpu_custom_call" | custom-call | tf_op jit(solution)/shard_map/pallas_call | solution.py:50
  31.9 1.3 %collective-permute-done.7 = f32[256,128]{1,0:T(8,128)S(1)} collective-permute-done((f32[256,128]{1,0:T(8,128)S(1)}, f32[256,128]{1,0:T(8,128)S(1)}, u32[]{:S(2)}, u32[]{:S(2)}) %collective-permute-start.7) | collective-permute-done | bytes 131104 | tf_op jit(solution)/shard_map/ppermute | solution.py:166
  33.2 2.6 %collective-permute-start.8 = (f32[256,128]{1,0:T(8,128)S(1)}, f32[256,128]{1,0:T(8,128)S(1)}, u32[]{:S(2)}, u32[]{:S(2)}) collective-permute-start(f32[256,128]{1,0:T(8,128)S(1)} %add.26), channel_id=1, source_target_pairs={{0,8},{4,20},{8,0},{12,28},{16,24},{20,4},{24,16},{28,12},{1,9},{5... | collective-permute-start | bytes 393224 | tf_op jit(solution)/shard_map/ppermute | solution.py:169
  35.8 2.9 %collective-permute-done.8 = f32[256,128]{1,0:T(8,128)S(1)} collective-permute-done((f32[256,128]{1,0:T(8,128)S(1)}, f32[256,128]{1,0:T(8,128)S(1)}, u32[]{:S(2)}, u32[]{:S(2)}) %collective-permute-start.8) | collective-permute-done | bytes 131104 | tf_op jit(solution)/shard_map/ppermute | solution.py:169
  38.8 0.7 %collective-permute-start.9 = (f32[256,128]{1,0:T(8,128)S(1)}, f32[256,128]{1,0:T(8,128)S(1)}, u32[]{:S(2)}, u32[]{:S(2)}) collective-permute-start(f32[256,128]{1,0:T(8,128)S(1)} %add.27), channel_id=1, source_target_pairs={{0,16},{4,12},{8,24},{12,4},{16,0},{20,28},{24,8},{28,20},{1,17},{... | collective-permute-start | bytes 393224 | tf_op jit(solution)/shard_map/ppermute | solution.py:169
  39.5 4.3 %collective-permute-done.9 = f32[256,128]{1,0:T(8,128)S(1)} collective-permute-done((f32[256,128]{1,0:T(8,128)S(1)}, f32[256,128]{1,0:T(8,128)S(1)}, u32[]{:S(2)}, u32[]{:S(2)}) %collective-permute-start.9) | collective-permute-done | bytes 131104 | tf_op jit(solution)/shard_map/ppermute | solution.py:169
  43.9 1.3 %collective-permute-done.10.other = f32[256,128]{1,0:T(8,128)S(1)} collective-permute-done((f32[256,128]{1,0:T(8,128)S(1)}, f32[256,128]{1,0:T(8,128)S(1)}, u32[]{:S(2)}, u32[]{:S(2)}) %collective-permute-start.10) | collective-permute-done | bytes 131104 | tf_op jit(solution)/shard_map/ppermute | solution.py:170
  45.2 1.7 %shard_map.105 = f32[384,128]{1,0:T(8,128)} custom-call(s32[2]{0:T(128)S(1)} %pad_add_fusion.refs_0_.place, f32[384,128]{1,0:T(8,128)S(1)} %get-tuple-element.18.diffused, f32[256,128]{1,0:T(8,128)S(1)} %add.28.mine, f32[256,128]{1,0:T(8,128)S(1)} %collective-permute-done.10.other, bf16[2,384,256]{2,1,0:T(8,128)(2,1)S(1)} %get-tuple-element.21.bg_high, ...), custom_call_target="tpu_custom_call" | custom-call | tf_op jit(solution)/shard_map/pallas_call | solution.py:50
  (32 shorter events, 1.0 us)
Async XLA Ops:
  0.0 14.2 %copy-start.3 = (f32[384,1,128]{2,1,0:T(1,128)S(1)}, f32[384,1,128]{2,1,0:T(1,128)}, u32[]{:S(2)}) copy-start(f32[384,1,128]{2,1,0:T(1,128)} %param.10) | copy-start | bytes 589828
  0.0 12.4 %copy-start.9 = (s32[512]{0:T(512)S(1)}, s32[512]{0:T(512)}, u32[]{:S(2)}) copy-start(s32[512]{0:T(512)} %param.17) | copy-start | bytes 6148
  0.0 12.4 %copy-start.8 = (f32[384]{0:T(512)S(1)}, f32[384]{0:T(512)}, u32[]{:S(2)}) copy-start(f32[384]{0:T(512)} %param.15) | copy-start | bytes 4612
  1.0 5.7 %collective-permute-start.1 = (bf16[384,128]{1,0:T(8,128)(2,1)S(1)}, bf16[384,128]{1,0:T(8,128)(2,1)S(1)}, u32[]{:S(2)}, u32[]{:S(2)}) collective-permute-start(bf16[384,128]{1,0:T(8,128)(2,1)S(1)} %convert_element_type.6.own), channel_id=1, source_target_pairs={{0,28},{4,0},{8,4},{12,8},{16,12},{20,16},{24,20},{28,24},{1,29},{... | collective-permute-start | bytes 294920 | tf_op jit(solution)/shard_map/ppermute | solution.py:159
  4.4 4.9 %collective-permute-start = (bf16[384,128]{1,0:T(8,128)(2,1)S(1)}, bf16[384,128]{1,0:T(8,128)(2,1)S(1)}, u32[]{:S(2)}, u32[]{:S(2)}) collective-permute-start(bf16[384,128]{1,0:T(8,128)(2,1)S(1)} %convert_element_type.6.own), channel_id=1, source_target_pairs={{0,4},{4,8},{8,12},{12,16},{16,20},{20,24},{24,28},{28,0},{1,5},{5... | collective-permute-start | bytes 294920 | tf_op jit(solution)/shard_map/ppermute | solution.py:159
  9.3 1.6 %copy-start = (bf16[3,3,128,896]{3,2,1,0:T(8,128)(2,1)S(1)}, bf16[3,3,128,896]{3,2,1,0:T(8,128)(2,1)}, u32[]{:S(2)}) copy-start(bf16[3,3,128,896]{3,2,1,0:T(8,128)(2,1)} %ops.5) | copy-start | bytes 6193156
  10.9 3.3 %copy-start.1 = (bf16[3,3,128,896]{3,2,1,0:T(8,128)(2,1)S(1)}, bf16[3,3,128,896]{3,2,1,0:T(8,128)(2,1)}, u32[]{:S(2)}) copy-start(bf16[3,3,128,896]{3,2,1,0:T(8,128)(2,1)} %ops.5) | copy-start | bytes 6193156
  10.9 3.3 %copy-start.6 = (f32[384,2,128]{2,1,0:T(2,128)S(1)}, f32[384,2,128]{2,1,0:T(2,128)}, u32[]{:S(2)}) copy-start(f32[384,2,128]{2,1,0:T(2,128)} %param.11) | copy-start | bytes 1179652
  11.9 3.6 %collective-permute-start.3 = (bf16[384,128]{1,0:T(8,128)(2,1)S(1)}, bf16[384,128]{1,0:T(8,128)(2,1)S(1)}, u32[]{:S(2)}, u32[]{:S(2)}) collective-permute-start(bf16[384,128]{1,0:T(8,128)(2,1)S(1)} %shard_map.100.own), channel_id=1, source_target_pairs={{0,28},{4,0},{8,4},{12,8},{16,12},{20,16},{24,20},{28,24},{1,29},{... | collective-permute-start | bytes 294920 | tf_op jit(solution)/shard_map/ppermute | solution.py:159
  12.1 4.9 %collective-permute-start.2 = (bf16[384,128]{1,0:T(8,128)(2,1)S(1)}, bf16[384,128]{1,0:T(8,128)(2,1)S(1)}, u32[]{:S(2)}, u32[]{:S(2)}) collective-permute-start(bf16[384,128]{1,0:T(8,128)(2,1)S(1)} %shard_map.100.own), channel_id=1, source_target_pairs={{0,4},{4,8},{8,12},{12,16},{16,20},{20,24},{24,28},{28,0},{1,5},{5... | collective-permute-start | bytes 294920 | tf_op jit(solution)/shard_map/ppermute | solution.py:159
  12.6 1.1 %copy-start.2 = (f32[384,512]{1,0:T(8,128)S(1)}, f32[384,512]{1,0:T(8,128)}, u32[]{:S(2)}) copy-start(f32[384,512]{1,0:T(8,128)} %basis.1) | copy-start | bytes 2359300
  15.4 14.1 %copy-start.4 = (bf16[4,512,128]{2,1,0:T(8,128)(2,1)S(1)}, bf16[4,512,128]{2,1,0:T(8,128)(2,1)}, u32[]{:S(2)}) copy-start(bf16[4,512,128]{2,1,0:T(8,128)(2,1)} %constant.54.clone.refs_7_) | copy-start | bytes 1572868
  15.4 14.1 %copy-start.5 = (bf16[4,512,128]{2,1,0:T(8,128)(2,1)S(1)}, bf16[4,512,128]{2,1,0:T(8,128)(2,1)}, u32[]{:S(2)}) copy-start(bf16[4,512,128]{2,1,0:T(8,128)(2,1)} %constant.53.clone.refs_6_) | copy-start | bytes 1572868
  15.4 14.1 %copy-start.7 = (f32[512]{0:T(512)S(1)}, f32[512]{0:T(512)}, u32[]{:S(2)}) copy-start(f32[512]{0:T(512)} %param.14) | copy-start | bytes 6148
  17.9 6.5 %collective-permute-start.6 = (bf16[384,128]{1,0:T(8,128)(2,1)S(1)}, bf16[384,128]{1,0:T(8,128)(2,1)S(1)}, u32[]{:S(2)}, u32[]{:S(2)}) collective-permute-start(bf16[384,128]{1,0:T(8,128)(2,1)S(1)} %get-tuple-element.14.refs_1_), channel_id=1, source_target_pairs={{0,3},{1,0},{2,1},{3,2},{4,7},{5,4},{6,5},{7,6},{8,11},{9,8},{10,9... | collective-permute-start | bytes 294920 | tf_op jit(solution)/shard_map/ppermute | solution.py:212
  21.6 7.9 %collective-permute-start.5 = (bf16[384,128]{1,0:T(8,128)(2,1)S(1)}, bf16[384,128]{1,0:T(8,128)(2,1)S(1)}, u32[]{:S(2)}, u32[]{:S(2)}) collective-permute-start(bf16[384,128]{1,0:T(8,128)(2,1)S(1)} %get-tuple-element.14.refs_1_), channel_id=1, source_target_pairs={{0,2},{1,3},{2,0},{3,1},{4,6},{5,7},{6,4},{7,5},{8,10},{9,11},{10,... | collective-permute-start | bytes 294920 | tf_op jit(solution)/shard_map/ppermute | solution.py:212
  21.6 7.9 %collective-permute-start.4 = (bf16[384,128]{1,0:T(8,128)(2,1)S(1)}, bf16[384,128]{1,0:T(8,128)(2,1)S(1)}, u32[]{:S(2)}, u32[]{:S(2)}) collective-permute-start(bf16[384,128]{1,0:T(8,128)(2,1)S(1)} %get-tuple-element.14.refs_1_), channel_id=1, source_target_pairs={{0,1},{1,2},{2,3},{3,0},{4,5},{5,6},{6,7},{7,4},{8,9},{9,10},{10,1... | collective-permute-start | bytes 294920 | tf_op jit(solution)/shard_map/ppermute | solution.py:212
  31.8 1.4 %collective-permute-start.7 = (f32[256,128]{1,0:T(8,128)S(1)}, f32[256,128]{1,0:T(8,128)S(1)}, u32[]{:S(2)}, u32[]{:S(2)}) collective-permute-start(f32[256,128]{1,0:T(8,128)S(1)} %get-tuple-element.20), channel_id=1, source_target_pairs={{0,4},{4,0},{8,12},{12,8},{16,20},{20,16},{24,28},{28,24},{1,5},{5... | collective-permute-start | bytes 393224 | tf_op jit(solution)/shard_map/ppermute | solution.py:166
  33.2 5.5 %collective-permute-start.8 = (f32[256,128]{1,0:T(8,128)S(1)}, f32[256,128]{1,0:T(8,128)S(1)}, u32[]{:S(2)}, u32[]{:S(2)}) collective-permute-start(f32[256,128]{1,0:T(8,128)S(1)} %add.26), channel_id=1, source_target_pairs={{0,8},{4,20},{8,0},{12,28},{16,24},{20,4},{24,16},{28,12},{1,9},{5... | collective-permute-start | bytes 393224 | tf_op jit(solution)/shard_map/ppermute | solution.py:169
  38.8 5.0 %collective-permute-start.9 = (f32[256,128]{1,0:T(8,128)S(1)}, f32[256,128]{1,0:T(8,128)S(1)}, u32[]{:S(2)}, u32[]{:S(2)}) collective-permute-start(f32[256,128]{1,0:T(8,128)S(1)} %add.27), channel_id=1, source_target_pairs={{0,16},{4,12},{8,24},{12,4},{16,0},{20,28},{24,8},{28,20},{1,17},{... | collective-permute-start | bytes 393224 | tf_op jit(solution)/shard_map/ppermute | solution.py:169
  43.8 1.4 %collective-permute-start.10 = (f32[256,128]{1,0:T(8,128)S(1)}, f32[256,128]{1,0:T(8,128)S(1)}, u32[]{:S(2)}, u32[]{:S(2)}) collective-permute-start(f32[256,128]{1,0:T(8,128)S(1)} %add.28.mine), channel_id=1, source_target_pairs={{0,4},{4,0},{8,12},{12,8},{16,20},{20,16},{24,28},{28,24},{1,5},{5... | collective-permute-start | bytes 393224 | tf_op jit(solution)/shard_map/ppermute | solution.py:170

commit v2 on v1

v2 whole, which is shorter than its diff:
```python
import jax
import jax.numpy as jnp
import numpy as np
from jax import lax
from jax.experimental import pallas as pl
from jax.experimental.pallas import tpu as pltpu
from jax.sharding import PartitionSpec as P

DEGMAX = 22

advect_step = 0.25
hyper_rate = 0.1
radial_step = 0.25

BF = jnp.bfloat16
F32 = jnp.float32
VMEM = pl.BlockSpec(memory_space=pltpu.VMEM)
SMEM = pl.BlockSpec(memory_space=pltpu.SMEM)
HBM = pl.BlockSpec(memory_space=pl.ANY)
PARAMS = pltpu.CompilerParams(vmem_limit_bytes=32 * 1024 * 1024)


def cheb_matrix(count):
    points = np.arange(count)
    angles = np.pi * points / (count - 1)
    upper, lower = angles[:, None], angles[None, :]
    spacing = -2.0 * np.sin((upper + lower) / 2.0) * np.sin((upper - lower) / 2.0)
    np.fill_diagonal(spacing, 1.0)
    weights = np.where((points == 0) | (points == count - 1), 2.0, 1.0)
    parity = np.where((upper * 0 + points[:, None] + points[None, :]) % 2 == 0, 1.0, -1.0)
    entries = weights[:, None] / weights[None, :] * parity / spacing
    np.fill_diagonal(entries, 0.0)
    matrix = entries - np.diag(entries.sum(axis=1))
    return (np.sin(angles)[:, None] * matrix / count).T.astype(np.float32)


def split(value):
    high = value.astype(BF)
    return high, (value - high.astype(F32)).astype(BF)


def dot(left, right):
    return jnp.dot(left, right, preferred_element_type=F32)


def dot3(left, right):
    wide = dot(left[0], jnp.concatenate(right, axis=1))
    count = right[0].shape[1]
    return wide[:, :count] + (wide[:, count:] + dot(left[1], right[0]))


def call(kernel, outs, args, spaces=None, scratch=()):
    return pl.pallas_call(
        kernel,
        out_shape=outs,
        in_specs=[{"s": SMEM, "h": HBM, "v": VMEM}[c] for c in spaces or "v" * len(args)],
        out_specs=jax.tree.map(lambda _: VMEM, outs),
        scratch_shapes=list(scratch),
        compiler_params=PARAMS,
    )(*args)


def shape(dims, kind):
    return jax.ShapeDtypeStruct(dims, kind)


def beside(dense, kind, first, count):
    return jnp.concatenate([dense[kind, first + s] for s in range(count)], axis=1)


def round_kernel(fields, wide, narrow, sems):
    parts = sems.shape[0]
    rows = wide.shape[0] // parts
    copies = []
    for p in range(parts):
        piece = pl.ds(p * rows, rows)
        copies.append(pltpu.make_async_copy(fields.at[piece], wide.at[piece], sems.at[p]))
        copies[-1].start()
    for p in range(parts):
        copies[p].wait()
        piece = slice(p * rows, (p + 1) * rows)
        narrow[piece] = wide[piece].astype(BF)


def prepare_kernel(ids, ops, basis, velocity, weight, gain, own, dense, lap_own, wbt_high, wbt_low, bg_high, bg_low,
                   vel, held, sems, op_sems):
    blocks, kinds, size, wide = ops.shape
    near = wide // size
    held_copy = pltpu.make_async_copy(basis, held, sems.at[0])
    held_copy.start()
    dense[...] = jnp.zeros(dense.shape, BF)
    total = blocks * lax.axis_size("tile")
    first = (lax.axis_index("tile") - 1) * blocks
    copies = []
    for b in range(blocks):
        for k in range(near):
            source = lax.rem(ids[b, k] - first + total, total)
            copies.append(
                pltpu.make_async_copy(
                    ops.at[b, :, :, pl.ds(k * size, size)],
                    dense.at[:, source, pl.ds(b * size, size), :],
                    op_sems.at[b, k],
                )
            )
            copies[-1].start()
    vel_copy = pltpu.make_async_copy(velocity, vel, sems.at[1])
    vel_copy.start()
    held_copy.wait()
    half = held.shape[1] // 2
    high, low = split(held[...].T * weight[...])
    wbt_high[...] = high
    wbt_low[...] = low
    for c in range(2):
        cols = slice(c * half, (c + 1) * half)
        high, low = split(held[:, cols] * gain[:, cols])
        bg_high[c] = high
        bg_low[c] = low
    for copy in copies:
        copy.wait()
    lap_own[...] = dot(beside(dense, 2, blocks, blocks), own[...])
    vel_copy.wait()


def first_lap_kernel(dense, lap_own, low, high, lap):
    blocks = dense.shape[1] // 3
    total = dot(beside(dense, 2, 0, blocks), low[...]) + dot(beside(dense, 2, 2 * blocks, blocks), high[...])
    lap[...] = (lap_own[...] + total).astype(BF)


def advect_kernel(dense, low, own, high, lap, fields, velocity, out):
    nodes = own.shape[0]
    blocks = dense.shape[1] // 3
    value = fields[...]
    for k in range(2):
        grad = dot(beside(dense, k, 0, blocks), low[...]) + dot(beside(dense, k, blocks, blocks), own[...])
        grad = grad + dot(beside(dense, k, 2 * blocks, blocks), high[...])
        value = value - advect_step * (velocity[pl.ds(k, nodes, stride=2), :] * grad)
    out[...] = value - hyper_rate * dot(beside(dense, 2, blocks, blocks), lap[...])


def second_lap_kernel(dense, low, high, part, stepped, narrow):
    blocks = dense.shape[1] // 3
    total = dot(beside(dense, 2, 0, blocks), low[...]) + dot(beside(dense, 2, 2 * blocks, blocks), high[...])
    value = part[...] - hyper_rate * total
    stepped[...] = value
    narrow[...] = value.astype(BF)


def project_kernel(wbt_high, wbt_low, value, out):
    out[...] = dot3((wbt_high[...], wbt_low[...]), split(value[...]))


def diffuse_kernel(count, *refs):
    shards = refs[:count]
    stepped, dh_high, dh_low, kappa, wbt_high, wbt_low, partial, diffused, keep, send, levels = refs[count:]
    rad, core = lax.axis_index("rad"), lax.rem(lax.axis_index("tile"), 2)
    for d in range(count):
        levels[lax.rem(rad + count - d, count)] = shards[d][...]
    value = jnp.concatenate([levels[c] for c in range(count)], axis=1)
    width = levels.shape[2]
    term = None
    group = 2 if count % 2 == 0 else 1
    for first in range(0, count, group):
        some = range(first, first + group)
        slopes = dot(value, jnp.concatenate([dh_high[c] for c in some], axis=1))
        slopes = slopes + dot(value, jnp.concatenate([dh_low[c] for c in some], axis=1))
        cols = slice(first * width, (first + group) * width)
        fluxes = kappa[:, cols] * (1.0 + 0.5 * jnp.tanh(value[:, cols].astype(F32))) * slopes
        more = dot3(split(fluxes), (dh_high[rad, cols, :], dh_low[rad, cols, :]))
        term = more if term is None else term + more
    term = radial_step * term
    diffused[...] = stepped[...] + term
    parts = split(term)
    half = keep.shape[0]
    for out, which in ((send, 1 - core), (keep, core)):
        rows = pl.ds(pl.multiple_of(which * half, half), half)
        out[...] = partial[rows, :] + dot3((wbt_high[rows, :], wbt_low[rows, :]), parts)


def filter_kernel(swap, value, modes, bg_high, bg_low, out):
    which = lax.rem(lax.axis_index("tile") + swap, 2)
    out[...] = value[...] - dot3((bg_high[which], bg_low[which]), split(modes[...]))


def shift(axis, by):
    count = lax.axis_size(axis)
    return [(i, (i + by) % count) for i in range(count)]


def halo(block):
    return lax.ppermute(block, "tile", shift("tile", 1)), lax.ppermute(block, "tile", shift("tile", -1))


def tile_sum(keep, send):
    count = lax.axis_size("tile")
    swap = [(i, i ^ 1) for i in range(count)]
    bits = [1 << k for k in range(1, count.bit_length() - 1)]
    mine = keep + lax.ppermute(send, "tile", swap)
    for k in range(len(bits)):
        pairs = [(i, i ^ bits[(k + i % 2) % len(bits)]) for i in range(count)]
        mine = mine + lax.ppermute(mine, "tile", pairs)
    return mine, lax.ppermute(mine, "tile", swap)


def body(fields, velocity, operators, neighbours, kappa_ref, quad_weight, basis, degree):
    nodes, nfield, levels = fields.shape
    blocks, _, size, _ = operators.shape
    modes = basis.shape[1]
    tiles, rads = lax.axis_size("tile"), lax.axis_size("rad")
    fields = fields.reshape(nodes, levels)
    velocity = velocity.reshape(2 * nodes, levels)
    wide = shape((nodes, levels), F32)
    thin = shape((nodes, levels), BF)

    ratio = degree.astype(F32) / DEGMAX
    gain = 0.5 * jnp.sqrt(F32(modes) / (nodes * tiles)) * (1.0 - jnp.exp(-4.0 * ratio * ratio))
    dhat = cheb_matrix(rads * levels)
    dhat = np.stack([dhat[:, c * levels : (c + 1) * levels] for c in range(rads)])
    dh_high = dhat.astype(BF)
    dh_low = (dhat - dh_high.astype(np.float32)).astype(BF)

    fields, rounded = call(round_kernel, (wide, thin), (fields,), "h", (pltpu.SemaphoreType.DMA((3,)),))
    low, high = halo(rounded)
    dense, lap_own, wbt_high, wbt_low, bg_high, bg_low, velocity = call(
        prepare_kernel,
        (shape((3, 3 * blocks, nodes, size), BF), wide)
        + (shape((modes, nodes), BF),) * 2
        + (shape((2, nodes, modes // 2), BF),) * 2
        + (shape((2 * nodes, levels), F32),),
        (neighbours, operators, basis, velocity, quad_weight[None, :], gain[None, :], rounded),
        "shhhvvv",
        (pltpu.VMEM((nodes, modes), F32), pltpu.SemaphoreType.DMA((2,)), pltpu.SemaphoreType.DMA(neighbours.shape)),
    )
    lap = call(first_lap_kernel, thin, (dense, lap_own, low, high))
    low_two, high_two = halo(lap)
    part = call(advect_kernel, wide, (dense, low, rounded, high, lap, fields, velocity))
    stepped, narrow = call(second_lap_kernel, (wide, thin), (dense, low_two, high_two, part))
    shards = [narrow] + [lax.ppermute(narrow, "rad", shift("rad", d)) for d in range(1, rads)]
    partial = call(project_kernel, shape((modes, levels), F32), (wbt_high, wbt_low, stepped))
    diffused, keep, send = call(
        lambda *refs: diffuse_kernel(rads, *refs),
        (wide,) + (shape((modes // 2, levels), F32),) * 2,
        (*shards, stepped, jnp.asarray(dh_high), jnp.asarray(dh_low), kappa_ref[None, :], wbt_high, wbt_low, partial),
        None,
        (pltpu.VMEM((rads, nodes, levels), BF),),
    )
    mine, other = tile_sum(keep, send)
    some = call(lambda *refs: filter_kernel(0, *refs), wide, (diffused, mine, bg_high, bg_low))
    filtered = call(lambda *refs: filter_kernel(1, *refs), wide, (some, other, bg_high, bg_low))
    return filtered.reshape(nodes, nfield, levels)


def solution(mesh):
    return jax.shard_map(
        body,
        mesh=mesh,
        in_specs=(
            P("tile", None, "rad"),
            P("tile", None, "rad"),
            P("tile", None, None, None),
            P("tile", None),
            P(),
            P("tile"),
            P("tile", None),
            P(),
        ),
        out_specs=P("tile", None, "rad"),
        check_vma=False,
    )
```

time: 47.2 us -> 47.5 us (level)
  waiting for transfers between devices: 22.6 us -> 19 us
  local copies, waits for them, and re-layouts: 2.85 us -> 6.02 us
  starting transfers between devices: 12 us -> 13.7 us
  other arithmetic: 1.83 us -> 0.74 us
    unnamed x20 -> x16, local copies, waits for them, and re-layouts: 2.75 us -> 5.33 us
    ppermute x2, starting transfers between devices: 3.59 us -> 6.08 us  [halo(): lax.ppermute(block, 'tile', shift('tile', -1))]
    ppermute x3, waiting for transfers between devices: 6.8 us -> 5.16 us  [body(): lax.ppermute(narrow, 'rad', shift('rad', d))]
    ppermute x2, waiting for transfers between devices: 4.23 us -> 2.73 us  [halo(): lax.ppermute(block, 'tile', shift('tile', 1))]
    convert_element_type x1 -> x0, other arithmetic: 1.01 us -> none  [body(): rounded = fields.astype(BF)]
    select_n x1 -> x0, other arithmetic: 0.7 us -> none  [body(): ids = jnp.mod(neighbours - (tile - 1) * blocks + total, total)]
    mul x1, other arithmetic: 0.01 us -> 0.69 us  [body(): 0.5 * jnp.sqrt(F32(modes) / (nodes * tiles))]
    broadcast_in_dim x1, local copies, waits for them, and re-layouts: 0.1 us -> 0.69 us  [body(): quad_weight[None, :]]
  transfers between devices with their start and end apart: 11 -> 11, of which waited for: 9 -> 8; matrix products, arithmetic and copies ran while one was open for 2% -> 3% of each run, Pallas kernels for 3% -> 8%
where the time goes in v2:
time: 47.5 us; the launch traced here: 47.1 us
  waiting for transfers between devices  19 us (40%)
  starting transfers between devices  13.7 us (29%)
  Pallas kernels  7.51 us (16%)
  local copies, waits for them, and re-layouts  6.02 us (13%)
  other arithmetic  0.74 us (2%)
    pallas_call x9, Pallas kernels, call(): pl.pallas_call(kernel, out_shape=outs, in_specs=[{'s': SMEM, 'h': HBM, 'v...  7.51 us
    ppermute x2, waiting for transfers between devices, tile_sum(): mine = mine + lax.ppermute(mine, 'tile', pairs)  7.27 us
    ppermute x2, starting transfers between devices, halo(): lax.ppermute(block, 'tile', shift('tile', -1))  6.08 us
    unnamed x16, local copies, waits for them, and re-layouts  5.33 us
    ppermute x3, waiting for transfers between devices, body(): lax.ppermute(narrow, 'rad', shift('rad', d))  5.16 us
    ppermute x3, starting transfers between devices, body(): lax.ppermute(narrow, 'rad', shift('rad', d))  4.67 us
    ppermute x2, starting transfers between devices, tile_sum(): mine = mine + lax.ppermute(mine, 'tile', pairs)  2.79 us
    ppermute x2, waiting for transfers between devices, halo(): lax.ppermute(block, 'tile', shift('tile', 1))  2.73 us
  transfers between devices with their start and end apart: 11, of which 8 were waited for; matrix products, arithmetic and copies ran while one was open for 3% of the time, Pallas kernels for 8%

profile of v2, /device:TPU:0, one launch (start us, length us, event | category | flops | bytes accessed | tf_op | source)
XLA Modules:
  0.0 47.1 jit_solution(15011402151813925857)
XLA Ops:
  0.0 0.9 %copy-done.5 = f32[384,1,128]{2,1,0:T(1,128)S(1)} copy-done((f32[384,1,128]{2,1,0:T(1,128)S(1)}, f32[384,1,128]{2,1,0:T(1,128)}, u32[]{:S(2)}) %copy-start.5) | copy-done | bytes 196632
  1.2 3.4 %collective-permute-start.1 = (bf16[384,128]{1,0:T(8,128)(2,1)S(1)}, bf16[384,128]{1,0:T(8,128)(2,1)S(1)}, u32[]{:S(2)}, u32[]{:S(2)}) collective-permute-start(bf16[384,128]{1,0:T(8,128)(2,1)S(1)} %get-tuple-element.19.own), channel_id=1, source_target_pairs={{0,28},{4,0},{8,4},{12,8},{16,12},{20,16},{24,20},{28,24},{1,29},{... | collective-permute-start | bytes 294920 | tf_op jit(solution)/shard_map/ppermute | solution.py:191
  4.6 0.7 %subtract_multiply_fusion = f32[512]{0:T(512)S(1)} fusion(s32[512]{0:T(512)} %param.17), kind=kLoop, calls=%fused_computation | loop fusion | flops 3072 | bytes 4096 | tf_op jit(solution)/shard_map/mul | solution.py:216
  5.3 0.7 %broadcast_in_dim.9.weight = f32[1,384]{1,0:T(1,128)S(1)} reshape(f32[384]{0:T(512)} %param.15) | data formatting | bytes 3072 | tf_op jit(solution)/shard_map/broadcast_in_dim | solution.py:230
  6.0 1.6 %copy-done = bf16[3,3,128,896]{3,2,1,0:T(8,128)(2,1)S(1)} copy-done((bf16[3,3,128,896]{3,2,1,0:T(8,128)(2,1)S(1)}, bf16[3,3,128,896]{3,2,1,0:T(8,128)(2,1)}, u32[]{:S(2)}) %copy-start) | copy-done | bytes 2064408
  7.5 1.1 %copy-done.1 = f32[384,512]{1,0:T(8,128)S(1)} copy-done((f32[384,512]{1,0:T(8,128)S(1)}, f32[384,512]{1,0:T(8,128)}, u32[]{:S(2)}) %copy-start.1) | copy-done | bytes 786456
  8.7 1.0 %copy-done.4 = f32[384,2,128]{2,1,0:T(2,128)S(1)} copy-done((f32[384,2,128]{2,1,0:T(2,128)S(1)}, f32[384,2,128]{2,1,0:T(2,128)}, u32[]{:S(2)}) %copy-start.4) | copy-done | bytes 393240
  10.4 2.6 %shard_map.101 = (bf16[3,9,384,128]{3,2,1,0:T(8,128)(2,1)S(1)}, f32[384,128]{1,0:T(8,128)S(1)}, bf16[512,384]{1,0:T(8,128)(2,1)S(1)}, bf16[512,384]{1,0:T(8,128)...) custom-call(s32[3,7]{1,0:T(4,128)S(1)} %copy-done.7, ...), custom_call_target="tpu_custom_call" | custom-call | tf_op jit(solution)/shard_map/pallas_call | solution.py:53
  13.3 2.7 %collective-permute-start.3 = (bf16[384,128]{1,0:T(8,128)(2,1)S(1)}, bf16[384,128]{1,0:T(8,128)(2,1)S(1)}, u32[]{:S(2)}, u32[]{:S(2)}) collective-permute-start(bf16[384,128]{1,0:T(8,128)(2,1)S(1)} %shard_map.102.lap), channel_id=1, source_target_pairs={{0,28},{4,0},{8,4},{12,8},{16,12},{20,16},{24,20},{28,24},{1,29},{... | collective-permute-start | bytes 294920 | tf_op jit(solution)/shard_map/ppermute | solution.py:191
  16.0 0.7 %shard_map.103.part = f32[384,128]{1,0:T(8,128)S(1)} custom-call(bf16[3,9,384,128]{3,2,1,0:T(8,128)(2,1)S(1)} %get-tuple-element.20.dense, bf16[384,128]{1,0:T(8,128)(2,1)S(1)} %collective-permute-done.low, bf16[384,128]{1,0:T(8,128)(2,1)S(1)} %get-tuple-element.19.own, bf16[384,128]{1,0:T(8,128)(2,1)S(1)} %collective-permute-done.1.high, ...), custom_call_target="tpu_custom_call" | custom-call | tf_op jit(solution)/shard_map/pallas_call | solution.py:53
  16.7 1.5 %collective-permute-done.3.high = bf16[384,128]{1,0:T(8,128)(2,1)S(1)} collective-permute-done((bf16[384,128]{1,0:T(8,128)(2,1)S(1)}, bf16[384,128]{1,0:T(8,128)(2,1)S(1)}, u32[]{:S(2)}, u32[]{:S(2)}) %collective-permute-start.3) | collective-permute-done | bytes 98336 | tf_op jit(solution)/shard_map/ppermute | solution.py:191
  18.2 2.7 %collective-permute-done.2.low = bf16[384,128]{1,0:T(8,128)(2,1)S(1)} collective-permute-done((bf16[384,128]{1,0:T(8,128)(2,1)S(1)}, bf16[384,128]{1,0:T(8,128)(2,1)S(1)}, u32[]{:S(2)}, u32[]{:S(2)}) %collective-permute-start.2) | collective-permute-done | bytes 98336 | tf_op jit(solution)/shard_map/ppermute | solution.py:191
  21.2 3.7 %collective-permute-start.6 = (bf16[384,128]{1,0:T(8,128)(2,1)S(1)}, bf16[384,128]{1,0:T(8,128)(2,1)S(1)}, u32[]{:S(2)}, u32[]{:S(2)}) collective-permute-start(bf16[384,128]{1,0:T(8,128)(2,1)S(1)} %get-tuple-element.24.refs_0_), channel_id=1, source_target_pairs={{0,3},{1,0},{2,1},{3,2},{4,7},{5,4},{6,5},{7,6},{8,11},{9,8},{10,9... | collective-permute-start | bytes 294920 | tf_op jit(solution)/shard_map/ppermute | solution.py:238
  24.9 1.0 %collective-permute-start.4 = (bf16[384,128]{1,0:T(8,128)(2,1)S(1)}, bf16[384,128]{1,0:T(8,128)(2,1)S(1)}, u32[]{:S(2)}, u32[]{:S(2)}) collective-permute-start(bf16[384,128]{1,0:T(8,128)(2,1)S(1)} %get-tuple-element.24.refs_0_), channel_id=1, source_target_pairs={{0,1},{1,2},{2,3},{3,0},{4,5},{5,6},{6,7},{7,4},{8,9},{9,10},{10,1... | collective-permute-start | bytes 294920 | tf_op jit(solution)/shard_map/ppermute | solution.py:238
  26.3 1.3 %collective-permute-done.6.refs_3_ = bf16[384,128]{1,0:T(8,128)(2,1)S(1)} collective-permute-done((bf16[384,128]{1,0:T(8,128)(2,1)S(1)}, bf16[384,128]{1,0:T(8,128)(2,1)S(1)}, u32[]{:S(2)}, u32[]{:S(2)}) %collective-permute-start.6) | collective-permute-done | bytes 98336 | tf_op jit(solution)/shard_map/ppermute | solution.py:238
  27.6 3.8 %collective-permute-done.5.refs_2_ = bf16[384,128]{1,0:T(8,128)(2,1)S(1)} collective-permute-done((bf16[384,128]{1,0:T(8,128)(2,1)S(1)}, bf16[384,128]{1,0:T(8,128)(2,1)S(1)}, u32[]{:S(2)}, u32[]{:S(2)}) %collective-permute-start.5) | collective-permute-done | bytes 98336 | tf_op jit(solution)/shard_map/ppermute | solution.py:238
  31.5 1.8 %shard_map.106 = (f32[384,128]{1,0:T(8,128)S(1)}, f32[256,128]{1,0:T(8,128)S(1)}, f32[256,128]{1,0:T(8,128)S(1)}) custom-call(bf16[384,128]{1,0:T(8,128)(2,1)S(1)} %get-tuple-element.24.refs_0_, bf16[384,128]{1,0:T(8,128)(2,1)S(1)} %collective-permute-done.4.refs_1_, bf16[384,128]{1,0:T(8,128)(2,1)S(1)} %collective-permute-done.5.refs_2_, ...), custom_call_target="tpu_custom_call" | custom-call | tf_op jit(solution)/shard_map/pallas_call | solution.py:53
  33.3 1.3 %collective-permute-done.7 = f32[256,128]{1,0:T(8,128)S(1)} collective-permute-done((f32[256,128]{1,0:T(8,128)S(1)}, f32[256,128]{1,0:T(8,128)S(1)}, u32[]{:S(2)}, u32[]{:S(2)}) %collective-permute-start.7) | collective-permute-done | bytes 131104 | tf_op jit(solution)/shard_map/ppermute | solution.py:198
  34.7 1.2 %collective-permute-start.8 = (f32[256,128]{1,0:T(8,128)S(1)}, f32[256,128]{1,0:T(8,128)S(1)}, u32[]{:S(2)}, u32[]{:S(2)}) collective-permute-start(f32[256,128]{1,0:T(8,128)S(1)} %add.9), channel_id=1, source_target_pairs={{0,8},{4,20},{8,0},{12,28},{16,24},{20,4},{24,16},{28,12},{1,9},{5... | collective-permute-start | bytes 393224 | tf_op jit(solution)/shard_map/ppermute | solution.py:201
  35.9 3.8 %collective-permute-done.8 = f32[256,128]{1,0:T(8,128)S(1)} collective-permute-done((f32[256,128]{1,0:T(8,128)S(1)}, f32[256,128]{1,0:T(8,128)S(1)}, u32[]{:S(2)}, u32[]{:S(2)}) %collective-permute-start.8) | collective-permute-done | bytes 131104 | tf_op jit(solution)/shard_map/ppermute | solution.py:201
  39.7 1.6 %collective-permute-start.9 = (f32[256,128]{1,0:T(8,128)S(1)}, f32[256,128]{1,0:T(8,128)S(1)}, u32[]{:S(2)}, u32[]{:S(2)}) collective-permute-start(f32[256,128]{1,0:T(8,128)S(1)} %add.10), channel_id=1, source_target_pairs={{0,16},{4,12},{8,24},{12,4},{16,0},{20,28},{24,8},{28,20},{1,17},{... | collective-permute-start | bytes 393224 | tf_op jit(solution)/shard_map/ppermute | solution.py:201
  41.3 3.5 %collective-permute-done.9 = f32[256,128]{1,0:T(8,128)S(1)} collective-permute-done((f32[256,128]{1,0:T(8,128)S(1)}, f32[256,128]{1,0:T(8,128)S(1)}, u32[]{:S(2)}, u32[]{:S(2)}) %collective-permute-start.9) | collective-permute-done | bytes 131104 | tf_op jit(solution)/shard_map/ppermute | solution.py:201
  45.1 1.1 %collective-permute-done.10.refs_1_ = f32[256,128]{1,0:T(8,128)S(1)} collective-permute-done((f32[256,128]{1,0:T(8,128)S(1)}, f32[256,128]{1,0:T(8,128)S(1)}, u32[]{:S(2)}, u32[]{:S(2)}) %collective-permute-start.10) | collective-permute-done | bytes 131104 | tf_op jit(solution)/shard_map/ppermute | solution.py:202
  46.2 0.9 %shard_map.108 = f32[384,128]{1,0:T(8,128)} custom-call(f32[384,128]{1,0:T(8,128)S(1)} %shard_map.107.refs_0_, f32[256,128]{1,0:T(8,128)S(1)} %collective-permute-done.10.refs_1_, bf16[2,384,256]{2,1,0:T(8,128)(2,1)S(1)} %get-tuple-element.31.refs_2_, bf16[2,384,256]{2,1,0:T(8,128)(2,1)S(1)} %get-tuple-element.32.refs_3_), custom_call_target="tpu_custom_call" | custom-call | tf_op jit(solution)/shard_map/pallas_call | solution.py:53
  (28 shorter events, 2.5 us)
Async XLA Ops:
  0.0 0.9 %copy-start.5 = (f32[384,1,128]{2,1,0:T(1,128)S(1)}, f32[384,1,128]{2,1,0:T(1,128)}, u32[]{:S(2)}) copy-start(f32[384,1,128]{2,1,0:T(1,128)} %param.10) | copy-start | bytes 589828
  1.2 11.7 %collective-permute-start.1 = (bf16[384,128]{1,0:T(8,128)(2,1)S(1)}, bf16[384,128]{1,0:T(8,128)(2,1)S(1)}, u32[]{:S(2)}, u32[]{:S(2)}) collective-permute-start(bf16[384,128]{1,0:T(8,128)(2,1)S(1)} %get-tuple-element.19.own), channel_id=1, source_target_pairs={{0,28},{4,0},{8,4},{12,8},{16,12},{20,16},{24,20},{28,24},{1,29},{... | collective-permute-start | bytes 294920 | tf_op jit(solution)/shard_map/ppermute | solution.py:191
  4.6 8.4 %collective-permute-start = (bf16[384,128]{1,0:T(8,128)(2,1)S(1)}, bf16[384,128]{1,0:T(8,128)(2,1)S(1)}, u32[]{:S(2)}, u32[]{:S(2)}) collective-permute-start(bf16[384,128]{1,0:T(8,128)(2,1)S(1)} %get-tuple-element.19.own), channel_id=1, source_target_pairs={{0,4},{4,8},{8,12},{12,16},{16,20},{20,24},{24,28},{28,0},{1,5},{5... | collective-permute-start | bytes 294920 | tf_op jit(solution)/shard_map/ppermute | solution.py:191
  6.0 1.6 %copy-start = (bf16[3,3,128,896]{3,2,1,0:T(8,128)(2,1)S(1)}, bf16[3,3,128,896]{3,2,1,0:T(8,128)(2,1)}, u32[]{:S(2)}) copy-start(bf16[3,3,128,896]{3,2,1,0:T(8,128)(2,1)} %ops.1) | copy-start | bytes 6193156
  7.5 1.1 %copy-start.1 = (f32[384,512]{1,0:T(8,128)S(1)}, f32[384,512]{1,0:T(8,128)}, u32[]{:S(2)}) copy-start(f32[384,512]{1,0:T(8,128)} %basis.1) | copy-start | bytes 2359300
  8.7 1.0 %copy-start.4 = (f32[384,2,128]{2,1,0:T(2,128)S(1)}, f32[384,2,128]{2,1,0:T(2,128)}, u32[]{:S(2)}) copy-start(f32[384,2,128]{2,1,0:T(2,128)} %param.11) | copy-start | bytes 1179652
  9.7 0.7 %copy-start.7 = (s32[3,7]{1,0:T(4,128)S(1)}, s32[3,7]{1,0:T(4,128)}, u32[]{:S(2)}) copy-start(s32[3,7]{1,0:T(4,128)} %ids.1) | copy-start | bytes 256
  13.3 4.9 %collective-permute-start.3 = (bf16[384,128]{1,0:T(8,128)(2,1)S(1)}, bf16[384,128]{1,0:T(8,128)(2,1)S(1)}, u32[]{:S(2)}, u32[]{:S(2)}) collective-permute-start(bf16[384,128]{1,0:T(8,128)(2,1)S(1)} %shard_map.102.lap), channel_id=1, source_target_pairs={{0,28},{4,0},{8,4},{12,8},{16,12},{20,16},{24,20},{28,24},{1,29},{... | collective-permute-start | bytes 294920 | tf_op jit(solution)/shard_map/ppermute | solution.py:191
  16.0 4.9 %collective-permute-start.2 = (bf16[384,128]{1,0:T(8,128)(2,1)S(1)}, bf16[384,128]{1,0:T(8,128)(2,1)S(1)}, u32[]{:S(2)}, u32[]{:S(2)}) collective-permute-start(bf16[384,128]{1,0:T(8,128)(2,1)S(1)} %shard_map.102.lap), channel_id=1, source_target_pairs={{0,4},{4,8},{8,12},{12,16},{16,20},{20,24},{24,28},{28,0},{1,5},{5... | collective-permute-start | bytes 294920 | tf_op jit(solution)/shard_map/ppermute | solution.py:191
  16.7 14.8 %copy-start.2 = (bf16[4,512,128]{2,1,0:T(8,128)(2,1)S(1)}, bf16[4,512,128]{2,1,0:T(8,128)(2,1)}, u32[]{:S(2)}) copy-start(bf16[4,512,128]{2,1,0:T(8,128)(2,1)} %constant.15.clone.refs_6_) | copy-start | bytes 1572868
  16.7 14.8 %copy-start.3 = (bf16[4,512,128]{2,1,0:T(8,128)(2,1)S(1)}, bf16[4,512,128]{2,1,0:T(8,128)(2,1)}, u32[]{:S(2)}) copy-start(bf16[4,512,128]{2,1,0:T(8,128)(2,1)} %constant.14.clone.refs_5_) | copy-start | bytes 1572868
  16.7 14.8 %copy-start.6 = (f32[512]{0:T(512)S(1)}, f32[512]{0:T(512)}, u32[]{:S(2)}) copy-start(f32[512]{0:T(512)} %param.14) | copy-start | bytes 6148
  21.2 6.4 %collective-permute-start.6 = (bf16[384,128]{1,0:T(8,128)(2,1)S(1)}, bf16[384,128]{1,0:T(8,128)(2,1)S(1)}, u32[]{:S(2)}, u32[]{:S(2)}) collective-permute-start(bf16[384,128]{1,0:T(8,128)(2,1)S(1)} %get-tuple-element.24.refs_0_), channel_id=1, source_target_pairs={{0,3},{1,0},{2,1},{3,2},{4,7},{5,4},{6,5},{7,6},{8,11},{9,8},{10,9... | collective-permute-start | bytes 294920 | tf_op jit(solution)/shard_map/ppermute | solution.py:238
  24.9 6.6 %collective-permute-start.5 = (bf16[384,128]{1,0:T(8,128)(2,1)S(1)}, bf16[384,128]{1,0:T(8,128)(2,1)S(1)}, u32[]{:S(2)}, u32[]{:S(2)}) collective-permute-start(bf16[384,128]{1,0:T(8,128)(2,1)S(1)} %get-tuple-element.24.refs_0_), channel_id=1, source_target_pairs={{0,2},{1,3},{2,0},{3,1},{4,6},{5,7},{6,4},{7,5},{8,10},{9,11},{10,... | collective-permute-start | bytes 294920 | tf_op jit(solution)/shard_map/ppermute | solution.py:238
  24.9 6.6 %collective-permute-start.4 = (bf16[384,128]{1,0:T(8,128)(2,1)S(1)}, bf16[384,128]{1,0:T(8,128)(2,1)S(1)}, u32[]{:S(2)}, u32[]{:S(2)}) collective-permute-start(bf16[384,128]{1,0:T(8,128)(2,1)S(1)} %get-tuple-element.24.refs_0_), channel_id=1, source_target_pairs={{0,1},{1,2},{2,3},{3,0},{4,5},{5,6},{6,7},{7,4},{8,9},{9,10},{10,1... | collective-permute-start | bytes 294920 | tf_op jit(solution)/shard_map/ppermute | solution.py:238
  33.2 1.4 %collective-permute-start.7 = (f32[256,128]{1,0:T(8,128)S(1)}, f32[256,128]{1,0:T(8,128)S(1)}, u32[]{:S(2)}, u32[]{:S(2)}) collective-permute-start(f32[256,128]{1,0:T(8,128)S(1)} %get-tuple-element.30), channel_id=1, source_target_pairs={{0,4},{4,0},{8,12},{12,8},{16,20},{20,16},{24,28},{28,24},{1,5},{5... | collective-permute-start | bytes 393224 | tf_op jit(solution)/shard_map/ppermute | solution.py:198
  34.7 5.0 %collective-permute-start.8 = (f32[256,128]{1,0:T(8,128)S(1)}, f32[256,128]{1,0:T(8,128)S(1)}, u32[]{:S(2)}, u32[]{:S(2)}) collective-permute-start(f32[256,128]{1,0:T(8,128)S(1)} %add.9), channel_id=1, source_target_pairs={{0,8},{4,20},{8,0},{12,28},{16,24},{20,4},{24,16},{28,12},{1,9},{5... | collective-permute-start | bytes 393224 | tf_op jit(solution)/shard_map/ppermute | solution.py:201
  39.7 5.0 %collective-permute-start.9 = (f32[256,128]{1,0:T(8,128)S(1)}, f32[256,128]{1,0:T(8,128)S(1)}, u32[]{:S(2)}, u32[]{:S(2)}) collective-permute-start(f32[256,128]{1,0:T(8,128)S(1)} %add.10), channel_id=1, source_target_pairs={{0,16},{4,12},{8,24},{12,4},{16,0},{20,28},{24,8},{28,20},{1,17},{... | collective-permute-start | bytes 393224 | tf_op jit(solution)/shard_map/ppermute | solution.py:201
  44.8 1.4 %collective-permute-start.10 = (f32[256,128]{1,0:T(8,128)S(1)}, f32[256,128]{1,0:T(8,128)S(1)}, u32[]{:S(2)}, u32[]{:S(2)}) collective-permute-start(f32[256,128]{1,0:T(8,128)S(1)} %add.11.refs_1_), channel_id=1, source_target_pairs={{0,4},{4,0},{8,12},{12,8},{16,20},{20,16},{24,28},{28,24},{1,5},{5... | collective-permute-start | bytes 393224 | tf_op jit(solution)/shard_map/ppermute | solution.py:202

commit v3 on v2

--- a/solution.py
+++ b/solution.py
@@ -1,3 +1,5 @@
+import math
+
 import jax
 import jax.numpy as jnp
 import numpy as np
@@ -16,7 +18,7 @@
 F32 = jnp.float32
 VMEM = pl.BlockSpec(memory_space=pltpu.VMEM)
 SMEM = pl.BlockSpec(memory_space=pltpu.SMEM)
-HBM = pl.BlockSpec(memory_space=pl.ANY)
+HBM = pl.BlockSpec(memory_space=pltpu.HBM)
 PARAMS = pltpu.CompilerParams(vmem_limit_bytes=32 * 1024 * 1024)
 
 
@@ -82,12 +84,15 @@
         narrow[piece] = wide[piece].astype(BF)
 
 
-def prepare_kernel(ids, ops, basis, velocity, weight, gain, own, dense, lap_own, wbt_high, wbt_low, bg_high, bg_low,
-                   vel, held, sems, op_sems):
-    blocks, kinds, size, wide = ops.shape
+def prepare_kernel(ids, ops, basis, velocity, weight, degree, own, dense, lap_own, wbt_high, wbt_low, bg_high, bg_low,
+                   vel, held, weight_held, degree_held, sems, op_sems):
+    blocks, _, size, wide = ops.shape
     near = wide // size
-    held_copy = pltpu.make_async_copy(basis, held, sems.at[0])
-    held_copy.start()
+    nodes, modes = held.shape
+    pairs = ((basis, held), (weight, weight_held), (degree, degree_held), (velocity, vel))
+    held_copies = [pltpu.make_async_copy(*pair, sems.at[k]) for k, pair in enumerate(pairs)]
+    for copy in held_copies:
+        copy.start()
     dense[...] = jnp.zeros(dense.shape, BF)
     total = blocks * lax.axis_size("tile")
     first = (lax.axis_index("tile") - 1) * blocks
@@ -103,11 +108,12 @@
                 )
             )
             copies[-1].start()
-    vel_copy = pltpu.make_async_copy(velocity, vel, sems.at[1])
-    vel_copy.start()
-    held_copy.wait()
-    half = held.shape[1] // 2
-    high, low = split(held[...].T * weight[...])
+    for copy in held_copies:
+        copy.wait()
+    ratio = degree_held[...].astype(F32) / DEGMAX
+    gain = 0.5 * math.sqrt(modes / (nodes * lax.axis_size("tile"))) * (1.0 - jnp.exp(-4.0 * ratio * ratio))
+    half = modes // 2
+    high, low = split(held[...].T * weight_held[...])
     wbt_high[...] = high
     wbt_low[...] = low
     for c in range(2):
@@ -118,7 +124,6 @@
     for copy in copies:
         copy.wait()
     lap_own[...] = dot(beside(dense, 2, blocks, blocks), own[...])
-    vel_copy.wait()
 
 
 def first_lap_kernel(dense, lap_own, low, high, lap):
@@ -206,14 +211,12 @@
     nodes, nfield, levels = fields.shape
     blocks, _, size, _ = operators.shape
     modes = basis.shape[1]
-    tiles, rads = lax.axis_size("tile"), lax.axis_size("rad")
+    rads = lax.axis_size("rad")
     fields = fields.reshape(nodes, levels)
     velocity = velocity.reshape(2 * nodes, levels)
     wide = shape((nodes, levels), F32)
     thin = shape((nodes, levels), BF)
 
-    ratio = degree.astype(F32) / DEGMAX
-    gain = 0.5 * jnp.sqrt(F32(modes) / (nodes * tiles)) * (1.0 - jnp.exp(-4.0 * ratio * ratio))
     dhat = cheb_matrix(rads * levels)
     dhat = np.stack([dhat[:, c * levels : (c + 1) * levels] for c in range(rads)])
     dh_high = dhat.astype(BF)
@@ -227,9 +230,15 @@
         + (shape((modes, nodes), BF),) * 2
         + (shape((2, nodes, modes // 2), BF),) * 2
         + (shape((2 * nodes, levels), F32),),
-        (neighbours, operators, basis, velocity, quad_weight[None, :], gain[None, :], rounded),
-        "shhhvvv",
-        (pltpu.VMEM((nodes, modes), F32), pltpu.SemaphoreType.DMA((2,)), pltpu.SemaphoreType.DMA(neighbours.shape)),
+        (neighbours, operators, basis, velocity, quad_weight[None, :], degree[None, :], rounded),
+        "shhhhhv",
+        (
+            pltpu.VMEM((nodes, modes), F32),
+            pltpu.VMEM((1, nodes), F32),
+            pltpu.VMEM((1, modes), jnp.int32),
+            pltpu.SemaphoreType.DMA((4,)),
+            pltpu.SemaphoreType.DMA(neighbours.shape),
+        ),
     )
     lap = call(first_lap_kernel, thin, (dense, lap_own, low, high))
     low_two, high_two = halo(lap)

time: 47.5 us -> 47.5 us (level)
  other arithmetic: 0.74 us -> 0.05 us
  local copies, waits for them, and re-layouts: 6.02 us -> 6.7 us
    mul x1 -> x0, other arithmetic: 0.69 us -> none  [body(): 0.5 * jnp.sqrt(F32(modes) / (nodes * tiles))]
    unnamed x16 -> x18, local copies, waits for them, and re-layouts: 5.33 us -> 6.02 us
  transfers between devices with their start and end apart: 11 -> 11, of which waited for: 8 -> 8; matrix products, arithmetic and copies ran while one was open for 3% -> 1% of each run, Pallas kernels for 8% -> 8%
where the time goes in v3:
time: 47.5 us; the launch traced here: 47.2 us
  waiting for transfers between devices  19 us (40%)
  starting transfers between devices  13.7 us (29%)
  Pallas kernels  7.54 us (16%)
  local copies, waits for them, and re-layouts  6.7 us (14%)
    pallas_call x9, Pallas kernels, call(): pl.pallas_call(kernel, out_shape=outs, in_specs=[{'s': SMEM, 'h': HBM, 'v...  7.54 us
    ppermute x2, waiting for transfers between devices, tile_sum(): mine = mine + lax.ppermute(mine, 'tile', pairs)  7.27 us
    ppermute x2, starting transfers between devices, halo(): lax.ppermute(block, 'tile', shift('tile', -1))  6.08 us
    unnamed x18, local copies, waits for them, and re-layouts  6.02 us
    ppermute x3, waiting for transfers between devices, body(): lax.ppermute(narrow, 'rad', shift('rad', d))  5.16 us
    ppermute x3, starting transfers between devices, body(): lax.ppermute(narrow, 'rad', shift('rad', d))  4.67 us
    ppermute x2, starting transfers between devices, tile_sum(): mine = mine + lax.ppermute(mine, 'tile', pairs)  2.79 us
    ppermute x2, waiting for transfers between devices, halo(): lax.ppermute(block, 'tile', shift('tile', 1))  2.73 us
  transfers between devices with their start and end apart: 11, of which 8 were waited for; matrix products, arithmetic and copies ran while one was open for 1% of the time, Pallas kernels for 8%

profile of v3, /device:TPU:0, one launch (start us, length us, event | category | flops | bytes accessed | tf_op | source)
XLA Modules:
  0.0 47.2 jit_solution(15971446656379279026)
XLA Ops:
  0.0 0.9 %copy-done.5 = f32[384,1,128]{2,1,0:T(1,128)S(1)} copy-done((f32[384,1,128]{2,1,0:T(1,128)S(1)}, f32[384,1,128]{2,1,0:T(1,128)}, u32[]{:S(2)}) %copy-start.5) | copy-done | bytes 196632
  1.2 3.4 %collective-permute-start.1 = (bf16[384,128]{1,0:T(8,128)(2,1)S(1)}, bf16[384,128]{1,0:T(8,128)(2,1)S(1)}, u32[]{:S(2)}, u32[]{:S(2)}) collective-permute-start(bf16[384,128]{1,0:T(8,128)(2,1)S(1)} %get-tuple-element.19.own), channel_id=1, source_target_pairs={{0,28},{4,0},{8,4},{12,8},{16,12},{20,16},{24,20},{28,24},{1,29},{... | collective-permute-start | bytes 294920 | tf_op jit(solution)/shard_map/ppermute | solution.py:196
  4.6 0.7 %broadcast_in_dim.9.weight = f32[1,384]{1,0:T(1,128)S(1)} reshape(f32[384]{0:T(512)} %param.15) | data formatting | bytes 3072 | tf_op jit(solution)/shard_map/broadcast_in_dim | solution.py:233
  5.3 1.6 %copy-done = bf16[3,3,128,896]{3,2,1,0:T(8,128)(2,1)S(1)} copy-done((bf16[3,3,128,896]{3,2,1,0:T(8,128)(2,1)S(1)}, bf16[3,3,128,896]{3,2,1,0:T(8,128)(2,1)}, u32[]{:S(2)}) %copy-start) | copy-done | bytes 2064408
  6.9 1.1 %copy-done.1 = f32[384,512]{1,0:T(8,128)S(1)} copy-done((f32[384,512]{1,0:T(8,128)S(1)}, f32[384,512]{1,0:T(8,128)}, u32[]{:S(2)}) %copy-start.1) | copy-done | bytes 786456
  8.0 1.0 %copy-done.4 = f32[384,2,128]{2,1,0:T(2,128)S(1)} copy-done((f32[384,2,128]{2,1,0:T(2,128)S(1)}, f32[384,2,128]{2,1,0:T(2,128)}, u32[]{:S(2)}) %copy-start.4) | copy-done | bytes 393240
  9.0 0.7 %copy-done.7 = s32[3,7]{1,0:T(4,128)S(1)} copy-done((s32[3,7]{1,0:T(4,128)S(1)}, s32[3,7]{1,0:T(4,128)}, u32[]{:S(2)}) %copy-start.7) | copy-done | bytes 108
  10.3 2.6 %shard_map.101 = (bf16[3,9,384,128]{3,2,1,0:T(8,128)(2,1)S(1)}, f32[384,128]{1,0:T(8,128)S(1)}, bf16[512,384]{1,0:T(8,128)(2,1)S(1)}, bf16[512,384]{1,0:T(8,128)...) custom-call(s32[3,7]{1,0:T(4,128)S(1)} %copy-done.7, ...), custom_call_target="tpu_custom_call" | custom-call | tf_op jit(solution)/shard_map/pallas_call | solution.py:55
  13.3 2.7 %collective-permute-start.3 = (bf16[384,128]{1,0:T(8,128)(2,1)S(1)}, bf16[384,128]{1,0:T(8,128)(2,1)S(1)}, u32[]{:S(2)}, u32[]{:S(2)}) collective-permute-start(bf16[384,128]{1,0:T(8,128)(2,1)S(1)} %shard_map.102.lap), channel_id=1, source_target_pairs={{0,28},{4,0},{8,4},{12,8},{16,12},{20,16},{24,20},{28,24},{1,29},{... | collective-permute-start | bytes 294920 | tf_op jit(solution)/shard_map/ppermute | solution.py:196
  16.0 0.7 %shard_map.103.part = f32[384,128]{1,0:T(8,128)S(1)} custom-call(bf16[3,9,384,128]{3,2,1,0:T(8,128)(2,1)S(1)} %get-tuple-element.20.dense, bf16[384,128]{1,0:T(8,128)(2,1)S(1)} %collective-permute-done.low, bf16[384,128]{1,0:T(8,128)(2,1)S(1)} %get-tuple-element.19.own, bf16[384,128]{1,0:T(8,128)(2,1)S(1)} %collective-permute-done.1.high, ...), custom_call_target="tpu_custom_call" | custom-call | tf_op jit(solution)/shard_map/pallas_call | solution.py:55
  16.7 1.5 %collective-permute-done.3.high = bf16[384,128]{1,0:T(8,128)(2,1)S(1)} collective-permute-done((bf16[384,128]{1,0:T(8,128)(2,1)S(1)}, bf16[384,128]{1,0:T(8,128)(2,1)S(1)}, u32[]{:S(2)}, u32[]{:S(2)}) %collective-permute-start.3) | collective-permute-done | bytes 98336 | tf_op jit(solution)/shard_map/ppermute | solution.py:196
  18.2 2.7 %collective-permute-done.2.low = bf16[384,128]{1,0:T(8,128)(2,1)S(1)} collective-permute-done((bf16[384,128]{1,0:T(8,128)(2,1)S(1)}, bf16[384,128]{1,0:T(8,128)(2,1)S(1)}, u32[]{:S(2)}, u32[]{:S(2)}) %collective-permute-start.2) | collective-permute-done | bytes 98336 | tf_op jit(solution)/shard_map/ppermute | solution.py:196
  21.2 3.7 %collective-permute-start.6 = (bf16[384,128]{1,0:T(8,128)(2,1)S(1)}, bf16[384,128]{1,0:T(8,128)(2,1)S(1)}, u32[]{:S(2)}, u32[]{:S(2)}) collective-permute-start(bf16[384,128]{1,0:T(8,128)(2,1)S(1)} %get-tuple-element.24.refs_0_), channel_id=1, source_target_pairs={{0,3},{1,0},{2,1},{3,2},{4,7},{5,4},{6,5},{7,6},{8,11},{9,8},{10,9... | collective-permute-start | bytes 294920 | tf_op jit(solution)/shard_map/ppermute | solution.py:247
  24.9 1.0 %collective-permute-start.4 = (bf16[384,128]{1,0:T(8,128)(2,1)S(1)}, bf16[384,128]{1,0:T(8,128)(2,1)S(1)}, u32[]{:S(2)}, u32[]{:S(2)}) collective-permute-start(bf16[384,128]{1,0:T(8,128)(2,1)S(1)} %get-tuple-element.24.refs_0_), channel_id=1, source_target_pairs={{0,1},{1,2},{2,3},{3,0},{4,5},{5,6},{6,7},{7,4},{8,9},{9,10},{10,1... | collective-permute-start | bytes 294920 | tf_op jit(solution)/shard_map/ppermute | solution.py:247
  26.3 1.3 %collective-permute-done.6.refs_3_ = bf16[384,128]{1,0:T(8,128)(2,1)S(1)} collective-permute-done((bf16[384,128]{1,0:T(8,128)(2,1)S(1)}, bf16[384,128]{1,0:T(8,128)(2,1)S(1)}, u32[]{:S(2)}, u32[]{:S(2)}) %collective-permute-start.6) | collective-permute-done | bytes 98336 | tf_op jit(solution)/shard_map/ppermute | solution.py:247
  27.6 3.8 %collective-permute-done.5.refs_2_ = bf16[384,128]{1,0:T(8,128)(2,1)S(1)} collective-permute-done((bf16[384,128]{1,0:T(8,128)(2,1)S(1)}, bf16[384,128]{1,0:T(8,128)(2,1)S(1)}, u32[]{:S(2)}, u32[]{:S(2)}) %collective-permute-start.5) | collective-permute-done | bytes 98336 | tf_op jit(solution)/shard_map/ppermute | solution.py:247
  31.5 1.8 %shard_map.106 = (f32[384,128]{1,0:T(8,128)S(1)}, f32[256,128]{1,0:T(8,128)S(1)}, f32[256,128]{1,0:T(8,128)S(1)}) custom-call(bf16[384,128]{1,0:T(8,128)(2,1)S(1)} %get-tuple-element.24.refs_0_, bf16[384,128]{1,0:T(8,128)(2,1)S(1)} %collective-permute-done.4.refs_1_, bf16[384,128]{1,0:T(8,128)(2,1)S(1)} %collective-permute-done.5.refs_2_, ...), custom_call_target="tpu_custom_call" | custom-call | tf_op jit(solution)/shard_map/pallas_call | solution.py:55
  33.3 1.3 %collective-permute-done.7 = f32[256,128]{1,0:T(8,128)S(1)} collective-permute-done((f32[256,128]{1,0:T(8,128)S(1)}, f32[256,128]{1,0:T(8,128)S(1)}, u32[]{:S(2)}, u32[]{:S(2)}) %collective-permute-start.7) | collective-permute-done | bytes 131104 | tf_op jit(solution)/shard_map/ppermute | solution.py:203
  34.7 1.2 %collective-permute-start.8 = (f32[256,128]{1,0:T(8,128)S(1)}, f32[256,128]{1,0:T(8,128)S(1)}, u32[]{:S(2)}, u32[]{:S(2)}) collective-permute-start(f32[256,128]{1,0:T(8,128)S(1)} %add.9), channel_id=1, source_target_pairs={{0,8},{4,20},{8,0},{12,28},{16,24},{20,4},{24,16},{28,12},{1,9},{5... | collective-permute-start | bytes 393224 | tf_op jit(solution)/shard_map/ppermute | solution.py:206
  35.9 3.8 %collective-permute-done.8 = f32[256,128]{1,0:T(8,128)S(1)} collective-permute-done((f32[256,128]{1,0:T(8,128)S(1)}, f32[256,128]{1,0:T(8,128)S(1)}, u32[]{:S(2)}, u32[]{:S(2)}) %collective-permute-start.8) | collective-permute-done | bytes 131104 | tf_op jit(solution)/shard_map/ppermute | solution.py:206
  39.7 1.6 %collective-permute-start.9 = (f32[256,128]{1,0:T(8,128)S(1)}, f32[256,128]{1,0:T(8,128)S(1)}, u32[]{:S(2)}, u32[]{:S(2)}) collective-permute-start(f32[256,128]{1,0:T(8,128)S(1)} %add.10), channel_id=1, source_target_pairs={{0,16},{4,12},{8,24},{12,4},{16,0},{20,28},{24,8},{28,20},{1,17},{... | collective-permute-start | bytes 393224 | tf_op jit(solution)/shard_map/ppermute | solution.py:206
  41.3 3.5 %collective-permute-done.9 = f32[256,128]{1,0:T(8,128)S(1)} collective-permute-done((f32[256,128]{1,0:T(8,128)S(1)}, f32[256,128]{1,0:T(8,128)S(1)}, u32[]{:S(2)}, u32[]{:S(2)}) %collective-permute-start.9) | collective-permute-done | bytes 131104 | tf_op jit(solution)/shard_map/ppermute | solution.py:206
  45.2 1.1 %collective-permute-done.10.refs_1_ = f32[256,128]{1,0:T(8,128)S(1)} collective-permute-done((f32[256,128]{1,0:T(8,128)S(1)}, f32[256,128]{1,0:T(8,128)S(1)}, u32[]{:S(2)}, u32[]{:S(2)}) %collective-permute-start.10) | collective-permute-done | bytes 131104 | tf_op jit(solution)/shard_map/ppermute | solution.py:207
  46.2 0.9 %shard_map.108 = f32[384,128]{1,0:T(8,128)} custom-call(f32[384,128]{1,0:T(8,128)S(1)} %shard_map.107.refs_0_, f32[256,128]{1,0:T(8,128)S(1)} %collective-permute-done.10.refs_1_, bf16[2,384,256]{2,1,0:T(8,128)(2,1)S(1)} %get-tuple-element.31.refs_2_, bf16[2,384,256]{2,1,0:T(8,128)(2,1)S(1)} %get-tuple-element.32.refs_3_), custom_call_target="tpu_custom_call" | custom-call | tf_op jit(solution)/shard_map/pallas_call | solution.py:55
  (29 shorter events, 2.5 us)
Async XLA Ops:
  0.0 0.9 %copy-start.5 = (f32[384,1,128]{2,1,0:T(1,128)S(1)}, f32[384,1,128]{2,1,0:T(1,128)}, u32[]{:S(2)}) copy-start(f32[384,1,128]{2,1,0:T(1,128)} %param.10) | copy-start | bytes 589828
  1.2 11.8 %collective-permute-start.1 = (bf16[384,128]{1,0:T(8,128)(2,1)S(1)}, bf16[384,128]{1,0:T(8,128)(2,1)S(1)}, u32[]{:S(2)}, u32[]{:S(2)}) collective-permute-start(bf16[384,128]{1,0:T(8,128)(2,1)S(1)} %get-tuple-element.19.own), channel_id=1, source_target_pairs={{0,28},{4,0},{8,4},{12,8},{16,12},{20,16},{24,20},{28,24},{1,29},{... | collective-permute-start | bytes 294920 | tf_op jit(solution)/shard_map/ppermute | solution.py:196
  4.6 8.4 %collective-permute-start = (bf16[384,128]{1,0:T(8,128)(2,1)S(1)}, bf16[384,128]{1,0:T(8,128)(2,1)S(1)}, u32[]{:S(2)}, u32[]{:S(2)}) collective-permute-start(bf16[384,128]{1,0:T(8,128)(2,1)S(1)} %get-tuple-element.19.own), channel_id=1, source_target_pairs={{0,4},{4,8},{8,12},{12,16},{16,20},{20,24},{24,28},{28,0},{1,5},{5... | collective-permute-start | bytes 294920 | tf_op jit(solution)/shard_map/ppermute | solution.py:196
  5.3 1.6 %copy-start = (bf16[3,3,128,896]{3,2,1,0:T(8,128)(2,1)S(1)}, bf16[3,3,128,896]{3,2,1,0:T(8,128)(2,1)}, u32[]{:S(2)}) copy-start(bf16[3,3,128,896]{3,2,1,0:T(8,128)(2,1)} %ops.1) | copy-start | bytes 6193156
  6.9 1.1 %copy-start.1 = (f32[384,512]{1,0:T(8,128)S(1)}, f32[384,512]{1,0:T(8,128)}, u32[]{:S(2)}) copy-start(f32[384,512]{1,0:T(8,128)} %basis.1) | copy-start | bytes 2359300
  8.0 1.0 %copy-start.4 = (f32[384,2,128]{2,1,0:T(2,128)S(1)}, f32[384,2,128]{2,1,0:T(2,128)}, u32[]{:S(2)}) copy-start(f32[384,2,128]{2,1,0:T(2,128)} %param.11) | copy-start | bytes 1179652
  9.0 0.7 %copy-start.7 = (s32[3,7]{1,0:T(4,128)S(1)}, s32[3,7]{1,0:T(4,128)}, u32[]{:S(2)}) copy-start(s32[3,7]{1,0:T(4,128)} %ids.1) | copy-start | bytes 256
  9.7 0.7 %copy-start.8 = (s32[512]{0:T(512)S(1)}, s32[512]{0:T(512)}, u32[]{:S(2)}) copy-start(s32[512]{0:T(512)} %param.17) | copy-start | bytes 6148
  13.3 4.9 %collective-permute-start.3 = (bf16[384,128]{1,0:T(8,128)(2,1)S(1)}, bf16[384,128]{1,0:T(8,128)(2,1)S(1)}, u32[]{:S(2)}, u32[]{:S(2)}) collective-permute-start(bf16[384,128]{1,0:T(8,128)(2,1)S(1)} %shard_map.102.lap), channel_id=1, source_target_pairs={{0,28},{4,0},{8,4},{12,8},{16,12},{20,16},{24,20},{28,24},{1,29},{... | collective-permute-start | bytes 294920 | tf_op jit(solution)/shard_map/ppermute | solution.py:196
  16.0 4.9 %collective-permute-start.2 = (bf16[384,128]{1,0:T(8,128)(2,1)S(1)}, bf16[384,128]{1,0:T(8,128)(2,1)S(1)}, u32[]{:S(2)}, u32[]{:S(2)}) collective-permute-start(bf16[384,128]{1,0:T(8,128)(2,1)S(1)} %shard_map.102.lap), channel_id=1, source_target_pairs={{0,4},{4,8},{8,12},{12,16},{16,20},{20,24},{24,28},{28,0},{1,5},{5... | collective-permute-start | bytes 294920 | tf_op jit(solution)/shard_map/ppermute | solution.py:196
  16.7 14.8 %copy-start.2 = (bf16[4,512,128]{2,1,0:T(8,128)(2,1)S(1)}, bf16[4,512,128]{2,1,0:T(8,128)(2,1)}, u32[]{:S(2)}) copy-start(bf16[4,512,128]{2,1,0:T(8,128)(2,1)} %constant.5.clone.refs_6_) | copy-start | bytes 1572868
  16.7 14.8 %copy-start.3 = (bf16[4,512,128]{2,1,0:T(8,128)(2,1)S(1)}, bf16[4,512,128]{2,1,0:T(8,128)(2,1)}, u32[]{:S(2)}) copy-start(bf16[4,512,128]{2,1,0:T(8,128)(2,1)} %constant.4.clone.refs_5_) | copy-start | bytes 1572868
  16.7 14.8 %copy-start.6 = (f32[512]{0:T(512)S(1)}, f32[512]{0:T(512)}, u32[]{:S(2)}) copy-start(f32[512]{0:T(512)} %param.14) | copy-start | bytes 6148
  21.2 6.4 %collective-permute-start.6 = (bf16[384,128]{1,0:T(8,128)(2,1)S(1)}, bf16[384,128]{1,0:T(8,128)(2,1)S(1)}, u32[]{:S(2)}, u32[]{:S(2)}) collective-permute-start(bf16[384,128]{1,0:T(8,128)(2,1)S(1)} %get-tuple-element.24.refs_0_), channel_id=1, source_target_pairs={{0,3},{1,0},{2,1},{3,2},{4,7},{5,4},{6,5},{7,6},{8,11},{9,8},{10,9... | collective-permute-start | bytes 294920 | tf_op jit(solution)/shard_map/ppermute | solution.py:247
  24.9 6.6 %collective-permute-start.5 = (bf16[384,128]{1,0:T(8,128)(2,1)S(1)}, bf16[384,128]{1,0:T(8,128)(2,1)S(1)}, u32[]{:S(2)}, u32[]{:S(2)}) collective-permute-start(bf16[384,128]{1,0:T(8,128)(2,1)S(1)} %get-tuple-element.24.refs_0_), channel_id=1, source_target_pairs={{0,2},{1,3},{2,0},{3,1},{4,6},{5,7},{6,4},{7,5},{8,10},{9,11},{10,... | collective-permute-start | bytes 294920 | tf_op jit(solution)/shard_map/ppermute | solution.py:247
  24.9 6.6 %collective-permute-start.4 = (bf16[384,128]{1,0:T(8,128)(2,1)S(1)}, bf16[384,128]{1,0:T(8,128)(2,1)S(1)}, u32[]{:S(2)}, u32[]{:S(2)}) collective-permute-start(bf16[384,128]{1,0:T(8,128)(2,1)S(1)} %get-tuple-element.24.refs_0_), channel_id=1, source_target_pairs={{0,1},{1,2},{2,3},{3,0},{4,5},{5,6},{6,7},{7,4},{8,9},{9,10},{10,1... | collective-permute-start | bytes 294920 | tf_op jit(solution)/shard_map/ppermute | solution.py:247
  33.3 1.4 %collective-permute-start.7 = (f32[256,128]{1,0:T(8,128)S(1)}, f32[256,128]{1,0:T(8,128)S(1)}, u32[]{:S(2)}, u32[]{:S(2)}) collective-permute-start(f32[256,128]{1,0:T(8,128)S(1)} %get-tuple-element.30), channel_id=1, source_target_pairs={{0,4},{4,0},{8,12},{12,8},{16,20},{20,16},{24,28},{28,24},{1,5},{5... | collective-permute-start | bytes 393224 | tf_op jit(solution)/shard_map/ppermute | solution.py:203
  34.7 5.0 %collective-permute-start.8 = (f32[256,128]{1,0:T(8,128)S(1)}, f32[256,128]{1,0:T(8,128)S(1)}, u32[]{:S(2)}, u32[]{:S(2)}) collective-permute-start(f32[256,128]{1,0:T(8,128)S(1)} %add.9), channel_id=1, source_target_pairs={{0,8},{4,20},{8,0},{12,28},{16,24},{20,4},{24,16},{28,12},{1,9},{5... | collective-permute-start | bytes 393224 | tf_op jit(solution)/shard_map/ppermute | solution.py:206
  39.7 5.0 %collective-permute-start.9 = (f32[256,128]{1,0:T(8,128)S(1)}, f32[256,128]{1,0:T(8,128)S(1)}, u32[]{:S(2)}, u32[]{:S(2)}) collective-permute-start(f32[256,128]{1,0:T(8,128)S(1)} %add.10), channel_id=1, source_target_pairs={{0,16},{4,12},{8,24},{12,4},{16,0},{20,28},{24,8},{28,20},{1,17},{... | collective-permute-start | bytes 393224 | tf_op jit(solution)/shard_map/ppermute | solution.py:206
  44.8 1.4 %collective-permute-start.10 = (f32[256,128]{1,0:T(8,128)S(1)}, f32[256,128]{1,0:T(8,128)S(1)}, u32[]{:S(2)}, u32[]{:S(2)}) collective-permute-start(f32[256,128]{1,0:T(8,128)S(1)} %add.11.refs_1_), channel_id=1, source_target_pairs={{0,4},{4,0},{8,12},{12,8},{16,20},{20,16},{24,28},{28,24},{1,5},{5... | collective-permute-start | bytes 393224 | tf_op jit(solution)/shard_map/ppermute | solution.py:207

commit v4 on v3

--- a/solution.py
+++ b/solution.py
@@ -52,10 +52,12 @@
 
 
 def call(kernel, outs, args, spaces=None, scratch=()):
+    spaces = spaces or "v" * len(args)
+    args = [pltpu.with_memory_space_constraint(a, pltpu.HBM) if c == "h" else a for a, c in zip(args, spaces)]
     return pl.pallas_call(
         kernel,
         out_shape=outs,
-        in_specs=[{"s": SMEM, "h": HBM, "v": VMEM}[c] for c in spaces or "v" * len(args)],
+        in_specs=[{"s": SMEM, "h": HBM, "v": VMEM}[c] for c in spaces],
         out_specs=jax.tree.map(lambda _: VMEM, outs),
         scratch_shapes=list(scratch),
         compiler_params=PARAMS,

time: 47.5 us -> 43.8 us (0.922)
  local copies, waits for them, and re-layouts: 6.7 us -> 1.95 us
  Pallas kernels: 7.54 us -> 8.72 us
    unnamed x18 -> x8, local copies, waits for them, and re-layouts: 6.02 us -> 0.7 us
    pallas_call x9, Pallas kernels: 7.54 us -> 8.72 us  [call(): pl.pallas_call(kernel, out_shape=outs, in_specs=[{'s': SMEM, 'h': HBM, 'v...]
    broadcast_in_dim x1, local copies, waits for them, and re-layouts: 0.68 us -> 1.24 us  [body(): quad_weight[None, :]]
  transfers between devices with their start and end apart: 11 -> 11, of which waited for: 8 -> 8; matrix products, arithmetic and copies ran while one was open for 1% -> 3% of each run, Pallas kernels for 8% -> 10%
where the time goes in v4:
time: 43.8 us; the launch traced here: 43.6 us
  waiting for transfers between devices  19 us (43%)
  starting transfers between devices  13.7 us (31%)
  Pallas kernels  8.72 us (20%)
  local copies, waits for them, and re-layouts  1.95 us (4%)
    pallas_call x9, Pallas kernels, call(): pl.pallas_call(kernel, out_shape=outs, in_specs=[{'s': SMEM, 'h': HBM, 'v...  8.72 us
    ppermute x2, waiting for transfers between devices, tile_sum(): mine = mine + lax.ppermute(mine, 'tile', pairs)  7.28 us
    ppermute x2, starting transfers between devices, halo(): lax.ppermute(block, 'tile', shift('tile', -1))  6.08 us
    ppermute x3, waiting for transfers between devices, body(): lax.ppermute(narrow, 'rad', shift('rad', d))  5.16 us
    ppermute x3, starting transfers between devices, body(): lax.ppermute(narrow, 'rad', shift('rad', d))  4.67 us
    ppermute x2, starting transfers between devices, tile_sum(): mine = mine + lax.ppermute(mine, 'tile', pairs)  2.78 us
    ppermute x2, waiting for transfers between devices, halo(): lax.ppermute(block, 'tile', shift('tile', 1))  2.73 us
    ppermute x2, waiting for transfers between devices, halo(): lax.ppermute(block, 'tile', shift('tile', -1))  1.47 us
  transfers between devices with their start and end apart: 11, of which 8 were waited for; matrix products, arithmetic and copies ran while one was open for 3% of the time, Pallas kernels for 10%

profile of v4, /device:TPU:0, one launch (start us, length us, event | category | flops | bytes accessed | tf_op | source)
XLA Modules:
  0.0 43.6 jit_solution(88420612551015130)
XLA Ops:
  0.0 0.9 %shard_map.100 = (f32[384,128]{1,0:T(8,128)S(1)}, bf16[384,128]{1,0:T(8,128)(2,1)S(1)}) custom-call(f32[384,128]{1,0:T(8,128)} %bitcast.9), custom_call_target="tpu_custom_call" | custom-call | tf_op jit(solution)/shard_map/pallas_call | solution.py:57
  0.9 3.4 %collective-permute-start.1 = (bf16[384,128]{1,0:T(8,128)(2,1)S(1)}, bf16[384,128]{1,0:T(8,128)(2,1)S(1)}, u32[]{:S(2)}, u32[]{:S(2)}) collective-permute-start(bf16[384,128]{1,0:T(8,128)(2,1)S(1)} %get-tuple-element.19.own), channel_id=1, source_target_pairs={{0,28},{4,0},{8,4},{12,8},{16,12},{20,16},{24,20},{28,24},{1,29},{... | collective-permute-start | bytes 294920 | tf_op jit(solution)/shard_map/ppermute | solution.py:198
  4.3 1.2 %broadcast_in_dim.9.weight = f32[1,384]{1,0:T(1,128)} reshape(f32[384]{0:T(512)} %param.15) | data formatting | bytes 3072 | tf_op jit(solution)/shard_map/broadcast_in_dim | solution.py:235
  5.6 0.7 %copy-done.3 = s32[3,7]{1,0:T(4,128)S(1)} copy-done((s32[3,7]{1,0:T(4,128)S(1)}, s32[3,7]{1,0:T(4,128)}, u32[]{:S(2)}) %copy-start.3) | copy-done | bytes 108
  6.3 3.1 %shard_map.101 = (bf16[3,9,384,128]{3,2,1,0:T(8,128)(2,1)S(1)}, f32[384,128]{1,0:T(8,128)S(1)}, bf16[512,384]{1,0:T(8,128)(2,1)S(1)}, bf16[512,384]{1,0:T(8,128)...) custom-call(s32[3,7]{1,0:T(4,128)S(1)} %copy-done.3, ...), custom_call_target="tpu_custom_call" | custom-call | tf_op jit(solution)/shard_map/pallas_call | solution.py:57
  9.4 0.3 shard_map.102.lap
  9.7 2.7 %collective-permute-start.3 = (bf16[384,128]{1,0:T(8,128)(2,1)S(1)}, bf16[384,128]{1,0:T(8,128)(2,1)S(1)}, u32[]{:S(2)}, u32[]{:S(2)}) collective-permute-start(bf16[384,128]{1,0:T(8,128)(2,1)S(1)} %shard_map.102.lap), channel_id=1, source_target_pairs={{0,28},{4,0},{8,4},{12,8},{16,12},{20,16},{24,20},{28,24},{1,29},{... | collective-permute-start | bytes 294920 | tf_op jit(solution)/shard_map/ppermute | solution.py:198
  12.4 0.7 %shard_map.103.part = f32[384,128]{1,0:T(8,128)S(1)} custom-call(bf16[3,9,384,128]{3,2,1,0:T(8,128)(2,1)S(1)} %get-tuple-element.20.dense, bf16[384,128]{1,0:T(8,128)(2,1)S(1)} %collective-permute-done.low, bf16[384,128]{1,0:T(8,128)(2,1)S(1)} %get-tuple-element.19.own, bf16[384,128]{1,0:T(8,128)(2,1)S(1)} %collective-permute-done.1.high, ...), custom_call_target="tpu_custom_call" | custom-call | tf_op jit(solution)/shard_map/pallas_call | solution.py:57
  13.1 1.5 %collective-permute-done.3.high = bf16[384,128]{1,0:T(8,128)(2,1)S(1)} collective-permute-done((bf16[384,128]{1,0:T(8,128)(2,1)S(1)}, bf16[384,128]{1,0:T(8,128)(2,1)S(1)}, u32[]{:S(2)}, u32[]{:S(2)}) %collective-permute-start.3) | collective-permute-done | bytes 98336 | tf_op jit(solution)/shard_map/ppermute | solution.py:198
  14.6 2.7 %collective-permute-done.2.low = bf16[384,128]{1,0:T(8,128)(2,1)S(1)} collective-permute-done((bf16[384,128]{1,0:T(8,128)(2,1)S(1)}, bf16[384,128]{1,0:T(8,128)(2,1)S(1)}, u32[]{:S(2)}, u32[]{:S(2)}) %collective-permute-start.2) | collective-permute-done | bytes 98336 | tf_op jit(solution)/shard_map/ppermute | solution.py:198
  17.3 0.3 shard_map.104
  17.6 3.7 %collective-permute-start.6 = (bf16[384,128]{1,0:T(8,128)(2,1)S(1)}, bf16[384,128]{1,0:T(8,128)(2,1)S(1)}, u32[]{:S(2)}, u32[]{:S(2)}) collective-permute-start(bf16[384,128]{1,0:T(8,128)(2,1)S(1)} %get-tuple-element.24.refs_0_), channel_id=1, source_target_pairs={{0,3},{1,0},{2,1},{3,2},{4,7},{5,4},{6,5},{7,6},{8,11},{9,8},{10,9... | collective-permute-start | bytes 294920 | tf_op jit(solution)/shard_map/ppermute | solution.py:249
  21.3 1.0 %collective-permute-start.4 = (bf16[384,128]{1,0:T(8,128)(2,1)S(1)}, bf16[384,128]{1,0:T(8,128)(2,1)S(1)}, u32[]{:S(2)}, u32[]{:S(2)}) collective-permute-start(bf16[384,128]{1,0:T(8,128)(2,1)S(1)} %get-tuple-element.24.refs_0_), channel_id=1, source_target_pairs={{0,1},{1,2},{2,3},{3,0},{4,5},{5,6},{6,7},{7,4},{8,9},{9,10},{10,1... | collective-permute-start | bytes 294920 | tf_op jit(solution)/shard_map/ppermute | solution.py:249
  22.3 0.4 shard_map.105.refs_10_
  22.7 1.3 %collective-permute-done.6.refs_3_ = bf16[384,128]{1,0:T(8,128)(2,1)S(1)} collective-permute-done((bf16[384,128]{1,0:T(8,128)(2,1)S(1)}, bf16[384,128]{1,0:T(8,128)(2,1)S(1)}, u32[]{:S(2)}, u32[]{:S(2)}) %collective-permute-start.6) | collective-permute-done | bytes 98336 | tf_op jit(solution)/shard_map/ppermute | solution.py:249
  24.0 3.8 %collective-permute-done.5.refs_2_ = bf16[384,128]{1,0:T(8,128)(2,1)S(1)} collective-permute-done((bf16[384,128]{1,0:T(8,128)(2,1)S(1)}, bf16[384,128]{1,0:T(8,128)(2,1)S(1)}, u32[]{:S(2)}, u32[]{:S(2)}) %collective-permute-start.5) | collective-permute-done | bytes 98336 | tf_op jit(solution)/shard_map/ppermute | solution.py:249
  27.9 1.8 %shard_map.106 = (f32[384,128]{1,0:T(8,128)S(1)}, f32[256,128]{1,0:T(8,128)S(1)}, f32[256,128]{1,0:T(8,128)S(1)}) custom-call(bf16[384,128]{1,0:T(8,128)(2,1)S(1)} %get-tuple-element.24.refs_0_, bf16[384,128]{1,0:T(8,128)(2,1)S(1)} %collective-permute-done.4.refs_1_, bf16[384,128]{1,0:T(8,128)(2,1)S(1)} %collective-permute-done.5.refs_2_, ...), custom_call_target="tpu_custom_call" | custom-call | tf_op jit(solution)/shard_map/pallas_call | solution.py:57
  29.7 1.3 %collective-permute-done.7 = f32[256,128]{1,0:T(8,128)S(1)} collective-permute-done((f32[256,128]{1,0:T(8,128)S(1)}, f32[256,128]{1,0:T(8,128)S(1)}, u32[]{:S(2)}, u32[]{:S(2)}) %collective-permute-start.7) | collective-permute-done | bytes 131104 | tf_op jit(solution)/shard_map/ppermute | solution.py:205
  31.1 1.2 %collective-permute-start.8 = (f32[256,128]{1,0:T(8,128)S(1)}, f32[256,128]{1,0:T(8,128)S(1)}, u32[]{:S(2)}, u32[]{:S(2)}) collective-permute-start(f32[256,128]{1,0:T(8,128)S(1)} %add.9), channel_id=1, source_target_pairs={{0,8},{4,20},{8,0},{12,28},{16,24},{20,4},{24,16},{28,12},{1,9},{5... | collective-permute-start | bytes 393224 | tf_op jit(solution)/shard_map/ppermute | solution.py:208
  32.3 3.8 %collective-permute-done.8 = f32[256,128]{1,0:T(8,128)S(1)} collective-permute-done((f32[256,128]{1,0:T(8,128)S(1)}, f32[256,128]{1,0:T(8,128)S(1)}, u32[]{:S(2)}, u32[]{:S(2)}) %collective-permute-start.8) | collective-permute-done | bytes 131104 | tf_op jit(solution)/shard_map/ppermute | solution.py:208
  36.2 1.6 %collective-permute-start.9 = (f32[256,128]{1,0:T(8,128)S(1)}, f32[256,128]{1,0:T(8,128)S(1)}, u32[]{:S(2)}, u32[]{:S(2)}) collective-permute-start(f32[256,128]{1,0:T(8,128)S(1)} %add.10), channel_id=1, source_target_pairs={{0,16},{4,12},{8,24},{12,4},{16,0},{20,28},{24,8},{28,20},{1,17},{... | collective-permute-start | bytes 393224 | tf_op jit(solution)/shard_map/ppermute | solution.py:208
  37.7 3.5 %collective-permute-done.9 = f32[256,128]{1,0:T(8,128)S(1)} collective-permute-done((f32[256,128]{1,0:T(8,128)S(1)}, f32[256,128]{1,0:T(8,128)S(1)}, u32[]{:S(2)}, u32[]{:S(2)}) %collective-permute-start.9) | collective-permute-done | bytes 131104 | tf_op jit(solution)/shard_map/ppermute | solution.py:208
  41.6 1.1 %collective-permute-done.10.refs_1_ = f32[256,128]{1,0:T(8,128)S(1)} collective-permute-done((f32[256,128]{1,0:T(8,128)S(1)}, f32[256,128]{1,0:T(8,128)S(1)}, u32[]{:S(2)}, u32[]{:S(2)}) %collective-permute-start.10) | collective-permute-done | bytes 131104 | tf_op jit(solution)/shard_map/ppermute | solution.py:209
  42.6 0.9 %shard_map.108 = f32[384,128]{1,0:T(8,128)} custom-call(f32[384,128]{1,0:T(8,128)S(1)} %shard_map.107.refs_0_, f32[256,128]{1,0:T(8,128)S(1)} %collective-permute-done.10.refs_1_, bf16[2,384,256]{2,1,0:T(8,128)(2,1)S(1)} %get-tuple-element.31.refs_2_, bf16[2,384,256]{2,1,0:T(8,128)(2,1)S(1)} %get-tuple-element.32.refs_3_), custom_call_target="tpu_custom_call" | custom-call | tf_op jit(solution)/shard_map/pallas_call | solution.py:57
  (19 shorter events, 0.5 us)
Async XLA Ops:
  0.9 8.4 %collective-permute-start.1 = (bf16[384,128]{1,0:T(8,128)(2,1)S(1)}, bf16[384,128]{1,0:T(8,128)(2,1)S(1)}, u32[]{:S(2)}, u32[]{:S(2)}) collective-permute-start(bf16[384,128]{1,0:T(8,128)(2,1)S(1)} %get-tuple-element.19.own), channel_id=1, source_target_pairs={{0,28},{4,0},{8,4},{12,8},{16,12},{20,16},{24,20},{28,24},{1,29},{... | collective-permute-start | bytes 294920 | tf_op jit(solution)/shard_map/ppermute | solution.py:198
  4.3 5.0 %collective-permute-start = (bf16[384,128]{1,0:T(8,128)(2,1)S(1)}, bf16[384,128]{1,0:T(8,128)(2,1)S(1)}, u32[]{:S(2)}, u32[]{:S(2)}) collective-permute-start(bf16[384,128]{1,0:T(8,128)(2,1)S(1)} %get-tuple-element.19.own), channel_id=1, source_target_pairs={{0,4},{4,8},{8,12},{12,16},{16,20},{20,24},{24,28},{28,0},{1,5},{5... | collective-permute-start | bytes 294920 | tf_op jit(solution)/shard_map/ppermute | solution.py:198
  5.6 0.7 %copy-start.3 = (s32[3,7]{1,0:T(4,128)S(1)}, s32[3,7]{1,0:T(4,128)}, u32[]{:S(2)}) copy-start(s32[3,7]{1,0:T(4,128)} %ids.1) | copy-start | bytes 256
  9.7 4.9 %collective-permute-start.3 = (bf16[384,128]{1,0:T(8,128)(2,1)S(1)}, bf16[384,128]{1,0:T(8,128)(2,1)S(1)}, u32[]{:S(2)}, u32[]{:S(2)}) collective-permute-start(bf16[384,128]{1,0:T(8,128)(2,1)S(1)} %shard_map.102.lap), channel_id=1, source_target_pairs={{0,28},{4,0},{8,4},{12,8},{16,12},{20,16},{24,20},{28,24},{1,29},{... | collective-permute-start | bytes 294920 | tf_op jit(solution)/shard_map/ppermute | solution.py:198
  12.4 4.9 %collective-permute-start.2 = (bf16[384,128]{1,0:T(8,128)(2,1)S(1)}, bf16[384,128]{1,0:T(8,128)(2,1)S(1)}, u32[]{:S(2)}, u32[]{:S(2)}) collective-permute-start(bf16[384,128]{1,0:T(8,128)(2,1)S(1)} %shard_map.102.lap), channel_id=1, source_target_pairs={{0,4},{4,8},{8,12},{12,16},{16,20},{20,24},{24,28},{28,0},{1,5},{5... | collective-permute-start | bytes 294920 | tf_op jit(solution)/shard_map/ppermute | solution.py:198
  13.1 14.8 %copy-start = (bf16[4,512,128]{2,1,0:T(8,128)(2,1)S(1)}, bf16[4,512,128]{2,1,0:T(8,128)(2,1)}, u32[]{:S(2)}) copy-start(bf16[4,512,128]{2,1,0:T(8,128)(2,1)} %constant.5.clone.refs_6_) | copy-start | bytes 1572868
  13.1 14.8 %copy-start.1 = (bf16[4,512,128]{2,1,0:T(8,128)(2,1)S(1)}, bf16[4,512,128]{2,1,0:T(8,128)(2,1)}, u32[]{:S(2)}) copy-start(bf16[4,512,128]{2,1,0:T(8,128)(2,1)} %constant.4.clone.refs_5_) | copy-start | bytes 1572868
  13.1 14.8 %copy-start.2 = (f32[512]{0:T(512)S(1)}, f32[512]{0:T(512)}, u32[]{:S(2)}) copy-start(f32[512]{0:T(512)} %param.14) | copy-start | bytes 6148
  17.6 6.4 %collective-permute-start.6 = (bf16[384,128]{1,0:T(8,128)(2,1)S(1)}, bf16[384,128]{1,0:T(8,128)(2,1)S(1)}, u32[]{:S(2)}, u32[]{:S(2)}) collective-permute-start(bf16[384,128]{1,0:T(8,128)(2,1)S(1)} %get-tuple-element.24.refs_0_), channel_id=1, source_target_pairs={{0,3},{1,0},{2,1},{3,2},{4,7},{5,4},{6,5},{7,6},{8,11},{9,8},{10,9... | collective-permute-start | bytes 294920 | tf_op jit(solution)/shard_map/ppermute | solution.py:249
  21.3 6.6 %collective-permute-start.5 = (bf16[384,128]{1,0:T(8,128)(2,1)S(1)}, bf16[384,128]{1,0:T(8,128)(2,1)S(1)}, u32[]{:S(2)}, u32[]{:S(2)}) collective-permute-start(bf16[384,128]{1,0:T(8,128)(2,1)S(1)} %get-tuple-element.24.refs_0_), channel_id=1, source_target_pairs={{0,2},{1,3},{2,0},{3,1},{4,6},{5,7},{6,4},{7,5},{8,10},{9,11},{10,... | collective-permute-start | bytes 294920 | tf_op jit(solution)/shard_map/ppermute | solution.py:249
  21.3 6.6 %collective-permute-start.4 = (bf16[384,128]{1,0:T(8,128)(2,1)S(1)}, bf16[384,128]{1,0:T(8,128)(2,1)S(1)}, u32[]{:S(2)}, u32[]{:S(2)}) collective-permute-start(bf16[384,128]{1,0:T(8,128)(2,1)S(1)} %get-tuple-element.24.refs_0_), channel_id=1, source_target_pairs={{0,1},{1,2},{2,3},{3,0},{4,5},{5,6},{6,7},{7,4},{8,9},{9,10},{10,1... | collective-permute-start | bytes 294920 | tf_op jit(solution)/shard_map/ppermute | solution.py:249
  29.7 1.4 %collective-permute-start.7 = (f32[256,128]{1,0:T(8,128)S(1)}, f32[256,128]{1,0:T(8,128)S(1)}, u32[]{:S(2)}, u32[]{:S(2)}) collective-permute-start(f32[256,128]{1,0:T(8,128)S(1)} %get-tuple-element.30), channel_id=1, source_target_pairs={{0,4},{4,0},{8,12},{12,8},{16,20},{20,16},{24,28},{28,24},{1,5},{5... | collective-permute-start | bytes 393224 | tf_op jit(solution)/shard_map/ppermute | solution.py:205
  31.1 5.0 %collective-permute-start.8 = (f32[256,128]{1,0:T(8,128)S(1)}, f32[256,128]{1,0:T(8,128)S(1)}, u32[]{:S(2)}, u32[]{:S(2)}) collective-permute-start(f32[256,128]{1,0:T(8,128)S(1)} %add.9), channel_id=1, source_target_pairs={{0,8},{4,20},{8,0},{12,28},{16,24},{20,4},{24,16},{28,12},{1,9},{5... | collective-permute-start | bytes 393224 | tf_op jit(solution)/shard_map/ppermute | solution.py:208
  36.2 5.0 %collective-permute-start.9 = (f32[256,128]{1,0:T(8,128)S(1)}, f32[256,128]{1,0:T(8,128)S(1)}, u32[]{:S(2)}, u32[]{:S(2)}) collective-permute-start(f32[256,128]{1,0:T(8,128)S(1)} %add.10), channel_id=1, source_target_pairs={{0,16},{4,12},{8,24},{12,4},{16,0},{20,28},{24,8},{28,20},{1,17},{... | collective-permute-start | bytes 393224 | tf_op jit(solution)/shard_map/ppermute | solution.py:208
  41.2 1.4 %collective-permute-start.10 = (f32[256,128]{1,0:T(8,128)S(1)}, f32[256,128]{1,0:T(8,128)S(1)}, u32[]{:S(2)}, u32[]{:S(2)}) collective-permute-start(f32[256,128]{1,0:T(8,128)S(1)} %add.11.refs_1_), channel_id=1, source_target_pairs={{0,4},{4,0},{8,12},{12,8},{16,20},{20,16},{24,28},{28,24},{1,5},{5... | collective-permute-start | bytes 393224 | tf_op jit(solution)/shard_map/ppermute | solution.py:209

commit v5 on v4

v5 whole, which is shorter than its diff:
```python
import math

import jax
import jax.numpy as jnp
import numpy as np
from jax import lax
from jax.experimental import pallas as pl
from jax.experimental.pallas import tpu as pltpu
from jax.sharding import PartitionSpec as P

DEGMAX = 22

advect_step = 0.25
hyper_rate = 0.1
radial_step = 0.25

BF = jnp.bfloat16
F32 = jnp.float32
VMEM = pl.BlockSpec(memory_space=pltpu.VMEM)
SMEM = pl.BlockSpec(memory_space=pltpu.SMEM)
HBM = pl.BlockSpec(memory_space=pltpu.HBM)
PARAMS = pltpu.CompilerParams(vmem_limit_bytes=32 * 1024 * 1024)


def cheb_matrix(count):
    points = np.arange(count)
    angles = np.pi * points / (count - 1)
    upper, lower = angles[:, None], angles[None, :]
    spacing = -2.0 * np.sin((upper + lower) / 2.0) * np.sin((upper - lower) / 2.0)
    np.fill_diagonal(spacing, 1.0)
    weights = np.where((points == 0) | (points == count - 1), 2.0, 1.0)
    parity = np.where((upper * 0 + points[:, None] + points[None, :]) % 2 == 0, 1.0, -1.0)
    entries = weights[:, None] / weights[None, :] * parity / spacing
    np.fill_diagonal(entries, 0.0)
    matrix = entries - np.diag(entries.sum(axis=1))
    return (np.sin(angles)[:, None] * matrix / count).T.astype(np.float32)


def split(value):
    high = value.astype(BF)
    return high, (value - high.astype(F32)).astype(BF)


def dot(left, right):
    return jnp.dot(left, right, preferred_element_type=F32)


def dot3(left, right):
    wide = dot(left[0], jnp.concatenate(right, axis=1))
    count = right[0].shape[1]
    return wide[:, :count] + (wide[:, count:] + dot(left[1], right[0]))


def call(kernel, outs, args, spaces=None, scratch=()):
    spaces = spaces or "v" * len(args)
    args = [pltpu.with_memory_space_constraint(a, pltpu.HBM) if c == "h" else a for a, c in zip(args, spaces)]
    return pl.pallas_call(
        kernel,
        out_shape=outs,
        in_specs=[{"s": SMEM, "h": HBM, "v": VMEM}[c] for c in spaces],
        out_specs=jax.tree.map(lambda _: VMEM, outs),
        scratch_shapes=list(scratch),
        compiler_params=PARAMS,
    )(*args)


def shape(dims, kind):
    return jax.ShapeDtypeStruct(dims, kind)


def beside(dense, first, count):
    return jnp.concatenate([dense[first + s] for s in range(count)], axis=1)


def stencil_copies(ids, ops, kinds, dense, sems):
    blocks, _, size, wide = ops.shape
    total = blocks * lax.axis_size("tile")
    first = (lax.axis_index("tile") - 1) * blocks
    dense[...] = jnp.zeros(dense.shape, BF)
    copies = []
    for b in range(blocks):
        for k in range(wide // size):
            source = lax.rem(ids[b, k] - first + total, total)
            copy = pltpu.make_async_copy(
                ops.at[b, kinds, :, pl.ds(k * size, size)],
                dense.at[:, source, pl.ds(b * size, size), :],
                sems.at[b, k],
            )
            copy.start()
            copies.append(copy)
    return copies


def round_kernel(fields, neighbours, wide, narrow, ids, sems, ids_sem):
    parts = sems.shape[0]
    rows = wide.shape[0] // parts
    copies = []
    for p in range(parts):
        piece = pl.ds(p * rows, rows)
        copies.append(pltpu.make_async_copy(fields.at[piece], wide.at[piece], sems.at[p]))
        copies[-1].start()
    ids_copy = pltpu.make_async_copy(neighbours, ids, ids_sem)
    ids_copy.start()
    for p in range(parts):
        copies[p].wait()
        piece = slice(p * rows, (p + 1) * rows)
        narrow[piece] = wide[piece].astype(BF)
    ids_copy.wait()


def prepare_kernel(ids, ops, own, dense, lap_own, sems):
    blocks = ops.shape[0]
    for copy in stencil_copies(ids, ops, pl.ds(2, 1), dense, sems):
        copy.wait()
    lap_own[...] = dot(beside(dense.at[0], blocks, blocks), own[...])


def around(dense, low, high):
    blocks = dense.shape[0] // 3
    return dot(beside(dense, 0, blocks), low[...]) + dot(beside(dense, 2 * blocks, blocks), high[...])


def first_lap_kernel(dense, lap_own, low, high, lap):
    lap[...] = (lap_own[...] + around(dense.at[0], low, high)).astype(BF)


def advect_kernel(ids, ops, velocity, basis, weight, degree, lap_dense, low, own, high, lap, fields,
                  out, wbt_high, wbt_low, bg_high, bg_low, dense, vel, held, weight_held, degree_held, sems, op_sems):
    blocks = ops.shape[0]
    nodes, modes = held.shape
    pairs = ((basis, held), (weight, weight_held), (degree, degree_held), (velocity, vel))
    held_copies = [pltpu.make_async_copy(*pair, sems.at[k]) for k, pair in enumerate(pairs)]
    for copy in held_copies:
        copy.start()
    copies = stencil_copies(ids, ops, pl.ds(0, 2), dense, op_sems)
    for copy in held_copies:
        copy.wait()
    ratio = degree_held[...].astype(F32) / DEGMAX
    gain = 0.5 * math.sqrt(modes / (nodes * lax.axis_size("tile"))) * (1.0 - jnp.exp(-4.0 * ratio * ratio))
    half = modes // 2
    for c in range(2):
        cols = slice(c * half, (c + 1) * half)
        high_part, low_part = split(held[:, cols] * gain[:, cols])
        bg_high[c] = high_part
        bg_low[c] = low_part
    high_part, low_part = split(held[...].T * weight_held[...])
    wbt_high[...] = high_part
    wbt_low[...] = low_part
    for copy in copies:
        copy.wait()
    value = fields[...] - hyper_rate * dot(beside(lap_dense.at[0], blocks, blocks), lap[...])
    for k in range(2):
        grad = dot(beside(dense.at[k], blocks, blocks), own[...]) + around(dense.at[k], low, high)
        value = value - advect_step * (vel[pl.ds(k, nodes, stride=2), :] * grad)
    out[...] = value


def second_lap_kernel(dense, low, high, part, stepped, narrow):
    value = part[...] - hyper_rate * around(dense.at[0], low, high)
    stepped[...] = value
    narrow[...] = value.astype(BF)


def project_kernel(wbt_high, wbt_low, value, out):
    out[...] = dot3((wbt_high[...], wbt_low[...]), split(value[...]))


def diffuse_kernel(count, *refs):
    shards = refs[:count]
    stepped, dh_high, dh_low, kappa, wbt, early, diffused, keep, send = refs[count:]
    rad, core = lax.axis_index("rad"), lax.rem(lax.axis_index("tile"), 2)
    width = stepped.shape[1]
    chunk = [lax.rem(rad + count - d, count) for d in range(count)]
    rows = [pl.ds(pl.multiple_of(c * width, width), width) for c in chunk]
    value = jnp.concatenate([shard[...] for shard in shards], axis=1)
    term = None
    group = 2 if count % 2 == 0 else 1
    for first in range(0, count, group):
        some = range(first, first + group)
        slopes = None
        for table in (dh_high, dh_low):
            weights = [jnp.concatenate([table[chunk[i], rows[j], :] for j in range(count)], axis=0) for i in some]
            more = dot(value, jnp.concatenate(weights, axis=1))
            slopes = more if slopes is None else slopes + more
        rate = jnp.concatenate([kappa[chunk[i]] for i in some], axis=1)
        bend = jnp.tanh(value[:, first * width : (first + group) * width].astype(F32))
        fluxes = (rate + (0.5 * rate) * bend) * slopes
        own = [jnp.concatenate([table[rad, rows[i], :] for i in some], axis=0) for table in (dh_high, dh_low)]
        more = dot3(split(fluxes), own)
        term = more if term is None else term + more
    term = radial_step * term
    diffused[...] = stepped[...] + term
    late = jnp.concatenate(split(term), axis=1)
    half = keep.shape[0]
    for out, which in ((send, 1 - core), (keep, core)):
        modes = pl.ds(pl.multiple_of(which * half, half), half)
        total = dot(wbt[modes, :], late)
        out[...] = early[modes, :] + total[:, :width] + total[:, width:]


def filter_kernel(swap, value, modes, bg_high, bg_low, out):
    which = lax.rem(lax.axis_index("tile") + swap, 2)
    out[...] = value[...] - dot3((bg_high[which], bg_low[which]), split(modes[...]))


def shift(axis, by):
    count = lax.axis_size(axis)
    return [(i, (i + by) % count) for i in range(count)]


def halo(block):
    return lax.ppermute(block, "tile", shift("tile", 1)), lax.ppermute(block, "tile", shift("tile", -1))


def swap(block):
    return lax.ppermute(block, "tile", [(i, i ^ 1) for i in range(lax.axis_size("tile"))])


def chip_sum(block):
    count = lax.axis_size("tile")
    bits = [1 << k for k in range(1, count.bit_length() - 1)]
    for k in range(len(bits)):
        pairs = [(i, i ^ bits[(k + i % 2) % len(bits)]) for i in range(count)]
        block = block + lax.ppermute(block, "tile", pairs)
    return block


def body(fields, velocity, operators, neighbours, kappa_ref, quad_weight, basis, degree):
    nodes, nfield, levels = fields.shape
    blocks, _, size, _ = operators.shape
    modes = basis.shape[1]
    rads = lax.axis_size("rad")
    fields = fields.reshape(nodes, levels)
    velocity = velocity.reshape(2 * nodes, levels)
    wide = shape((nodes, levels), F32)
    thin = shape((nodes, levels), BF)

    dhat = cheb_matrix(rads * levels)
    dhat = np.stack([dhat[:, c * levels : (c + 1) * levels] for c in range(rads)])
    dh_high = dhat.astype(BF)
    dh_low = (dhat - dh_high.astype(np.float32)).astype(BF)

    half = shape((modes // 2, levels), F32)
    dma = pltpu.SemaphoreType.DMA
    fields, rounded, ids = call(
        round_kernel,
        (wide, thin, shape(neighbours.shape, neighbours.dtype)),
        (fields, neighbours),
        "hh",
        (dma((3,)), dma(())),
    )
    low, high = halo(rounded)
    lap_dense, lap_own = call(
        prepare_kernel,
        (shape((1, 3 * blocks, nodes, size), BF), wide),
        (ids, operators, rounded),
        "shv",
        (dma(neighbours.shape),),
    )
    lap = call(first_lap_kernel, thin, (lap_dense, lap_own, low, high))
    low_two, high_two = halo(lap)
    part, wbt_high, wbt_low, bg_high, bg_low = call(
        advect_kernel,
        (wide,) + (shape((modes, nodes), BF),) * 2 + (shape((2, nodes, modes // 2), BF),) * 2,
        (ids, operators, velocity, basis, quad_weight[None, :], degree[None, :])
        + (lap_dense, low, rounded, high, lap, fields),
        "shhhhhvvvvvv",
        (
            pltpu.VMEM((2, 3 * blocks, nodes, size), BF),
            pltpu.VMEM((2 * nodes, levels), F32),
            pltpu.VMEM((nodes, modes), F32),
            pltpu.VMEM((1, nodes), F32),
            pltpu.VMEM((1, modes), jnp.int32),
            dma((4,)),
            dma(neighbours.shape),
        ),
    )
    stepped, narrow = call(second_lap_kernel, (wide, thin), (lap_dense, low_two, high_two, part))
    shards = [narrow] + [lax.ppermute(narrow, "rad", shift("rad", d)) for d in range(1, rads)]
    early = call(project_kernel, shape((modes, levels), F32), (wbt_high, wbt_low, stepped))
    diffused, keep, send = call(
        lambda *refs: diffuse_kernel(rads, *refs),
        (wide, half, half),
        (*shards, stepped, jnp.asarray(dh_high), jnp.asarray(dh_low), kappa_ref.reshape(rads, 1, levels))
        + (wbt_high, early),
    )
    mine = chip_sum(keep + swap(send))
    other = swap(mine)
    some = call(lambda *refs: filter_kernel(0, *refs), wide, (diffused, mine, bg_high, bg_low))
    filtered = call(lambda *refs: filter_kernel(1, *refs), wide, (some, other, bg_high, bg_low))
    return filtered.reshape(nodes, nfield, levels)


def solution(mesh):
    return jax.shard_map(
        body,
        mesh=mesh,
        in_specs=(
            P("tile", None, "rad"),
            P("tile", None, "rad"),
            P("tile", None, None, None),
            P("tile", None),
            P(),
            P("tile"),
            P("tile", None),
            P(),
        ),
        out_specs=P("tile", None, "rad"),
        check_vma=False,
    )
```

time: 43.8 us -> 41.3 us (0.943)
  waiting for transfers between devices: 19 us -> 14.4 us
  starting transfers between devices: 13.7 us -> 15.5 us
  Pallas kernels: 8.72 us -> 10.3 us
  local copies, waits for them, and re-layouts: 1.95 us -> 0.59 us
    ppermute x2, waiting for transfers between devices: 2.73 us -> 0.05 us  [halo(): lax.ppermute(block, 'tile', shift('tile', 1))]
    ppermute x2, starting transfers between devices: 0.01 us -> 2.24 us  [halo(): lax.ppermute(block, 'tile', shift('tile', 1))]
    ppermute x2, starting transfers between devices: 6.08 us -> 4.05 us  [halo(): lax.ppermute(block, 'tile', shift('tile', -1))]
    ppermute x3, starting transfers between devices: 4.67 us -> 6.25 us  [body(): lax.ppermute(narrow, 'rad', shift('rad', d))]
    pallas_call x9, Pallas kernels: 8.72 us -> 10.3 us  [call(): pl.pallas_call(kernel, out_shape=outs, in_specs=[{'s': SMEM, 'h': HBM, 'v...]
    ppermute x2, waiting for transfers between devices: 1.47 us -> 0.01 us  [halo(): lax.ppermute(block, 'tile', shift('tile', -1))]
    broadcast_in_dim x1, local copies, waits for them, and re-layouts: 1.24 us -> 0.56 us  [body(): quad_weight[None, :]]
    unnamed x8, local copies, waits for them, and re-layouts: 0.7 us -> 0.02 us
  transfers between devices with their start and end apart: 11 -> 11, of which waited for: 8 -> 7; matrix products, arithmetic and copies ran while one was open for 3% -> 1% of each run, Pallas kernels for 10% -> 15%
where the time goes in v5:
time: 41.3 us; the launch traced here: 40.9 us
  starting transfers between devices  15.5 us (38%)
  waiting for transfers between devices  14.4 us (35%)
  Pallas kernels  10.3 us (25%)
  local copies, waits for them, and re-layouts  0.59 us (1%)
    pallas_call x9, Pallas kernels, call(): pl.pallas_call(kernel, out_shape=outs, in_specs=[{'s': SMEM, 'h': HBM, 'v...  10.3 us
    ppermute x2, waiting for transfers between devices, chip_sum(): block = block + lax.ppermute(block, 'tile', pairs)  7.25 us
    ppermute x3, starting transfers between devices, body(): lax.ppermute(narrow, 'rad', shift('rad', d))  6.25 us
    ppermute x3, waiting for transfers between devices, body(): lax.ppermute(narrow, 'rad', shift('rad', d))  4.7 us
    ppermute x2, starting transfers between devices, halo(): lax.ppermute(block, 'tile', shift('tile', -1))  4.05 us
    ppermute x2, starting transfers between devices, chip_sum(): block = block + lax.ppermute(block, 'tile', pairs)  2.81 us
    ppermute x2, waiting for transfers between devices, swap(): lax.ppermute(block, 'tile', [(i, i ^ 1) for i in range(lax.axis_size('til...  2.4 us
    ppermute x2, starting transfers between devices, halo(): lax.ppermute(block, 'tile', shift('tile', 1))  2.24 us
  transfers between devices with their start and end apart: 11, of which 7 were waited for; matrix products, arithmetic and copies ran while one was open for 1% of the time, Pallas kernels for 15%

profile of v5, /device:TPU:0, one launch (start us, length us, event | category | flops | bytes accessed | tf_op | source)
XLA Modules:
  0.0 40.9 jit_solution(529192290924635668)
XLA Ops:
  0.0 1.0 %shard_map.100 = (f32[384,128]{1,0:T(8,128)S(1)}, bf16[384,128]{1,0:T(8,128)(2,1)S(1)}, s32[3,7]{1,0:T(4,128)S(1)}) custom-call(f32[384,128]{1,0:T(8,128)} %bitcast.9, s32[3,7]{1,0:T(4,128)} %neighbours.1), custom_call_target="tpu_custom_call" | custom-call | tf_op jit(solution)/shard_map/pallas_call | solution.py:57
  1.0 0.5 %collective-permute-start = (bf16[384,128]{1,0:T(8,128)(2,1)S(1)}, bf16[384,128]{1,0:T(8,128)(2,1)S(1)}, u32[]{:S(2)}, u32[]{:S(2)}) collective-permute-start(bf16[384,128]{1,0:T(8,128)(2,1)S(1)} %get-tuple-element.21.own), channel_id=1, source_target_pairs={{0,4},{4,8},{8,12},{12,16},{16,20},{20,24},{24,28},{28,0},{1,5},{5... | collective-permute-start | bytes 294920 | tf_op jit(solution)/shard_map/ppermute | solution.py:212
  1.5 2.9 %collective-permute-start.1 = (bf16[384,128]{1,0:T(8,128)(2,1)S(1)}, bf16[384,128]{1,0:T(8,128)(2,1)S(1)}, u32[]{:S(2)}, u32[]{:S(2)}) collective-permute-start(bf16[384,128]{1,0:T(8,128)(2,1)S(1)} %get-tuple-element.21.own), channel_id=1, source_target_pairs={{0,28},{4,0},{8,4},{12,8},{16,12},{20,16},{24,20},{28,24},{1,29},{... | collective-permute-start | bytes 294920 | tf_op jit(solution)/shard_map/ppermute | solution.py:212
  4.4 2.2 %shard_map.101 = (bf16[1,9,384,128]{3,2,1,0:T(8,128)(2,1)S(1)}, f32[384,128]{1,0:T(8,128)S(1)}) custom-call(s32[3,7]{1,0:T(4,128)S(1)} %get-tuple-element.20.ids, bf16[3,3,128,896]{3,2,1,0:T(8,128)(2,1)} %ops.3, bf16[384,128]{1,0:T(8,128)(2,1)S(1)} %get-tuple-element.21.own), custom_call_target="tpu_custom_call" | custom-call | tf_op jit(solution)/shard_map/pallas_call | solution.py:57
  6.7 0.3 shard_map.102.lap
  7.0 1.7 %collective-permute-start.2 = (bf16[384,128]{1,0:T(8,128)(2,1)S(1)}, bf16[384,128]{1,0:T(8,128)(2,1)S(1)}, u32[]{:S(2)}, u32[]{:S(2)}) collective-permute-start(bf16[384,128]{1,0:T(8,128)(2,1)S(1)} %shard_map.102.lap), channel_id=1, source_target_pairs={{0,4},{4,8},{8,12},{12,16},{16,20},{20,24},{24,28},{28,0},{1,5},{5... | collective-permute-start | bytes 294920 | tf_op jit(solution)/shard_map/ppermute | solution.py:212
  8.7 1.1 %collective-permute-start.3 = (bf16[384,128]{1,0:T(8,128)(2,1)S(1)}, bf16[384,128]{1,0:T(8,128)(2,1)S(1)}, u32[]{:S(2)}, u32[]{:S(2)}) collective-permute-start(bf16[384,128]{1,0:T(8,128)(2,1)S(1)} %shard_map.102.lap), channel_id=1, source_target_pairs={{0,28},{4,0},{8,4},{12,8},{16,12},{20,16},{24,20},{28,24},{1,29},{... | collective-permute-start | bytes 294920 | tf_op jit(solution)/shard_map/ppermute | solution.py:212
  9.8 0.6 %broadcast_in_dim.6.weight = f32[1,384]{1,0:T(1,128)} reshape(f32[384]{0:T(512)S(1)} %copy-done.3) | data formatting | bytes 3072 | tf_op jit(solution)/shard_map/broadcast_in_dim | solution.py:265
  10.4 3.3 %shard_map.103 = (f32[384,128]{1,0:T(8,128)S(1)}, bf16[512,384]{1,0:T(8,128)(2,1)S(1)}, bf16[512,384]{1,0:T(8,128)(2,1)S(1)}, bf16[2,384,256]{2,1,0:T(8,128)(2,1)S(1)}, bf16[2,384,256]{2,1,0:T(8,128)(2,1)S(1)}) custom-call(s32[3,7]{1,0:T(4,128)S(1)} %get-tuple-element.20.ids, bf16[3,3,128,896]{3,2,1,0:T(8,128)(2,1)} %ops.3, f32[768,128]{1,0:T(8,128)} %bitcast.8, ...), custom_call_target="tpu_custom_call" | custom-call | tf_op jit(solution)/shard_map/pallas_call | solution.py:57
  13.7 0.3 shard_map.104
  14.0 2.3 %collective-permute-start.4 = (bf16[384,128]{1,0:T(8,128)(2,1)S(1)}, bf16[384,128]{1,0:T(8,128)(2,1)S(1)}, u32[]{:S(2)}, u32[]{:S(2)}) collective-permute-start(bf16[384,128]{1,0:T(8,128)(2,1)S(1)} %get-tuple-element.26.refs_0_), channel_id=1, source_target_pairs={{0,1},{1,2},{2,3},{3,0},{4,5},{5,6},{6,7},{7,4},{8,9},{9,10},{10,1... | collective-permute-start | bytes 294920 | tf_op jit(solution)/shard_map/ppermute | solution.py:279
  16.3 2.6 %collective-permute-start.5 = (bf16[384,128]{1,0:T(8,128)(2,1)S(1)}, bf16[384,128]{1,0:T(8,128)(2,1)S(1)}, u32[]{:S(2)}, u32[]{:S(2)}) collective-permute-start(bf16[384,128]{1,0:T(8,128)(2,1)S(1)} %get-tuple-element.26.refs_0_), channel_id=1, source_target_pairs={{0,2},{1,3},{2,0},{3,1},{4,6},{5,7},{6,4},{7,5},{8,10},{9,11},{10,... | collective-permute-start | bytes 294920 | tf_op jit(solution)/shard_map/ppermute | solution.py:279
  18.9 1.3 %collective-permute-start.6 = (bf16[384,128]{1,0:T(8,128)(2,1)S(1)}, bf16[384,128]{1,0:T(8,128)(2,1)S(1)}, u32[]{:S(2)}, u32[]{:S(2)}) collective-permute-start(bf16[384,128]{1,0:T(8,128)(2,1)S(1)} %get-tuple-element.26.refs_0_), channel_id=1, source_target_pairs={{0,3},{1,0},{2,1},{3,2},{4,7},{5,4},{6,5},{7,6},{8,11},{9,8},{10,9... | collective-permute-start | bytes 294920 | tf_op jit(solution)/shard_map/ppermute | solution.py:279
  20.3 0.4 shard_map.105.refs_9_
  20.7 1.2 %collective-permute-done.4.refs_1_ = bf16[384,128]{1,0:T(8,128)(2,1)S(1)} collective-permute-done((bf16[384,128]{1,0:T(8,128)(2,1)S(1)}, bf16[384,128]{1,0:T(8,128)(2,1)S(1)}, u32[]{:S(2)}, u32[]{:S(2)}) %collective-permute-start.4) | collective-permute-done | bytes 98336 | tf_op jit(solution)/shard_map/ppermute | solution.py:279
  21.8 3.4 %collective-permute-done.5.refs_2_ = bf16[384,128]{1,0:T(8,128)(2,1)S(1)} collective-permute-done((bf16[384,128]{1,0:T(8,128)(2,1)S(1)}, bf16[384,128]{1,0:T(8,128)(2,1)S(1)}, u32[]{:S(2)}, u32[]{:S(2)}) %collective-permute-start.5) | collective-permute-done | bytes 98336 | tf_op jit(solution)/shard_map/ppermute | solution.py:279
  25.4 1.7 %shard_map.106 = (f32[384,128]{1,0:T(8,128)S(1)}, f32[256,128]{1,0:T(8,128)S(1)}, f32[256,128]{1,0:T(8,128)S(1)}) custom-call(bf16[384,128]{1,0:T(8,128)(2,1)S(1)} %get-tuple-element.26.refs_0_, bf16[384,128]{1,0:T(8,128)(2,1)S(1)} %collective-permute-done.4.refs_1_, bf16[384,128]{1,0:T(8,128)(2,1)S(1)} %collective-permute-done.5.refs_2_, ...), custom_call_target="tpu_custom_call" | custom-call | tf_op jit(solution)/shard_map/pallas_call | solution.py:57
  27.1 1.3 %collective-permute-done.7 = f32[256,128]{1,0:T(8,128)S(1)} collective-permute-done((f32[256,128]{1,0:T(8,128)S(1)}, f32[256,128]{1,0:T(8,128)S(1)}, u32[]{:S(2)}, u32[]{:S(2)}) %collective-permute-start.7) | collective-permute-done | bytes 131104 | tf_op jit(solution)/shard_map/ppermute | solution.py:216
  28.5 1.6 %collective-permute-start.8 = (f32[256,128]{1,0:T(8,128)S(1)}, f32[256,128]{1,0:T(8,128)S(1)}, u32[]{:S(2)}, u32[]{:S(2)}) collective-permute-start(f32[256,128]{1,0:T(8,128)S(1)} %add.9), channel_id=1, source_target_pairs={{0,8},{4,20},{8,0},{12,28},{16,24},{20,4},{24,16},{28,12},{1,9},{5... | collective-permute-start | bytes 393224 | tf_op jit(solution)/shard_map/ppermute | solution.py:224
  30.1 3.4 %collective-permute-done.8 = f32[256,128]{1,0:T(8,128)S(1)} collective-permute-done((f32[256,128]{1,0:T(8,128)S(1)}, f32[256,128]{1,0:T(8,128)S(1)}, u32[]{:S(2)}, u32[]{:S(2)}) %collective-permute-start.8) | collective-permute-done | bytes 131104 | tf_op jit(solution)/shard_map/ppermute | solution.py:224
  33.5 1.2 %collective-permute-start.9 = (f32[256,128]{1,0:T(8,128)S(1)}, f32[256,128]{1,0:T(8,128)S(1)}, u32[]{:S(2)}, u32[]{:S(2)}) collective-permute-start(f32[256,128]{1,0:T(8,128)S(1)} %add.10), channel_id=1, source_target_pairs={{0,16},{4,12},{8,24},{12,4},{16,0},{20,28},{24,8},{28,20},{1,17},{... | collective-permute-start | bytes 393224 | tf_op jit(solution)/shard_map/ppermute | solution.py:224
  34.7 3.8 %collective-permute-done.9 = f32[256,128]{1,0:T(8,128)S(1)} collective-permute-done((f32[256,128]{1,0:T(8,128)S(1)}, f32[256,128]{1,0:T(8,128)S(1)}, u32[]{:S(2)}, u32[]{:S(2)}) %collective-permute-start.9) | collective-permute-done | bytes 131104 | tf_op jit(solution)/shard_map/ppermute | solution.py:224
  38.9 1.1 %collective-permute-done.10.refs_1_ = f32[256,128]{1,0:T(8,128)S(1)} collective-permute-done((f32[256,128]{1,0:T(8,128)S(1)}, f32[256,128]{1,0:T(8,128)S(1)}, u32[]{:S(2)}, u32[]{:S(2)}) %collective-permute-start.10) | collective-permute-done | bytes 131104 | tf_op jit(solution)/shard_map/ppermute | solution.py:216
  40.0 0.9 %shard_map.108 = f32[384,128]{1,0:T(8,128)} custom-call(f32[384,128]{1,0:T(8,128)S(1)} %shard_map.107.refs_0_, f32[256,128]{1,0:T(8,128)S(1)} %collective-permute-done.10.refs_1_, bf16[2,384,256]{2,1,0:T(8,128)(2,1)S(1)} %get-tuple-element.33.refs_2_, bf16[2,384,256]{2,1,0:T(8,128)(2,1)S(1)} %get-tuple-element.34.refs_3_), custom_call_target="tpu_custom_call" | custom-call | tf_op jit(solution)/shard_map/pallas_call | solution.py:57
  (19 shorter events, 0.7 us)
Async XLA Ops:
  0.0 9.8 %copy-start.3 = (f32[384]{0:T(512)S(1)}, f32[384]{0:T(512)}, u32[]{:S(2)}) copy-start(f32[384]{0:T(512)} %param.15) | copy-start | bytes 4612
  1.0 5.7 %collective-permute-start = (bf16[384,128]{1,0:T(8,128)(2,1)S(1)}, bf16[384,128]{1,0:T(8,128)(2,1)S(1)}, u32[]{:S(2)}, u32[]{:S(2)}) collective-permute-start(bf16[384,128]{1,0:T(8,128)(2,1)S(1)} %get-tuple-element.21.own), channel_id=1, source_target_pairs={{0,4},{4,8},{8,12},{12,16},{16,20},{20,24},{24,28},{28,0},{1,5},{5... | collective-permute-start | bytes 294920 | tf_op jit(solution)/shard_map/ppermute | solution.py:212
  1.5 5.2 %collective-permute-start.1 = (bf16[384,128]{1,0:T(8,128)(2,1)S(1)}, bf16[384,128]{1,0:T(8,128)(2,1)S(1)}, u32[]{:S(2)}, u32[]{:S(2)}) collective-permute-start(bf16[384,128]{1,0:T(8,128)(2,1)S(1)} %get-tuple-element.21.own), channel_id=1, source_target_pairs={{0,28},{4,0},{8,4},{12,8},{16,12},{20,16},{24,20},{28,24},{1,29},{... | collective-permute-start | bytes 294920 | tf_op jit(solution)/shard_map/ppermute | solution.py:212
  7.0 6.7 %collective-permute-start.2 = (bf16[384,128]{1,0:T(8,128)(2,1)S(1)}, bf16[384,128]{1,0:T(8,128)(2,1)S(1)}, u32[]{:S(2)}, u32[]{:S(2)}) collective-permute-start(bf16[384,128]{1,0:T(8,128)(2,1)S(1)} %shard_map.102.lap), channel_id=1, source_target_pairs={{0,4},{4,8},{8,12},{12,16},{16,20},{20,24},{24,28},{28,0},{1,5},{5... | collective-permute-start | bytes 294920 | tf_op jit(solution)/shard_map/ppermute | solution.py:212
  8.7 5.0 %collective-permute-start.3 = (bf16[384,128]{1,0:T(8,128)(2,1)S(1)}, bf16[384,128]{1,0:T(8,128)(2,1)S(1)}, u32[]{:S(2)}, u32[]{:S(2)}) collective-permute-start(bf16[384,128]{1,0:T(8,128)(2,1)S(1)} %shard_map.102.lap), channel_id=1, source_target_pairs={{0,28},{4,0},{8,4},{12,8},{16,12},{20,16},{24,20},{28,24},{1,29},{... | collective-permute-start | bytes 294920 | tf_op jit(solution)/shard_map/ppermute | solution.py:212
  13.6 11.7 %copy-start = (bf16[4,512,128]{2,1,0:T(8,128)(2,1)S(1)}, bf16[4,512,128]{2,1,0:T(8,128)(2,1)}, u32[]{:S(2)}) copy-start(bf16[4,512,128]{2,1,0:T(8,128)(2,1)} %constant.4.clone.refs_5_) | copy-start | bytes 1572868
  13.7 11.7 %copy-start.1 = (bf16[4,512,128]{2,1,0:T(8,128)(2,1)S(1)}, bf16[4,512,128]{2,1,0:T(8,128)(2,1)}, u32[]{:S(2)}) copy-start(bf16[4,512,128]{2,1,0:T(8,128)(2,1)} %constant.5.clone.refs_6_) | copy-start | bytes 1572868
  13.7 11.7 %copy-start.2 = (f32[512]{0:T(512)S(1)}, f32[512]{0:T(512)}, u32[]{:S(2)}) copy-start(f32[512]{0:T(512)} %param.14) | copy-start | bytes 6148
  14.0 7.8 %collective-permute-start.4 = (bf16[384,128]{1,0:T(8,128)(2,1)S(1)}, bf16[384,128]{1,0:T(8,128)(2,1)S(1)}, u32[]{:S(2)}, u32[]{:S(2)}) collective-permute-start(bf16[384,128]{1,0:T(8,128)(2,1)S(1)} %get-tuple-element.26.refs_0_), channel_id=1, source_target_pairs={{0,1},{1,2},{2,3},{3,0},{4,5},{5,6},{6,7},{7,4},{8,9},{9,10},{10,1... | collective-permute-start | bytes 294920 | tf_op jit(solution)/shard_map/ppermute | solution.py:279
  16.3 8.9 %collective-permute-start.5 = (bf16[384,128]{1,0:T(8,128)(2,1)S(1)}, bf16[384,128]{1,0:T(8,128)(2,1)S(1)}, u32[]{:S(2)}, u32[]{:S(2)}) collective-permute-start(bf16[384,128]{1,0:T(8,128)(2,1)S(1)} %get-tuple-element.26.refs_0_), channel_id=1, source_target_pairs={{0,2},{1,3},{2,0},{3,1},{4,6},{5,7},{6,4},{7,5},{8,10},{9,11},{10,... | collective-permute-start | bytes 294920 | tf_op jit(solution)/shard_map/ppermute | solution.py:279
  18.9 6.4 %collective-permute-start.6 = (bf16[384,128]{1,0:T(8,128)(2,1)S(1)}, bf16[384,128]{1,0:T(8,128)(2,1)S(1)}, u32[]{:S(2)}, u32[]{:S(2)}) collective-permute-start(bf16[384,128]{1,0:T(8,128)(2,1)S(1)} %get-tuple-element.26.refs_0_), channel_id=1, source_target_pairs={{0,3},{1,0},{2,1},{3,2},{4,7},{5,4},{6,5},{7,6},{8,11},{9,8},{10,9... | collective-permute-start | bytes 294920 | tf_op jit(solution)/shard_map/ppermute | solution.py:279
  27.1 1.4 %collective-permute-start.7 = (f32[256,128]{1,0:T(8,128)S(1)}, f32[256,128]{1,0:T(8,128)S(1)}, u32[]{:S(2)}, u32[]{:S(2)}) collective-permute-start(f32[256,128]{1,0:T(8,128)S(1)} %get-tuple-element.32), channel_id=1, source_target_pairs={{0,4},{4,0},{8,12},{12,8},{16,20},{20,16},{24,28},{28,24},{1,5},{5... | collective-permute-start | bytes 393224 | tf_op jit(solution)/shard_map/ppermute | solution.py:216
  28.5 5.0 %collective-permute-start.8 = (f32[256,128]{1,0:T(8,128)S(1)}, f32[256,128]{1,0:T(8,128)S(1)}, u32[]{:S(2)}, u32[]{:S(2)}) collective-permute-start(f32[256,128]{1,0:T(8,128)S(1)} %add.9), channel_id=1, source_target_pairs={{0,8},{4,20},{8,0},{12,28},{16,24},{20,4},{24,16},{28,12},{1,9},{5... | collective-permute-start | bytes 393224 | tf_op jit(solution)/shard_map/ppermute | solution.py:224
  33.5 5.0 %collective-permute-start.9 = (f32[256,128]{1,0:T(8,128)S(1)}, f32[256,128]{1,0:T(8,128)S(1)}, u32[]{:S(2)}, u32[]{:S(2)}) collective-permute-start(f32[256,128]{1,0:T(8,128)S(1)} %add.10), channel_id=1, source_target_pairs={{0,16},{4,12},{8,24},{12,4},{16,0},{20,28},{24,8},{28,20},{1,17},{... | collective-permute-start | bytes 393224 | tf_op jit(solution)/shard_map/ppermute | solution.py:224
  38.6 1.4 %collective-permute-start.10 = (f32[256,128]{1,0:T(8,128)S(1)}, f32[256,128]{1,0:T(8,128)S(1)}, u32[]{:S(2)}, u32[]{:S(2)}) collective-permute-start(f32[256,128]{1,0:T(8,128)S(1)} %add.11.refs_1_), channel_id=1, source_target_pairs={{0,4},{4,0},{8,12},{12,8},{16,20},{20,16},{24,28},{28,24},{1,5},{5... | collective-permute-start | bytes 393224 | tf_op jit(solution)/shard_map/ppermute | solution.py:216

commit v6 on v5

--- a/solution.py
+++ b/solution.py
@@ -124,45 +124,45 @@
     lap[...] = (lap_own[...] + around(dense.at[0], low, high)).astype(BF)
 
 
-def advect_kernel(ids, ops, velocity, basis, weight, degree, lap_dense, low, own, high, lap, fields,
-                  out, wbt_high, wbt_low, bg_high, bg_low, dense, vel, held, weight_held, degree_held, sems, op_sems):
+def advect_kernel(ids, ops, velocity, lap_dense, low, own, high, lap, fields, out, dense, vel, vel_sem, op_sems):
     blocks = ops.shape[0]
+    nodes = own.shape[0]
+    vel_copy = pltpu.make_async_copy(velocity, vel, vel_sem)
+    vel_copy.start()
+    copies = stencil_copies(ids, ops, pl.ds(0, 2), dense, op_sems)
+    value = fields[...] - hyper_rate * dot(beside(lap_dense.at[0], blocks, blocks), lap[...])
+    vel_copy.wait()
+    for copy in copies:
+        copy.wait()
+    for k in range(2):
+        grad = dot(beside(dense.at[k], blocks, blocks), own[...]) + around(dense.at[k], low, high)
+        value = value - advect_step * (vel[pl.ds(k, nodes, stride=2), :] * grad)
+    out[...] = value
+
+
+def second_lap_kernel(dense, low, high, part, stepped, narrow):
+    value = part[...] - hyper_rate * around(dense.at[0], low, high)
+    stepped[...] = value
+    narrow[...] = value.astype(BF)
+
+
+def project_kernel(basis, weight, degree, value, wbt, early, bg_high, bg_low, held, weight_held, degree_held, sems):
     nodes, modes = held.shape
-    pairs = ((basis, held), (weight, weight_held), (degree, degree_held), (velocity, vel))
-    held_copies = [pltpu.make_async_copy(*pair, sems.at[k]) for k, pair in enumerate(pairs)]
-    for copy in held_copies:
+    pairs = ((basis, held), (weight, weight_held), (degree, degree_held))
+    copies = [pltpu.make_async_copy(*pair, sems.at[k]) for k, pair in enumerate(pairs)]
+    for copy in copies:
         copy.start()
-    copies = stencil_copies(ids, ops, pl.ds(0, 2), dense, op_sems)
-    for copy in held_copies:
+    for copy in copies:
         copy.wait()
+    parts = split(held[...].T * weight_held[...])
+    wbt[...] = parts[0]
+    early[...] = dot3(parts, split(value[...]))
     ratio = degree_held[...].astype(F32) / DEGMAX
     gain = 0.5 * math.sqrt(modes / (nodes * lax.axis_size("tile"))) * (1.0 - jnp.exp(-4.0 * ratio * ratio))
     half = modes // 2
     for c in range(2):
         cols = slice(c * half, (c + 1) * half)
-        high_part, low_part = split(held[:, cols] * gain[:, cols])
-        bg_high[c] = high_part
-        bg_low[c] = low_part
-    high_part, low_part = split(held[...].T * weight_held[...])
-    wbt_high[...] = high_part
-    wbt_low[...] = low_part
-    for copy in copies:
-        copy.wait()
-    value = fields[...] - hyper_rate * dot(beside(lap_dense.at[0], blocks, blocks), lap[...])
-    for k in range(2):
-        grad = dot(beside(dense.at[k], blocks, blocks), own[...]) + around(dense.at[k], low, high)
-        value = value - advect_step * (vel[pl.ds(k, nodes, stride=2), :] * grad)
-    out[...] = value
-
-
-def second_lap_kernel(dense, low, high, part, stepped, narrow):
-    value = part[...] - hyper_rate * around(dense.at[0], low, high)
-    stepped[...] = value
-    narrow[...] = value.astype(BF)
-
-
-def project_kernel(wbt_high, wbt_low, value, out):
-    out[...] = dot3((wbt_high[...], wbt_low[...]), split(value[...]))
+        bg_high[c], bg_low[c] = split(held[:, cols] * gain[:, cols])
 
 
 def diffuse_kernel(count, *refs):
@@ -216,12 +216,26 @@
     return lax.ppermute(block, "tile", [(i, i ^ 1) for i in range(lax.axis_size("tile"))])
 
 
+def packed(block):
+    top = jnp.max(jnp.abs(block), keepdims=True)
+    power = jnp.round(jnp.log2(jnp.maximum(top, 1e-30)))
+    tail = jnp.broadcast_to(power, (16, block.shape[1]))
+    return jnp.concatenate([block * jnp.exp2(8.0 - power), tail], axis=0).astype(jnp.float16)
+
+
+def unpacked(sent):
+    rows = sent.shape[0] - 16
+    return sent[:rows].astype(F32) * jnp.exp2(sent[rows : rows + 1].astype(F32) - 8.0)
+
+
 def chip_sum(block):
     count = lax.axis_size("tile")
-    bits = [1 << k for k in range(1, count.bit_length() - 1)]
-    for k in range(len(bits)):
-        pairs = [(i, i ^ bits[(k + i % 2) % len(bits)]) for i in range(count)]
-        block = block + lax.ppermute(block, "tile", pairs)
+    if count <= 8:
+        sent = packed(block)
+        parts = [lax.ppermute(sent, "tile", [(i, i ^ m) for i in range(count)]) for m in range(2, count, 2)]
+        return sum((unpacked(part) for part in parts), block)
+    for m in [1 << k for k in range(1, count.bit_length() - 1)]:
+        block = block + lax.ppermute(block, "tile", [(i, i ^ m) for i in range(count)])
     return block
 
 
@@ -259,30 +273,32 @@
     )
     lap = call(first_lap_kernel, thin, (lap_dense, lap_own, low, high))
     low_two, high_two = halo(lap)
-    part, wbt_high, wbt_low, bg_high, bg_low = call(
+    part = call(
         advect_kernel,
-        (wide,) + (shape((modes, nodes), BF),) * 2 + (shape((2, nodes, modes // 2), BF),) * 2,
-        (ids, operators, velocity, basis, quad_weight[None, :], degree[None, :])
-        + (lap_dense, low, rounded, high, lap, fields),
-        "shhhhhvvvvvv",
+        wide,
+        (ids, operators, velocity, lap_dense, low, rounded, high, lap, fields),
+        "shhvvvvvv",
         (
             pltpu.VMEM((2, 3 * blocks, nodes, size), BF),
             pltpu.VMEM((2 * nodes, levels), F32),
-            pltpu.VMEM((nodes, modes), F32),
-            pltpu.VMEM((1, nodes), F32),
-            pltpu.VMEM((1, modes), jnp.int32),
-            dma((4,)),
+            dma(()),
             dma(neighbours.shape),
         ),
     )
     stepped, narrow = call(second_lap_kernel, (wide, thin), (lap_dense, low_two, high_two, part))
     shards = [narrow] + [lax.ppermute(narrow, "rad", shift("rad", d)) for d in range(1, rads)]
-    early = call(project_kernel, shape((modes, levels), F32), (wbt_high, wbt_low, stepped))
+    wbt, early, bg_high, bg_low = call(
+        project_kernel,
+        (shape((modes, nodes), BF), shape((modes, levels), F32)) + (shape((2, nodes, modes // 2), BF),) * 2,
+        (basis, quad_weight[None, :], degree[None, :], stepped),
+        "hhhv",
+        (pltpu.VMEM((nodes, modes), F32), pltpu.VMEM((1, nodes), F32), pltpu.VMEM((1, modes), jnp.int32), dma((3,))),
+    )
     diffused, keep, send = call(
         lambda *refs: diffuse_kernel(rads, *refs),
         (wide, half, half),
         (*shards, stepped, jnp.asarray(dh_high), jnp.asarray(dh_low), kappa_ref.reshape(rads, 1, levels))
-        + (wbt_high, early),
+        + (wbt, early),
     )
     mine = chip_sum(keep + swap(send))
     other = swap(mine)

time: 41.3 us -> 42.3 us (1.024)
  starting transfers between devices: 15.5 us -> 12.8 us
  Pallas kernels: 10.3 us -> 11.5 us
  waiting for transfers between devices: 14.4 us -> 15.5 us
  between operations: 0.14 us -> 0.91 us
  other arithmetic: 0.05 us -> 0.7 us
    ppermute x2, waiting for transfers between devices: 0.05 us -> 4.14 us  [halo(): lax.ppermute(block, 'tile', shift('tile', 1))]
    ppermute x2 -> x3, waiting for transfers between devices: 7.25 us -> 4.29 us  [chip_sum(): lax.ppermute(sent, 'tile', [(i, i ^ m) for i in range(count)])]
    ppermute x2, starting transfers between devices: 2.24 us -> 0.36 us  [halo(): lax.ppermute(block, 'tile', shift('tile', 1))]
    ppermute x3, starting transfers between devices: 6.25 us -> 4.67 us  [body(): lax.ppermute(narrow, 'rad', shift('rad', d))]
    ppermute x2 -> x3, starting transfers between devices: 2.81 us -> 4.03 us  [chip_sum(): lax.ppermute(sent, 'tile', [(i, i ^ m) for i in range(count)])]
    pallas_call x9, Pallas kernels: 10.3 us -> 11.5 us  [call(): pl.pallas_call(kernel, out_shape=outs, in_specs=[{'s': SMEM, 'h': HBM, 'v...]
    reduce_max x0 -> x1, other arithmetic: none -> 0.61 us  [packed(): top = jnp.max(jnp.abs(block), keepdims=True)]
    ppermute x2, starting transfers between devices: 4.05 us -> 3.59 us  [halo(): lax.ppermute(block, 'tile', shift('tile', -1))]
  transfers between devices with their start and end apart: 11 -> 12, of which waited for: 7 -> 9; matrix products, arithmetic and copies ran while one was open for 1% -> 1% of each run, Pallas kernels for 15% -> 17%
where the time goes in v6:
time: 42.3 us; the launch traced here: 42 us
  waiting for transfers between devices  15.5 us (37%)
  starting transfers between devices  12.8 us (30%)
  Pallas kernels  11.5 us (27%)
  between operations  0.91 us (2%)
  other arithmetic  0.7 us (2%)
  local copies, waits for them, and re-layouts  0.61 us (1%)
    pallas_call x9, Pallas kernels, call(): pl.pallas_call(kernel, out_shape=outs, in_specs=[{'s': SMEM, 'h': HBM, 'v...  11.5 us
    ppermute x3, starting transfers between devices, body(): lax.ppermute(narrow, 'rad', shift('rad', d))  4.67 us
    ppermute x3, waiting for transfers between devices, body(): lax.ppermute(narrow, 'rad', shift('rad', d))  4.56 us
    ppermute x3, waiting for transfers between devices, chip_sum(): lax.ppermute(sent, 'tile', [(i, i ^ m) for i in range(count)])  4.29 us
    ppermute x2, waiting for transfers between devices, halo(): lax.ppermute(block, 'tile', shift('tile', 1))  4.14 us
    ppermute x3, starting transfers between devices, chip_sum(): lax.ppermute(sent, 'tile', [(i, i ^ m) for i in range(count)])  4.03 us
    ppermute x2, starting transfers between devices, halo(): lax.ppermute(block, 'tile', shift('tile', -1))  3.59 us
    ppermute x2, waiting for transfers between devices, swap(): lax.ppermute(block, 'tile', [(i, i ^ 1) for i in range(lax.axis_size('til...  2.4 us
  transfers between devices with their start and end apart: 12, of which 9 were waited for; matrix products, arithmetic and copies ran while one was open for 1% of the time, Pallas kernels for 17%

profile of v6, /device:TPU:0, one launch (start us, length us, event | category | flops | bytes accessed | tf_op | source)
XLA Modules:
  0.0 42.0 jit_solution(10707062000024578989)
XLA Ops:
  0.0 0.9 %shard_map.100 = (f32[384,128]{1,0:T(8,128)S(1)}, bf16[384,128]{1,0:T(8,128)(2,1)S(1)}, s32[3,7]{1,0:T(4,128)S(1)}) custom-call(f32[384,128]{1,0:T(8,128)} %bitcast.15, s32[3,7]{1,0:T(4,128)} %neighbours.1), custom_call_target="tpu_custom_call" | custom-call | tf_op jit(solution)/shard_map/pallas_call | solution.py:57
  0.9 3.4 %collective-permute-start.1 = (bf16[384,128]{1,0:T(8,128)(2,1)S(1)}, bf16[384,128]{1,0:T(8,128)(2,1)S(1)}, u32[]{:S(2)}, u32[]{:S(2)}) collective-permute-start(bf16[384,128]{1,0:T(8,128)(2,1)S(1)} %get-tuple-element.20.own), channel_id=1, source_target_pairs={{0,28},{4,0},{8,4},{12,8},{16,12},{20,16},{24,20},{28,24},{1,29},{... | collective-permute-start | bytes 294920 | tf_op jit(solution)/shard_map/ppermute | solution.py:212
  4.3 2.2 %shard_map.101 = (bf16[1,9,384,128]{3,2,1,0:T(8,128)(2,1)S(1)}, f32[384,128]{1,0:T(8,128)S(1)}) custom-call(s32[3,7]{1,0:T(4,128)S(1)} %get-tuple-element.19.ids, bf16[3,3,128,896]{3,2,1,0:T(8,128)(2,1)} %ops.3, bf16[384,128]{1,0:T(8,128)(2,1)S(1)} %get-tuple-element.20.own), custom_call_target="tpu_custom_call" | custom-call | tf_op jit(solution)/shard_map/pallas_call | solution.py:57
  6.6 2.7 %collective-permute-done.low = bf16[384,128]{1,0:T(8,128)(2,1)S(1)} collective-permute-done((bf16[384,128]{1,0:T(8,128)(2,1)S(1)}, bf16[384,128]{1,0:T(8,128)(2,1)S(1)}, u32[]{:S(2)}, u32[]{:S(2)}) %collective-permute-start) | collective-permute-done | bytes 98336 | tf_op jit(solution)/shard_map/ppermute | solution.py:212
  9.3 0.3 shard_map.102.lap
  9.8 0.4 collective-permute-start.2
  10.2 3.0 %shard_map.103.part = f32[384,128]{1,0:T(8,128)S(1)} custom-call(s32[3,7]{1,0:T(4,128)S(1)} %get-tuple-element.19.ids, bf16[3,3,128,896]{3,2,1,0:T(8,128)(2,1)} %ops.3, f32[768,128]{1,0:T(8,128)} %bitcast.14, bf16[1,9,384,128]{3,2,1,0:T(8,128)(2,1)S(1)} %get-tuple-element.21.dense.lap_dense, bf16[384,128]{1,0:T(8,128)(2,1)S(1)} %collective-permute-done.low, ...), custom_call_target="tpu_custom_call" | custom-call | tf_op jit(solution)/shard_map/pallas_call | solution.py:57
  13.3 1.5 %collective-permute-done.2.low = bf16[384,128]{1,0:T(8,128)(2,1)S(1)} collective-permute-done((bf16[384,128]{1,0:T(8,128)(2,1)S(1)}, bf16[384,128]{1,0:T(8,128)(2,1)S(1)}, u32[]{:S(2)}, u32[]{:S(2)}) %collective-permute-start.2) | collective-permute-done | bytes 98336 | tf_op jit(solution)/shard_map/ppermute | solution.py:212
  14.7 0.3 shard_map.104
  15.1 3.7 %collective-permute-start.6 = (bf16[384,128]{1,0:T(8,128)(2,1)S(1)}, bf16[384,128]{1,0:T(8,128)(2,1)S(1)}, u32[]{:S(2)}, u32[]{:S(2)}) collective-permute-start(bf16[384,128]{1,0:T(8,128)(2,1)S(1)} %get-tuple-element.24.refs_0_), channel_id=1, source_target_pairs={{0,3},{1,0},{2,1},{3,2},{4,7},{5,4},{6,5},{7,6},{8,11},{9,8},{10,9... | collective-permute-start | bytes 294920 | tf_op jit(solution)/shard_map/ppermute | solution.py:289
  18.7 1.0 %collective-permute-start.4 = (bf16[384,128]{1,0:T(8,128)(2,1)S(1)}, bf16[384,128]{1,0:T(8,128)(2,1)S(1)}, u32[]{:S(2)}, u32[]{:S(2)}) collective-permute-start(bf16[384,128]{1,0:T(8,128)(2,1)S(1)} %get-tuple-element.24.refs_0_), channel_id=1, source_target_pairs={{0,1},{1,2},{2,3},{3,0},{4,5},{5,6},{6,7},{7,4},{8,9},{9,10},{10,1... | collective-permute-start | bytes 294920 | tf_op jit(solution)/shard_map/ppermute | solution.py:289
  19.7 0.6 %broadcast_in_dim.4.weight = f32[1,384]{1,0:T(1,128)} reshape(f32[384]{0:T(512)S(1)} %copy-done.3) | data formatting | bytes 3072 | tf_op jit(solution)/shard_map/broadcast_in_dim | solution.py:293
  20.3 1.8 %shard_map.105 = (bf16[512,384]{1,0:T(8,128)(2,1)S(1)}, f32[512,128]{1,0:T(8,128)S(1)}, bf16[2,384,256]{2,1,0:T(8,128)(2,1)S(1)}, bf16[2,384,256]{2,1,0:T(8,128)(2,1)S(1)}) custom-call(f32[384,512]{1,0:T(8,128)} %basis.1, f32[1,384]{1,0:T(1,128)} %broadcast_in_dim.4.weight, s32[1,512]{1,0:T(1,128)} %bitcast.16, f32[384,128]{1,0:T(8,128)S(1)} %get-tuple-element.25.value.refs_4_), custom_call_target="tpu_custom_call" | custom-call | tf_op jit(solution)/shard_map/pallas_call | solution.py:57
  22.1 4.6 %collective-permute-done.5.refs_2_ = bf16[384,128]{1,0:T(8,128)(2,1)S(1)} collective-permute-done((bf16[384,128]{1,0:T(8,128)(2,1)S(1)}, bf16[384,128]{1,0:T(8,128)(2,1)S(1)}, u32[]{:S(2)}, u32[]{:S(2)}) %collective-permute-start.5) | collective-permute-done | bytes 98336 | tf_op jit(solution)/shard_map/ppermute | solution.py:289
  26.7 1.7 %shard_map.106 = (f32[384,128]{1,0:T(8,128)S(1)}, f32[256,128]{1,0:T(8,128)S(1)}, f32[256,128]{1,0:T(8,128)S(1)}) custom-call(bf16[384,128]{1,0:T(8,128)(2,1)S(1)} %get-tuple-element.24.refs_0_, bf16[384,128]{1,0:T(8,128)(2,1)S(1)} %collective-permute-done.4.refs_1_, bf16[384,128]{1,0:T(8,128)(2,1)S(1)} %collective-permute-done.5.refs_2_, ...), custom_call_target="tpu_custom_call" | custom-call | tf_op jit(solution)/shard_map/pallas_call | solution.py:57
  28.5 1.3 %collective-permute-done.7 = f32[256,128]{1,0:T(8,128)S(1)} collective-permute-done((f32[256,128]{1,0:T(8,128)S(1)}, f32[256,128]{1,0:T(8,128)S(1)}, u32[]{:S(2)}, u32[]{:S(2)}) %collective-permute-start.7) | collective-permute-done | bytes 131104 | tf_op jit(solution)/shard_map/ppermute | solution.py:216
  29.8 0.6 %abs_reduce_fusion = (f32[]{:T(128)}, f32[256,128]{1,0:T(8,128)S(1)}) fusion(f32[256,128]{1,0:T(8,128)S(1)} %get-tuple-element.29, f32[256,128]{1,0:T(8,128)S(1)} %collective-permute-done.7), kind=kLoop, calls=%fused_computation.2 | loop fusion | flops 98303 | bytes 393220 | tf_op jit(solution)/shard_map/reduce_max | solution.py:220
  31.2 2.5 %collective-permute-start.10 = (f16[272,128]{1,0:T(8,128)(2,1)S(1)}, f16[272,128]{1,0:T(8,128)(2,1)S(1)}, u32[]{:S(2)}, u32[]{:S(2)}) collective-permute-start(f16[272,128]{1,0:T(8,128)(2,1)S(1)} %concatenate.3), channel_id=1, source_target_pairs={{0,24},{4,28},{8,16},{12,20},{16,8},{20,12},{24,0},{28,4},{1,25},{... | collective-permute-start | bytes 208904 | tf_op jit(solution)/shard_map/ppermute | solution.py:235
  33.8 1.5 %collective-permute-start.9 = (f16[272,128]{1,0:T(8,128)(2,1)S(1)}, f16[272,128]{1,0:T(8,128)(2,1)S(1)}, u32[]{:S(2)}, u32[]{:S(2)}) collective-permute-start(f16[272,128]{1,0:T(8,128)(2,1)S(1)} %concatenate.3), channel_id=1, source_target_pairs={{0,16},{4,20},{8,24},{12,28},{16,0},{20,4},{24,8},{28,12},{1,17},{... | collective-permute-start | bytes 208904 | tf_op jit(solution)/shard_map/ppermute | solution.py:235
  35.2 1.3 %collective-permute-done.10 = f16[272,128]{1,0:T(8,128)(2,1)S(1)} collective-permute-done((f16[272,128]{1,0:T(8,128)(2,1)S(1)}, f16[272,128]{1,0:T(8,128)(2,1)S(1)}, u32[]{:S(2)}, u32[]{:S(2)}) %collective-permute-start.10) | collective-permute-done | bytes 69664 | tf_op jit(solution)/shard_map/ppermute | solution.py:235
  36.5 1.5 %collective-permute-done.9 = f16[272,128]{1,0:T(8,128)(2,1)S(1)} collective-permute-done((f16[272,128]{1,0:T(8,128)(2,1)S(1)}, f16[272,128]{1,0:T(8,128)(2,1)S(1)}, u32[]{:S(2)}, u32[]{:S(2)}) %collective-permute-start.9) | collective-permute-done | bytes 69664 | tf_op jit(solution)/shard_map/ppermute | solution.py:235
  38.1 1.5 %collective-permute-done.8 = f16[272,128]{1,0:T(8,128)(2,1)S(1)} collective-permute-done((f16[272,128]{1,0:T(8,128)(2,1)S(1)}, f16[272,128]{1,0:T(8,128)(2,1)S(1)}, u32[]{:S(2)}, u32[]{:S(2)}) %collective-permute-start.8) | collective-permute-done | bytes 69664 | tf_op jit(solution)/shard_map/ppermute | solution.py:235
  40.0 1.1 %collective-permute-done.11.refs_1_ = f32[256,128]{1,0:T(8,128)S(1)} collective-permute-done((f32[256,128]{1,0:T(8,128)S(1)}, f32[256,128]{1,0:T(8,128)S(1)}, u32[]{:S(2)}, u32[]{:S(2)}) %collective-permute-start.11) | collective-permute-done | bytes 131104 | tf_op jit(solution)/shard_map/ppermute | solution.py:216
  41.0 0.9 %shard_map.108 = f32[384,128]{1,0:T(8,128)} custom-call(f32[384,128]{1,0:T(8,128)S(1)} %shard_map.107.refs_0_, f32[256,128]{1,0:T(8,128)S(1)} %collective-permute-done.11.refs_1_, bf16[2,384,256]{2,1,0:T(8,128)(2,1)S(1)} %get-tuple-element.31.refs_2_, bf16[2,384,256]{2,1,0:T(8,128)(2,1)S(1)} %get-tuple-element.32.refs_3_), custom_call_target="tpu_custom_call" | custom-call | tf_op jit(solution)/shard_map/pallas_call | solution.py:57
  (25 shorter events, 0.9 us)
Async XLA Ops:
  0.9 5.7 %collective-permute-start.1 = (bf16[384,128]{1,0:T(8,128)(2,1)S(1)}, bf16[384,128]{1,0:T(8,128)(2,1)S(1)}, u32[]{:S(2)}, u32[]{:S(2)}) collective-permute-start(bf16[384,128]{1,0:T(8,128)(2,1)S(1)} %get-tuple-element.20.own), channel_id=1, source_target_pairs={{0,28},{4,0},{8,4},{12,8},{16,12},{20,16},{24,20},{28,24},{1,29},{... | collective-permute-start | bytes 294920 | tf_op jit(solution)/shard_map/ppermute | solution.py:212
  4.3 4.9 %collective-permute-start = (bf16[384,128]{1,0:T(8,128)(2,1)S(1)}, bf16[384,128]{1,0:T(8,128)(2,1)S(1)}, u32[]{:S(2)}, u32[]{:S(2)}) collective-permute-start(bf16[384,128]{1,0:T(8,128)(2,1)S(1)} %get-tuple-element.20.own), channel_id=1, source_target_pairs={{0,4},{4,8},{8,12},{12,16},{16,20},{20,24},{24,28},{28,0},{1,5},{5... | collective-permute-start | bytes 294920 | tf_op jit(solution)/shard_map/ppermute | solution.py:212
  9.6 3.7 %collective-permute-start.3 = (bf16[384,128]{1,0:T(8,128)(2,1)S(1)}, bf16[384,128]{1,0:T(8,128)(2,1)S(1)}, u32[]{:S(2)}, u32[]{:S(2)}) collective-permute-start(bf16[384,128]{1,0:T(8,128)(2,1)S(1)} %shard_map.102.lap), channel_id=1, source_target_pairs={{0,28},{4,0},{8,4},{12,8},{16,12},{20,16},{24,20},{28,24},{1,29},{... | collective-permute-start | bytes 294920 | tf_op jit(solution)/shard_map/ppermute | solution.py:212
  9.8 4.9 %collective-permute-start.2 = (bf16[384,128]{1,0:T(8,128)(2,1)S(1)}, bf16[384,128]{1,0:T(8,128)(2,1)S(1)}, u32[]{:S(2)}, u32[]{:S(2)}) collective-permute-start(bf16[384,128]{1,0:T(8,128)(2,1)S(1)} %shard_map.102.lap), channel_id=1, source_target_pairs={{0,4},{4,8},{8,12},{12,16},{16,20},{20,24},{24,28},{28,0},{1,5},{5... | collective-permute-start | bytes 294920 | tf_op jit(solution)/shard_map/ppermute | solution.py:212
  10.2 9.6 %copy-start.3 = (f32[384]{0:T(512)S(1)}, f32[384]{0:T(512)}, u32[]{:S(2)}) copy-start(f32[384]{0:T(512)} %param.15) | copy-start | bytes 4612
  13.2 13.5 %copy-start = (bf16[4,512,128]{2,1,0:T(8,128)(2,1)S(1)}, bf16[4,512,128]{2,1,0:T(8,128)(2,1)}, u32[]{:S(2)}) copy-start(bf16[4,512,128]{2,1,0:T(8,128)(2,1)} %constant.24.clone.refs_6_) | copy-start | bytes 1572868
  13.2 13.5 %copy-start.1 = (bf16[4,512,128]{2,1,0:T(8,128)(2,1)S(1)}, bf16[4,512,128]{2,1,0:T(8,128)(2,1)}, u32[]{:S(2)}) copy-start(bf16[4,512,128]{2,1,0:T(8,128)(2,1)} %constant.23.clone.refs_5_) | copy-start | bytes 1572868
  13.2 13.5 %copy-start.2 = (f32[512]{0:T(512)S(1)}, f32[512]{0:T(512)}, u32[]{:S(2)}) copy-start(f32[512]{0:T(512)} %param.14) | copy-start | bytes 6148
  15.1 7.1 %collective-permute-start.6 = (bf16[384,128]{1,0:T(8,128)(2,1)S(1)}, bf16[384,128]{1,0:T(8,128)(2,1)S(1)}, u32[]{:S(2)}, u32[]{:S(2)}) collective-permute-start(bf16[384,128]{1,0:T(8,128)(2,1)S(1)} %get-tuple-element.24.refs_0_), channel_id=1, source_target_pairs={{0,3},{1,0},{2,1},{3,2},{4,7},{5,4},{6,5},{7,6},{8,11},{9,8},{10,9... | collective-permute-start | bytes 294920 | tf_op jit(solution)/shard_map/ppermute | solution.py:289
  18.7 8.0 %collective-permute-start.5 = (bf16[384,128]{1,0:T(8,128)(2,1)S(1)}, bf16[384,128]{1,0:T(8,128)(2,1)S(1)}, u32[]{:S(2)}, u32[]{:S(2)}) collective-permute-start(bf16[384,128]{1,0:T(8,128)(2,1)S(1)} %get-tuple-element.24.refs_0_), channel_id=1, source_target_pairs={{0,2},{1,3},{2,0},{3,1},{4,6},{5,7},{6,4},{7,5},{8,10},{9,11},{10,... | collective-permute-start | bytes 294920 | tf_op jit(solution)/shard_map/ppermute | solution.py:289
  18.7 8.0 %collective-permute-start.4 = (bf16[384,128]{1,0:T(8,128)(2,1)S(1)}, bf16[384,128]{1,0:T(8,128)(2,1)S(1)}, u32[]{:S(2)}, u32[]{:S(2)}) collective-permute-start(bf16[384,128]{1,0:T(8,128)(2,1)S(1)} %get-tuple-element.24.refs_0_), channel_id=1, source_target_pairs={{0,1},{1,2},{2,3},{3,0},{4,5},{5,6},{6,7},{7,4},{8,9},{9,10},{10,1... | collective-permute-start | bytes 294920 | tf_op jit(solution)/shard_map/ppermute | solution.py:289
  28.4 1.4 %collective-permute-start.7 = (f32[256,128]{1,0:T(8,128)S(1)}, f32[256,128]{1,0:T(8,128)S(1)}, u32[]{:S(2)}, u32[]{:S(2)}) collective-permute-start(f32[256,128]{1,0:T(8,128)S(1)} %get-tuple-element.30), channel_id=1, source_target_pairs={{0,4},{4,0},{8,12},{12,8},{16,20},{20,16},{24,28},{28,24},{1,5},{5... | collective-permute-start | bytes 393224 | tf_op jit(solution)/shard_map/ppermute | solution.py:216
  31.2 5.3 %collective-permute-start.10 = (f16[272,128]{1,0:T(8,128)(2,1)S(1)}, f16[272,128]{1,0:T(8,128)(2,1)S(1)}, u32[]{:S(2)}, u32[]{:S(2)}) collective-permute-start(f16[272,128]{1,0:T(8,128)(2,1)S(1)} %concatenate.3), channel_id=1, source_target_pairs={{0,24},{4,28},{8,16},{12,20},{16,8},{20,12},{24,0},{28,4},{1,25},{... | collective-permute-start | bytes 208904 | tf_op jit(solution)/shard_map/ppermute | solution.py:235
  33.8 4.3 %collective-permute-start.9 = (f16[272,128]{1,0:T(8,128)(2,1)S(1)}, f16[272,128]{1,0:T(8,128)(2,1)S(1)}, u32[]{:S(2)}, u32[]{:S(2)}) collective-permute-start(f16[272,128]{1,0:T(8,128)(2,1)S(1)} %concatenate.3), channel_id=1, source_target_pairs={{0,16},{4,20},{8,24},{12,28},{16,0},{20,4},{24,8},{28,12},{1,17},{... | collective-permute-start | bytes 208904 | tf_op jit(solution)/shard_map/ppermute | solution.py:235
  35.2 4.3 %collective-permute-start.8 = (f16[272,128]{1,0:T(8,128)(2,1)S(1)}, f16[272,128]{1,0:T(8,128)(2,1)S(1)}, u32[]{:S(2)}, u32[]{:S(2)}) collective-permute-start(f16[272,128]{1,0:T(8,128)(2,1)S(1)} %concatenate.3), channel_id=1, source_target_pairs={{0,8},{4,12},{8,0},{12,4},{16,24},{20,28},{24,16},{28,20},{1,9},{5... | collective-permute-start | bytes 208904 | tf_op jit(solution)/shard_map/ppermute | solution.py:235
  39.6 1.4 %collective-permute-start.11 = (f32[256,128]{1,0:T(8,128)S(1)}, f32[256,128]{1,0:T(8,128)S(1)}, u32[]{:S(2)}, u32[]{:S(2)}) collective-permute-start(f32[256,128]{1,0:T(8,128)S(1)} %multiply_add_fusion.refs_1_), channel_id=1, source_target_pairs={{0,4},{4,0},{8,12},{12,8},{16,20},{20,16},{24,28},{28,24},{1,5},{5... | collective-permute-start | bytes 393224 | tf_op jit(solution)/shard_map/ppermute | solution.py:216

commit v7 on v6

--- a/solution.py
+++ b/solution.py
@@ -72,23 +72,9 @@
     return jnp.concatenate([dense[first + s] for s in range(count)], axis=1)
 
 
-def stencil_copies(ids, ops, kinds, dense, sems):
-    blocks, _, size, wide = ops.shape
+def local_id(ids, b, k, blocks):
     total = blocks * lax.axis_size("tile")
-    first = (lax.axis_index("tile") - 1) * blocks
-    dense[...] = jnp.zeros(dense.shape, BF)
-    copies = []
-    for b in range(blocks):
-        for k in range(wide // size):
-            source = lax.rem(ids[b, k] - first + total, total)
-            copy = pltpu.make_async_copy(
-                ops.at[b, kinds, :, pl.ds(k * size, size)],
-                dense.at[:, source, pl.ds(b * size, size), :],
-                sems.at[b, k],
-            )
-            copy.start()
-            copies.append(copy)
-    return copies
+    return lax.rem(ids[b, k] - (lax.axis_index("tile") - 1) * blocks + total, total)
 
 
 def round_kernel(fields, neighbours, wide, narrow, ids, sems, ids_sem):
@@ -108,11 +94,17 @@
     ids_copy.wait()
 
 
-def prepare_kernel(ids, ops, own, dense, lap_own, sems):
-    blocks = ops.shape[0]
-    for copy in stencil_copies(ids, ops, pl.ds(2, 1), dense, sems):
-        copy.wait()
-    lap_own[...] = dot(beside(dense.at[0], blocks, blocks), own[...])
+def prepare_kernel(ids, ops, own, dense, lap_own, held, sems):
+    blocks, _, size, wide = ops.shape
+    copies = [pltpu.make_async_copy(ops.at[b, 2], held.at[b], sems.at[b]) for b in range(blocks)]
+    for copy in copies:
+        copy.start()
+    dense[...] = jnp.zeros(dense.shape, BF)
+    for b in range(blocks):
+        copies[b].wait()
+        for k in range(wide // size):
+            dense[local_id(ids, b, k, blocks), b * size : (b + 1) * size, :] = held[b, :, k * size : (k + 1) * size]
+    lap_own[...] = dot(beside(dense, blocks, blocks), own[...])
 
 
 def around(dense, low, high):
@@ -121,27 +113,28 @@
 
 
 def first_lap_kernel(dense, lap_own, low, high, lap):
-    lap[...] = (lap_own[...] + around(dense.at[0], low, high)).astype(BF)
-
-
-def advect_kernel(ids, ops, velocity, lap_dense, low, own, high, lap, fields, out, dense, vel, vel_sem, op_sems):
-    blocks = ops.shape[0]
+    lap[...] = (lap_own[...] + around(dense, low, high)).astype(BF)
+
+
+def advect_kernel(ids, ops, velocity, lap_dense, low, own, high, lap, fields, out, window):
+    blocks, _, size, wide = ops.shape
     nodes = own.shape[0]
-    vel_copy = pltpu.make_async_copy(velocity, vel, vel_sem)
-    vel_copy.start()
-    copies = stencil_copies(ids, ops, pl.ds(0, 2), dense, op_sems)
-    value = fields[...] - hyper_rate * dot(beside(lap_dense.at[0], blocks, blocks), lap[...])
-    vel_copy.wait()
-    for copy in copies:
-        copy.wait()
-    for k in range(2):
-        grad = dot(beside(dense.at[k], blocks, blocks), own[...]) + around(dense.at[k], low, high)
-        value = value - advect_step * (vel[pl.ds(k, nodes, stride=2), :] * grad)
-    out[...] = value
+    for k, tile in enumerate((low, own, high)):
+        window[k * nodes : (k + 1) * nodes] = tile[...]
+    lap_two = dot(beside(lap_dense, blocks, blocks), lap[...])
+    for b in range(blocks):
+        starts = [pl.multiple_of(local_id(ids, b, k, blocks) * size, size) for k in range(wide // size)]
+        nearby = jnp.concatenate([window[pl.ds(start, size), :] for start in starts], axis=0)
+        grad = dot(ops[b, 0:2].reshape(2 * size, wide), nearby)
+        vel_x = velocity[pl.ds(2 * b * size, size, stride=2), :]
+        vel_y = velocity[pl.ds(2 * b * size + 1, size, stride=2), :]
+        rows = slice(b * size, (b + 1) * size)
+        value = fields[rows] - advect_step * (vel_x * grad[:size] + vel_y * grad[size:])
+        out[rows] = value - hyper_rate * lap_two[rows]
 
 
 def second_lap_kernel(dense, low, high, part, stepped, narrow):
-    value = part[...] - hyper_rate * around(dense.at[0], low, high)
+    value = part[...] - hyper_rate * around(dense, low, high)
     stepped[...] = value
     narrow[...] = value.astype(BF)
 
@@ -198,6 +191,16 @@
         out[...] = early[modes, :] + total[:, :width] + total[:, width:]
 
 
+def pack_kernel(keep, received, out, scaled):
+    value = keep[...] + received[...]
+    out[...] = value
+    top = jnp.max(jnp.abs(value), axis=(0, 1), keepdims=True)
+    power = jnp.round(jnp.log2(jnp.maximum(top, 1e-30)))
+    rows = value.shape[0]
+    scaled[0:rows] = value * jnp.exp2(8.0 - power)
+    scaled[rows:] = jnp.broadcast_to(power, (16, value.shape[1]))
+
+
 def filter_kernel(swap, value, modes, bg_high, bg_low, out):
     which = lax.rem(lax.axis_index("tile") + swap, 2)
     out[...] = value[...] - dot3((bg_high[which], bg_low[which]), split(modes[...]))
@@ -209,18 +212,13 @@
 
 
 def halo(block):
-    return lax.ppermute(block, "tile", shift("tile", 1)), lax.ppermute(block, "tile", shift("tile", -1))
+    high = lax.ppermute(block, "tile", shift("tile", -1))
+    low = lax.ppermute(block, "tile", shift("tile", 1))
+    return low, high
 
 
 def swap(block):
     return lax.ppermute(block, "tile", [(i, i ^ 1) for i in range(lax.axis_size("tile"))])
-
-
-def packed(block):
-    top = jnp.max(jnp.abs(block), keepdims=True)
-    power = jnp.round(jnp.log2(jnp.maximum(top, 1e-30)))
-    tail = jnp.broadcast_to(power, (16, block.shape[1]))
-    return jnp.concatenate([block * jnp.exp2(8.0 - power), tail], axis=0).astype(jnp.float16)
 
 
 def unpacked(sent):
@@ -228,12 +226,16 @@
     return sent[:rows].astype(F32) * jnp.exp2(sent[rows : rows + 1].astype(F32) - 8.0)
 
 
-def chip_sum(block):
+def tile_sum(keep, send):
     count = lax.axis_size("tile")
+    received = swap(send)
     if count <= 8:
-        sent = packed(block)
-        parts = [lax.ppermute(sent, "tile", [(i, i ^ m) for i in range(count)]) for m in range(2, count, 2)]
+        rows, levels = keep.shape
+        block, scaled = call(pack_kernel, (shape(keep.shape, F32), shape((rows + 16, levels), F32)), (keep, received))
+        sent = scaled.astype(jnp.float16)
+        parts = [lax.ppermute(sent, "tile", [(i, i ^ m) for i in range(count)]) for m in reversed(range(2, count, 2))]
         return sum((unpacked(part) for part in parts), block)
+    block = keep + received
     for m in [1 << k for k in range(1, count.bit_length() - 1)]:
         block = block + lax.ppermute(block, "tile", [(i, i ^ m) for i in range(count)])
     return block
@@ -266,10 +268,10 @@
     low, high = halo(rounded)
     lap_dense, lap_own = call(
         prepare_kernel,
-        (shape((1, 3 * blocks, nodes, size), BF), wide),
+        (shape((3 * blocks, nodes, size), BF), wide),
         (ids, operators, rounded),
         "shv",
-        (dma(neighbours.shape),),
+        (pltpu.VMEM((blocks, size, operators.shape[3]), BF), dma((blocks,))),
     )
     lap = call(first_lap_kernel, thin, (lap_dense, lap_own, low, high))
     low_two, high_two = halo(lap)
@@ -277,13 +279,8 @@
         advect_kernel,
         wide,
         (ids, operators, velocity, lap_dense, low, rounded, high, lap, fields),
-        "shhvvvvvv",
-        (
-            pltpu.VMEM((2, 3 * blocks, nodes, size), BF),
-            pltpu.VMEM((2 * nodes, levels), F32),
-            dma(()),
-            dma(neighbours.shape),
-        ),
+        "svvvvvvvv",
+        (pltpu.VMEM((3 * nodes, levels), BF),),
     )
     stepped, narrow = call(second_lap_kernel, (wide, thin), (lap_dense, low_two, high_two, part))
     shards = [narrow] + [lax.ppermute(narrow, "rad", shift("rad", d)) for d in range(1, rads)]
@@ -300,7 +297,7 @@
         (*shards, stepped, jnp.asarray(dh_high), jnp.asarray(dh_low), kappa_ref.reshape(rads, 1, levels))
         + (wbt, early),
     )
-    mine = chip_sum(keep + swap(send))
+    mine = tile_sum(keep, send)
     other = swap(mine)
     some = call(lambda *refs: filter_kernel(0, *refs), wide, (diffused, mine, bg_high, bg_low))
     filtered = call(lambda *refs: filter_kernel(1, *refs), wide, (some, other, bg_high, bg_low))

time: 42.3 us -> 41 us (0.969)
  waiting for transfers between devices: 15.5 us -> 17.3 us
  Pallas kernels: 11.5 us -> 9.74 us
  between operations: 0.91 us -> 0.16 us
  other arithmetic: 0.7 us -> 0.08 us
    ppermute x7, waiting for transfers between devices: 8.52 us -> 11.1 us  [the longest x3 4.81 us: tile_sum(): lax.ppermute(sent, 'tile', [(i, i ^ m) for i in range(count)])]
    pallas_call x9 -> x10, Pallas kernels: 11.5 us -> 9.74 us  [call(): pl.pallas_call(kernel, out_shape=outs, in_specs=[{'s': SMEM, 'h': HBM, 'v...]
    ppermute x3, waiting for transfers between devices: 4.56 us -> 3.81 us  [body(): lax.ppermute(narrow, 'rad', shift('rad', d))]
    reduce_max x1 -> x0, other arithmetic: 0.61 us -> none  [packed(): top = jnp.max(jnp.abs(block), keepdims=True)]
  transfers between devices with their start and end apart: 12 -> 12, of which waited for: 9 -> 10; matrix products, arithmetic and copies ran while one was open for 1% -> 1% of each run, Pallas kernels for 17% -> 13%
where the time goes in v7:
time: 41 us; the launch traced here: 40.9 us
  waiting for transfers between devices  17.3 us (42%)
  starting transfers between devices  13 us (32%)
  Pallas kernels  9.74 us (24%)
  local copies, waits for them, and re-layouts  0.59 us (1%)
    pallas_call x10, Pallas kernels, call(): pl.pallas_call(kernel, out_shape=outs, in_specs=[{'s': SMEM, 'h': HBM, 'v...  9.74 us
    ppermute x3, waiting for transfers between devices, tile_sum(): lax.ppermute(sent, 'tile', [(i, i ^ m) for i in range(count)])  4.81 us
    ppermute x2, waiting for transfers between devices, halo(): low = lax.ppermute(block, 'tile', shift('tile', 1))  4.74 us
    ppermute x3, starting transfers between devices, body(): lax.ppermute(narrow, 'rad', shift('rad', d))  4.67 us
    ppermute x3, starting transfers between devices, tile_sum(): lax.ppermute(sent, 'tile', [(i, i ^ m) for i in range(count)])  4.23 us
    ppermute x3, waiting for transfers between devices, body(): lax.ppermute(narrow, 'rad', shift('rad', d))  3.81 us
    ppermute x2, starting transfers between devices, halo(): high = lax.ppermute(block, 'tile', shift('tile', -1))  3.59 us
    ppermute x2, waiting for transfers between devices, swap(): lax.ppermute(block, 'tile', [(i, i ^ 1) for i in range(lax.axis_size('til...  2.4 us
  transfers between devices with their start and end apart: 12, of which 10 were waited for; matrix products, arithmetic and copies ran while one was open for 1% of the time, Pallas kernels for 13%

profile of v7, /device:TPU:0, one launch (start us, length us, event | category | flops | bytes accessed | tf_op | source)
XLA Modules:
  0.0 40.9 jit_solution(11005875696080892778)
XLA Ops:
  0.0 1.1 %shard_map.100 = (f32[384,128]{1,0:T(8,128)S(1)}, bf16[384,128]{1,0:T(8,128)(2,1)S(1)}, s32[3,7]{1,0:T(4,128)S(1)}) custom-call(f32[384,128]{1,0:T(8,128)} %bitcast.15, s32[3,7]{1,0:T(4,128)} %neighbours.1), custom_call_target="tpu_custom_call" | custom-call | tf_op jit(solution)/shard_map/pallas_call | solution.py:57
  1.1 3.4 %collective-permute-start.1 = (bf16[384,128]{1,0:T(8,128)(2,1)S(1)}, bf16[384,128]{1,0:T(8,128)(2,1)S(1)}, u32[]{:S(2)}, u32[]{:S(2)}) collective-permute-start(bf16[384,128]{1,0:T(8,128)(2,1)S(1)} %get-tuple-element.22.own), channel_id=1, source_target_pairs={{0,28},{4,0},{8,4},{12,8},{16,12},{20,16},{24,20},{28,24},{1,29},{... | collective-permute-start | bytes 294920 | tf_op jit(solution)/shard_map/ppermute | solution.py:215
  4.5 2.0 %shard_map.101 = (bf16[9,384,128]{2,1,0:T(8,128)(2,1)S(1)}, f32[384,128]{1,0:T(8,128)S(1)}) custom-call(s32[3,7]{1,0:T(4,128)S(1)} %get-tuple-element.21.ids, bf16[3,3,128,896]{3,2,1,0:T(8,128)(2,1)} %ops.3, bf16[384,128]{1,0:T(8,128)(2,1)S(1)} %get-tuple-element.22.own), custom_call_target="tpu_custom_call" | custom-call | tf_op jit(solution)/shard_map/pallas_call | solution.py:57
  6.8 2.7 %collective-permute-done.low = bf16[384,128]{1,0:T(8,128)(2,1)S(1)} collective-permute-done((bf16[384,128]{1,0:T(8,128)(2,1)S(1)}, bf16[384,128]{1,0:T(8,128)(2,1)S(1)}, u32[]{:S(2)}, u32[]{:S(2)}) %collective-permute-start) | collective-permute-done | bytes 98336 | tf_op jit(solution)/shard_map/ppermute | solution.py:216
  10.0 0.4 collective-permute-start.2
  10.3 1.2 %shard_map.103.part = f32[384,128]{1,0:T(8,128)S(1)} custom-call(s32[3,7]{1,0:T(4,128)S(1)} %get-tuple-element.21.ids, bf16[3,3,128,896]{3,2,1,0:T(8,128)(2,1)S(1)} %copy-done, f32[768,128]{1,0:T(8,128)S(1)} %bitcast.13, bf16[9,384,128]{2,1,0:T(8,128)(2,1)S(1)} %get-tuple-element.23.dense.lap_dense, bf16[384,128]{1,0:T(8,128)(2,1)S(1)} %collective-permute-done.low, ...), custom_call_target="tpu_custom_call" | custom-call | tf_op jit(solution)/shard_map/pallas_call | solution.py:57
  11.5 1.3 %collective-permute-done.3.high = bf16[384,128]{1,0:T(8,128)(2,1)S(1)} collective-permute-done((bf16[384,128]{1,0:T(8,128)(2,1)S(1)}, bf16[384,128]{1,0:T(8,128)(2,1)S(1)}, u32[]{:S(2)}, u32[]{:S(2)}) %collective-permute-start.3) | collective-permute-done | bytes 98336 | tf_op jit(solution)/shard_map/ppermute | solution.py:215
  12.8 2.1 %collective-permute-done.2.low = bf16[384,128]{1,0:T(8,128)(2,1)S(1)} collective-permute-done((bf16[384,128]{1,0:T(8,128)(2,1)S(1)}, bf16[384,128]{1,0:T(8,128)(2,1)S(1)}, u32[]{:S(2)}, u32[]{:S(2)}) %collective-permute-start.2) | collective-permute-done | bytes 98336 | tf_op jit(solution)/shard_map/ppermute | solution.py:216
  14.9 0.3 shard_map.104
  15.2 3.7 %collective-permute-start.6 = (bf16[384,128]{1,0:T(8,128)(2,1)S(1)}, bf16[384,128]{1,0:T(8,128)(2,1)S(1)}, u32[]{:S(2)}, u32[]{:S(2)}) collective-permute-start(bf16[384,128]{1,0:T(8,128)(2,1)S(1)} %get-tuple-element.26.refs_0_), channel_id=1, source_target_pairs={{0,3},{1,0},{2,1},{3,2},{4,7},{5,4},{6,5},{7,6},{8,11},{9,8},{10,9... | collective-permute-start | bytes 294920 | tf_op jit(solution)/shard_map/ppermute | solution.py:286
  18.9 1.0 %collective-permute-start.4 = (bf16[384,128]{1,0:T(8,128)(2,1)S(1)}, bf16[384,128]{1,0:T(8,128)(2,1)S(1)}, u32[]{:S(2)}, u32[]{:S(2)}) collective-permute-start(bf16[384,128]{1,0:T(8,128)(2,1)S(1)} %get-tuple-element.26.refs_0_), channel_id=1, source_target_pairs={{0,1},{1,2},{2,3},{3,0},{4,5},{5,6},{6,7},{7,4},{8,9},{9,10},{10,1... | collective-permute-start | bytes 294920 | tf_op jit(solution)/shard_map/ppermute | solution.py:286
  19.9 0.6 %broadcast_in_dim.6.weight = f32[1,384]{1,0:T(1,128)} reshape(f32[384]{0:T(512)S(1)} %copy-done.5) | data formatting | bytes 3072 | tf_op jit(solution)/shard_map/broadcast_in_dim | solution.py:290
  20.4 1.8 %shard_map.105 = (bf16[512,384]{1,0:T(8,128)(2,1)S(1)}, f32[512,128]{1,0:T(8,128)S(1)}, bf16[2,384,256]{2,1,0:T(8,128)(2,1)S(1)}, bf16[2,384,256]{2,1,0:T(8,128)(2,1)S(1)}) custom-call(f32[384,512]{1,0:T(8,128)} %basis.1, f32[1,384]{1,0:T(1,128)} %broadcast_in_dim.6.weight, s32[1,512]{1,0:T(1,128)} %bitcast.16, f32[384,128]{1,0:T(8,128)S(1)} %get-tuple-element.27.value.refs_4_), custom_call_target="tpu_custom_call" | custom-call | tf_op jit(solution)/shard_map/pallas_call | solution.py:57
  22.3 3.8 %collective-permute-done.5.refs_2_ = bf16[384,128]{1,0:T(8,128)(2,1)S(1)} collective-permute-done((bf16[384,128]{1,0:T(8,128)(2,1)S(1)}, bf16[384,128]{1,0:T(8,128)(2,1)S(1)}, u32[]{:S(2)}, u32[]{:S(2)}) %collective-permute-start.5) | collective-permute-done | bytes 98336 | tf_op jit(solution)/shard_map/ppermute | solution.py:286
  26.1 1.7 %shard_map.106 = (f32[384,128]{1,0:T(8,128)S(1)}, f32[256,128]{1,0:T(8,128)S(1)}, f32[256,128]{1,0:T(8,128)S(1)}) custom-call(bf16[384,128]{1,0:T(8,128)(2,1)S(1)} %get-tuple-element.26.refs_0_, bf16[384,128]{1,0:T(8,128)(2,1)S(1)} %collective-permute-done.4.refs_1_, bf16[384,128]{1,0:T(8,128)(2,1)S(1)} %collective-permute-done.5.refs_2_, ...), custom_call_target="tpu_custom_call" | custom-call | tf_op jit(solution)/shard_map/pallas_call | solution.py:57
  27.9 1.3 %collective-permute-done.7.received = f32[256,128]{1,0:T(8,128)S(1)} collective-permute-done((f32[256,128]{1,0:T(8,128)S(1)}, f32[256,128]{1,0:T(8,128)S(1)}, u32[]{:S(2)}, u32[]{:S(2)}) %collective-permute-start.7) | collective-permute-done | bytes 131104 | tf_op jit(solution)/shard_map/ppermute | solution.py:221
  29.4 2.7 %collective-permute-start.10 = (f16[272,128]{1,0:T(8,128)(2,1)S(1)}, f16[272,128]{1,0:T(8,128)(2,1)S(1)}, u32[]{:S(2)}, u32[]{:S(2)}) collective-permute-start(f16[272,128]{1,0:T(8,128)(2,1)S(1)} %convert_element_type.21), channel_id=1, source_target_pairs={{0,8},{4,12},{8,0},{12,4},{16,24},{20,28},{24,16},{28,20},{1,9},{5... | collective-permute-start | bytes 208904 | tf_op jit(solution)/shard_map/ppermute | solution.py:236
  32.1 1.2 %collective-permute-start.9 = (f16[272,128]{1,0:T(8,128)(2,1)S(1)}, f16[272,128]{1,0:T(8,128)(2,1)S(1)}, u32[]{:S(2)}, u32[]{:S(2)}) collective-permute-start(f16[272,128]{1,0:T(8,128)(2,1)S(1)} %convert_element_type.21), channel_id=1, source_target_pairs={{0,16},{4,20},{8,24},{12,28},{16,0},{20,4},{24,8},{28,12},{1,17},{... | collective-permute-start | bytes 208904 | tf_op jit(solution)/shard_map/ppermute | solution.py:236
  33.2 0.4 collective-permute-start.8
  33.6 1.0 %collective-permute-done.10 = f16[272,128]{1,0:T(8,128)(2,1)S(1)} collective-permute-done((f16[272,128]{1,0:T(8,128)(2,1)S(1)}, f16[272,128]{1,0:T(8,128)(2,1)S(1)}, u32[]{:S(2)}, u32[]{:S(2)}) %collective-permute-start.10) | collective-permute-done | bytes 69664 | tf_op jit(solution)/shard_map/ppermute | solution.py:236
  34.6 1.8 %collective-permute-done.9 = f16[272,128]{1,0:T(8,128)(2,1)S(1)} collective-permute-done((f16[272,128]{1,0:T(8,128)(2,1)S(1)}, f16[272,128]{1,0:T(8,128)(2,1)S(1)}, u32[]{:S(2)}, u32[]{:S(2)}) %collective-permute-start.9) | collective-permute-done | bytes 69664 | tf_op jit(solution)/shard_map/ppermute | solution.py:236
  36.4 2.0 %collective-permute-done.8 = f16[272,128]{1,0:T(8,128)(2,1)S(1)} collective-permute-done((f16[272,128]{1,0:T(8,128)(2,1)S(1)}, f16[272,128]{1,0:T(8,128)(2,1)S(1)}, u32[]{:S(2)}, u32[]{:S(2)}) %collective-permute-start.8) | collective-permute-done | bytes 69664 | tf_op jit(solution)/shard_map/ppermute | solution.py:236
  38.9 1.1 %collective-permute-done.11.refs_1_ = f32[256,128]{1,0:T(8,128)S(1)} collective-permute-done((f32[256,128]{1,0:T(8,128)S(1)}, f32[256,128]{1,0:T(8,128)S(1)}, u32[]{:S(2)}, u32[]{:S(2)}) %collective-permute-start.11) | collective-permute-done | bytes 131104 | tf_op jit(solution)/shard_map/ppermute | solution.py:221
  39.9 0.9 %shard_map.109 = f32[384,128]{1,0:T(8,128)} custom-call(f32[384,128]{1,0:T(8,128)S(1)} %shard_map.108.refs_0_, f32[256,128]{1,0:T(8,128)S(1)} %collective-permute-done.11.refs_1_, bf16[2,384,256]{2,1,0:T(8,128)(2,1)S(1)} %get-tuple-element.35.refs_2_, bf16[2,384,256]{2,1,0:T(8,128)(2,1)S(1)} %get-tuple-element.36.refs_3_), custom_call_target="tpu_custom_call" | custom-call | tf_op jit(solution)/shard_map/pallas_call | solution.py:57
  (28 shorter events, 1.5 us)
Async XLA Ops:
  0.0 10.3 %copy-start = (bf16[3,3,128,896]{3,2,1,0:T(8,128)(2,1)S(1)}, bf16[3,3,128,896]{3,2,1,0:T(8,128)(2,1)}, u32[]{:S(2)}) copy-start(bf16[3,3,128,896]{3,2,1,0:T(8,128)(2,1)} %ops.3) | copy-start | bytes 6193156
  0.0 10.3 %copy-start.3 = (f32[384,2,128]{2,1,0:T(2,128)S(1)}, f32[384,2,128]{2,1,0:T(2,128)}, u32[]{:S(2)}) copy-start(f32[384,2,128]{2,1,0:T(2,128)} %param.11) | copy-start | bytes 1179652
  1.1 5.7 %collective-permute-start.1 = (bf16[384,128]{1,0:T(8,128)(2,1)S(1)}, bf16[384,128]{1,0:T(8,128)(2,1)S(1)}, u32[]{:S(2)}, u32[]{:S(2)}) collective-permute-start(bf16[384,128]{1,0:T(8,128)(2,1)S(1)} %get-tuple-element.22.own), channel_id=1, source_target_pairs={{0,28},{4,0},{8,4},{12,8},{16,12},{20,16},{24,20},{28,24},{1,29},{... | collective-permute-start | bytes 294920 | tf_op jit(solution)/shard_map/ppermute | solution.py:215
  4.5 4.9 %collective-permute-start = (bf16[384,128]{1,0:T(8,128)(2,1)S(1)}, bf16[384,128]{1,0:T(8,128)(2,1)S(1)}, u32[]{:S(2)}, u32[]{:S(2)}) collective-permute-start(bf16[384,128]{1,0:T(8,128)(2,1)S(1)} %get-tuple-element.22.own), channel_id=1, source_target_pairs={{0,4},{4,8},{8,12},{12,16},{16,20},{20,24},{24,28},{28,0},{1,5},{5... | collective-permute-start | bytes 294920 | tf_op jit(solution)/shard_map/ppermute | solution.py:216
  9.7 3.1 %collective-permute-start.3 = (bf16[384,128]{1,0:T(8,128)(2,1)S(1)}, bf16[384,128]{1,0:T(8,128)(2,1)S(1)}, u32[]{:S(2)}, u32[]{:S(2)}) collective-permute-start(bf16[384,128]{1,0:T(8,128)(2,1)S(1)} %shard_map.102.lap), channel_id=1, source_target_pairs={{0,28},{4,0},{8,4},{12,8},{16,12},{20,16},{24,20},{28,24},{1,29},{... | collective-permute-start | bytes 294920 | tf_op jit(solution)/shard_map/ppermute | solution.py:215
  10.0 4.9 %collective-permute-start.2 = (bf16[384,128]{1,0:T(8,128)(2,1)S(1)}, bf16[384,128]{1,0:T(8,128)(2,1)S(1)}, u32[]{:S(2)}, u32[]{:S(2)}) collective-permute-start(bf16[384,128]{1,0:T(8,128)(2,1)S(1)} %shard_map.102.lap), channel_id=1, source_target_pairs={{0,4},{4,8},{8,12},{12,16},{16,20},{20,24},{24,28},{28,0},{1,5},{5... | collective-permute-start | bytes 294920 | tf_op jit(solution)/shard_map/ppermute | solution.py:216
  10.3 9.6 %copy-start.5 = (f32[384]{0:T(512)S(1)}, f32[384]{0:T(512)}, u32[]{:S(2)}) copy-start(f32[384]{0:T(512)} %param.15) | copy-start | bytes 4612
  11.5 14.6 %copy-start.1 = (bf16[4,512,128]{2,1,0:T(8,128)(2,1)S(1)}, bf16[4,512,128]{2,1,0:T(8,128)(2,1)}, u32[]{:S(2)}) copy-start(bf16[4,512,128]{2,1,0:T(8,128)(2,1)} %constant.12.clone.refs_6_) | copy-start | bytes 1572868
  11.5 14.6 %copy-start.2 = (bf16[4,512,128]{2,1,0:T(8,128)(2,1)S(1)}, bf16[4,512,128]{2,1,0:T(8,128)(2,1)}, u32[]{:S(2)}) copy-start(bf16[4,512,128]{2,1,0:T(8,128)(2,1)} %constant.11.clone.refs_5_) | copy-start | bytes 1572868
  11.5 14.6 %copy-start.4 = (f32[512]{0:T(512)S(1)}, f32[512]{0:T(512)}, u32[]{:S(2)}) copy-start(f32[512]{0:T(512)} %param.14) | copy-start | bytes 6148
  15.2 7.1 %collective-permute-start.6 = (bf16[384,128]{1,0:T(8,128)(2,1)S(1)}, bf16[384,128]{1,0:T(8,128)(2,1)S(1)}, u32[]{:S(2)}, u32[]{:S(2)}) collective-permute-start(bf16[384,128]{1,0:T(8,128)(2,1)S(1)} %get-tuple-element.26.refs_0_), channel_id=1, source_target_pairs={{0,3},{1,0},{2,1},{3,2},{4,7},{5,4},{6,5},{7,6},{8,11},{9,8},{10,9... | collective-permute-start | bytes 294920 | tf_op jit(solution)/shard_map/ppermute | solution.py:286
  18.9 7.2 %collective-permute-start.5 = (bf16[384,128]{1,0:T(8,128)(2,1)S(1)}, bf16[384,128]{1,0:T(8,128)(2,1)S(1)}, u32[]{:S(2)}, u32[]{:S(2)}) collective-permute-start(bf16[384,128]{1,0:T(8,128)(2,1)S(1)} %get-tuple-element.26.refs_0_), channel_id=1, source_target_pairs={{0,2},{1,3},{2,0},{3,1},{4,6},{5,7},{6,4},{7,5},{8,10},{9,11},{10,... | collective-permute-start | bytes 294920 | tf_op jit(solution)/shard_map/ppermute | solution.py:286
  18.9 7.2 %collective-permute-start.4 = (bf16[384,128]{1,0:T(8,128)(2,1)S(1)}, bf16[384,128]{1,0:T(8,128)(2,1)S(1)}, u32[]{:S(2)}, u32[]{:S(2)}) collective-permute-start(bf16[384,128]{1,0:T(8,128)(2,1)S(1)} %get-tuple-element.26.refs_0_), channel_id=1, source_target_pairs={{0,1},{1,2},{2,3},{3,0},{4,5},{5,6},{6,7},{7,4},{8,9},{9,10},{10,1... | collective-permute-start | bytes 294920 | tf_op jit(solution)/shard_map/ppermute | solution.py:286
  27.8 1.4 %collective-permute-start.7 = (f32[256,128]{1,0:T(8,128)S(1)}, f32[256,128]{1,0:T(8,128)S(1)}, u32[]{:S(2)}, u32[]{:S(2)}) collective-permute-start(f32[256,128]{1,0:T(8,128)S(1)} %get-tuple-element.32), channel_id=1, source_target_pairs={{0,4},{4,0},{8,12},{12,8},{16,20},{20,16},{24,28},{28,24},{1,5},{5... | collective-permute-start | bytes 393224 | tf_op jit(solution)/shard_map/ppermute | solution.py:221
  29.4 5.2 %collective-permute-start.10 = (f16[272,128]{1,0:T(8,128)(2,1)S(1)}, f16[272,128]{1,0:T(8,128)(2,1)S(1)}, u32[]{:S(2)}, u32[]{:S(2)}) collective-permute-start(f16[272,128]{1,0:T(8,128)(2,1)S(1)} %convert_element_type.21), channel_id=1, source_target_pairs={{0,8},{4,12},{8,0},{12,4},{16,24},{20,28},{24,16},{28,20},{1,9},{5... | collective-permute-start | bytes 208904 | tf_op jit(solution)/shard_map/ppermute | solution.py:236
  32.1 4.3 %collective-permute-start.9 = (f16[272,128]{1,0:T(8,128)(2,1)S(1)}, f16[272,128]{1,0:T(8,128)(2,1)S(1)}, u32[]{:S(2)}, u32[]{:S(2)}) collective-permute-start(f16[272,128]{1,0:T(8,128)(2,1)S(1)} %convert_element_type.21), channel_id=1, source_target_pairs={{0,16},{4,20},{8,24},{12,28},{16,0},{20,4},{24,8},{28,12},{1,17},{... | collective-permute-start | bytes 208904 | tf_op jit(solution)/shard_map/ppermute | solution.py:236
  33.2 5.2 %collective-permute-start.8 = (f16[272,128]{1,0:T(8,128)(2,1)S(1)}, f16[272,128]{1,0:T(8,128)(2,1)S(1)}, u32[]{:S(2)}, u32[]{:S(2)}) collective-permute-start(f16[272,128]{1,0:T(8,128)(2,1)S(1)} %convert_element_type.21), channel_id=1, source_target_pairs={{0,24},{4,28},{8,16},{12,20},{16,8},{20,12},{24,0},{28,4},{1,25},{... | collective-permute-start | bytes 208904 | tf_op jit(solution)/shard_map/ppermute | solution.py:236
  38.5 1.4 %collective-permute-start.11 = (f32[256,128]{1,0:T(8,128)S(1)}, f32[256,128]{1,0:T(8,128)S(1)}, u32[]{:S(2)}, u32[]{:S(2)}) collective-permute-start(f32[256,128]{1,0:T(8,128)S(1)} %multiply_add_fusion.refs_1_), channel_id=1, source_target_pairs={{0,4},{4,0},{8,12},{12,8},{16,20},{20,16},{24,28},{28,24},{1,5},{5... | collective-permute-start | bytes 393224 | tf_op jit(solution)/shard_map/ppermute | solution.py:221

commit v8 on v7

--- a/solution.py
+++ b/solution.py
@@ -112,7 +112,7 @@
     return dot(beside(dense, 0, blocks), low[...]) + dot(beside(dense, 2 * blocks, blocks), high[...])
 
 
-def first_lap_kernel(dense, lap_own, low, high, lap):
+def first_lap_kernel(dense, lap_own, high, low, lap):
     lap[...] = (lap_own[...] + around(dense, low, high)).astype(BF)
 
 
@@ -133,7 +133,7 @@
         out[rows] = value - hyper_rate * lap_two[rows]
 
 
-def second_lap_kernel(dense, low, high, part, stepped, narrow):
+def second_lap_kernel(dense, high, low, part, stepped, narrow):
     value = part[...] - hyper_rate * around(dense, low, high)
     stepped[...] = value
     narrow[...] = value.astype(BF)
@@ -273,7 +273,7 @@
         "shv",
         (pltpu.VMEM((blocks, size, operators.shape[3]), BF), dma((blocks,))),
     )
-    lap = call(first_lap_kernel, thin, (lap_dense, lap_own, low, high))
+    lap = call(first_lap_kernel, thin, (lap_dense, lap_own, high, low))
     low_two, high_two = halo(lap)
     part = call(
         advect_kernel,
@@ -282,7 +282,7 @@
         "svvvvvvvv",
         (pltpu.VMEM((3 * nodes, levels), BF),),
     )
-    stepped, narrow = call(second_lap_kernel, (wide, thin), (lap_dense, low_two, high_two, part))
+    stepped, narrow = call(second_lap_kernel, (wide, thin), (lap_dense, high_two, low_two, part))
     shards = [narrow] + [lax.ppermute(narrow, "rad", shift("rad", d)) for d in range(1, rads)]
     wbt, early, bg_high, bg_low = call(
         project_kernel,

time: 41 us -> 39.1 us (0.954)
  waiting for transfers between devices: 17.3 us -> 12.9 us
  starting transfers between devices: 13 us -> 15.5 us
    ppermute x2, waiting for transfers between devices: 4.74 us -> 1.24 us  [halo(): low = lax.ppermute(block, 'tile', shift('tile', 1))]
    ppermute x3, waiting for transfers between devices: 3.81 us -> 6.99 us  [body(): lax.ppermute(narrow, 'rad', shift('rad', d))]
    ppermute x3, waiting for transfers between devices: 4.81 us -> 2.39 us  [tile_sum(): lax.ppermute(sent, 'tile', [(i, i ^ m) for i in range(count)])]
    ppermute x2, starting transfers between devices: 0.36 us -> 2.24 us  [halo(): low = lax.ppermute(block, 'tile', shift('tile', 1))]
    ppermute x2, waiting for transfers between devices: 1.55 us -> 0.01 us  [halo(): high = lax.ppermute(block, 'tile', shift('tile', -1))]
    ppermute x3, starting transfers between devices: 4.67 us -> 5.39 us  [body(): lax.ppermute(narrow, 'rad', shift('rad', d))]
    ppermute x3, starting transfers between devices: 4.23 us -> 3.55 us  [tile_sum(): lax.ppermute(sent, 'tile', [(i, i ^ m) for i in range(count)])]
    ppermute x2, starting transfers between devices: 3.59 us -> 4.05 us  [halo(): high = lax.ppermute(block, 'tile', shift('tile', -1))]
  transfers between devices with their start and end apart: 12 -> 12, of which waited for: 10 -> 7; matrix products, arithmetic and copies ran while one was open for 1% -> 1% of each run, Pallas kernels for 13% -> 14%
where the time goes in v8:
time: 39.1 us; the launch traced here: 39 us
  starting transfers between devices  15.5 us (40%)
  waiting for transfers between devices  12.9 us (33%)
  Pallas kernels  9.73 us (25%)
  local copies, waits for them, and re-layouts  0.59 us (2%)
    pallas_call x10, Pallas kernels, call(): pl.pallas_call(kernel, out_shape=outs, in_specs=[{'s': SMEM, 'h': HBM, 'v...  9.73 us
    ppermute x3, waiting for transfers between devices, body(): lax.ppermute(narrow, 'rad', shift('rad', d))  6.99 us
    ppermute x3, starting transfers between devices, body(): lax.ppermute(narrow, 'rad', shift('rad', d))  5.39 us
    ppermute x2, starting transfers between devices, halo(): high = lax.ppermute(block, 'tile', shift('tile', -1))  4.05 us
    ppermute x3, starting transfers between devices, tile_sum(): lax.ppermute(sent, 'tile', [(i, i ^ m) for i in range(count)])  3.55 us
    ppermute x3, waiting for transfers between devices, tile_sum(): lax.ppermute(sent, 'tile', [(i, i ^ m) for i in range(count)])  2.39 us
    ppermute x2, waiting for transfers between devices, swap(): lax.ppermute(block, 'tile', [(i, i ^ 1) for i in range(lax.axis_size('til...  2.3 us
    ppermute x2, starting transfers between devices, halo(): low = lax.ppermute(block, 'tile', shift('tile', 1))  2.24 us
  transfers between devices with their start and end apart: 12, of which 7 were waited for; matrix products, arithmetic and copies ran while one was open for 1% of the time, Pallas kernels for 14%

profile of v8, /device:TPU:0, one launch (start us, length us, event | category | flops | bytes accessed | tf_op | source)
XLA Modules:
  0.0 39.0 jit_solution(3958227893151390699)
XLA Ops:
  0.0 1.1 %shard_map.100 = (f32[384,128]{1,0:T(8,128)S(1)}, bf16[384,128]{1,0:T(8,128)(2,1)S(1)}, s32[3,7]{1,0:T(4,128)S(1)}) custom-call(f32[384,128]{1,0:T(8,128)} %bitcast.15, s32[3,7]{1,0:T(4,128)} %neighbours.1), custom_call_target="tpu_custom_call" | custom-call | tf_op jit(solution)/shard_map/pallas_call | solution.py:57
  1.1 0.5 %collective-permute-start.1 = (bf16[384,128]{1,0:T(8,128)(2,1)S(1)}, bf16[384,128]{1,0:T(8,128)(2,1)S(1)}, u32[]{:S(2)}, u32[]{:S(2)}) collective-permute-start(bf16[384,128]{1,0:T(8,128)(2,1)S(1)} %get-tuple-element.22.own), channel_id=1, source_target_pairs={{0,4},{4,8},{8,12},{12,16},{16,20},{20,24},{24,28},{28,0},{1,5},{5... | collective-permute-start | bytes 294920 | tf_op jit(solution)/shard_map/ppermute | solution.py:216
  1.6 2.9 %collective-permute-start = (bf16[384,128]{1,0:T(8,128)(2,1)S(1)}, bf16[384,128]{1,0:T(8,128)(2,1)S(1)}, u32[]{:S(2)}, u32[]{:S(2)}) collective-permute-start(bf16[384,128]{1,0:T(8,128)(2,1)S(1)} %get-tuple-element.22.own), channel_id=1, source_target_pairs={{0,28},{4,0},{8,4},{12,8},{16,12},{20,16},{24,20},{28,24},{1,29},{... | collective-permute-start | bytes 294920 | tf_op jit(solution)/shard_map/ppermute | solution.py:215
  4.6 2.0 %shard_map.101 = (bf16[9,384,128]{2,1,0:T(8,128)(2,1)S(1)}, f32[384,128]{1,0:T(8,128)S(1)}) custom-call(s32[3,7]{1,0:T(4,128)S(1)} %get-tuple-element.21.ids, bf16[3,3,128,896]{3,2,1,0:T(8,128)(2,1)} %ops.3, bf16[384,128]{1,0:T(8,128)(2,1)S(1)} %get-tuple-element.22.own), custom_call_target="tpu_custom_call" | custom-call | tf_op jit(solution)/shard_map/pallas_call | solution.py:57
  6.8 0.3 shard_map.102.lap
  7.1 1.7 %collective-permute-start.3 = (bf16[384,128]{1,0:T(8,128)(2,1)S(1)}, bf16[384,128]{1,0:T(8,128)(2,1)S(1)}, u32[]{:S(2)}, u32[]{:S(2)}) collective-permute-start(bf16[384,128]{1,0:T(8,128)(2,1)S(1)} %shard_map.102.lap), channel_id=1, source_target_pairs={{0,4},{4,8},{8,12},{12,16},{16,20},{20,24},{24,28},{28,0},{1,5},{5... | collective-permute-start | bytes 294920 | tf_op jit(solution)/shard_map/ppermute | solution.py:216
  8.8 1.1 %collective-permute-start.2 = (bf16[384,128]{1,0:T(8,128)(2,1)S(1)}, bf16[384,128]{1,0:T(8,128)(2,1)S(1)}, u32[]{:S(2)}, u32[]{:S(2)}) collective-permute-start(bf16[384,128]{1,0:T(8,128)(2,1)S(1)} %shard_map.102.lap), channel_id=1, source_target_pairs={{0,28},{4,0},{8,4},{12,8},{16,12},{20,16},{24,20},{28,24},{1,29},{... | collective-permute-start | bytes 294920 | tf_op jit(solution)/shard_map/ppermute | solution.py:215
  10.0 1.2 %shard_map.103.part = f32[384,128]{1,0:T(8,128)S(1)} custom-call(s32[3,7]{1,0:T(4,128)S(1)} %get-tuple-element.21.ids, bf16[3,3,128,896]{3,2,1,0:T(8,128)(2,1)S(1)} %copy-done, f32[768,128]{1,0:T(8,128)S(1)} %bitcast.13, bf16[9,384,128]{2,1,0:T(8,128)(2,1)S(1)} %get-tuple-element.23.dense.lap_dense, bf16[384,128]{1,0:T(8,128)(2,1)S(1)} %collective-permute-done.1.low, ...), custom_call_target="tpu_custom_call" | custom-call | tf_op jit(solution)/shard_map/pallas_call | solution.py:57
  11.2 1.0 %collective-permute-done.3.low = bf16[384,128]{1,0:T(8,128)(2,1)S(1)} collective-permute-done((bf16[384,128]{1,0:T(8,128)(2,1)S(1)}, bf16[384,128]{1,0:T(8,128)(2,1)S(1)}, u32[]{:S(2)}, u32[]{:S(2)}) %collective-permute-start.3) | collective-permute-done | bytes 98336 | tf_op jit(solution)/shard_map/ppermute | solution.py:216
  12.2 0.3 shard_map.104
  12.5 4.4 %collective-permute-start.6 = (bf16[384,128]{1,0:T(8,128)(2,1)S(1)}, bf16[384,128]{1,0:T(8,128)(2,1)S(1)}, u32[]{:S(2)}, u32[]{:S(2)}) collective-permute-start(bf16[384,128]{1,0:T(8,128)(2,1)S(1)} %get-tuple-element.26.refs_0_), channel_id=1, source_target_pairs={{0,3},{1,0},{2,1},{3,2},{4,7},{5,4},{6,5},{7,6},{8,11},{9,8},{10,9... | collective-permute-start | bytes 294920 | tf_op jit(solution)/shard_map/ppermute | solution.py:286
  16.9 1.0 %collective-permute-start.4 = (bf16[384,128]{1,0:T(8,128)(2,1)S(1)}, bf16[384,128]{1,0:T(8,128)(2,1)S(1)}, u32[]{:S(2)}, u32[]{:S(2)}) collective-permute-start(bf16[384,128]{1,0:T(8,128)(2,1)S(1)} %get-tuple-element.26.refs_0_), channel_id=1, source_target_pairs={{0,1},{1,2},{2,3},{3,0},{4,5},{5,6},{6,7},{7,4},{8,9},{9,10},{10,1... | collective-permute-start | bytes 294920 | tf_op jit(solution)/shard_map/ppermute | solution.py:286
  17.9 0.6 %broadcast_in_dim.6.weight = f32[1,384]{1,0:T(1,128)} reshape(f32[384]{0:T(512)S(1)} %copy-done.5) | data formatting | bytes 3072 | tf_op jit(solution)/shard_map/broadcast_in_dim | solution.py:290
  18.5 1.8 %shard_map.105 = (bf16[512,384]{1,0:T(8,128)(2,1)S(1)}, f32[512,128]{1,0:T(8,128)S(1)}, bf16[2,384,256]{2,1,0:T(8,128)(2,1)S(1)}, bf16[2,384,256]{2,1,0:T(8,128)(2,1)S(1)}) custom-call(f32[384,512]{1,0:T(8,128)} %basis.1, f32[1,384]{1,0:T(1,128)} %broadcast_in_dim.6.weight, s32[1,512]{1,0:T(1,128)} %bitcast.16, f32[384,128]{1,0:T(8,128)S(1)} %get-tuple-element.27.value.refs_4_), custom_call_target="tpu_custom_call" | custom-call | tf_op jit(solution)/shard_map/pallas_call | solution.py:57
  20.3 7.0 %collective-permute-done.5.refs_2_ = bf16[384,128]{1,0:T(8,128)(2,1)S(1)} collective-permute-done((bf16[384,128]{1,0:T(8,128)(2,1)S(1)}, bf16[384,128]{1,0:T(8,128)(2,1)S(1)}, u32[]{:S(2)}, u32[]{:S(2)}) %collective-permute-start.5) | collective-permute-done | bytes 98336 | tf_op jit(solution)/shard_map/ppermute | solution.py:286
  27.3 1.7 %shard_map.106 = (f32[384,128]{1,0:T(8,128)S(1)}, f32[256,128]{1,0:T(8,128)S(1)}, f32[256,128]{1,0:T(8,128)S(1)}) custom-call(bf16[384,128]{1,0:T(8,128)(2,1)S(1)} %get-tuple-element.26.refs_0_, bf16[384,128]{1,0:T(8,128)(2,1)S(1)} %collective-permute-done.4.refs_1_, bf16[384,128]{1,0:T(8,128)(2,1)S(1)} %collective-permute-done.5.refs_2_, ...), custom_call_target="tpu_custom_call" | custom-call | tf_op jit(solution)/shard_map/pallas_call | solution.py:57
  29.2 1.2 %collective-permute-done.7.received = f32[256,128]{1,0:T(8,128)S(1)} collective-permute-done((f32[256,128]{1,0:T(8,128)S(1)}, f32[256,128]{1,0:T(8,128)S(1)}, u32[]{:S(2)}, u32[]{:S(2)}) %collective-permute-start.7) | collective-permute-done | bytes 131104 | tf_op jit(solution)/shard_map/ppermute | solution.py:221
  30.7 0.4 %collective-permute-start.9 = (f16[272,128]{1,0:T(8,128)(2,1)S(1)}, f16[272,128]{1,0:T(8,128)(2,1)S(1)}, u32[]{:S(2)}, u32[]{:S(2)}) collective-permute-start(f16[272,128]{1,0:T(8,128)(2,1)S(1)} %convert_element_type.21), channel_id=1, source_target_pairs={{0,16},{4,20},{8,24},{12,28},{16,0},{20,4},{24,8},{28,12},{1,17},{... | collective-permute-start | bytes 208904 | tf_op jit(solution)/shard_map/ppermute | solution.py:236
  31.1 3.1 %collective-permute-start.8 = (f16[272,128]{1,0:T(8,128)(2,1)S(1)}, f16[272,128]{1,0:T(8,128)(2,1)S(1)}, u32[]{:S(2)}, u32[]{:S(2)}) collective-permute-start(f16[272,128]{1,0:T(8,128)(2,1)S(1)} %convert_element_type.21), channel_id=1, source_target_pairs={{0,24},{4,28},{8,16},{12,20},{16,8},{20,12},{24,0},{28,4},{1,25},{... | collective-permute-start | bytes 208904 | tf_op jit(solution)/shard_map/ppermute | solution.py:236
  34.1 1.2 %collective-permute-done.10 = f16[272,128]{1,0:T(8,128)(2,1)S(1)} collective-permute-done((f16[272,128]{1,0:T(8,128)(2,1)S(1)}, f16[272,128]{1,0:T(8,128)(2,1)S(1)}, u32[]{:S(2)}, u32[]{:S(2)}) %collective-permute-start.10) | collective-permute-done | bytes 69664 | tf_op jit(solution)/shard_map/ppermute | solution.py:236
  35.3 1.2 %collective-permute-done.9 = f16[272,128]{1,0:T(8,128)(2,1)S(1)} collective-permute-done((f16[272,128]{1,0:T(8,128)(2,1)S(1)}, f16[272,128]{1,0:T(8,128)(2,1)S(1)}, u32[]{:S(2)}, u32[]{:S(2)}) %collective-permute-start.9) | collective-permute-done | bytes 69664 | tf_op jit(solution)/shard_map/ppermute | solution.py:236
  36.7 0.3 shard_map.108.refs_0_
  37.0 1.1 %collective-permute-done.11.refs_1_ = f32[256,128]{1,0:T(8,128)S(1)} collective-permute-done((f32[256,128]{1,0:T(8,128)S(1)}, f32[256,128]{1,0:T(8,128)S(1)}, u32[]{:S(2)}, u32[]{:S(2)}) %collective-permute-start.11) | collective-permute-done | bytes 131104 | tf_op jit(solution)/shard_map/ppermute | solution.py:221
  38.0 0.9 %shard_map.109 = f32[384,128]{1,0:T(8,128)} custom-call(f32[384,128]{1,0:T(8,128)S(1)} %shard_map.108.refs_0_, f32[256,128]{1,0:T(8,128)S(1)} %collective-permute-done.11.refs_1_, bf16[2,384,256]{2,1,0:T(8,128)(2,1)S(1)} %get-tuple-element.35.refs_2_, bf16[2,384,256]{2,1,0:T(8,128)(2,1)S(1)} %get-tuple-element.36.refs_3_), custom_call_target="tpu_custom_call" | custom-call | tf_op jit(solution)/shard_map/pallas_call | solution.py:57
  (28 shorter events, 0.8 us)
Async XLA Ops:
  0.0 9.9 %copy-start = (bf16[3,3,128,896]{3,2,1,0:T(8,128)(2,1)S(1)}, bf16[3,3,128,896]{3,2,1,0:T(8,128)(2,1)}, u32[]{:S(2)}) copy-start(bf16[3,3,128,896]{3,2,1,0:T(8,128)(2,1)} %ops.3) | copy-start | bytes 6193156
  0.0 9.9 %copy-start.3 = (f32[384,2,128]{2,1,0:T(2,128)S(1)}, f32[384,2,128]{2,1,0:T(2,128)}, u32[]{:S(2)}) copy-start(f32[384,2,128]{2,1,0:T(2,128)} %param.11) | copy-start | bytes 1179652
  1.1 5.7 %collective-permute-start.1 = (bf16[384,128]{1,0:T(8,128)(2,1)S(1)}, bf16[384,128]{1,0:T(8,128)(2,1)S(1)}, u32[]{:S(2)}, u32[]{:S(2)}) collective-permute-start(bf16[384,128]{1,0:T(8,128)(2,1)S(1)} %get-tuple-element.22.own), channel_id=1, source_target_pairs={{0,4},{4,8},{8,12},{12,16},{16,20},{20,24},{24,28},{28,0},{1,5},{5... | collective-permute-start | bytes 294920 | tf_op jit(solution)/shard_map/ppermute | solution.py:216
  1.6 5.2 %collective-permute-start = (bf16[384,128]{1,0:T(8,128)(2,1)S(1)}, bf16[384,128]{1,0:T(8,128)(2,1)S(1)}, u32[]{:S(2)}, u32[]{:S(2)}) collective-permute-start(bf16[384,128]{1,0:T(8,128)(2,1)S(1)} %get-tuple-element.22.own), channel_id=1, source_target_pairs={{0,28},{4,0},{8,4},{12,8},{16,12},{20,16},{24,20},{28,24},{1,29},{... | collective-permute-start | bytes 294920 | tf_op jit(solution)/shard_map/ppermute | solution.py:215
  7.1 5.1 %collective-permute-start.3 = (bf16[384,128]{1,0:T(8,128)(2,1)S(1)}, bf16[384,128]{1,0:T(8,128)(2,1)S(1)}, u32[]{:S(2)}, u32[]{:S(2)}) collective-permute-start(bf16[384,128]{1,0:T(8,128)(2,1)S(1)} %shard_map.102.lap), channel_id=1, source_target_pairs={{0,4},{4,8},{8,12},{12,16},{16,20},{20,24},{24,28},{28,0},{1,5},{5... | collective-permute-start | bytes 294920 | tf_op jit(solution)/shard_map/ppermute | solution.py:216
  8.8 3.3 %collective-permute-start.2 = (bf16[384,128]{1,0:T(8,128)(2,1)S(1)}, bf16[384,128]{1,0:T(8,128)(2,1)S(1)}, u32[]{:S(2)}, u32[]{:S(2)}) collective-permute-start(bf16[384,128]{1,0:T(8,128)(2,1)S(1)} %shard_map.102.lap), channel_id=1, source_target_pairs={{0,28},{4,0},{8,4},{12,8},{16,12},{20,16},{24,20},{28,24},{1,29},{... | collective-permute-start | bytes 294920 | tf_op jit(solution)/shard_map/ppermute | solution.py:215
  10.0 7.9 %copy-start.5 = (f32[384]{0:T(512)S(1)}, f32[384]{0:T(512)}, u32[]{:S(2)}) copy-start(f32[384]{0:T(512)} %param.15) | copy-start | bytes 4612
  11.1 16.2 %copy-start.1 = (bf16[4,512,128]{2,1,0:T(8,128)(2,1)S(1)}, bf16[4,512,128]{2,1,0:T(8,128)(2,1)}, u32[]{:S(2)}) copy-start(bf16[4,512,128]{2,1,0:T(8,128)(2,1)} %constant.12.clone.refs_6_) | copy-start | bytes 1572868
  11.1 16.2 %copy-start.2 = (bf16[4,512,128]{2,1,0:T(8,128)(2,1)S(1)}, bf16[4,512,128]{2,1,0:T(8,128)(2,1)}, u32[]{:S(2)}) copy-start(bf16[4,512,128]{2,1,0:T(8,128)(2,1)} %constant.11.clone.refs_5_) | copy-start | bytes 1572868
  11.2 16.2 %copy-start.4 = (f32[512]{0:T(512)S(1)}, f32[512]{0:T(512)}, u32[]{:S(2)}) copy-start(f32[512]{0:T(512)} %param.14) | copy-start | bytes 6148
  12.5 7.8 %collective-permute-start.6 = (bf16[384,128]{1,0:T(8,128)(2,1)S(1)}, bf16[384,128]{1,0:T(8,128)(2,1)S(1)}, u32[]{:S(2)}, u32[]{:S(2)}) collective-permute-start(bf16[384,128]{1,0:T(8,128)(2,1)S(1)} %get-tuple-element.26.refs_0_), channel_id=1, source_target_pairs={{0,3},{1,0},{2,1},{3,2},{4,7},{5,4},{6,5},{7,6},{8,11},{9,8},{10,9... | collective-permute-start | bytes 294920 | tf_op jit(solution)/shard_map/ppermute | solution.py:286
  16.9 10.4 %collective-permute-start.5 = (bf16[384,128]{1,0:T(8,128)(2,1)S(1)}, bf16[384,128]{1,0:T(8,128)(2,1)S(1)}, u32[]{:S(2)}, u32[]{:S(2)}) collective-permute-start(bf16[384,128]{1,0:T(8,128)(2,1)S(1)} %get-tuple-element.26.refs_0_), channel_id=1, source_target_pairs={{0,2},{1,3},{2,0},{3,1},{4,6},{5,7},{6,4},{7,5},{8,10},{9,11},{10,... | collective-permute-start | bytes 294920 | tf_op jit(solution)/shard_map/ppermute | solution.py:286
  16.9 10.4 %collective-permute-start.4 = (bf16[384,128]{1,0:T(8,128)(2,1)S(1)}, bf16[384,128]{1,0:T(8,128)(2,1)S(1)}, u32[]{:S(2)}, u32[]{:S(2)}) collective-permute-start(bf16[384,128]{1,0:T(8,128)(2,1)S(1)} %get-tuple-element.26.refs_0_), channel_id=1, source_target_pairs={{0,1},{1,2},{2,3},{3,0},{4,5},{5,6},{6,7},{7,4},{8,9},{9,10},{10,1... | collective-permute-start | bytes 294920 | tf_op jit(solution)/shard_map/ppermute | solution.py:286
  29.0 1.4 %collective-permute-start.7 = (f32[256,128]{1,0:T(8,128)S(1)}, f32[256,128]{1,0:T(8,128)S(1)}, u32[]{:S(2)}, u32[]{:S(2)}) collective-permute-start(f32[256,128]{1,0:T(8,128)S(1)} %get-tuple-element.32), channel_id=1, source_target_pairs={{0,4},{4,0},{8,12},{12,8},{16,20},{20,16},{24,28},{28,24},{1,5},{5... | collective-permute-start | bytes 393224 | tf_op jit(solution)/shard_map/ppermute | solution.py:221
  30.6 4.8 %collective-permute-start.10 = (f16[272,128]{1,0:T(8,128)(2,1)S(1)}, f16[272,128]{1,0:T(8,128)(2,1)S(1)}, u32[]{:S(2)}, u32[]{:S(2)}) collective-permute-start(f16[272,128]{1,0:T(8,128)(2,1)S(1)} %convert_element_type.21), channel_id=1, source_target_pairs={{0,8},{4,12},{8,0},{12,4},{16,24},{20,28},{24,16},{28,20},{1,9},{5... | collective-permute-start | bytes 208904 | tf_op jit(solution)/shard_map/ppermute | solution.py:236
  30.7 5.9 %collective-permute-start.9 = (f16[272,128]{1,0:T(8,128)(2,1)S(1)}, f16[272,128]{1,0:T(8,128)(2,1)S(1)}, u32[]{:S(2)}, u32[]{:S(2)}) collective-permute-start(f16[272,128]{1,0:T(8,128)(2,1)S(1)} %convert_element_type.21), channel_id=1, source_target_pairs={{0,16},{4,20},{8,24},{12,28},{16,0},{20,4},{24,8},{28,12},{1,17},{... | collective-permute-start | bytes 208904 | tf_op jit(solution)/shard_map/ppermute | solution.py:236
  31.1 5.5 %collective-permute-start.8 = (f16[272,128]{1,0:T(8,128)(2,1)S(1)}, f16[272,128]{1,0:T(8,128)(2,1)S(1)}, u32[]{:S(2)}, u32[]{:S(2)}) collective-permute-start(f16[272,128]{1,0:T(8,128)(2,1)S(1)} %convert_element_type.21), channel_id=1, source_target_pairs={{0,24},{4,28},{8,16},{12,20},{16,8},{20,12},{24,0},{28,4},{1,25},{... | collective-permute-start | bytes 208904 | tf_op jit(solution)/shard_map/ppermute | solution.py:236
  36.6 1.4 %collective-permute-start.11 = (f32[256,128]{1,0:T(8,128)S(1)}, f32[256,128]{1,0:T(8,128)S(1)}, u32[]{:S(2)}, u32[]{:S(2)}) collective-permute-start(f32[256,128]{1,0:T(8,128)S(1)} %multiply_add_fusion.refs_1_), channel_id=1, source_target_pairs={{0,4},{4,0},{8,12},{12,8},{16,20},{20,16},{24,28},{28,24},{1,5},{5... | collective-permute-start | bytes 393224 | tf_op jit(solution)/shard_map/ppermute | solution.py:221

commit v9 on v8

--- a/solution.py
+++ b/solution.py
@@ -158,29 +158,29 @@
         bg_high[c], bg_low[c] = split(held[:, cols] * gain[:, cols])
 
 
-def diffuse_kernel(count, *refs):
+def source(rad, d):
+    count = lax.axis_size("rad")
+    return (rad + count - d) % count if isinstance(rad, int) else lax.rem(rad + count - d, count)
+
+
+def diffuse_kernel(order, *refs):
+    count = len(order)
     shards = refs[:count]
     stepped, dh_high, dh_low, kappa, wbt, early, diffused, keep, send = refs[count:]
     rad, core = lax.axis_index("rad"), lax.rem(lax.axis_index("tile"), 2)
     width = stepped.shape[1]
-    chunk = [lax.rem(rad + count - d, count) for d in range(count)]
+    chunk = [source(rad, d) for d in order]
     rows = [pl.ds(pl.multiple_of(c * width, width), width) for c in chunk]
     value = jnp.concatenate([shard[...] for shard in shards], axis=1)
-    term = None
-    group = 2 if count % 2 == 0 else 1
-    for first in range(0, count, group):
-        some = range(first, first + group)
-        slopes = None
-        for table in (dh_high, dh_low):
-            weights = [jnp.concatenate([table[chunk[i], rows[j], :] for j in range(count)], axis=0) for i in some]
-            more = dot(value, jnp.concatenate(weights, axis=1))
-            slopes = more if slopes is None else slopes + more
-        rate = jnp.concatenate([kappa[chunk[i]] for i in some], axis=1)
-        bend = jnp.tanh(value[:, first * width : (first + group) * width].astype(F32))
-        fluxes = (rate + (0.5 * rate) * bend) * slopes
-        own = [jnp.concatenate([table[rad, rows[i], :] for i in some], axis=0) for table in (dh_high, dh_low)]
-        more = dot3(split(fluxes), own)
-        term = more if term is None else term + more
+    slopes = None
+    for table in (dh_high, dh_low):
+        weights = [jnp.concatenate([table[c, r, :] for r in rows], axis=0) for c in chunk]
+        more = dot(value, jnp.concatenate(weights, axis=1))
+        slopes = more if slopes is None else slopes + more
+    rate = jnp.concatenate([kappa[c] for c in chunk], axis=1)
+    fluxes = (rate + (0.5 * rate) * jnp.tanh(value.astype(F32))) * slopes
+    own = [jnp.concatenate([table[rad, r, :] for r in rows], axis=0) for table in (dh_high, dh_low)]
+    term = dot3(split(fluxes), own)
     term = radial_step * term
     diffused[...] = stepped[...] + term
     late = jnp.concatenate(split(term), axis=1)
@@ -283,7 +283,8 @@
         (pltpu.VMEM((3 * nodes, levels), BF),),
     )
     stepped, narrow = call(second_lap_kernel, (wide, thin), (lap_dense, high_two, low_two, part))
-    shards = [narrow] + [lax.ppermute(narrow, "rad", shift("rad", d)) for d in range(1, rads)]
+    order = [0, 1, *reversed(range(2, rads))]
+    shards = [narrow] + [lax.ppermute(narrow, "rad", [(source(i, d), i) for i in range(rads)]) for d in order[1:]]
     wbt, early, bg_high, bg_low = call(
         project_kernel,
         (shape((modes, nodes), BF), shape((modes, levels), F32)) + (shape((2, nodes, modes // 2), BF),) * 2,
@@ -292,7 +293,7 @@
         (pltpu.VMEM((nodes, modes), F32), pltpu.VMEM((1, nodes), F32), pltpu.VMEM((1, modes), jnp.int32), dma((3,))),
     )
     diffused, keep, send = call(
-        lambda *refs: diffuse_kernel(rads, *refs),
+        lambda *refs: diffuse_kernel(order, *refs),
         (wide, half, half),
         (*shards, stepped, jnp.asarray(dh_high), jnp.asarray(dh_low), kappa_ref.reshape(rads, 1, levels))
         + (wbt, early),

time: 39.1 us -> 36.9 us (0.944)
  waiting for transfers between devices: 12.9 us -> 11.2 us
  Pallas kernels: 9.73 us -> 9.17 us
    ppermute x3, waiting for transfers between devices: 6.99 us -> 4.77 us  [body(): lax.ppermute(narrow, 'rad', [(source(i, d), i) for i in range(rads)])]
    pallas_call x10, Pallas kernels: 9.73 us -> 9.17 us  [call(): pl.pallas_call(kernel, out_shape=outs, in_specs=[{'s': SMEM, 'h': HBM, 'v...]
    ppermute x3, waiting for transfers between devices: 2.39 us -> 2.81 us  [tile_sum(): lax.ppermute(sent, 'tile', [(i, i ^ m) for i in range(count)])]
  transfers between devices with their start and end apart: 12 -> 12, of which waited for: 7 -> 10; matrix products, arithmetic and copies ran while one was open for 1% -> 2% of each run, Pallas kernels for 14% -> 14%
where the time goes in v9:
time: 36.9 us; the launch traced here: 36.6 us
  starting transfers between devices  15.4 us (42%)
  waiting for transfers between devices  11.2 us (30%)
  Pallas kernels  9.17 us (25%)
  local copies, waits for them, and re-layouts  0.59 us (2%)
    pallas_call x10, Pallas kernels, call(): pl.pallas_call(kernel, out_shape=outs, in_specs=[{'s': SMEM, 'h': HBM, 'v...  9.17 us
    ppermute x3, starting transfers between devices, body(): lax.ppermute(narrow, 'rad', [(source(i, d), i) for i in range(rads)])  5.4 us
    ppermute x3, waiting for transfers between devices, body(): lax.ppermute(narrow, 'rad', [(source(i, d), i) for i in range(rads)])  4.77 us
    ppermute x2, starting transfers between devices, halo(): high = lax.ppermute(block, 'tile', shift('tile', -1))  4.05 us
    ppermute x3, starting transfers between devices, tile_sum(): lax.ppermute(sent, 'tile', [(i, i ^ m) for i in range(count)])  3.55 us
    ppermute x3, waiting for transfers between devices, tile_sum(): lax.ppermute(sent, 'tile', [(i, i ^ m) for i in range(count)])  2.81 us
    ppermute x2, waiting for transfers between devices, swap(): lax.ppermute(block, 'tile', [(i, i ^ 1) for i in range(lax.axis_size('til...  2.35 us
    ppermute x2, starting transfers between devices, halo(): low = lax.ppermute(block, 'tile', shift('tile', 1))  2.24 us
  transfers between devices with their start and end apart: 12, of which 10 were waited for; matrix products, arithmetic and copies ran while one was open for 2% of the time, Pallas kernels for 14%

profile of v9, /device:TPU:0, one launch (start us, length us, event | category | flops | bytes accessed | tf_op | source)
XLA Modules:
  0.0 36.6 jit_solution(6429069490371265284)
XLA Ops:
  0.0 1.1 %shard_map.100 = (f32[384,128]{1,0:T(8,128)S(1)}, bf16[384,128]{1,0:T(8,128)(2,1)S(1)}, s32[3,7]{1,0:T(4,128)S(1)}) custom-call(f32[384,128]{1,0:T(8,128)} %bitcast.15, s32[3,7]{1,0:T(4,128)} %neighbours.1), custom_call_target="tpu_custom_call" | custom-call | tf_op jit(solution)/shard_map/pallas_call | solution.py:57
  1.6 2.9 %collective-permute-start = (bf16[384,128]{1,0:T(8,128)(2,1)S(1)}, bf16[384,128]{1,0:T(8,128)(2,1)S(1)}, u32[]{:S(2)}, u32[]{:S(2)}) collective-permute-start(bf16[384,128]{1,0:T(8,128)(2,1)S(1)} %get-tuple-element.22.own), channel_id=1, source_target_pairs={{0,28},{4,0},{8,4},{12,8},{16,12},{20,16},{24,20},{28,24},{1,29},{... | collective-permute-start | bytes 294920 | tf_op jit(solution)/shard_map/ppermute | solution.py:215
  4.6 2.0 %shard_map.101 = (bf16[9,384,128]{2,1,0:T(8,128)(2,1)S(1)}, f32[384,128]{1,0:T(8,128)S(1)}) custom-call(s32[3,7]{1,0:T(4,128)S(1)} %get-tuple-element.21.ids, bf16[3,3,128,896]{3,2,1,0:T(8,128)(2,1)} %ops.3, bf16[384,128]{1,0:T(8,128)(2,1)S(1)} %get-tuple-element.22.own), custom_call_target="tpu_custom_call" | custom-call | tf_op jit(solution)/shard_map/pallas_call | solution.py:57
  7.1 1.7 %collective-permute-start.3 = (bf16[384,128]{1,0:T(8,128)(2,1)S(1)}, bf16[384,128]{1,0:T(8,128)(2,1)S(1)}, u32[]{:S(2)}, u32[]{:S(2)}) collective-permute-start(bf16[384,128]{1,0:T(8,128)(2,1)S(1)} %shard_map.102.lap), channel_id=1, source_target_pairs={{0,4},{4,8},{8,12},{12,16},{16,20},{20,24},{24,28},{28,0},{1,5},{5... | collective-permute-start | bytes 294920 | tf_op jit(solution)/shard_map/ppermute | solution.py:216
  8.8 1.1 %collective-permute-start.2 = (bf16[384,128]{1,0:T(8,128)(2,1)S(1)}, bf16[384,128]{1,0:T(8,128)(2,1)S(1)}, u32[]{:S(2)}, u32[]{:S(2)}) collective-permute-start(bf16[384,128]{1,0:T(8,128)(2,1)S(1)} %shard_map.102.lap), channel_id=1, source_target_pairs={{0,28},{4,0},{8,4},{12,8},{16,12},{20,16},{24,20},{28,24},{1,29},{... | collective-permute-start | bytes 294920 | tf_op jit(solution)/shard_map/ppermute | solution.py:215
  10.0 1.2 %shard_map.103.part = f32[384,128]{1,0:T(8,128)S(1)} custom-call(s32[3,7]{1,0:T(4,128)S(1)} %get-tuple-element.21.ids, bf16[3,3,128,896]{3,2,1,0:T(8,128)(2,1)S(1)} %copy-done, f32[768,128]{1,0:T(8,128)S(1)} %bitcast.13, bf16[9,384,128]{2,1,0:T(8,128)(2,1)S(1)} %get-tuple-element.23.dense.lap_dense, bf16[384,128]{1,0:T(8,128)(2,1)S(1)} %collective-permute-done.1.low, ...), custom_call_target="tpu_custom_call" | custom-call | tf_op jit(solution)/shard_map/pallas_call | solution.py:57
  11.2 1.0 %collective-permute-done.3.low = bf16[384,128]{1,0:T(8,128)(2,1)S(1)} collective-permute-done((bf16[384,128]{1,0:T(8,128)(2,1)S(1)}, bf16[384,128]{1,0:T(8,128)(2,1)S(1)}, u32[]{:S(2)}, u32[]{:S(2)}) %collective-permute-start.3) | collective-permute-done | bytes 98336 | tf_op jit(solution)/shard_map/ppermute | solution.py:216
  12.5 3.4 %collective-permute-start.6 = (bf16[384,128]{1,0:T(8,128)(2,1)S(1)}, bf16[384,128]{1,0:T(8,128)(2,1)S(1)}, u32[]{:S(2)}, u32[]{:S(2)}) collective-permute-start(bf16[384,128]{1,0:T(8,128)(2,1)S(1)} %get-tuple-element.26.refs_0_), channel_id=1, source_target_pairs={{2,0},{3,1},{0,2},{1,3},{6,4},{7,5},{4,6},{5,7},{10,8},{11,9},{8,1... | collective-permute-start | bytes 294920 | tf_op jit(solution)/shard_map/ppermute | solution.py:287
  15.9 1.4 %collective-permute-start.5 = (bf16[384,128]{1,0:T(8,128)(2,1)S(1)}, bf16[384,128]{1,0:T(8,128)(2,1)S(1)}, u32[]{:S(2)}, u32[]{:S(2)}) collective-permute-start(bf16[384,128]{1,0:T(8,128)(2,1)S(1)} %get-tuple-element.26.refs_0_), channel_id=1, source_target_pairs={{1,0},{2,1},{3,2},{0,3},{5,4},{6,5},{7,6},{4,7},{9,8},{10,9},{11,1... | collective-permute-start | bytes 294920 | tf_op jit(solution)/shard_map/ppermute | solution.py:287
  17.2 0.7 %collective-permute-start.4 = (bf16[384,128]{1,0:T(8,128)(2,1)S(1)}, bf16[384,128]{1,0:T(8,128)(2,1)S(1)}, u32[]{:S(2)}, u32[]{:S(2)}) collective-permute-start(bf16[384,128]{1,0:T(8,128)(2,1)S(1)} %get-tuple-element.26.refs_0_), channel_id=1, source_target_pairs={{3,0},{0,1},{1,2},{2,3},{7,4},{4,5},{5,6},{6,7},{11,8},{8,9},{9,10... | collective-permute-start | bytes 294920 | tf_op jit(solution)/shard_map/ppermute | solution.py:287
  17.9 0.6 %broadcast_in_dim.6.weight = f32[1,384]{1,0:T(1,128)} reshape(f32[384]{0:T(512)S(1)} %copy-done.5) | data formatting | bytes 3072 | tf_op jit(solution)/shard_map/broadcast_in_dim | solution.py:291
  18.5 1.8 %shard_map.105 = (bf16[512,384]{1,0:T(8,128)(2,1)S(1)}, f32[512,128]{1,0:T(8,128)S(1)}, bf16[2,384,256]{2,1,0:T(8,128)(2,1)S(1)}, bf16[2,384,256]{2,1,0:T(8,128)(2,1)S(1)}) custom-call(f32[384,512]{1,0:T(8,128)} %basis.1, f32[1,384]{1,0:T(1,128)} %broadcast_in_dim.6.weight, s32[1,512]{1,0:T(1,128)} %bitcast.16, f32[384,128]{1,0:T(8,128)S(1)} %get-tuple-element.27.value.refs_4_), custom_call_target="tpu_custom_call" | custom-call | tf_op jit(solution)/shard_map/pallas_call | solution.py:57
  20.3 1.0 %collective-permute-done.6.refs_3_ = bf16[384,128]{1,0:T(8,128)(2,1)S(1)} collective-permute-done((bf16[384,128]{1,0:T(8,128)(2,1)S(1)}, bf16[384,128]{1,0:T(8,128)(2,1)S(1)}, u32[]{:S(2)}, u32[]{:S(2)}) %collective-permute-start.6) | collective-permute-done | bytes 98336 | tf_op jit(solution)/shard_map/ppermute | solution.py:287
  21.3 0.8 %collective-permute-done.5.refs_2_ = bf16[384,128]{1,0:T(8,128)(2,1)S(1)} collective-permute-done((bf16[384,128]{1,0:T(8,128)(2,1)S(1)}, bf16[384,128]{1,0:T(8,128)(2,1)S(1)}, u32[]{:S(2)}, u32[]{:S(2)}) %collective-permute-start.5) | collective-permute-done | bytes 98336 | tf_op jit(solution)/shard_map/ppermute | solution.py:287
  22.1 3.0 %collective-permute-done.4.refs_1_ = bf16[384,128]{1,0:T(8,128)(2,1)S(1)} collective-permute-done((bf16[384,128]{1,0:T(8,128)(2,1)S(1)}, bf16[384,128]{1,0:T(8,128)(2,1)S(1)}, u32[]{:S(2)}, u32[]{:S(2)}) %collective-permute-start.4) | collective-permute-done | bytes 98336 | tf_op jit(solution)/shard_map/ppermute | solution.py:287
  25.1 1.1 %shard_map.106 = (f32[384,128]{1,0:T(8,128)S(1)}, f32[256,128]{1,0:T(8,128)S(1)}, f32[256,128]{1,0:T(8,128)S(1)}) custom-call(bf16[384,128]{1,0:T(8,128)(2,1)S(1)} %get-tuple-element.26.refs_0_, bf16[384,128]{1,0:T(8,128)(2,1)S(1)} %collective-permute-done.4.refs_1_, bf16[384,128]{1,0:T(8,128)(2,1)S(1)} %collective-permute-done.5.refs_2_, ...), custom_call_target="tpu_custom_call" | custom-call | tf_op jit(solution)/shard_map/pallas_call | solution.py:57
  26.3 1.3 %collective-permute-done.7.received = f32[256,128]{1,0:T(8,128)S(1)} collective-permute-done((f32[256,128]{1,0:T(8,128)S(1)}, f32[256,128]{1,0:T(8,128)S(1)}, u32[]{:S(2)}, u32[]{:S(2)}) %collective-permute-start.7) | collective-permute-done | bytes 131104 | tf_op jit(solution)/shard_map/ppermute | solution.py:221
  28.3 0.7 %collective-permute-start.9 = (f16[272,128]{1,0:T(8,128)(2,1)S(1)}, f16[272,128]{1,0:T(8,128)(2,1)S(1)}, u32[]{:S(2)}, u32[]{:S(2)}) collective-permute-start(f16[272,128]{1,0:T(8,128)(2,1)S(1)} %convert_element_type.21), channel_id=1, source_target_pairs={{0,16},{4,20},{8,24},{12,28},{16,0},{20,4},{24,8},{28,12},{1,17},{... | collective-permute-start | bytes 208904 | tf_op jit(solution)/shard_map/ppermute | solution.py:236
  29.0 2.4 %collective-permute-start.8 = (f16[272,128]{1,0:T(8,128)(2,1)S(1)}, f16[272,128]{1,0:T(8,128)(2,1)S(1)}, u32[]{:S(2)}, u32[]{:S(2)}) collective-permute-start(f16[272,128]{1,0:T(8,128)(2,1)S(1)} %convert_element_type.21), channel_id=1, source_target_pairs={{0,24},{4,28},{8,16},{12,20},{16,8},{20,12},{24,0},{28,4},{1,25},{... | collective-permute-start | bytes 208904 | tf_op jit(solution)/shard_map/ppermute | solution.py:236
  31.4 0.9 %collective-permute-done.10 = f16[272,128]{1,0:T(8,128)(2,1)S(1)} collective-permute-done((f16[272,128]{1,0:T(8,128)(2,1)S(1)}, f16[272,128]{1,0:T(8,128)(2,1)S(1)}, u32[]{:S(2)}, u32[]{:S(2)}) %collective-permute-start.10) | collective-permute-done | bytes 69664 | tf_op jit(solution)/shard_map/ppermute | solution.py:236
  32.3 0.7 %collective-permute-done.9 = f16[272,128]{1,0:T(8,128)(2,1)S(1)} collective-permute-done((f16[272,128]{1,0:T(8,128)(2,1)S(1)}, f16[272,128]{1,0:T(8,128)(2,1)S(1)}, u32[]{:S(2)}, u32[]{:S(2)}) %collective-permute-start.9) | collective-permute-done | bytes 69664 | tf_op jit(solution)/shard_map/ppermute | solution.py:236
  33.0 1.2 %collective-permute-done.8 = f16[272,128]{1,0:T(8,128)(2,1)S(1)} collective-permute-done((f16[272,128]{1,0:T(8,128)(2,1)S(1)}, f16[272,128]{1,0:T(8,128)(2,1)S(1)}, u32[]{:S(2)}, u32[]{:S(2)}) %collective-permute-start.8) | collective-permute-done | bytes 69664 | tf_op jit(solution)/shard_map/ppermute | solution.py:236
  34.6 1.1 %collective-permute-done.11.refs_1_ = f32[256,128]{1,0:T(8,128)S(1)} collective-permute-done((f32[256,128]{1,0:T(8,128)S(1)}, f32[256,128]{1,0:T(8,128)S(1)}, u32[]{:S(2)}, u32[]{:S(2)}) %collective-permute-start.11) | collective-permute-done | bytes 131104 | tf_op jit(solution)/shard_map/ppermute | solution.py:221
  35.7 0.9 %shard_map.109 = f32[384,128]{1,0:T(8,128)} custom-call(f32[384,128]{1,0:T(8,128)S(1)} %shard_map.108.refs_0_, f32[256,128]{1,0:T(8,128)S(1)} %collective-permute-done.11.refs_1_, bf16[2,384,256]{2,1,0:T(8,128)(2,1)S(1)} %get-tuple-element.35.refs_2_, bf16[2,384,256]{2,1,0:T(8,128)(2,1)S(1)} %get-tuple-element.36.refs_3_), custom_call_target="tpu_custom_call" | custom-call | tf_op jit(solution)/shard_map/pallas_call | solution.py:57
  (28 shorter events, 2.6 us)
Async XLA Ops:
  0.0 9.9 %copy-start = (bf16[3,3,128,896]{3,2,1,0:T(8,128)(2,1)S(1)}, bf16[3,3,128,896]{3,2,1,0:T(8,128)(2,1)}, u32[]{:S(2)}) copy-start(bf16[3,3,128,896]{3,2,1,0:T(8,128)(2,1)} %ops.3) | copy-start | bytes 6193156
  0.0 9.9 %copy-start.3 = (f32[384,2,128]{2,1,0:T(2,128)S(1)}, f32[384,2,128]{2,1,0:T(2,128)}, u32[]{:S(2)}) copy-start(f32[384,2,128]{2,1,0:T(2,128)} %param.11) | copy-start | bytes 1179652
  1.1 5.7 %collective-permute-start.1 = (bf16[384,128]{1,0:T(8,128)(2,1)S(1)}, bf16[384,128]{1,0:T(8,128)(2,1)S(1)}, u32[]{:S(2)}, u32[]{:S(2)}) collective-permute-start(bf16[384,128]{1,0:T(8,128)(2,1)S(1)} %get-tuple-element.22.own), channel_id=1, source_target_pairs={{0,4},{4,8},{8,12},{12,16},{16,20},{20,24},{24,28},{28,0},{1,5},{5... | collective-permute-start | bytes 294920 | tf_op jit(solution)/shard_map/ppermute | solution.py:216
  1.6 5.2 %collective-permute-start = (bf16[384,128]{1,0:T(8,128)(2,1)S(1)}, bf16[384,128]{1,0:T(8,128)(2,1)S(1)}, u32[]{:S(2)}, u32[]{:S(2)}) collective-permute-start(bf16[384,128]{1,0:T(8,128)(2,1)S(1)} %get-tuple-element.22.own), channel_id=1, source_target_pairs={{0,28},{4,0},{8,4},{12,8},{16,12},{20,16},{24,20},{28,24},{1,29},{... | collective-permute-start | bytes 294920 | tf_op jit(solution)/shard_map/ppermute | solution.py:215
  7.1 5.1 %collective-permute-start.3 = (bf16[384,128]{1,0:T(8,128)(2,1)S(1)}, bf16[384,128]{1,0:T(8,128)(2,1)S(1)}, u32[]{:S(2)}, u32[]{:S(2)}) collective-permute-start(bf16[384,128]{1,0:T(8,128)(2,1)S(1)} %shard_map.102.lap), channel_id=1, source_target_pairs={{0,4},{4,8},{8,12},{12,16},{16,20},{20,24},{24,28},{28,0},{1,5},{5... | collective-permute-start | bytes 294920 | tf_op jit(solution)/shard_map/ppermute | solution.py:216
  8.8 3.3 %collective-permute-start.2 = (bf16[384,128]{1,0:T(8,128)(2,1)S(1)}, bf16[384,128]{1,0:T(8,128)(2,1)S(1)}, u32[]{:S(2)}, u32[]{:S(2)}) collective-permute-start(bf16[384,128]{1,0:T(8,128)(2,1)S(1)} %shard_map.102.lap), channel_id=1, source_target_pairs={{0,28},{4,0},{8,4},{12,8},{16,12},{20,16},{24,20},{28,24},{1,29},{... | collective-permute-start | bytes 294920 | tf_op jit(solution)/shard_map/ppermute | solution.py:215
  10.0 8.0 %copy-start.5 = (f32[384]{0:T(512)S(1)}, f32[384]{0:T(512)}, u32[]{:S(2)}) copy-start(f32[384]{0:T(512)} %param.15) | copy-start | bytes 4612
  11.1 14.0 %copy-start.1 = (bf16[4,512,128]{2,1,0:T(8,128)(2,1)S(1)}, bf16[4,512,128]{2,1,0:T(8,128)(2,1)}, u32[]{:S(2)}) copy-start(bf16[4,512,128]{2,1,0:T(8,128)(2,1)} %constant.12.clone.refs_6_) | copy-start | bytes 1572868
  11.1 13.9 %copy-start.2 = (bf16[4,512,128]{2,1,0:T(8,128)(2,1)S(1)}, bf16[4,512,128]{2,1,0:T(8,128)(2,1)}, u32[]{:S(2)}) copy-start(bf16[4,512,128]{2,1,0:T(8,128)(2,1)} %constant.11.clone.refs_5_) | copy-start | bytes 1572868
  11.2 13.9 %copy-start.4 = (f32[512]{0:T(512)S(1)}, f32[512]{0:T(512)}, u32[]{:S(2)}) copy-start(f32[512]{0:T(512)} %param.14) | copy-start | bytes 6148
  12.5 8.8 %collective-permute-start.6 = (bf16[384,128]{1,0:T(8,128)(2,1)S(1)}, bf16[384,128]{1,0:T(8,128)(2,1)S(1)}, u32[]{:S(2)}, u32[]{:S(2)}) collective-permute-start(bf16[384,128]{1,0:T(8,128)(2,1)S(1)} %get-tuple-element.26.refs_0_), channel_id=1, source_target_pairs={{2,0},{3,1},{0,2},{1,3},{6,4},{7,5},{4,6},{5,7},{10,8},{11,9},{8,1... | collective-permute-start | bytes 294920 | tf_op jit(solution)/shard_map/ppermute | solution.py:287
  15.9 6.2 %collective-permute-start.5 = (bf16[384,128]{1,0:T(8,128)(2,1)S(1)}, bf16[384,128]{1,0:T(8,128)(2,1)S(1)}, u32[]{:S(2)}, u32[]{:S(2)}) collective-permute-start(bf16[384,128]{1,0:T(8,128)(2,1)S(1)} %get-tuple-element.26.refs_0_), channel_id=1, source_target_pairs={{1,0},{2,1},{3,2},{0,3},{5,4},{6,5},{7,6},{4,7},{9,8},{10,9},{11,1... | collective-permute-start | bytes 294920 | tf_op jit(solution)/shard_map/ppermute | solution.py:287
  17.2 7.8 %collective-permute-start.4 = (bf16[384,128]{1,0:T(8,128)(2,1)S(1)}, bf16[384,128]{1,0:T(8,128)(2,1)S(1)}, u32[]{:S(2)}, u32[]{:S(2)}) collective-permute-start(bf16[384,128]{1,0:T(8,128)(2,1)S(1)} %get-tuple-element.26.refs_0_), channel_id=1, source_target_pairs={{3,0},{0,1},{1,2},{2,3},{7,4},{4,5},{5,6},{6,7},{11,8},{8,9},{9,10... | collective-permute-start | bytes 294920 | tf_op jit(solution)/shard_map/ppermute | solution.py:287
  26.2 1.4 %collective-permute-start.7 = (f32[256,128]{1,0:T(8,128)S(1)}, f32[256,128]{1,0:T(8,128)S(1)}, u32[]{:S(2)}, u32[]{:S(2)}) collective-permute-start(f32[256,128]{1,0:T(8,128)S(1)} %get-tuple-element.32), channel_id=1, source_target_pairs={{0,4},{4,0},{8,12},{12,8},{16,20},{20,16},{24,28},{28,24},{1,5},{5... | collective-permute-start | bytes 393224 | tf_op jit(solution)/shard_map/ppermute | solution.py:221
  27.8 4.4 %collective-permute-start.10 = (f16[272,128]{1,0:T(8,128)(2,1)S(1)}, f16[272,128]{1,0:T(8,128)(2,1)S(1)}, u32[]{:S(2)}, u32[]{:S(2)}) collective-permute-start(f16[272,128]{1,0:T(8,128)(2,1)S(1)} %convert_element_type.21), channel_id=1, source_target_pairs={{0,8},{4,12},{8,0},{12,4},{16,24},{20,28},{24,16},{28,20},{1,9},{5... | collective-permute-start | bytes 208904 | tf_op jit(solution)/shard_map/ppermute | solution.py:236
  28.3 4.7 %collective-permute-start.9 = (f16[272,128]{1,0:T(8,128)(2,1)S(1)}, f16[272,128]{1,0:T(8,128)(2,1)S(1)}, u32[]{:S(2)}, u32[]{:S(2)}) collective-permute-start(f16[272,128]{1,0:T(8,128)(2,1)S(1)} %convert_element_type.21), channel_id=1, source_target_pairs={{0,16},{4,20},{8,24},{12,28},{16,0},{20,4},{24,8},{28,12},{1,17},{... | collective-permute-start | bytes 208904 | tf_op jit(solution)/shard_map/ppermute | solution.py:236
  29.0 5.2 %collective-permute-start.8 = (f16[272,128]{1,0:T(8,128)(2,1)S(1)}, f16[272,128]{1,0:T(8,128)(2,1)S(1)}, u32[]{:S(2)}, u32[]{:S(2)}) collective-permute-start(f16[272,128]{1,0:T(8,128)(2,1)S(1)} %convert_element_type.21), channel_id=1, source_target_pairs={{0,24},{4,28},{8,16},{12,20},{16,8},{20,12},{24,0},{28,4},{1,25},{... | collective-permute-start | bytes 208904 | tf_op jit(solution)/shard_map/ppermute | solution.py:236
  34.2 1.4 %collective-permute-start.11 = (f32[256,128]{1,0:T(8,128)S(1)}, f32[256,128]{1,0:T(8,128)S(1)}, u32[]{:S(2)}, u32[]{:S(2)}) collective-permute-start(f32[256,128]{1,0:T(8,128)S(1)} %multiply_add_fusion.refs_1_), channel_id=1, source_target_pairs={{0,4},{4,0},{8,12},{12,8},{16,20},{20,16},{24,28},{28,24},{1,5},{5... | collective-permute-start | bytes 393224 | tf_op jit(solution)/shard_map/ppermute | solution.py:221

commit v10 on v9

--- a/solution.py
+++ b/solution.py
@@ -163,25 +163,41 @@
     return (rad + count - d) % count if isinstance(rad, int) else lax.rem(rad + count - d, count)
 
 
-def diffuse_kernel(order, *refs):
+def gathered(order, width):
+    rad = lax.axis_index("rad")
+    chunk = [source(rad, d) for d in order]
+    return rad, chunk, [pl.ds(pl.multiple_of(c * width, width), width) for c in chunk]
+
+
+def early_diffuse_kernel(order, *refs):
     count = len(order)
-    shards = refs[:count]
-    stepped, dh_high, dh_low, kappa, wbt, early, diffused, keep, send = refs[count:]
-    rad, core = lax.axis_index("rad"), lax.rem(lax.axis_index("tile"), 2)
+    shards = refs[: count - 1]
+    dh_high, dh_low, kappa, slopes, rates = refs[count - 1 :]
+    width = kappa.shape[2]
+    _, chunk, rows = gathered(order, width)
+    value = jnp.concatenate([shard[...] for shard in shards], axis=1)
+    total = None
+    for table in (dh_high, dh_low):
+        weights = [jnp.concatenate([table[c, r, :] for r in rows[:-1]], axis=0) for c in chunk]
+        more = dot(value, jnp.concatenate(weights, axis=1))
+        total = more if total is None else total + more
+    slopes[...] = total
+    rate = jnp.concatenate([kappa[c] for c in chunk[:-1]], axis=1)
+    rates[...] = rate + (0.5 * rate) * jnp.tanh(value.astype(F32))
+
+
+def diffuse_kernel(order, last, stepped, dh_high, dh_low, kappa, wbt, early, slopes, rates, diffused, keep, send):
     width = stepped.shape[1]
-    chunk = [source(rad, d) for d in order]
-    rows = [pl.ds(pl.multiple_of(c * width, width), width) for c in chunk]
-    value = jnp.concatenate([shard[...] for shard in shards], axis=1)
-    slopes = None
-    for table in (dh_high, dh_low):
-        weights = [jnp.concatenate([table[c, r, :] for r in rows], axis=0) for c in chunk]
-        more = dot(value, jnp.concatenate(weights, axis=1))
-        slopes = more if slopes is None else slopes + more
-    rate = jnp.concatenate([kappa[c] for c in chunk], axis=1)
-    fluxes = (rate + (0.5 * rate) * jnp.tanh(value.astype(F32))) * slopes
+    rad, chunk, rows = gathered(order, width)
+    core = lax.rem(lax.axis_index("tile"), 2)
+    value = last[...]
+    weights = [jnp.concatenate([dh_high[c, rows[-1], :], dh_low[c, rows[-1], :]], axis=0) for c in chunk]
+    total = slopes[...] + dot(jnp.concatenate([value, value], axis=1), jnp.concatenate(weights, axis=1))
+    rate = kappa[chunk[-1]]
+    last_rates = rate + (0.5 * rate) * jnp.tanh(value.astype(F32))
+    fluxes = jnp.concatenate([rates[...], last_rates], axis=1) * total
     own = [jnp.concatenate([table[rad, r, :] for r in rows], axis=0) for table in (dh_high, dh_low)]
-    term = dot3(split(fluxes), own)
-    term = radial_step * term
+    term = radial_step * dot3(split(fluxes), own)
     diffused[...] = stepped[...] + term
     late = jnp.concatenate(split(term), axis=1)
     half = keep.shape[0]
@@ -283,7 +299,7 @@
         (pltpu.VMEM((3 * nodes, levels), BF),),
     )
     stepped, narrow = call(second_lap_kernel, (wide, thin), (lap_dense, high_two, low_two, part))
-    order = [0, 1, *reversed(range(2, rads))]
+    order = [0, *reversed(range(1, rads))]
     shards = [narrow] + [lax.ppermute(narrow, "rad", [(source(i, d), i) for i in range(rads)]) for d in order[1:]]
     wbt, early, bg_high, bg_low = call(
         project_kernel,
@@ -292,11 +308,16 @@
         "hhhv",
         (pltpu.VMEM((nodes, modes), F32), pltpu.VMEM((1, nodes), F32), pltpu.VMEM((1, modes), jnp.int32), dma((3,))),
     )
+    dhat = (jnp.asarray(dh_high), jnp.asarray(dh_low), kappa_ref.reshape(rads, 1, levels))
+    slopes, rates = call(
+        lambda *refs: early_diffuse_kernel(order, *refs),
+        (shape((nodes, rads * levels), F32), shape((nodes, (rads - 1) * levels), F32)),
+        (*shards[:-1], *dhat),
+    )
     diffused, keep, send = call(
         lambda *refs: diffuse_kernel(order, *refs),
         (wide, half, half),
-        (*shards, stepped, jnp.asarray(dh_high), jnp.asarray(dh_low), kappa_ref.reshape(rads, 1, levels))
-        + (wbt, early),
+        (shards[-1], stepped, *dhat, wbt, early, slopes, rates),
     )
     mine = tile_sum(keep, send)
     other = swap(mine)

time: 36.9 us -> 36.5 us (0.989)
  waiting for transfers between devices: 11.2 us -> 10.6 us
    ppermute x3, waiting for transfers between devices: 4.77 us -> 4.16 us  [body(): lax.ppermute(narrow, 'rad', [(source(i, d), i) for i in range(rads)])]
    pallas_call x10 -> x11, Pallas kernels: 9.17 us -> 9.41 us  [call(): pl.pallas_call(kernel, out_shape=outs, in_specs=[{'s': SMEM, 'h': HBM, 'v...]
  transfers between devices with their start and end apart: 12 -> 12, of which waited for: 10 -> 10; matrix products, arithmetic and copies ran while one was open for 2% -> 2% of each run, Pallas kernels for 14% -> 16%
where the time goes in v10:
time: 36.5 us; the launch traced here: 36.2 us
  starting transfers between devices  15.4 us (42%)
  waiting for transfers between devices  10.6 us (29%)
  Pallas kernels  9.41 us (26%)
  local copies, waits for them, and re-layouts  0.59 us (2%)
    pallas_call x11, Pallas kernels, call(): pl.pallas_call(kernel, out_shape=outs, in_specs=[{'s': SMEM, 'h': HBM, 'v...  9.41 us
    ppermute x3, starting transfers between devices, body(): lax.ppermute(narrow, 'rad', [(source(i, d), i) for i in range(rads)])  5.4 us
    ppermute x3, waiting for transfers between devices, body(): lax.ppermute(narrow, 'rad', [(source(i, d), i) for i in range(rads)])  4.16 us
    ppermute x2, starting transfers between devices, halo(): high = lax.ppermute(block, 'tile', shift('tile', -1))  4.05 us
    ppermute x3, starting transfers between devices, tile_sum(): lax.ppermute(sent, 'tile', [(i, i ^ m) for i in range(count)])  3.55 us
    ppermute x3, waiting for transfers between devices, tile_sum(): lax.ppermute(sent, 'tile', [(i, i ^ m) for i in range(count)])  2.81 us
    ppermute x2, waiting for transfers between devices, swap(): lax.ppermute(block, 'tile', [(i, i ^ 1) for i in range(lax.axis_size('til...  2.34 us
    ppermute x2, starting transfers between devices, halo(): low = lax.ppermute(block, 'tile', shift('tile', 1))  2.24 us
  transfers between devices with their start and end apart: 12, of which 10 were waited for; matrix products, arithmetic and copies ran while one was open for 2% of the time, Pallas kernels for 16%

profile of v10, /device:TPU:0, one launch (start us, length us, event | category | flops | bytes accessed | tf_op | source)
XLA Modules:
  0.0 36.2 jit_solution(9635138678277167113)
XLA Ops:
  0.0 1.1 %shard_map.100 = (f32[384,128]{1,0:T(8,128)S(1)}, bf16[384,128]{1,0:T(8,128)(2,1)S(1)}, s32[3,7]{1,0:T(4,128)S(1)}) custom-call(f32[384,128]{1,0:T(8,128)} %bitcast.16, s32[3,7]{1,0:T(4,128)} %neighbours.1), custom_call_target="tpu_custom_call" | custom-call | tf_op jit(solution)/shard_map/pallas_call | solution.py:57
  1.6 2.9 %collective-permute-start = (bf16[384,128]{1,0:T(8,128)(2,1)S(1)}, bf16[384,128]{1,0:T(8,128)(2,1)S(1)}, u32[]{:S(2)}, u32[]{:S(2)}) collective-permute-start(bf16[384,128]{1,0:T(8,128)(2,1)S(1)} %get-tuple-element.24.own), channel_id=1, source_target_pairs={{0,28},{4,0},{8,4},{12,8},{16,12},{20,16},{24,20},{28,24},{1,29},{... | collective-permute-start | bytes 294920 | tf_op jit(solution)/shard_map/ppermute | solution.py:231
  4.6 2.0 %shard_map.101 = (bf16[9,384,128]{2,1,0:T(8,128)(2,1)S(1)}, f32[384,128]{1,0:T(8,128)S(1)}) custom-call(s32[3,7]{1,0:T(4,128)S(1)} %get-tuple-element.23.ids, bf16[3,3,128,896]{3,2,1,0:T(8,128)(2,1)} %ops.3, bf16[384,128]{1,0:T(8,128)(2,1)S(1)} %get-tuple-element.24.own), custom_call_target="tpu_custom_call" | custom-call | tf_op jit(solution)/shard_map/pallas_call | solution.py:57
  7.1 1.7 %collective-permute-start.3 = (bf16[384,128]{1,0:T(8,128)(2,1)S(1)}, bf16[384,128]{1,0:T(8,128)(2,1)S(1)}, u32[]{:S(2)}, u32[]{:S(2)}) collective-permute-start(bf16[384,128]{1,0:T(8,128)(2,1)S(1)} %shard_map.102.lap), channel_id=1, source_target_pairs={{0,4},{4,8},{8,12},{12,16},{16,20},{20,24},{24,28},{28,0},{1,5},{5... | collective-permute-start | bytes 294920 | tf_op jit(solution)/shard_map/ppermute | solution.py:232
  8.8 1.1 %collective-permute-start.2 = (bf16[384,128]{1,0:T(8,128)(2,1)S(1)}, bf16[384,128]{1,0:T(8,128)(2,1)S(1)}, u32[]{:S(2)}, u32[]{:S(2)}) collective-permute-start(bf16[384,128]{1,0:T(8,128)(2,1)S(1)} %shard_map.102.lap), channel_id=1, source_target_pairs={{0,28},{4,0},{8,4},{12,8},{16,12},{20,16},{24,20},{28,24},{1,29},{... | collective-permute-start | bytes 294920 | tf_op jit(solution)/shard_map/ppermute | solution.py:231
  10.0 1.2 %shard_map.103.part = f32[384,128]{1,0:T(8,128)S(1)} custom-call(s32[3,7]{1,0:T(4,128)S(1)} %get-tuple-element.23.ids, bf16[3,3,128,896]{3,2,1,0:T(8,128)(2,1)S(1)} %copy-done, f32[768,128]{1,0:T(8,128)S(1)} %bitcast.13, bf16[9,384,128]{2,1,0:T(8,128)(2,1)S(1)} %get-tuple-element.25.dense.lap_dense, bf16[384,128]{1,0:T(8,128)(2,1)S(1)} %collective-permute-done.1.low, ...), custom_call_target="tpu_custom_call" | custom-call | tf_op jit(solution)/shard_map/pallas_call | solution.py:57
  11.2 1.0 %collective-permute-done.3.low = bf16[384,128]{1,0:T(8,128)(2,1)S(1)} collective-permute-done((bf16[384,128]{1,0:T(8,128)(2,1)S(1)}, bf16[384,128]{1,0:T(8,128)(2,1)S(1)}, u32[]{:S(2)}, u32[]{:S(2)}) %collective-permute-start.3) | collective-permute-done | bytes 98336 | tf_op jit(solution)/shard_map/ppermute | solution.py:232
  12.5 3.4 %collective-permute-start.6 = (bf16[384,128]{1,0:T(8,128)(2,1)S(1)}, bf16[384,128]{1,0:T(8,128)(2,1)S(1)}, u32[]{:S(2)}, u32[]{:S(2)}) collective-permute-start(bf16[384,128]{1,0:T(8,128)(2,1)S(1)} %get-tuple-element.28.refs_0_), channel_id=1, source_target_pairs={{2,0},{3,1},{0,2},{1,3},{6,4},{7,5},{4,6},{5,7},{10,8},{11,9},{8,1... | collective-permute-start | bytes 294920 | tf_op jit(solution)/shard_map/ppermute | solution.py:303
  15.9 1.4 %collective-permute-start.5 = (bf16[384,128]{1,0:T(8,128)(2,1)S(1)}, bf16[384,128]{1,0:T(8,128)(2,1)S(1)}, u32[]{:S(2)}, u32[]{:S(2)}) collective-permute-start(bf16[384,128]{1,0:T(8,128)(2,1)S(1)} %get-tuple-element.28.refs_0_), channel_id=1, source_target_pairs={{1,0},{2,1},{3,2},{0,3},{5,4},{6,5},{7,6},{4,7},{9,8},{10,9},{11,1... | collective-permute-start | bytes 294920 | tf_op jit(solution)/shard_map/ppermute | solution.py:303
  17.2 0.7 %collective-permute-start.4 = (bf16[384,128]{1,0:T(8,128)(2,1)S(1)}, bf16[384,128]{1,0:T(8,128)(2,1)S(1)}, u32[]{:S(2)}, u32[]{:S(2)}) collective-permute-start(bf16[384,128]{1,0:T(8,128)(2,1)S(1)} %get-tuple-element.28.refs_0_), channel_id=1, source_target_pairs={{3,0},{0,1},{1,2},{2,3},{7,4},{4,5},{5,6},{6,7},{11,8},{8,9},{9,10... | collective-permute-start | bytes 294920 | tf_op jit(solution)/shard_map/ppermute | solution.py:303
  18.5 1.8 %shard_map.105 = (bf16[512,384]{1,0:T(8,128)(2,1)S(1)}, f32[512,128]{1,0:T(8,128)S(1)}, bf16[2,384,256]{2,1,0:T(8,128)(2,1)S(1)}, bf16[2,384,256]{2,1,0:T(8,128)(2,1)S(1)}) custom-call(f32[384,512]{1,0:T(8,128)} %basis.1, f32[1,384]{1,0:T(1,128)} %broadcast_in_dim.6.weight, s32[1,512]{1,0:T(1,128)} %bitcast.17, f32[384,128]{1,0:T(8,128)S(1)} %get-tuple-element.29.value.refs_1_), custom_call_target="tpu_custom_call" | custom-call | tf_op jit(solution)/shard_map/pallas_call | solution.py:57
  20.3 1.0 %collective-permute-done.6.refs_2_ = bf16[384,128]{1,0:T(8,128)(2,1)S(1)} collective-permute-done((bf16[384,128]{1,0:T(8,128)(2,1)S(1)}, bf16[384,128]{1,0:T(8,128)(2,1)S(1)}, u32[]{:S(2)}, u32[]{:S(2)}) %collective-permute-start.6) | collective-permute-done | bytes 98336 | tf_op jit(solution)/shard_map/ppermute | solution.py:303
  21.3 0.8 %collective-permute-done.5.refs_1_ = bf16[384,128]{1,0:T(8,128)(2,1)S(1)} collective-permute-done((bf16[384,128]{1,0:T(8,128)(2,1)S(1)}, bf16[384,128]{1,0:T(8,128)(2,1)S(1)}, u32[]{:S(2)}, u32[]{:S(2)}) %collective-permute-start.5) | collective-permute-done | bytes 98336 | tf_op jit(solution)/shard_map/ppermute | solution.py:303
  22.1 0.6 %shard_map.106 = (f32[384,512]{1,0:T(8,128)S(1)}, f32[384,384]{1,0:T(8,128)S(1)}) custom-call(bf16[384,128]{1,0:T(8,128)(2,1)S(1)} %get-tuple-element.28.refs_0_, bf16[384,128]{1,0:T(8,128)(2,1)S(1)} %collective-permute-done.5.refs_1_, bf16[384,128]{1,0:T(8,128)(2,1)S(1)} %collective-permute-done.6.refs_2_, bf16[4,512,128]{2,1,0:T(8,128)(2,1)S(1)} %copy-done.2, ...), custom_call_target="tpu_custom_call" | custom-call | tf_op jit(solution)/shard_map/pallas_call | solution.py:57
  22.7 2.4 %collective-permute-done.4.refs_0_ = bf16[384,128]{1,0:T(8,128)(2,1)S(1)} collective-permute-done((bf16[384,128]{1,0:T(8,128)(2,1)S(1)}, bf16[384,128]{1,0:T(8,128)(2,1)S(1)}, u32[]{:S(2)}, u32[]{:S(2)}) %collective-permute-start.4) | collective-permute-done | bytes 98336 | tf_op jit(solution)/shard_map/ppermute | solution.py:303
  25.1 0.7 %shard_map.107 = (f32[384,128]{1,0:T(8,128)S(1)}, f32[256,128]{1,0:T(8,128)S(1)}, f32[256,128]{1,0:T(8,128)S(1)}) custom-call(bf16[384,128]{1,0:T(8,128)(2,1)S(1)} %collective-permute-done.4.refs_0_, f32[384,128]{1,0:T(8,128)S(1)} %get-tuple-element.29.value.refs_1_, bf16[4,512,128]{2,1,0:T(8,128)(2,1)S(1)} %copy-done.2, bf16[4,512,128]{2,1,0:T(8,128)(2,1)S(1)} %copy-done.1, ...), custom_call_target="tpu_custom_call" | custom-call | tf_op jit(solution)/shard_map/pallas_call | solution.py:57
  26.0 1.3 %collective-permute-done.7.received = f32[256,128]{1,0:T(8,128)S(1)} collective-permute-done((f32[256,128]{1,0:T(8,128)S(1)}, f32[256,128]{1,0:T(8,128)S(1)}, u32[]{:S(2)}, u32[]{:S(2)}) %collective-permute-start.7) | collective-permute-done | bytes 131104 | tf_op jit(solution)/shard_map/ppermute | solution.py:237
  27.9 0.7 %collective-permute-start.9 = (f16[272,128]{1,0:T(8,128)(2,1)S(1)}, f16[272,128]{1,0:T(8,128)(2,1)S(1)}, u32[]{:S(2)}, u32[]{:S(2)}) collective-permute-start(f16[272,128]{1,0:T(8,128)(2,1)S(1)} %convert_element_type.21), channel_id=1, source_target_pairs={{0,16},{4,20},{8,24},{12,28},{16,0},{20,4},{24,8},{28,12},{1,17},{... | collective-permute-start | bytes 208904 | tf_op jit(solution)/shard_map/ppermute | solution.py:252
  28.6 2.4 %collective-permute-start.8 = (f16[272,128]{1,0:T(8,128)(2,1)S(1)}, f16[272,128]{1,0:T(8,128)(2,1)S(1)}, u32[]{:S(2)}, u32[]{:S(2)}) collective-permute-start(f16[272,128]{1,0:T(8,128)(2,1)S(1)} %convert_element_type.21), channel_id=1, source_target_pairs={{0,24},{4,28},{8,16},{12,20},{16,8},{20,12},{24,0},{28,4},{1,25},{... | collective-permute-start | bytes 208904 | tf_op jit(solution)/shard_map/ppermute | solution.py:252
  31.0 0.9 %collective-permute-done.10 = f16[272,128]{1,0:T(8,128)(2,1)S(1)} collective-permute-done((f16[272,128]{1,0:T(8,128)(2,1)S(1)}, f16[272,128]{1,0:T(8,128)(2,1)S(1)}, u32[]{:S(2)}, u32[]{:S(2)}) %collective-permute-start.10) | collective-permute-done | bytes 69664 | tf_op jit(solution)/shard_map/ppermute | solution.py:252
  31.9 0.7 %collective-permute-done.9 = f16[272,128]{1,0:T(8,128)(2,1)S(1)} collective-permute-done((f16[272,128]{1,0:T(8,128)(2,1)S(1)}, f16[272,128]{1,0:T(8,128)(2,1)S(1)}, u32[]{:S(2)}, u32[]{:S(2)}) %collective-permute-start.9) | collective-permute-done | bytes 69664 | tf_op jit(solution)/shard_map/ppermute | solution.py:252
  32.6 1.2 %collective-permute-done.8 = f16[272,128]{1,0:T(8,128)(2,1)S(1)} collective-permute-done((f16[272,128]{1,0:T(8,128)(2,1)S(1)}, f16[272,128]{1,0:T(8,128)(2,1)S(1)}, u32[]{:S(2)}, u32[]{:S(2)}) %collective-permute-start.8) | collective-permute-done | bytes 69664 | tf_op jit(solution)/shard_map/ppermute | solution.py:252
  34.2 1.1 %collective-permute-done.11.refs_1_ = f32[256,128]{1,0:T(8,128)S(1)} collective-permute-done((f32[256,128]{1,0:T(8,128)S(1)}, f32[256,128]{1,0:T(8,128)S(1)}, u32[]{:S(2)}, u32[]{:S(2)}) %collective-permute-start.11) | collective-permute-done | bytes 131104 | tf_op jit(solution)/shard_map/ppermute | solution.py:237
  35.3 0.9 %shard_map.110 = f32[384,128]{1,0:T(8,128)} custom-call(f32[384,128]{1,0:T(8,128)S(1)} %shard_map.109.refs_0_, f32[256,128]{1,0:T(8,128)S(1)} %collective-permute-done.11.refs_1_, bf16[2,384,256]{2,1,0:T(8,128)(2,1)S(1)} %get-tuple-element.39.refs_2_, bf16[2,384,256]{2,1,0:T(8,128)(2,1)S(1)} %get-tuple-element.40.refs_3_), custom_call_target="tpu_custom_call" | custom-call | tf_op jit(solution)/shard_map/pallas_call | solution.py:57
  (29 shorter events, 3.2 us)
Async XLA Ops:
  0.0 9.9 %copy-start = (bf16[3,3,128,896]{3,2,1,0:T(8,128)(2,1)S(1)}, bf16[3,3,128,896]{3,2,1,0:T(8,128)(2,1)}, u32[]{:S(2)}) copy-start(bf16[3,3,128,896]{3,2,1,0:T(8,128)(2,1)} %ops.3) | copy-start | bytes 6193156
  0.0 9.9 %copy-start.3 = (f32[384,2,128]{2,1,0:T(2,128)S(1)}, f32[384,2,128]{2,1,0:T(2,128)}, u32[]{:S(2)}) copy-start(f32[384,2,128]{2,1,0:T(2,128)} %param.11) | copy-start | bytes 1179652
  1.1 5.7 %collective-permute-start.1 = (bf16[384,128]{1,0:T(8,128)(2,1)S(1)}, bf16[384,128]{1,0:T(8,128)(2,1)S(1)}, u32[]{:S(2)}, u32[]{:S(2)}) collective-permute-start(bf16[384,128]{1,0:T(8,128)(2,1)S(1)} %get-tuple-element.24.own), channel_id=1, source_target_pairs={{0,4},{4,8},{8,12},{12,16},{16,20},{20,24},{24,28},{28,0},{1,5},{5... | collective-permute-start | bytes 294920 | tf_op jit(solution)/shard_map/ppermute | solution.py:232
  1.6 5.2 %collective-permute-start = (bf16[384,128]{1,0:T(8,128)(2,1)S(1)}, bf16[384,128]{1,0:T(8,128)(2,1)S(1)}, u32[]{:S(2)}, u32[]{:S(2)}) collective-permute-start(bf16[384,128]{1,0:T(8,128)(2,1)S(1)} %get-tuple-element.24.own), channel_id=1, source_target_pairs={{0,28},{4,0},{8,4},{12,8},{16,12},{20,16},{24,20},{28,24},{1,29},{... | collective-permute-start | bytes 294920 | tf_op jit(solution)/shard_map/ppermute | solution.py:231
  7.1 5.1 %collective-permute-start.3 = (bf16[384,128]{1,0:T(8,128)(2,1)S(1)}, bf16[384,128]{1,0:T(8,128)(2,1)S(1)}, u32[]{:S(2)}, u32[]{:S(2)}) collective-permute-start(bf16[384,128]{1,0:T(8,128)(2,1)S(1)} %shard_map.102.lap), channel_id=1, source_target_pairs={{0,4},{4,8},{8,12},{12,16},{16,20},{20,24},{24,28},{28,0},{1,5},{5... | collective-permute-start | bytes 294920 | tf_op jit(solution)/shard_map/ppermute | solution.py:232
  8.8 3.3 %collective-permute-start.2 = (bf16[384,128]{1,0:T(8,128)(2,1)S(1)}, bf16[384,128]{1,0:T(8,128)(2,1)S(1)}, u32[]{:S(2)}, u32[]{:S(2)}) collective-permute-start(bf16[384,128]{1,0:T(8,128)(2,1)S(1)} %shard_map.102.lap), channel_id=1, source_target_pairs={{0,28},{4,0},{8,4},{12,8},{16,12},{20,16},{24,20},{28,24},{1,29},{... | collective-permute-start | bytes 294920 | tf_op jit(solution)/shard_map/ppermute | solution.py:231
  10.0 8.0 %copy-start.5 = (f32[384]{0:T(512)S(1)}, f32[384]{0:T(512)}, u32[]{:S(2)}) copy-start(f32[384]{0:T(512)} %param.15) | copy-start | bytes 4612
  11.1 11.0 %copy-start.1 = (bf16[4,512,128]{2,1,0:T(8,128)(2,1)S(1)}, bf16[4,512,128]{2,1,0:T(8,128)(2,1)}, u32[]{:S(2)}) copy-start(bf16[4,512,128]{2,1,0:T(8,128)(2,1)} %constant.12.clone.refs_4_.refs_3_) | copy-start | bytes 1572868
  11.1 10.9 %copy-start.2 = (bf16[4,512,128]{2,1,0:T(8,128)(2,1)S(1)}, bf16[4,512,128]{2,1,0:T(8,128)(2,1)}, u32[]{:S(2)}) copy-start(bf16[4,512,128]{2,1,0:T(8,128)(2,1)} %constant.11.clone.refs_3_.refs_2_) | copy-start | bytes 1572868
  11.2 10.9 %copy-start.4 = (f32[512]{0:T(512)S(1)}, f32[512]{0:T(512)}, u32[]{:S(2)}) copy-start(f32[512]{0:T(512)} %param.14) | copy-start | bytes 6148
  12.5 8.8 %collective-permute-start.6 = (bf16[384,128]{1,0:T(8,128)(2,1)S(1)}, bf16[384,128]{1,0:T(8,128)(2,1)S(1)}, u32[]{:S(2)}, u32[]{:S(2)}) collective-permute-start(bf16[384,128]{1,0:T(8,128)(2,1)S(1)} %get-tuple-element.28.refs_0_), channel_id=1, source_target_pairs={{2,0},{3,1},{0,2},{1,3},{6,4},{7,5},{4,6},{5,7},{10,8},{11,9},{8,1... | collective-permute-start | bytes 294920 | tf_op jit(solution)/shard_map/ppermute | solution.py:303
  15.9 6.2 %collective-permute-start.5 = (bf16[384,128]{1,0:T(8,128)(2,1)S(1)}, bf16[384,128]{1,0:T(8,128)(2,1)S(1)}, u32[]{:S(2)}, u32[]{:S(2)}) collective-permute-start(bf16[384,128]{1,0:T(8,128)(2,1)S(1)} %get-tuple-element.28.refs_0_), channel_id=1, source_target_pairs={{1,0},{2,1},{3,2},{0,3},{5,4},{6,5},{7,6},{4,7},{9,8},{10,9},{11,1... | collective-permute-start | bytes 294920 | tf_op jit(solution)/shard_map/ppermute | solution.py:303
  17.2 7.8 %collective-permute-start.4 = (bf16[384,128]{1,0:T(8,128)(2,1)S(1)}, bf16[384,128]{1,0:T(8,128)(2,1)S(1)}, u32[]{:S(2)}, u32[]{:S(2)}) collective-permute-start(bf16[384,128]{1,0:T(8,128)(2,1)S(1)} %get-tuple-element.28.refs_0_), channel_id=1, source_target_pairs={{3,0},{0,1},{1,2},{2,3},{7,4},{4,5},{5,6},{6,7},{11,8},{8,9},{9,10... | collective-permute-start | bytes 294920 | tf_op jit(solution)/shard_map/ppermute | solution.py:303
  25.8 1.4 %collective-permute-start.7 = (f32[256,128]{1,0:T(8,128)S(1)}, f32[256,128]{1,0:T(8,128)S(1)}, u32[]{:S(2)}, u32[]{:S(2)}) collective-permute-start(f32[256,128]{1,0:T(8,128)S(1)} %get-tuple-element.36), channel_id=1, source_target_pairs={{0,4},{4,0},{8,12},{12,8},{16,20},{20,16},{24,28},{28,24},{1,5},{5... | collective-permute-start | bytes 393224 | tf_op jit(solution)/shard_map/ppermute | solution.py:237
  27.4 4.4 %collective-permute-start.10 = (f16[272,128]{1,0:T(8,128)(2,1)S(1)}, f16[272,128]{1,0:T(8,128)(2,1)S(1)}, u32[]{:S(2)}, u32[]{:S(2)}) collective-permute-start(f16[272,128]{1,0:T(8,128)(2,1)S(1)} %convert_element_type.21), channel_id=1, source_target_pairs={{0,8},{4,12},{8,0},{12,4},{16,24},{20,28},{24,16},{28,20},{1,9},{5... | collective-permute-start | bytes 208904 | tf_op jit(solution)/shard_map/ppermute | solution.py:252
  27.9 4.7 %collective-permute-start.9 = (f16[272,128]{1,0:T(8,128)(2,1)S(1)}, f16[272,128]{1,0:T(8,128)(2,1)S(1)}, u32[]{:S(2)}, u32[]{:S(2)}) collective-permute-start(f16[272,128]{1,0:T(8,128)(2,1)S(1)} %convert_element_type.21), channel_id=1, source_target_pairs={{0,16},{4,20},{8,24},{12,28},{16,0},{20,4},{24,8},{28,12},{1,17},{... | collective-permute-start | bytes 208904 | tf_op jit(solution)/shard_map/ppermute | solution.py:252
  28.6 5.2 %collective-permute-start.8 = (f16[272,128]{1,0:T(8,128)(2,1)S(1)}, f16[272,128]{1,0:T(8,128)(2,1)S(1)}, u32[]{:S(2)}, u32[]{:S(2)}) collective-permute-start(f16[272,128]{1,0:T(8,128)(2,1)S(1)} %convert_element_type.21), channel_id=1, source_target_pairs={{0,24},{4,28},{8,16},{12,20},{16,8},{20,12},{24,0},{28,4},{1,25},{... | collective-permute-start | bytes 208904 | tf_op jit(solution)/shard_map/ppermute | solution.py:252
  33.9 1.4 %collective-permute-start.11 = (f32[256,128]{1,0:T(8,128)S(1)}, f32[256,128]{1,0:T(8,128)S(1)}, u32[]{:S(2)}, u32[]{:S(2)}) collective-permute-start(f32[256,128]{1,0:T(8,128)S(1)} %multiply_add_fusion.refs_1_), channel_id=1, source_target_pairs={{0,4},{4,0},{8,12},{12,8},{16,20},{20,16},{24,28},{28,24},{1,5},{5... | collective-permute-start | bytes 393224 | tf_op jit(solution)/shard_map/ppermute | solution.py:237

commit v11 on v10

--- a/solution.py
+++ b/solution.py
@@ -186,8 +186,8 @@
     rates[...] = rate + (0.5 * rate) * jnp.tanh(value.astype(F32))
 
 
-def diffuse_kernel(order, last, stepped, dh_high, dh_low, kappa, wbt, early, slopes, rates, diffused, keep, send):
-    width = stepped.shape[1]
+def diffuse_kernel(order, last, dh_high, dh_low, kappa, wbt, early, slopes, rates, late, send):
+    width = last.shape[1]
     rad, chunk, rows = gathered(order, width)
     core = lax.rem(lax.axis_index("tile"), 2)
     value = last[...]
@@ -197,14 +197,21 @@
     last_rates = rate + (0.5 * rate) * jnp.tanh(value.astype(F32))
     fluxes = jnp.concatenate([rates[...], last_rates], axis=1) * total
     own = [jnp.concatenate([table[rad, r, :] for r in rows], axis=0) for table in (dh_high, dh_low)]
-    term = radial_step * dot3(split(fluxes), own)
-    diffused[...] = stepped[...] + term
-    late = jnp.concatenate(split(term), axis=1)
-    half = keep.shape[0]
-    for out, which in ((send, 1 - core), (keep, core)):
-        modes = pl.ds(pl.multiple_of(which * half, half), half)
-        total = dot(wbt[modes, :], late)
-        out[...] = early[modes, :] + total[:, :width] + total[:, width:]
+    late[...] = jnp.concatenate(split(radial_step * dot3(split(fluxes), own)), axis=1)
+    send[...] = mode_half(wbt, early, late, 1 - core)
+
+
+def mode_half(wbt, early, late, which):
+    half, width = early.shape[0] // 2, early.shape[1]
+    modes = pl.ds(pl.multiple_of(which * half, half), half)
+    total = dot(wbt[modes, :], late[...])
+    return early[modes, :] + total[:, :width] + total[:, width:]
+
+
+def keep_kernel(wbt, early, late, stepped, keep, diffused):
+    width = stepped.shape[1]
+    keep[...] = mode_half(wbt, early, late, lax.rem(lax.axis_index("tile"), 2))
+    diffused[...] = stepped[...] + late[:, :width].astype(F32) + late[:, width:].astype(F32)
 
 
 def pack_kernel(keep, received, out, scaled):
@@ -249,7 +256,7 @@
         rows, levels = keep.shape
         block, scaled = call(pack_kernel, (shape(keep.shape, F32), shape((rows + 16, levels), F32)), (keep, received))
         sent = scaled.astype(jnp.float16)
-        parts = [lax.ppermute(sent, "tile", [(i, i ^ m) for i in range(count)]) for m in reversed(range(2, count, 2))]
+        parts = [lax.ppermute(sent, "tile", [(i, i ^ m) for i in range(count)]) for m in range(2, count, 2)]
         return sum((unpacked(part) for part in parts), block)
     block = keep + received
     for m in [1 << k for k in range(1, count.bit_length() - 1)]:
@@ -314,11 +321,12 @@
         (shape((nodes, rads * levels), F32), shape((nodes, (rads - 1) * levels), F32)),
         (*shards[:-1], *dhat),
     )
-    diffused, keep, send = call(
+    late, send = call(
         lambda *refs: diffuse_kernel(order, *refs),
-        (wide, half, half),
-        (shards[-1], stepped, *dhat, wbt, early, slopes, rates),
-    )
+        (shape((nodes, 2 * levels), BF), half),
+        (shards[-1], *dhat, wbt, early, slopes, rates),
+    )
+    keep, diffused = call(keep_kernel, (half, wide), (wbt, early, late, stepped))
     mine = tile_sum(keep, send)
     other = swap(mine)
     some = call(lambda *refs: filter_kernel(0, *refs), wide, (diffused, mine, bg_high, bg_low))

time: 36.5 us -> 36.4 us (level)
    pallas_call x11 -> x12, Pallas kernels: 9.41 us -> 9.68 us  [call(): pl.pallas_call(kernel, out_shape=outs, in_specs=[{'s': SMEM, 'h': HBM, 'v...]
  transfers between devices with their start and end apart: 12 -> 12, of which waited for: 10 -> 9; matrix products, arithmetic and copies ran while one was open for 2% -> 2% of each run, Pallas kernels for 16% -> 17%
where the time goes in v11:
time: 36.4 us; the launch traced here: 36.2 us
  starting transfers between devices  15.4 us (42%)
  waiting for transfers between devices  10.3 us (28%)
  Pallas kernels  9.68 us (27%)
  local copies, waits for them, and re-layouts  0.59 us (2%)
    pallas_call x12, Pallas kernels, call(): pl.pallas_call(kernel, out_shape=outs, in_specs=[{'s': SMEM, 'h': HBM, 'v...  9.68 us
    ppermute x3, starting transfers between devices, body(): lax.ppermute(narrow, 'rad', [(source(i, d), i) for i in range(rads)])  5.4 us
    ppermute x3, waiting for transfers between devices, body(): lax.ppermute(narrow, 'rad', [(source(i, d), i) for i in range(rads)])  4.15 us
    ppermute x2, starting transfers between devices, halo(): high = lax.ppermute(block, 'tile', shift('tile', -1))  4.05 us
    ppermute x3, starting transfers between devices, tile_sum(): lax.ppermute(sent, 'tile', [(i, i ^ m) for i in range(count)])  3.55 us
    ppermute x3, waiting for transfers between devices, tile_sum(): lax.ppermute(sent, 'tile', [(i, i ^ m) for i in range(count)])  2.76 us
    ppermute x2, starting transfers between devices, halo(): low = lax.ppermute(block, 'tile', shift('tile', 1))  2.24 us
    ppermute x2, waiting for transfers between devices, swap(): lax.ppermute(block, 'tile', [(i, i ^ 1) for i in range(lax.axis_size('til...  2.13 us
  transfers between devices with their start and end apart: 12, of which 9 were waited for; matrix products, arithmetic and copies ran while one was open for 2% of the time, Pallas kernels for 17%

profile of v11, /device:TPU:0, one launch (start us, length us, event | category | flops | bytes accessed | tf_op | source)
XLA Modules:
  0.0 36.2 jit_solution(5956014408828277989)
XLA Ops:
  0.0 1.1 %shard_map.100 = (f32[384,128]{1,0:T(8,128)S(1)}, bf16[384,128]{1,0:T(8,128)(2,1)S(1)}, s32[3,7]{1,0:T(4,128)S(1)}) custom-call(f32[384,128]{1,0:T(8,128)} %bitcast.16, s32[3,7]{1,0:T(4,128)} %neighbours.1), custom_call_target="tpu_custom_call" | custom-call | tf_op jit(solution)/shard_map/pallas_call | solution.py:57
  1.1 0.5 %collective-permute-start.1 = (bf16[384,128]{1,0:T(8,128)(2,1)S(1)}, bf16[384,128]{1,0:T(8,128)(2,1)S(1)}, u32[]{:S(2)}, u32[]{:S(2)}) collective-permute-start(bf16[384,128]{1,0:T(8,128)(2,1)S(1)} %get-tuple-element.25.own), channel_id=1, source_target_pairs={{0,4},{4,8},{8,12},{12,16},{16,20},{20,24},{24,28},{28,0},{1,5},{5... | collective-permute-start | bytes 294920 | tf_op jit(solution)/shard_map/ppermute | solution.py:239
  1.6 2.9 %collective-permute-start = (bf16[384,128]{1,0:T(8,128)(2,1)S(1)}, bf16[384,128]{1,0:T(8,128)(2,1)S(1)}, u32[]{:S(2)}, u32[]{:S(2)}) collective-permute-start(bf16[384,128]{1,0:T(8,128)(2,1)S(1)} %get-tuple-element.25.own), channel_id=1, source_target_pairs={{0,28},{4,0},{8,4},{12,8},{16,12},{20,16},{24,20},{28,24},{1,29},{... | collective-permute-start | bytes 294920 | tf_op jit(solution)/shard_map/ppermute | solution.py:238
  4.6 2.0 %shard_map.101 = (bf16[9,384,128]{2,1,0:T(8,128)(2,1)S(1)}, f32[384,128]{1,0:T(8,128)S(1)}) custom-call(s32[3,7]{1,0:T(4,128)S(1)} %get-tuple-element.24.ids, bf16[3,3,128,896]{3,2,1,0:T(8,128)(2,1)} %ops.3, bf16[384,128]{1,0:T(8,128)(2,1)S(1)} %get-tuple-element.25.own), custom_call_target="tpu_custom_call" | custom-call | tf_op jit(solution)/shard_map/pallas_call | solution.py:57
  7.1 1.7 %collective-permute-start.3 = (bf16[384,128]{1,0:T(8,128)(2,1)S(1)}, bf16[384,128]{1,0:T(8,128)(2,1)S(1)}, u32[]{:S(2)}, u32[]{:S(2)}) collective-permute-start(bf16[384,128]{1,0:T(8,128)(2,1)S(1)} %shard_map.102.lap), channel_id=1, source_target_pairs={{0,4},{4,8},{8,12},{12,16},{16,20},{20,24},{24,28},{28,0},{1,5},{5... | collective-permute-start | bytes 294920 | tf_op jit(solution)/shard_map/ppermute | solution.py:239
  8.8 1.1 %collective-permute-start.2 = (bf16[384,128]{1,0:T(8,128)(2,1)S(1)}, bf16[384,128]{1,0:T(8,128)(2,1)S(1)}, u32[]{:S(2)}, u32[]{:S(2)}) collective-permute-start(bf16[384,128]{1,0:T(8,128)(2,1)S(1)} %shard_map.102.lap), channel_id=1, source_target_pairs={{0,28},{4,0},{8,4},{12,8},{16,12},{20,16},{24,20},{28,24},{1,29},{... | collective-permute-start | bytes 294920 | tf_op jit(solution)/shard_map/ppermute | solution.py:238
  10.0 1.2 %shard_map.103.part = f32[384,128]{1,0:T(8,128)S(1)} custom-call(s32[3,7]{1,0:T(4,128)S(1)} %get-tuple-element.24.ids, bf16[3,3,128,896]{3,2,1,0:T(8,128)(2,1)S(1)} %copy-done, f32[768,128]{1,0:T(8,128)S(1)} %bitcast.13, bf16[9,384,128]{2,1,0:T(8,128)(2,1)S(1)} %get-tuple-element.26.dense.lap_dense, bf16[384,128]{1,0:T(8,128)(2,1)S(1)} %collective-permute-done.1.low, ...), custom_call_target="tpu_custom_call" | custom-call | tf_op jit(solution)/shard_map/pallas_call | solution.py:57
  11.2 1.0 %collective-permute-done.3.low = bf16[384,128]{1,0:T(8,128)(2,1)S(1)} collective-permute-done((bf16[384,128]{1,0:T(8,128)(2,1)S(1)}, bf16[384,128]{1,0:T(8,128)(2,1)S(1)}, u32[]{:S(2)}, u32[]{:S(2)}) %collective-permute-start.3) | collective-permute-done | bytes 98336 | tf_op jit(solution)/shard_map/ppermute | solution.py:239
  12.5 3.4 %collective-permute-start.6 = (bf16[384,128]{1,0:T(8,128)(2,1)S(1)}, bf16[384,128]{1,0:T(8,128)(2,1)S(1)}, u32[]{:S(2)}, u32[]{:S(2)}) collective-permute-start(bf16[384,128]{1,0:T(8,128)(2,1)S(1)} %get-tuple-element.32.refs_0_), channel_id=1, source_target_pairs={{2,0},{3,1},{0,2},{1,3},{6,4},{7,5},{4,6},{5,7},{10,8},{11,9},{8,1... | collective-permute-start | bytes 294920 | tf_op jit(solution)/shard_map/ppermute | solution.py:310
  15.9 1.4 %collective-permute-start.5 = (bf16[384,128]{1,0:T(8,128)(2,1)S(1)}, bf16[384,128]{1,0:T(8,128)(2,1)S(1)}, u32[]{:S(2)}, u32[]{:S(2)}) collective-permute-start(bf16[384,128]{1,0:T(8,128)(2,1)S(1)} %get-tuple-element.32.refs_0_), channel_id=1, source_target_pairs={{1,0},{2,1},{3,2},{0,3},{5,4},{6,5},{7,6},{4,7},{9,8},{10,9},{11,1... | collective-permute-start | bytes 294920 | tf_op jit(solution)/shard_map/ppermute | solution.py:310
  17.2 0.7 %collective-permute-start.4 = (bf16[384,128]{1,0:T(8,128)(2,1)S(1)}, bf16[384,128]{1,0:T(8,128)(2,1)S(1)}, u32[]{:S(2)}, u32[]{:S(2)}) collective-permute-start(bf16[384,128]{1,0:T(8,128)(2,1)S(1)} %get-tuple-element.32.refs_0_), channel_id=1, source_target_pairs={{3,0},{0,1},{1,2},{2,3},{7,4},{4,5},{5,6},{6,7},{11,8},{8,9},{9,10... | collective-permute-start | bytes 294920 | tf_op jit(solution)/shard_map/ppermute | solution.py:310
  17.9 0.6 %broadcast_in_dim.6.weight = f32[1,384]{1,0:T(1,128)} reshape(f32[384]{0:T(512)S(1)} %copy-done.5) | data formatting | bytes 3072 | tf_op jit(solution)/shard_map/broadcast_in_dim | solution.py:314
  18.5 1.8 %shard_map.105 = (bf16[512,384]{1,0:T(8,128)(2,1)S(1)}, f32[512,128]{1,0:T(8,128)S(1)}, bf16[2,384,256]{2,1,0:T(8,128)(2,1)S(1)}, bf16[2,384,256]{2,1,0:T(8,128)(2,1)S(1)}) custom-call(f32[384,512]{1,0:T(8,128)} %basis.1, f32[1,384]{1,0:T(1,128)} %broadcast_in_dim.6.weight, s32[1,512]{1,0:T(1,128)} %bitcast.17, f32[384,128]{1,0:T(8,128)S(1)} %get-tuple-element.29.value.stepped), custom_call_target="tpu_custom_call" | custom-call | tf_op jit(solution)/shard_map/pallas_call | solution.py:57
  20.3 1.0 %collective-permute-done.6.refs_2_ = bf16[384,128]{1,0:T(8,128)(2,1)S(1)} collective-permute-done((bf16[384,128]{1,0:T(8,128)(2,1)S(1)}, bf16[384,128]{1,0:T(8,128)(2,1)S(1)}, u32[]{:S(2)}, u32[]{:S(2)}) %collective-permute-start.6) | collective-permute-done | bytes 98336 | tf_op jit(solution)/shard_map/ppermute | solution.py:310
  21.3 0.8 %collective-permute-done.5.refs_1_ = bf16[384,128]{1,0:T(8,128)(2,1)S(1)} collective-permute-done((bf16[384,128]{1,0:T(8,128)(2,1)S(1)}, bf16[384,128]{1,0:T(8,128)(2,1)S(1)}, u32[]{:S(2)}, u32[]{:S(2)}) %collective-permute-start.5) | collective-permute-done | bytes 98336 | tf_op jit(solution)/shard_map/ppermute | solution.py:310
  22.1 0.6 %shard_map.106 = (f32[384,512]{1,0:T(8,128)S(1)}, f32[384,384]{1,0:T(8,128)S(1)}) custom-call(bf16[384,128]{1,0:T(8,128)(2,1)S(1)} %get-tuple-element.32.refs_0_, bf16[384,128]{1,0:T(8,128)(2,1)S(1)} %collective-permute-done.5.refs_1_, bf16[384,128]{1,0:T(8,128)(2,1)S(1)} %collective-permute-done.6.refs_2_, bf16[4,512,128]{2,1,0:T(8,128)(2,1)S(1)} %copy-done.2, ...), custom_call_target="tpu_custom_call" | custom-call | tf_op jit(solution)/shard_map/pallas_call | solution.py:57
  22.7 2.4 %collective-permute-done.4.refs_0_ = bf16[384,128]{1,0:T(8,128)(2,1)S(1)} collective-permute-done((bf16[384,128]{1,0:T(8,128)(2,1)S(1)}, bf16[384,128]{1,0:T(8,128)(2,1)S(1)}, u32[]{:S(2)}, u32[]{:S(2)}) %collective-permute-start.4) | collective-permute-done | bytes 98336 | tf_op jit(solution)/shard_map/ppermute | solution.py:310
  25.1 0.8 %shard_map.107 = (bf16[384,256]{1,0:T(8,128)(2,1)S(1)}, f32[256,128]{1,0:T(8,128)S(1)}) custom-call(bf16[384,128]{1,0:T(8,128)(2,1)S(1)} %collective-permute-done.4.refs_0_, bf16[4,512,128]{2,1,0:T(8,128)(2,1)S(1)} %copy-done.2, bf16[4,512,128]{2,1,0:T(8,128)(2,1)S(1)} %copy-done.1, f32[4,1,128]{2,1,0:T(1,128)S(1)} %bitcast.15, ...), custom_call_target="tpu_custom_call" | custom-call | tf_op jit(solution)/shard_map/pallas_call | solution.py:57
  26.2 1.1 %collective-permute-done.7.received = f32[256,128]{1,0:T(8,128)S(1)} collective-permute-done((f32[256,128]{1,0:T(8,128)S(1)}, f32[256,128]{1,0:T(8,128)S(1)}, u32[]{:S(2)}, u32[]{:S(2)}) %collective-permute-start.7) | collective-permute-done | bytes 131104 | tf_op jit(solution)/shard_map/ppermute | solution.py:244
  27.7 1.7 %collective-permute-start.9 = (f16[272,128]{1,0:T(8,128)(2,1)S(1)}, f16[272,128]{1,0:T(8,128)(2,1)S(1)}, u32[]{:S(2)}, u32[]{:S(2)}) collective-permute-start(f16[272,128]{1,0:T(8,128)(2,1)S(1)} %convert_element_type.21), channel_id=1, source_target_pairs={{0,16},{4,20},{8,24},{12,28},{16,0},{20,4},{24,8},{28,12},{1,17},{... | collective-permute-start | bytes 208904 | tf_op jit(solution)/shard_map/ppermute | solution.py:259
  29.4 1.6 %collective-permute-start.8 = (f16[272,128]{1,0:T(8,128)(2,1)S(1)}, f16[272,128]{1,0:T(8,128)(2,1)S(1)}, u32[]{:S(2)}, u32[]{:S(2)}) collective-permute-start(f16[272,128]{1,0:T(8,128)(2,1)S(1)} %convert_element_type.21), channel_id=1, source_target_pairs={{0,8},{4,12},{8,0},{12,4},{16,24},{20,28},{24,16},{28,20},{1,9},{5... | collective-permute-start | bytes 208904 | tf_op jit(solution)/shard_map/ppermute | solution.py:259
  31.0 2.4 %collective-permute-done.10 = f16[272,128]{1,0:T(8,128)(2,1)S(1)} collective-permute-done((f16[272,128]{1,0:T(8,128)(2,1)S(1)}, f16[272,128]{1,0:T(8,128)(2,1)S(1)}, u32[]{:S(2)}, u32[]{:S(2)}) %collective-permute-start.10) | collective-permute-done | bytes 69664 | tf_op jit(solution)/shard_map/ppermute | solution.py:259
  34.2 1.1 %collective-permute-done.11.refs_1_ = f32[256,128]{1,0:T(8,128)S(1)} collective-permute-done((f32[256,128]{1,0:T(8,128)S(1)}, f32[256,128]{1,0:T(8,128)S(1)}, u32[]{:S(2)}, u32[]{:S(2)}) %collective-permute-start.11) | collective-permute-done | bytes 131104 | tf_op jit(solution)/shard_map/ppermute | solution.py:244
  35.3 0.9 %shard_map.111 = f32[384,128]{1,0:T(8,128)} custom-call(f32[384,128]{1,0:T(8,128)S(1)} %shard_map.110.refs_0_, f32[256,128]{1,0:T(8,128)S(1)} %collective-permute-done.11.refs_1_, bf16[2,384,256]{2,1,0:T(8,128)(2,1)S(1)} %get-tuple-element.41.refs_2_, bf16[2,384,256]{2,1,0:T(8,128)(2,1)S(1)} %get-tuple-element.42.refs_3_), custom_call_target="tpu_custom_call" | custom-call | tf_op jit(solution)/shard_map/pallas_call | solution.py:57
  (30 shorter events, 2.4 us)
Async XLA Ops:
  0.0 9.9 %copy-start = (bf16[3,3,128,896]{3,2,1,0:T(8,128)(2,1)S(1)}, bf16[3,3,128,896]{3,2,1,0:T(8,128)(2,1)}, u32[]{:S(2)}) copy-start(bf16[3,3,128,896]{3,2,1,0:T(8,128)(2,1)} %ops.3) | copy-start | bytes 6193156
  0.0 9.9 %copy-start.3 = (f32[384,2,128]{2,1,0:T(2,128)S(1)}, f32[384,2,128]{2,1,0:T(2,128)}, u32[]{:S(2)}) copy-start(f32[384,2,128]{2,1,0:T(2,128)} %param.11) | copy-start | bytes 1179652
  1.1 5.7 %collective-permute-start.1 = (bf16[384,128]{1,0:T(8,128)(2,1)S(1)}, bf16[384,128]{1,0:T(8,128)(2,1)S(1)}, u32[]{:S(2)}, u32[]{:S(2)}) collective-permute-start(bf16[384,128]{1,0:T(8,128)(2,1)S(1)} %get-tuple-element.25.own), channel_id=1, source_target_pairs={{0,4},{4,8},{8,12},{12,16},{16,20},{20,24},{24,28},{28,0},{1,5},{5... | collective-permute-start | bytes 294920 | tf_op jit(solution)/shard_map/ppermute | solution.py:239
  1.6 5.2 %collective-permute-start = (bf16[384,128]{1,0:T(8,128)(2,1)S(1)}, bf16[384,128]{1,0:T(8,128)(2,1)S(1)}, u32[]{:S(2)}, u32[]{:S(2)}) collective-permute-start(bf16[384,128]{1,0:T(8,128)(2,1)S(1)} %get-tuple-element.25.own), channel_id=1, source_target_pairs={{0,28},{4,0},{8,4},{12,8},{16,12},{20,16},{24,20},{28,24},{1,29},{... | collective-permute-start | bytes 294920 | tf_op jit(solution)/shard_map/ppermute | solution.py:238
  7.1 5.1 %collective-permute-start.3 = (bf16[384,128]{1,0:T(8,128)(2,1)S(1)}, bf16[384,128]{1,0:T(8,128)(2,1)S(1)}, u32[]{:S(2)}, u32[]{:S(2)}) collective-permute-start(bf16[384,128]{1,0:T(8,128)(2,1)S(1)} %shard_map.102.lap), channel_id=1, source_target_pairs={{0,4},{4,8},{8,12},{12,16},{16,20},{20,24},{24,28},{28,0},{1,5},{5... | collective-permute-start | bytes 294920 | tf_op jit(solution)/shard_map/ppermute | solution.py:239
  8.8 3.3 %collective-permute-start.2 = (bf16[384,128]{1,0:T(8,128)(2,1)S(1)}, bf16[384,128]{1,0:T(8,128)(2,1)S(1)}, u32[]{:S(2)}, u32[]{:S(2)}) collective-permute-start(bf16[384,128]{1,0:T(8,128)(2,1)S(1)} %shard_map.102.lap), channel_id=1, source_target_pairs={{0,28},{4,0},{8,4},{12,8},{16,12},{20,16},{24,20},{28,24},{1,29},{... | collective-permute-start | bytes 294920 | tf_op jit(solution)/shard_map/ppermute | solution.py:238
  10.0 8.0 %copy-start.5 = (f32[384]{0:T(512)S(1)}, f32[384]{0:T(512)}, u32[]{:S(2)}) copy-start(f32[384]{0:T(512)} %param.15) | copy-start | bytes 4612
  11.1 11.0 %copy-start.1 = (bf16[4,512,128]{2,1,0:T(8,128)(2,1)S(1)}, bf16[4,512,128]{2,1,0:T(8,128)(2,1)}, u32[]{:S(2)}) copy-start(bf16[4,512,128]{2,1,0:T(8,128)(2,1)} %constant.12.clone.refs_4_.refs_2_) | copy-start | bytes 1572868
  11.1 11.0 %copy-start.2 = (bf16[4,512,128]{2,1,0:T(8,128)(2,1)S(1)}, bf16[4,512,128]{2,1,0:T(8,128)(2,1)}, u32[]{:S(2)}) copy-start(bf16[4,512,128]{2,1,0:T(8,128)(2,1)} %constant.11.clone.refs_3_.refs_1_) | copy-start | bytes 1572868
  11.2 10.9 %copy-start.4 = (f32[512]{0:T(512)S(1)}, f32[512]{0:T(512)}, u32[]{:S(2)}) copy-start(f32[512]{0:T(512)} %param.14) | copy-start | bytes 6148
  12.5 8.8 %collective-permute-start.6 = (bf16[384,128]{1,0:T(8,128)(2,1)S(1)}, bf16[384,128]{1,0:T(8,128)(2,1)S(1)}, u32[]{:S(2)}, u32[]{:S(2)}) collective-permute-start(bf16[384,128]{1,0:T(8,128)(2,1)S(1)} %get-tuple-element.32.refs_0_), channel_id=1, source_target_pairs={{2,0},{3,1},{0,2},{1,3},{6,4},{7,5},{4,6},{5,7},{10,8},{11,9},{8,1... | collective-permute-start | bytes 294920 | tf_op jit(solution)/shard_map/ppermute | solution.py:310
  15.9 6.2 %collective-permute-start.5 = (bf16[384,128]{1,0:T(8,128)(2,1)S(1)}, bf16[384,128]{1,0:T(8,128)(2,1)S(1)}, u32[]{:S(2)}, u32[]{:S(2)}) collective-permute-start(bf16[384,128]{1,0:T(8,128)(2,1)S(1)} %get-tuple-element.32.refs_0_), channel_id=1, source_target_pairs={{1,0},{2,1},{3,2},{0,3},{5,4},{6,5},{7,6},{4,7},{9,8},{10,9},{11,1... | collective-permute-start | bytes 294920 | tf_op jit(solution)/shard_map/ppermute | solution.py:310
  17.2 7.8 %collective-permute-start.4 = (bf16[384,128]{1,0:T(8,128)(2,1)S(1)}, bf16[384,128]{1,0:T(8,128)(2,1)S(1)}, u32[]{:S(2)}, u32[]{:S(2)}) collective-permute-start(bf16[384,128]{1,0:T(8,128)(2,1)S(1)} %get-tuple-element.32.refs_0_), channel_id=1, source_target_pairs={{3,0},{0,1},{1,2},{2,3},{7,4},{4,5},{5,6},{6,7},{11,8},{8,9},{9,10... | collective-permute-start | bytes 294920 | tf_op jit(solution)/shard_map/ppermute | solution.py:310
  25.9 1.4 %collective-permute-start.7 = (f32[256,128]{1,0:T(8,128)S(1)}, f32[256,128]{1,0:T(8,128)S(1)}, u32[]{:S(2)}, u32[]{:S(2)}) collective-permute-start(f32[256,128]{1,0:T(8,128)S(1)} %get-tuple-element.38), channel_id=1, source_target_pairs={{0,4},{4,0},{8,12},{12,8},{16,20},{20,16},{24,28},{28,24},{1,5},{5... | collective-permute-start | bytes 393224 | tf_op jit(solution)/shard_map/ppermute | solution.py:244
  27.5 6.0 %collective-permute-start.10 = (f16[272,128]{1,0:T(8,128)(2,1)S(1)}, f16[272,128]{1,0:T(8,128)(2,1)S(1)}, u32[]{:S(2)}, u32[]{:S(2)}) collective-permute-start(f16[272,128]{1,0:T(8,128)(2,1)S(1)} %convert_element_type.21), channel_id=1, source_target_pairs={{0,24},{4,28},{8,16},{12,20},{16,8},{20,12},{24,0},{28,4},{1,25},{... | collective-permute-start | bytes 208904 | tf_op jit(solution)/shard_map/ppermute | solution.py:259
  27.7 5.7 %collective-permute-start.9 = (f16[272,128]{1,0:T(8,128)(2,1)S(1)}, f16[272,128]{1,0:T(8,128)(2,1)S(1)}, u32[]{:S(2)}, u32[]{:S(2)}) collective-permute-start(f16[272,128]{1,0:T(8,128)(2,1)S(1)} %convert_element_type.21), channel_id=1, source_target_pairs={{0,16},{4,20},{8,24},{12,28},{16,0},{20,4},{24,8},{28,12},{1,17},{... | collective-permute-start | bytes 208904 | tf_op jit(solution)/shard_map/ppermute | solution.py:259
  29.4 4.4 %collective-permute-start.8 = (f16[272,128]{1,0:T(8,128)(2,1)S(1)}, f16[272,128]{1,0:T(8,128)(2,1)S(1)}, u32[]{:S(2)}, u32[]{:S(2)}) collective-permute-start(f16[272,128]{1,0:T(8,128)(2,1)S(1)} %convert_element_type.21), channel_id=1, source_target_pairs={{0,8},{4,12},{8,0},{12,4},{16,24},{20,28},{24,16},{28,20},{1,9},{5... | collective-permute-start | bytes 208904 | tf_op jit(solution)/shard_map/ppermute | solution.py:259
  33.9 1.4 %collective-permute-start.11 = (f32[256,128]{1,0:T(8,128)S(1)}, f32[256,128]{1,0:T(8,128)S(1)}, u32[]{:S(2)}, u32[]{:S(2)}) collective-permute-start(f32[256,128]{1,0:T(8,128)S(1)} %multiply_add_fusion.refs_1_), channel_id=1, source_target_pairs={{0,4},{4,0},{8,12},{12,8},{16,20},{20,16},{24,28},{28,24},{1,5},{5... | collective-permute-start | bytes 393224 | tf_op jit(solution)/shard_map/ppermute | solution.py:244

commit v12 on v11

--- a/solution.py
+++ b/solution.py
@@ -109,7 +109,8 @@
 
 def around(dense, low, high):
     blocks = dense.shape[0] // 3
-    return dot(beside(dense, 0, blocks), low[...]) + dot(beside(dense, 2 * blocks, blocks), high[...])
+    weights = jnp.concatenate([beside(dense, 0, blocks), beside(dense, 2 * blocks, blocks)], axis=1)
+    return dot(weights, jnp.concatenate([low[...], high[...]], axis=0))
 
 
 def first_lap_kernel(dense, lap_own, high, low, lap):

time: 36.4 us -> 36.5 us (level)
  no operation moved by 1% of the time
where the time goes in v12:
time: 36.5 us; the launch traced here: 36.3 us
  starting transfers between devices  15.4 us (42%)
  waiting for transfers between devices  10.3 us (28%)
  Pallas kernels  9.69 us (27%)
  local copies, waits for them, and re-layouts  0.59 us (2%)
    pallas_call x12, Pallas kernels, call(): pl.pallas_call(kernel, out_shape=outs, in_specs=[{'s': SMEM, 'h': HBM, 'v...  9.69 us
    ppermute x3, starting transfers between devices, body(): lax.ppermute(narrow, 'rad', [(source(i, d), i) for i in range(rads)])  5.4 us
    ppermute x3, waiting for transfers between devices, body(): lax.ppermute(narrow, 'rad', [(source(i, d), i) for i in range(rads)])  4.16 us
    ppermute x2, starting transfers between devices, halo(): high = lax.ppermute(block, 'tile', shift('tile', -1))  4.05 us
    ppermute x3, starting transfers between devices, tile_sum(): lax.ppermute(sent, 'tile', [(i, i ^ m) for i in range(count)])  3.55 us
    ppermute x3, waiting for transfers between devices, tile_sum(): lax.ppermute(sent, 'tile', [(i, i ^ m) for i in range(count)])  2.75 us
    ppermute x2, starting transfers between devices, halo(): low = lax.ppermute(block, 'tile', shift('tile', 1))  2.24 us
    ppermute x2, waiting for transfers between devices, swap(): lax.ppermute(block, 'tile', [(i, i ^ 1) for i in range(lax.axis_size('til...  2.13 us
  transfers between devices with their start and end apart: 12, of which 9 were waited for; matrix products, arithmetic and copies ran while one was open for 2% of the time, Pallas kernels for 17%

profile of v12, /device:TPU:0, one launch (start us, length us, event | category | flops | bytes accessed | tf_op | source)
XLA Modules:
  0.0 36.3 jit_solution(17619311498746147717)
XLA Ops:
  0.0 1.1 %shard_map.100 = (f32[384,128]{1,0:T(8,128)S(1)}, bf16[384,128]{1,0:T(8,128)(2,1)S(1)}, s32[3,7]{1,0:T(4,128)S(1)}) custom-call(f32[384,128]{1,0:T(8,128)} %bitcast.16, s32[3,7]{1,0:T(4,128)} %neighbours.1), custom_call_target="tpu_custom_call" | custom-call | tf_op jit(solution)/shard_map/pallas_call | solution.py:57
  1.1 0.5 %collective-permute-start.1 = (bf16[384,128]{1,0:T(8,128)(2,1)S(1)}, bf16[384,128]{1,0:T(8,128)(2,1)S(1)}, u32[]{:S(2)}, u32[]{:S(2)}) collective-permute-start(bf16[384,128]{1,0:T(8,128)(2,1)S(1)} %get-tuple-element.25.own), channel_id=1, source_target_pairs={{0,4},{4,8},{8,12},{12,16},{16,20},{20,24},{24,28},{28,0},{1,5},{5... | collective-permute-start | bytes 294920 | tf_op jit(solution)/shard_map/ppermute | solution.py:240
  1.6 2.9 %collective-permute-start = (bf16[384,128]{1,0:T(8,128)(2,1)S(1)}, bf16[384,128]{1,0:T(8,128)(2,1)S(1)}, u32[]{:S(2)}, u32[]{:S(2)}) collective-permute-start(bf16[384,128]{1,0:T(8,128)(2,1)S(1)} %get-tuple-element.25.own), channel_id=1, source_target_pairs={{0,28},{4,0},{8,4},{12,8},{16,12},{20,16},{24,20},{28,24},{1,29},{... | collective-permute-start | bytes 294920 | tf_op jit(solution)/shard_map/ppermute | solution.py:239
  4.6 2.0 %shard_map.101 = (bf16[9,384,128]{2,1,0:T(8,128)(2,1)S(1)}, f32[384,128]{1,0:T(8,128)S(1)}) custom-call(s32[3,7]{1,0:T(4,128)S(1)} %get-tuple-element.24.ids, bf16[3,3,128,896]{3,2,1,0:T(8,128)(2,1)} %ops.3, bf16[384,128]{1,0:T(8,128)(2,1)S(1)} %get-tuple-element.25.own), custom_call_target="tpu_custom_call" | custom-call | tf_op jit(solution)/shard_map/pallas_call | solution.py:57
  7.1 1.7 %collective-permute-start.3 = (bf16[384,128]{1,0:T(8,128)(2,1)S(1)}, bf16[384,128]{1,0:T(8,128)(2,1)S(1)}, u32[]{:S(2)}, u32[]{:S(2)}) collective-permute-start(bf16[384,128]{1,0:T(8,128)(2,1)S(1)} %shard_map.102.lap), channel_id=1, source_target_pairs={{0,4},{4,8},{8,12},{12,16},{16,20},{20,24},{24,28},{28,0},{1,5},{5... | collective-permute-start | bytes 294920 | tf_op jit(solution)/shard_map/ppermute | solution.py:240
  8.9 1.1 %collective-permute-start.2 = (bf16[384,128]{1,0:T(8,128)(2,1)S(1)}, bf16[384,128]{1,0:T(8,128)(2,1)S(1)}, u32[]{:S(2)}, u32[]{:S(2)}) collective-permute-start(bf16[384,128]{1,0:T(8,128)(2,1)S(1)} %shard_map.102.lap), channel_id=1, source_target_pairs={{0,28},{4,0},{8,4},{12,8},{16,12},{20,16},{24,20},{28,24},{1,29},{... | collective-permute-start | bytes 294920 | tf_op jit(solution)/shard_map/ppermute | solution.py:239
  10.0 1.2 %shard_map.103.part = f32[384,128]{1,0:T(8,128)S(1)} custom-call(s32[3,7]{1,0:T(4,128)S(1)} %get-tuple-element.24.ids, bf16[3,3,128,896]{3,2,1,0:T(8,128)(2,1)S(1)} %copy-done, f32[768,128]{1,0:T(8,128)S(1)} %bitcast.13, bf16[9,384,128]{2,1,0:T(8,128)(2,1)S(1)} %get-tuple-element.26.dense.lap_dense, bf16[384,128]{1,0:T(8,128)(2,1)S(1)} %collective-permute-done.1.low, ...), custom_call_target="tpu_custom_call" | custom-call | tf_op jit(solution)/shard_map/pallas_call | solution.py:57
  11.2 1.0 %collective-permute-done.3.low = bf16[384,128]{1,0:T(8,128)(2,1)S(1)} collective-permute-done((bf16[384,128]{1,0:T(8,128)(2,1)S(1)}, bf16[384,128]{1,0:T(8,128)(2,1)S(1)}, u32[]{:S(2)}, u32[]{:S(2)}) %collective-permute-start.3) | collective-permute-done | bytes 98336 | tf_op jit(solution)/shard_map/ppermute | solution.py:240
  12.5 3.4 %collective-permute-start.6 = (bf16[384,128]{1,0:T(8,128)(2,1)S(1)}, bf16[384,128]{1,0:T(8,128)(2,1)S(1)}, u32[]{:S(2)}, u32[]{:S(2)}) collective-permute-start(bf16[384,128]{1,0:T(8,128)(2,1)S(1)} %get-tuple-element.32.refs_0_), channel_id=1, source_target_pairs={{2,0},{3,1},{0,2},{1,3},{6,4},{7,5},{4,6},{5,7},{10,8},{11,9},{8,1... | collective-permute-start | bytes 294920 | tf_op jit(solution)/shard_map/ppermute | solution.py:311
  15.9 1.4 %collective-permute-start.5 = (bf16[384,128]{1,0:T(8,128)(2,1)S(1)}, bf16[384,128]{1,0:T(8,128)(2,1)S(1)}, u32[]{:S(2)}, u32[]{:S(2)}) collective-permute-start(bf16[384,128]{1,0:T(8,128)(2,1)S(1)} %get-tuple-element.32.refs_0_), channel_id=1, source_target_pairs={{1,0},{2,1},{3,2},{0,3},{5,4},{6,5},{7,6},{4,7},{9,8},{10,9},{11,1... | collective-permute-start | bytes 294920 | tf_op jit(solution)/shard_map/ppermute | solution.py:311
  17.3 0.7 %collective-permute-start.4 = (bf16[384,128]{1,0:T(8,128)(2,1)S(1)}, bf16[384,128]{1,0:T(8,128)(2,1)S(1)}, u32[]{:S(2)}, u32[]{:S(2)}) collective-permute-start(bf16[384,128]{1,0:T(8,128)(2,1)S(1)} %get-tuple-element.32.refs_0_), channel_id=1, source_target_pairs={{3,0},{0,1},{1,2},{2,3},{7,4},{4,5},{5,6},{6,7},{11,8},{8,9},{9,10... | collective-permute-start | bytes 294920 | tf_op jit(solution)/shard_map/ppermute | solution.py:311
  17.9 0.6 %broadcast_in_dim.6.weight = f32[1,384]{1,0:T(1,128)} reshape(f32[384]{0:T(512)S(1)} %copy-done.5) | data formatting | bytes 3072 | tf_op jit(solution)/shard_map/broadcast_in_dim | solution.py:315
  18.5 1.8 %shard_map.105 = (bf16[512,384]{1,0:T(8,128)(2,1)S(1)}, f32[512,128]{1,0:T(8,128)S(1)}, bf16[2,384,256]{2,1,0:T(8,128)(2,1)S(1)}, bf16[2,384,256]{2,1,0:T(8,128)(2,1)S(1)}) custom-call(f32[384,512]{1,0:T(8,128)} %basis.1, f32[1,384]{1,0:T(1,128)} %broadcast_in_dim.6.weight, s32[1,512]{1,0:T(1,128)} %bitcast.17, f32[384,128]{1,0:T(8,128)S(1)} %get-tuple-element.29.value.stepped), custom_call_target="tpu_custom_call" | custom-call | tf_op jit(solution)/shard_map/pallas_call | solution.py:57
  20.3 1.0 %collective-permute-done.6.refs_2_ = bf16[384,128]{1,0:T(8,128)(2,1)S(1)} collective-permute-done((bf16[384,128]{1,0:T(8,128)(2,1)S(1)}, bf16[384,128]{1,0:T(8,128)(2,1)S(1)}, u32[]{:S(2)}, u32[]{:S(2)}) %collective-permute-start.6) | collective-permute-done | bytes 98336 | tf_op jit(solution)/shard_map/ppermute | solution.py:311
  21.3 0.8 %collective-permute-done.5.refs_1_ = bf16[384,128]{1,0:T(8,128)(2,1)S(1)} collective-permute-done((bf16[384,128]{1,0:T(8,128)(2,1)S(1)}, bf16[384,128]{1,0:T(8,128)(2,1)S(1)}, u32[]{:S(2)}, u32[]{:S(2)}) %collective-permute-start.5) | collective-permute-done | bytes 98336 | tf_op jit(solution)/shard_map/ppermute | solution.py:311
  22.1 0.6 %shard_map.106 = (f32[384,512]{1,0:T(8,128)S(1)}, f32[384,384]{1,0:T(8,128)S(1)}) custom-call(bf16[384,128]{1,0:T(8,128)(2,1)S(1)} %get-tuple-element.32.refs_0_, bf16[384,128]{1,0:T(8,128)(2,1)S(1)} %collective-permute-done.5.refs_1_, bf16[384,128]{1,0:T(8,128)(2,1)S(1)} %collective-permute-done.6.refs_2_, bf16[4,512,128]{2,1,0:T(8,128)(2,1)S(1)} %copy-done.2, ...), custom_call_target="tpu_custom_call" | custom-call | tf_op jit(solution)/shard_map/pallas_call | solution.py:57
  22.7 2.4 %collective-permute-done.4.refs_0_ = bf16[384,128]{1,0:T(8,128)(2,1)S(1)} collective-permute-done((bf16[384,128]{1,0:T(8,128)(2,1)S(1)}, bf16[384,128]{1,0:T(8,128)(2,1)S(1)}, u32[]{:S(2)}, u32[]{:S(2)}) %collective-permute-start.4) | collective-permute-done | bytes 98336 | tf_op jit(solution)/shard_map/ppermute | solution.py:311
  25.1 0.8 %shard_map.107 = (bf16[384,256]{1,0:T(8,128)(2,1)S(1)}, f32[256,128]{1,0:T(8,128)S(1)}) custom-call(bf16[384,128]{1,0:T(8,128)(2,1)S(1)} %collective-permute-done.4.refs_0_, bf16[4,512,128]{2,1,0:T(8,128)(2,1)S(1)} %copy-done.2, bf16[4,512,128]{2,1,0:T(8,128)(2,1)S(1)} %copy-done.1, f32[4,1,128]{2,1,0:T(1,128)S(1)} %bitcast.15, ...), custom_call_target="tpu_custom_call" | custom-call | tf_op jit(solution)/shard_map/pallas_call | solution.py:57
  26.2 1.1 %collective-permute-done.7.received = f32[256,128]{1,0:T(8,128)S(1)} collective-permute-done((f32[256,128]{1,0:T(8,128)S(1)}, f32[256,128]{1,0:T(8,128)S(1)}, u32[]{:S(2)}, u32[]{:S(2)}) %collective-permute-start.7) | collective-permute-done | bytes 131104 | tf_op jit(solution)/shard_map/ppermute | solution.py:245
  27.7 1.7 %collective-permute-start.9 = (f16[272,128]{1,0:T(8,128)(2,1)S(1)}, f16[272,128]{1,0:T(8,128)(2,1)S(1)}, u32[]{:S(2)}, u32[]{:S(2)}) collective-permute-start(f16[272,128]{1,0:T(8,128)(2,1)S(1)} %convert_element_type.21), channel_id=1, source_target_pairs={{0,16},{4,20},{8,24},{12,28},{16,0},{20,4},{24,8},{28,12},{1,17},{... | collective-permute-start | bytes 208904 | tf_op jit(solution)/shard_map/ppermute | solution.py:260
  29.4 1.6 %collective-permute-start.8 = (f16[272,128]{1,0:T(8,128)(2,1)S(1)}, f16[272,128]{1,0:T(8,128)(2,1)S(1)}, u32[]{:S(2)}, u32[]{:S(2)}) collective-permute-start(f16[272,128]{1,0:T(8,128)(2,1)S(1)} %convert_element_type.21), channel_id=1, source_target_pairs={{0,8},{4,12},{8,0},{12,4},{16,24},{20,28},{24,16},{28,20},{1,9},{5... | collective-permute-start | bytes 208904 | tf_op jit(solution)/shard_map/ppermute | solution.py:260
  31.0 2.4 %collective-permute-done.10 = f16[272,128]{1,0:T(8,128)(2,1)S(1)} collective-permute-done((f16[272,128]{1,0:T(8,128)(2,1)S(1)}, f16[272,128]{1,0:T(8,128)(2,1)S(1)}, u32[]{:S(2)}, u32[]{:S(2)}) %collective-permute-start.10) | collective-permute-done | bytes 69664 | tf_op jit(solution)/shard_map/ppermute | solution.py:260
  34.2 1.1 %collective-permute-done.11.refs_1_ = f32[256,128]{1,0:T(8,128)S(1)} collective-permute-done((f32[256,128]{1,0:T(8,128)S(1)}, f32[256,128]{1,0:T(8,128)S(1)}, u32[]{:S(2)}, u32[]{:S(2)}) %collective-permute-start.11) | collective-permute-done | bytes 131104 | tf_op jit(solution)/shard_map/ppermute | solution.py:245
  35.3 0.9 %shard_map.111 = f32[384,128]{1,0:T(8,128)} custom-call(f32[384,128]{1,0:T(8,128)S(1)} %shard_map.110.refs_0_, f32[256,128]{1,0:T(8,128)S(1)} %collective-permute-done.11.refs_1_, bf16[2,384,256]{2,1,0:T(8,128)(2,1)S(1)} %get-tuple-element.41.refs_2_, bf16[2,384,256]{2,1,0:T(8,128)(2,1)S(1)} %get-tuple-element.42.refs_3_), custom_call_target="tpu_custom_call" | custom-call | tf_op jit(solution)/shard_map/pallas_call | solution.py:57
  (30 shorter events, 2.4 us)
Async XLA Ops:
  0.0 10.0 %copy-start = (bf16[3,3,128,896]{3,2,1,0:T(8,128)(2,1)S(1)}, bf16[3,3,128,896]{3,2,1,0:T(8,128)(2,1)}, u32[]{:S(2)}) copy-start(bf16[3,3,128,896]{3,2,1,0:T(8,128)(2,1)} %ops.3) | copy-start | bytes 6193156
  0.0 10.0 %copy-start.3 = (f32[384,2,128]{2,1,0:T(2,128)S(1)}, f32[384,2,128]{2,1,0:T(2,128)}, u32[]{:S(2)}) copy-start(f32[384,2,128]{2,1,0:T(2,128)} %param.11) | copy-start | bytes 1179652
  1.1 5.7 %collective-permute-start.1 = (bf16[384,128]{1,0:T(8,128)(2,1)S(1)}, bf16[384,128]{1,0:T(8,128)(2,1)S(1)}, u32[]{:S(2)}, u32[]{:S(2)}) collective-permute-start(bf16[384,128]{1,0:T(8,128)(2,1)S(1)} %get-tuple-element.25.own), channel_id=1, source_target_pairs={{0,4},{4,8},{8,12},{12,16},{16,20},{20,24},{24,28},{28,0},{1,5},{5... | collective-permute-start | bytes 294920 | tf_op jit(solution)/shard_map/ppermute | solution.py:240
  1.6 5.2 %collective-permute-start = (bf16[384,128]{1,0:T(8,128)(2,1)S(1)}, bf16[384,128]{1,0:T(8,128)(2,1)S(1)}, u32[]{:S(2)}, u32[]{:S(2)}) collective-permute-start(bf16[384,128]{1,0:T(8,128)(2,1)S(1)} %get-tuple-element.25.own), channel_id=1, source_target_pairs={{0,28},{4,0},{8,4},{12,8},{16,12},{20,16},{24,20},{28,24},{1,29},{... | collective-permute-start | bytes 294920 | tf_op jit(solution)/shard_map/ppermute | solution.py:239
  7.1 5.1 %collective-permute-start.3 = (bf16[384,128]{1,0:T(8,128)(2,1)S(1)}, bf16[384,128]{1,0:T(8,128)(2,1)S(1)}, u32[]{:S(2)}, u32[]{:S(2)}) collective-permute-start(bf16[384,128]{1,0:T(8,128)(2,1)S(1)} %shard_map.102.lap), channel_id=1, source_target_pairs={{0,4},{4,8},{8,12},{12,16},{16,20},{20,24},{24,28},{28,0},{1,5},{5... | collective-permute-start | bytes 294920 | tf_op jit(solution)/shard_map/ppermute | solution.py:240
  8.9 3.3 %collective-permute-start.2 = (bf16[384,128]{1,0:T(8,128)(2,1)S(1)}, bf16[384,128]{1,0:T(8,128)(2,1)S(1)}, u32[]{:S(2)}, u32[]{:S(2)}) collective-permute-start(bf16[384,128]{1,0:T(8,128)(2,1)S(1)} %shard_map.102.lap), channel_id=1, source_target_pairs={{0,28},{4,0},{8,4},{12,8},{16,12},{20,16},{24,20},{28,24},{1,29},{... | collective-permute-start | bytes 294920 | tf_op jit(solution)/shard_map/ppermute | solution.py:239
  10.0 8.0 %copy-start.5 = (f32[384]{0:T(512)S(1)}, f32[384]{0:T(512)}, u32[]{:S(2)}) copy-start(f32[384]{0:T(512)} %param.15) | copy-start | bytes 4612
  11.1 11.0 %copy-start.1 = (bf16[4,512,128]{2,1,0:T(8,128)(2,1)S(1)}, bf16[4,512,128]{2,1,0:T(8,128)(2,1)}, u32[]{:S(2)}) copy-start(bf16[4,512,128]{2,1,0:T(8,128)(2,1)} %constant.12.clone.refs_4_.refs_2_) | copy-start | bytes 1572868
  11.1 11.0 %copy-start.2 = (bf16[4,512,128]{2,1,0:T(8,128)(2,1)S(1)}, bf16[4,512,128]{2,1,0:T(8,128)(2,1)}, u32[]{:S(2)}) copy-start(bf16[4,512,128]{2,1,0:T(8,128)(2,1)} %constant.11.clone.refs_3_.refs_1_) | copy-start | bytes 1572868
  11.2 11.0 %copy-start.4 = (f32[512]{0:T(512)S(1)}, f32[512]{0:T(512)}, u32[]{:S(2)}) copy-start(f32[512]{0:T(512)} %param.14) | copy-start | bytes 6148
  12.5 8.8 %collective-permute-start.6 = (bf16[384,128]{1,0:T(8,128)(2,1)S(1)}, bf16[384,128]{1,0:T(8,128)(2,1)S(1)}, u32[]{:S(2)}, u32[]{:S(2)}) collective-permute-start(bf16[384,128]{1,0:T(8,128)(2,1)S(1)} %get-tuple-element.32.refs_0_), channel_id=1, source_target_pairs={{2,0},{3,1},{0,2},{1,3},{6,4},{7,5},{4,6},{5,7},{10,8},{11,9},{8,1... | collective-permute-start | bytes 294920 | tf_op jit(solution)/shard_map/ppermute | solution.py:311
  15.9 6.2 %collective-permute-start.5 = (bf16[384,128]{1,0:T(8,128)(2,1)S(1)}, bf16[384,128]{1,0:T(8,128)(2,1)S(1)}, u32[]{:S(2)}, u32[]{:S(2)}) collective-permute-start(bf16[384,128]{1,0:T(8,128)(2,1)S(1)} %get-tuple-element.32.refs_0_), channel_id=1, source_target_pairs={{1,0},{2,1},{3,2},{0,3},{5,4},{6,5},{7,6},{4,7},{9,8},{10,9},{11,1... | collective-permute-start | bytes 294920 | tf_op jit(solution)/shard_map/ppermute | solution.py:311
  17.3 7.8 %collective-permute-start.4 = (bf16[384,128]{1,0:T(8,128)(2,1)S(1)}, bf16[384,128]{1,0:T(8,128)(2,1)S(1)}, u32[]{:S(2)}, u32[]{:S(2)}) collective-permute-start(bf16[384,128]{1,0:T(8,128)(2,1)S(1)} %get-tuple-element.32.refs_0_), channel_id=1, source_target_pairs={{3,0},{0,1},{1,2},{2,3},{7,4},{4,5},{5,6},{6,7},{11,8},{8,9},{9,10... | collective-permute-start | bytes 294920 | tf_op jit(solution)/shard_map/ppermute | solution.py:311
  25.9 1.4 %collective-permute-start.7 = (f32[256,128]{1,0:T(8,128)S(1)}, f32[256,128]{1,0:T(8,128)S(1)}, u32[]{:S(2)}, u32[]{:S(2)}) collective-permute-start(f32[256,128]{1,0:T(8,128)S(1)} %get-tuple-element.38), channel_id=1, source_target_pairs={{0,4},{4,0},{8,12},{12,8},{16,20},{20,16},{24,28},{28,24},{1,5},{5... | collective-permute-start | bytes 393224 | tf_op jit(solution)/shard_map/ppermute | solution.py:245
  27.5 5.9 %collective-permute-start.10 = (f16[272,128]{1,0:T(8,128)(2,1)S(1)}, f16[272,128]{1,0:T(8,128)(2,1)S(1)}, u32[]{:S(2)}, u32[]{:S(2)}) collective-permute-start(f16[272,128]{1,0:T(8,128)(2,1)S(1)} %convert_element_type.21), channel_id=1, source_target_pairs={{0,24},{4,28},{8,16},{12,20},{16,8},{20,12},{24,0},{28,4},{1,25},{... | collective-permute-start | bytes 208904 | tf_op jit(solution)/shard_map/ppermute | solution.py:260
  27.7 5.7 %collective-permute-start.9 = (f16[272,128]{1,0:T(8,128)(2,1)S(1)}, f16[272,128]{1,0:T(8,128)(2,1)S(1)}, u32[]{:S(2)}, u32[]{:S(2)}) collective-permute-start(f16[272,128]{1,0:T(8,128)(2,1)S(1)} %convert_element_type.21), channel_id=1, source_target_pairs={{0,16},{4,20},{8,24},{12,28},{16,0},{20,4},{24,8},{28,12},{1,17},{... | collective-permute-start | bytes 208904 | tf_op jit(solution)/shard_map/ppermute | solution.py:260
  29.4 4.4 %collective-permute-start.8 = (f16[272,128]{1,0:T(8,128)(2,1)S(1)}, f16[272,128]{1,0:T(8,128)(2,1)S(1)}, u32[]{:S(2)}, u32[]{:S(2)}) collective-permute-start(f16[272,128]{1,0:T(8,128)(2,1)S(1)} %convert_element_type.21), channel_id=1, source_target_pairs={{0,8},{4,12},{8,0},{12,4},{16,24},{20,28},{24,16},{28,20},{1,9},{5... | collective-permute-start | bytes 208904 | tf_op jit(solution)/shard_map/ppermute | solution.py:260
  33.9 1.4 %collective-permute-start.11 = (f32[256,128]{1,0:T(8,128)S(1)}, f32[256,128]{1,0:T(8,128)S(1)}, u32[]{:S(2)}, u32[]{:S(2)}) collective-permute-start(f32[256,128]{1,0:T(8,128)S(1)} %multiply_add_fusion.refs_1_), channel_id=1, source_target_pairs={{0,4},{4,0},{8,12},{12,8},{16,20},{20,16},{24,28},{28,24},{1,5},{5... | collective-permute-start | bytes 393224 | tf_op jit(solution)/shard_map/ppermute | solution.py:245

commit v13 on v12

--- a/solution.py
+++ b/solution.py
@@ -177,12 +177,9 @@
     width = kappa.shape[2]
     _, chunk, rows = gathered(order, width)
     value = jnp.concatenate([shard[...] for shard in shards], axis=1)
-    total = None
-    for table in (dh_high, dh_low):
-        weights = [jnp.concatenate([table[c, r, :] for r in rows[:-1]], axis=0) for c in chunk]
-        more = dot(value, jnp.concatenate(weights, axis=1))
-        total = more if total is None else total + more
-    slopes[...] = total
+    pieces = [(table, r) for table in (dh_high, dh_low) for r in rows[:-1]]
+    weights = [jnp.concatenate([table[c, r, :] for table, r in pieces], axis=0) for c in chunk]
+    slopes[...] = dot(jnp.concatenate([value, value], axis=1), jnp.concatenate(weights, axis=1))
     rate = jnp.concatenate([kappa[c] for c in chunk[:-1]], axis=1)
     rates[...] = rate + (0.5 * rate) * jnp.tanh(value.astype(F32))
 

time: 36.5 us -> 36.5 us (level)
  transfers between devices with their start and end apart: 12 -> 12, of which waited for: 9 -> 9; matrix products, arithmetic and copies ran while one was open for 2% -> 2% of each run, Pallas kernels for 17% -> 16%
where the time goes in v13:
time: 36.5 us; the launch traced here: 36.3 us
  starting transfers between devices  15.4 us (42%)
  waiting for transfers between devices  10.4 us (28%)
  Pallas kernels  9.59 us (26%)
  local copies, waits for them, and re-layouts  0.59 us (2%)
    pallas_call x12, Pallas kernels, call(): pl.pallas_call(kernel, out_shape=outs, in_specs=[{'s': SMEM, 'h': HBM, 'v...  9.59 us
    ppermute x3, starting transfers between devices, body(): lax.ppermute(narrow, 'rad', [(source(i, d), i) for i in range(rads)])  5.4 us
    ppermute x3, waiting for transfers between devices, body(): lax.ppermute(narrow, 'rad', [(source(i, d), i) for i in range(rads)])  4.26 us
    ppermute x2, starting transfers between devices, halo(): high = lax.ppermute(block, 'tile', shift('tile', -1))  4.05 us
    ppermute x3, starting transfers between devices, tile_sum(): lax.ppermute(sent, 'tile', [(i, i ^ m) for i in range(count)])  3.55 us
    ppermute x3, waiting for transfers between devices, tile_sum(): lax.ppermute(sent, 'tile', [(i, i ^ m) for i in range(count)])  2.75 us
    ppermute x2, starting transfers between devices, halo(): low = lax.ppermute(block, 'tile', shift('tile', 1))  2.24 us
    ppermute x2, waiting for transfers between devices, swap(): lax.ppermute(block, 'tile', [(i, i ^ 1) for i in range(lax.axis_size('til...  2.13 us
  transfers between devices with their start and end apart: 12, of which 9 were waited for; matrix products, arithmetic and copies ran while one was open for 2% of the time, Pallas kernels for 16%

profile of v13, /device:TPU:0, one launch (start us, length us, event | category | flops | bytes accessed | tf_op | source)
XLA Modules:
  0.0 36.3 jit_solution(8408351159047950433)
XLA Ops:
  0.0 1.1 %shard_map.100 = (f32[384,128]{1,0:T(8,128)S(1)}, bf16[384,128]{1,0:T(8,128)(2,1)S(1)}, s32[3,7]{1,0:T(4,128)S(1)}) custom-call(f32[384,128]{1,0:T(8,128)} %bitcast.16, s32[3,7]{1,0:T(4,128)} %neighbours.1), custom_call_target="tpu_custom_call" | custom-call | tf_op jit(solution)/shard_map/pallas_call | solution.py:57
  1.1 0.5 %collective-permute-start.1 = (bf16[384,128]{1,0:T(8,128)(2,1)S(1)}, bf16[384,128]{1,0:T(8,128)(2,1)S(1)}, u32[]{:S(2)}, u32[]{:S(2)}) collective-permute-start(bf16[384,128]{1,0:T(8,128)(2,1)S(1)} %get-tuple-element.25.own), channel_id=1, source_target_pairs={{0,4},{4,8},{8,12},{12,16},{16,20},{20,24},{24,28},{28,0},{1,5},{5... | collective-permute-start | bytes 294920 | tf_op jit(solution)/shard_map/ppermute | solution.py:237
  1.6 2.9 %collective-permute-start = (bf16[384,128]{1,0:T(8,128)(2,1)S(1)}, bf16[384,128]{1,0:T(8,128)(2,1)S(1)}, u32[]{:S(2)}, u32[]{:S(2)}) collective-permute-start(bf16[384,128]{1,0:T(8,128)(2,1)S(1)} %get-tuple-element.25.own), channel_id=1, source_target_pairs={{0,28},{4,0},{8,4},{12,8},{16,12},{20,16},{24,20},{28,24},{1,29},{... | collective-permute-start | bytes 294920 | tf_op jit(solution)/shard_map/ppermute | solution.py:236
  4.6 2.0 %shard_map.101 = (bf16[9,384,128]{2,1,0:T(8,128)(2,1)S(1)}, f32[384,128]{1,0:T(8,128)S(1)}) custom-call(s32[3,7]{1,0:T(4,128)S(1)} %get-tuple-element.24.ids, bf16[3,3,128,896]{3,2,1,0:T(8,128)(2,1)} %ops.3, bf16[384,128]{1,0:T(8,128)(2,1)S(1)} %get-tuple-element.25.own), custom_call_target="tpu_custom_call" | custom-call | tf_op jit(solution)/shard_map/pallas_call | solution.py:57
  7.1 1.7 %collective-permute-start.3 = (bf16[384,128]{1,0:T(8,128)(2,1)S(1)}, bf16[384,128]{1,0:T(8,128)(2,1)S(1)}, u32[]{:S(2)}, u32[]{:S(2)}) collective-permute-start(bf16[384,128]{1,0:T(8,128)(2,1)S(1)} %shard_map.102.lap), channel_id=1, source_target_pairs={{0,4},{4,8},{8,12},{12,16},{16,20},{20,24},{24,28},{28,0},{1,5},{5... | collective-permute-start | bytes 294920 | tf_op jit(solution)/shard_map/ppermute | solution.py:237
  8.9 1.1 %collective-permute-start.2 = (bf16[384,128]{1,0:T(8,128)(2,1)S(1)}, bf16[384,128]{1,0:T(8,128)(2,1)S(1)}, u32[]{:S(2)}, u32[]{:S(2)}) collective-permute-start(bf16[384,128]{1,0:T(8,128)(2,1)S(1)} %shard_map.102.lap), channel_id=1, source_target_pairs={{0,28},{4,0},{8,4},{12,8},{16,12},{20,16},{24,20},{28,24},{1,29},{... | collective-permute-start | bytes 294920 | tf_op jit(solution)/shard_map/ppermute | solution.py:236
  10.0 1.2 %shard_map.103.part = f32[384,128]{1,0:T(8,128)S(1)} custom-call(s32[3,7]{1,0:T(4,128)S(1)} %get-tuple-element.24.ids, bf16[3,3,128,896]{3,2,1,0:T(8,128)(2,1)S(1)} %copy-done, f32[768,128]{1,0:T(8,128)S(1)} %bitcast.13, bf16[9,384,128]{2,1,0:T(8,128)(2,1)S(1)} %get-tuple-element.26.dense.lap_dense, bf16[384,128]{1,0:T(8,128)(2,1)S(1)} %collective-permute-done.1.low, ...), custom_call_target="tpu_custom_call" | custom-call | tf_op jit(solution)/shard_map/pallas_call | solution.py:57
  11.2 1.0 %collective-permute-done.3.low = bf16[384,128]{1,0:T(8,128)(2,1)S(1)} collective-permute-done((bf16[384,128]{1,0:T(8,128)(2,1)S(1)}, bf16[384,128]{1,0:T(8,128)(2,1)S(1)}, u32[]{:S(2)}, u32[]{:S(2)}) %collective-permute-start.3) | collective-permute-done | bytes 98336 | tf_op jit(solution)/shard_map/ppermute | solution.py:237
  12.5 3.4 %collective-permute-start.6 = (bf16[384,128]{1,0:T(8,128)(2,1)S(1)}, bf16[384,128]{1,0:T(8,128)(2,1)S(1)}, u32[]{:S(2)}, u32[]{:S(2)}) collective-permute-start(bf16[384,128]{1,0:T(8,128)(2,1)S(1)} %get-tuple-element.32.refs_0_), channel_id=1, source_target_pairs={{2,0},{3,1},{0,2},{1,3},{6,4},{7,5},{4,6},{5,7},{10,8},{11,9},{8,1... | collective-permute-start | bytes 294920 | tf_op jit(solution)/shard_map/ppermute | solution.py:308
  15.9 1.4 %collective-permute-start.5 = (bf16[384,128]{1,0:T(8,128)(2,1)S(1)}, bf16[384,128]{1,0:T(8,128)(2,1)S(1)}, u32[]{:S(2)}, u32[]{:S(2)}) collective-permute-start(bf16[384,128]{1,0:T(8,128)(2,1)S(1)} %get-tuple-element.32.refs_0_), channel_id=1, source_target_pairs={{1,0},{2,1},{3,2},{0,3},{5,4},{6,5},{7,6},{4,7},{9,8},{10,9},{11,1... | collective-permute-start | bytes 294920 | tf_op jit(solution)/shard_map/ppermute | solution.py:308
  17.3 0.7 %collective-permute-start.4 = (bf16[384,128]{1,0:T(8,128)(2,1)S(1)}, bf16[384,128]{1,0:T(8,128)(2,1)S(1)}, u32[]{:S(2)}, u32[]{:S(2)}) collective-permute-start(bf16[384,128]{1,0:T(8,128)(2,1)S(1)} %get-tuple-element.32.refs_0_), channel_id=1, source_target_pairs={{3,0},{0,1},{1,2},{2,3},{7,4},{4,5},{5,6},{6,7},{11,8},{8,9},{9,10... | collective-permute-start | bytes 294920 | tf_op jit(solution)/shard_map/ppermute | solution.py:308
  17.9 0.6 %broadcast_in_dim.6.weight = f32[1,384]{1,0:T(1,128)} reshape(f32[384]{0:T(512)S(1)} %copy-done.5) | data formatting | bytes 3072 | tf_op jit(solution)/shard_map/broadcast_in_dim | solution.py:312
  18.5 1.8 %shard_map.105 = (bf16[512,384]{1,0:T(8,128)(2,1)S(1)}, f32[512,128]{1,0:T(8,128)S(1)}, bf16[2,384,256]{2,1,0:T(8,128)(2,1)S(1)}, bf16[2,384,256]{2,1,0:T(8,128)(2,1)S(1)}) custom-call(f32[384,512]{1,0:T(8,128)} %basis.1, f32[1,384]{1,0:T(1,128)} %broadcast_in_dim.6.weight, s32[1,512]{1,0:T(1,128)} %bitcast.17, f32[384,128]{1,0:T(8,128)S(1)} %get-tuple-element.29.value.stepped), custom_call_target="tpu_custom_call" | custom-call | tf_op jit(solution)/shard_map/pallas_call | solution.py:57
  20.3 1.0 %collective-permute-done.6.refs_2_ = bf16[384,128]{1,0:T(8,128)(2,1)S(1)} collective-permute-done((bf16[384,128]{1,0:T(8,128)(2,1)S(1)}, bf16[384,128]{1,0:T(8,128)(2,1)S(1)}, u32[]{:S(2)}, u32[]{:S(2)}) %collective-permute-start.6) | collective-permute-done | bytes 98336 | tf_op jit(solution)/shard_map/ppermute | solution.py:308
  21.3 0.8 %collective-permute-done.5.refs_1_ = bf16[384,128]{1,0:T(8,128)(2,1)S(1)} collective-permute-done((bf16[384,128]{1,0:T(8,128)(2,1)S(1)}, bf16[384,128]{1,0:T(8,128)(2,1)S(1)}, u32[]{:S(2)}, u32[]{:S(2)}) %collective-permute-start.5) | collective-permute-done | bytes 98336 | tf_op jit(solution)/shard_map/ppermute | solution.py:308
  22.1 0.5 %shard_map.106 = (f32[384,512]{1,0:T(8,128)S(1)}, f32[384,384]{1,0:T(8,128)S(1)}) custom-call(bf16[384,128]{1,0:T(8,128)(2,1)S(1)} %get-tuple-element.32.refs_0_, bf16[384,128]{1,0:T(8,128)(2,1)S(1)} %collective-permute-done.5.refs_1_, bf16[384,128]{1,0:T(8,128)(2,1)S(1)} %collective-permute-done.6.refs_2_, bf16[4,512,128]{2,1,0:T(8,128)(2,1)S(1)} %copy-done.2, ...), custom_call_target="tpu_custom_call" | custom-call | tf_op jit(solution)/shard_map/pallas_call | solution.py:57
  22.6 2.5 %collective-permute-done.4.refs_0_ = bf16[384,128]{1,0:T(8,128)(2,1)S(1)} collective-permute-done((bf16[384,128]{1,0:T(8,128)(2,1)S(1)}, bf16[384,128]{1,0:T(8,128)(2,1)S(1)}, u32[]{:S(2)}, u32[]{:S(2)}) %collective-permute-start.4) | collective-permute-done | bytes 98336 | tf_op jit(solution)/shard_map/ppermute | solution.py:308
  25.1 0.8 %shard_map.107 = (bf16[384,256]{1,0:T(8,128)(2,1)S(1)}, f32[256,128]{1,0:T(8,128)S(1)}) custom-call(bf16[384,128]{1,0:T(8,128)(2,1)S(1)} %collective-permute-done.4.refs_0_, bf16[4,512,128]{2,1,0:T(8,128)(2,1)S(1)} %copy-done.2, bf16[4,512,128]{2,1,0:T(8,128)(2,1)S(1)} %copy-done.1, f32[4,1,128]{2,1,0:T(1,128)S(1)} %bitcast.15, ...), custom_call_target="tpu_custom_call" | custom-call | tf_op jit(solution)/shard_map/pallas_call | solution.py:57
  26.2 1.1 %collective-permute-done.7.received = f32[256,128]{1,0:T(8,128)S(1)} collective-permute-done((f32[256,128]{1,0:T(8,128)S(1)}, f32[256,128]{1,0:T(8,128)S(1)}, u32[]{:S(2)}, u32[]{:S(2)}) %collective-permute-start.7) | collective-permute-done | bytes 131104 | tf_op jit(solution)/shard_map/ppermute | solution.py:242
  27.7 1.7 %collective-permute-start.9 = (f16[272,128]{1,0:T(8,128)(2,1)S(1)}, f16[272,128]{1,0:T(8,128)(2,1)S(1)}, u32[]{:S(2)}, u32[]{:S(2)}) collective-permute-start(f16[272,128]{1,0:T(8,128)(2,1)S(1)} %convert_element_type.21), channel_id=1, source_target_pairs={{0,16},{4,20},{8,24},{12,28},{16,0},{20,4},{24,8},{28,12},{1,17},{... | collective-permute-start | bytes 208904 | tf_op jit(solution)/shard_map/ppermute | solution.py:257
  29.4 1.6 %collective-permute-start.8 = (f16[272,128]{1,0:T(8,128)(2,1)S(1)}, f16[272,128]{1,0:T(8,128)(2,1)S(1)}, u32[]{:S(2)}, u32[]{:S(2)}) collective-permute-start(f16[272,128]{1,0:T(8,128)(2,1)S(1)} %convert_element_type.21), channel_id=1, source_target_pairs={{0,8},{4,12},{8,0},{12,4},{16,24},{20,28},{24,16},{28,20},{1,9},{5... | collective-permute-start | bytes 208904 | tf_op jit(solution)/shard_map/ppermute | solution.py:257
  31.0 2.4 %collective-permute-done.10 = f16[272,128]{1,0:T(8,128)(2,1)S(1)} collective-permute-done((f16[272,128]{1,0:T(8,128)(2,1)S(1)}, f16[272,128]{1,0:T(8,128)(2,1)S(1)}, u32[]{:S(2)}, u32[]{:S(2)}) %collective-permute-start.10) | collective-permute-done | bytes 69664 | tf_op jit(solution)/shard_map/ppermute | solution.py:257
  34.2 1.1 %collective-permute-done.11.refs_1_ = f32[256,128]{1,0:T(8,128)S(1)} collective-permute-done((f32[256,128]{1,0:T(8,128)S(1)}, f32[256,128]{1,0:T(8,128)S(1)}, u32[]{:S(2)}, u32[]{:S(2)}) %collective-permute-start.11) | collective-permute-done | bytes 131104 | tf_op jit(solution)/shard_map/ppermute | solution.py:242
  35.3 0.9 %shard_map.111 = f32[384,128]{1,0:T(8,128)} custom-call(f32[384,128]{1,0:T(8,128)S(1)} %shard_map.110.refs_0_, f32[256,128]{1,0:T(8,128)S(1)} %collective-permute-done.11.refs_1_, bf16[2,384,256]{2,1,0:T(8,128)(2,1)S(1)} %get-tuple-element.41.refs_2_, bf16[2,384,256]{2,1,0:T(8,128)(2,1)S(1)} %get-tuple-element.42.refs_3_), custom_call_target="tpu_custom_call" | custom-call | tf_op jit(solution)/shard_map/pallas_call | solution.py:57
  (30 shorter events, 2.4 us)
Async XLA Ops:
  0.0 10.0 %copy-start = (bf16[3,3,128,896]{3,2,1,0:T(8,128)(2,1)S(1)}, bf16[3,3,128,896]{3,2,1,0:T(8,128)(2,1)}, u32[]{:S(2)}) copy-start(bf16[3,3,128,896]{3,2,1,0:T(8,128)(2,1)} %ops.3) | copy-start | bytes 6193156
  0.0 10.0 %copy-start.3 = (f32[384,2,128]{2,1,0:T(2,128)S(1)}, f32[384,2,128]{2,1,0:T(2,128)}, u32[]{:S(2)}) copy-start(f32[384,2,128]{2,1,0:T(2,128)} %param.11) | copy-start | bytes 1179652
  1.1 5.7 %collective-permute-start.1 = (bf16[384,128]{1,0:T(8,128)(2,1)S(1)}, bf16[384,128]{1,0:T(8,128)(2,1)S(1)}, u32[]{:S(2)}, u32[]{:S(2)}) collective-permute-start(bf16[384,128]{1,0:T(8,128)(2,1)S(1)} %get-tuple-element.25.own), channel_id=1, source_target_pairs={{0,4},{4,8},{8,12},{12,16},{16,20},{20,24},{24,28},{28,0},{1,5},{5... | collective-permute-start | bytes 294920 | tf_op jit(solution)/shard_map/ppermute | solution.py:237
  1.6 5.2 %collective-permute-start = (bf16[384,128]{1,0:T(8,128)(2,1)S(1)}, bf16[384,128]{1,0:T(8,128)(2,1)S(1)}, u32[]{:S(2)}, u32[]{:S(2)}) collective-permute-start(bf16[384,128]{1,0:T(8,128)(2,1)S(1)} %get-tuple-element.25.own), channel_id=1, source_target_pairs={{0,28},{4,0},{8,4},{12,8},{16,12},{20,16},{24,20},{28,24},{1,29},{... | collective-permute-start | bytes 294920 | tf_op jit(solution)/shard_map/ppermute | solution.py:236
  7.1 5.1 %collective-permute-start.3 = (bf16[384,128]{1,0:T(8,128)(2,1)S(1)}, bf16[384,128]{1,0:T(8,128)(2,1)S(1)}, u32[]{:S(2)}, u32[]{:S(2)}) collective-permute-start(bf16[384,128]{1,0:T(8,128)(2,1)S(1)} %shard_map.102.lap), channel_id=1, source_target_pairs={{0,4},{4,8},{8,12},{12,16},{16,20},{20,24},{24,28},{28,0},{1,5},{5... | collective-permute-start | bytes 294920 | tf_op jit(solution)/shard_map/ppermute | solution.py:237
  8.9 3.3 %collective-permute-start.2 = (bf16[384,128]{1,0:T(8,128)(2,1)S(1)}, bf16[384,128]{1,0:T(8,128)(2,1)S(1)}, u32[]{:S(2)}, u32[]{:S(2)}) collective-permute-start(bf16[384,128]{1,0:T(8,128)(2,1)S(1)} %shard_map.102.lap), channel_id=1, source_target_pairs={{0,28},{4,0},{8,4},{12,8},{16,12},{20,16},{24,20},{28,24},{1,29},{... | collective-permute-start | bytes 294920 | tf_op jit(solution)/shard_map/ppermute | solution.py:236
  10.0 8.0 %copy-start.5 = (f32[384]{0:T(512)S(1)}, f32[384]{0:T(512)}, u32[]{:S(2)}) copy-start(f32[384]{0:T(512)} %param.15) | copy-start | bytes 4612
  11.1 11.0 %copy-start.1 = (bf16[4,512,128]{2,1,0:T(8,128)(2,1)S(1)}, bf16[4,512,128]{2,1,0:T(8,128)(2,1)}, u32[]{:S(2)}) copy-start(bf16[4,512,128]{2,1,0:T(8,128)(2,1)} %constant.12.clone.refs_4_.refs_2_) | copy-start | bytes 1572868
  11.1 11.0 %copy-start.2 = (bf16[4,512,128]{2,1,0:T(8,128)(2,1)S(1)}, bf16[4,512,128]{2,1,0:T(8,128)(2,1)}, u32[]{:S(2)}) copy-start(bf16[4,512,128]{2,1,0:T(8,128)(2,1)} %constant.11.clone.refs_3_.refs_1_) | copy-start | bytes 1572868
  11.2 11.0 %copy-start.4 = (f32[512]{0:T(512)S(1)}, f32[512]{0:T(512)}, u32[]{:S(2)}) copy-start(f32[512]{0:T(512)} %param.14) | copy-start | bytes 6148
  12.5 8.8 %collective-permute-start.6 = (bf16[384,128]{1,0:T(8,128)(2,1)S(1)}, bf16[384,128]{1,0:T(8,128)(2,1)S(1)}, u32[]{:S(2)}, u32[]{:S(2)}) collective-permute-start(bf16[384,128]{1,0:T(8,128)(2,1)S(1)} %get-tuple-element.32.refs_0_), channel_id=1, source_target_pairs={{2,0},{3,1},{0,2},{1,3},{6,4},{7,5},{4,6},{5,7},{10,8},{11,9},{8,1... | collective-permute-start | bytes 294920 | tf_op jit(solution)/shard_map/ppermute | solution.py:308
  15.9 6.2 %collective-permute-start.5 = (bf16[384,128]{1,0:T(8,128)(2,1)S(1)}, bf16[384,128]{1,0:T(8,128)(2,1)S(1)}, u32[]{:S(2)}, u32[]{:S(2)}) collective-permute-start(bf16[384,128]{1,0:T(8,128)(2,1)S(1)} %get-tuple-element.32.refs_0_), channel_id=1, source_target_pairs={{1,0},{2,1},{3,2},{0,3},{5,4},{6,5},{7,6},{4,7},{9,8},{10,9},{11,1... | collective-permute-start | bytes 294920 | tf_op jit(solution)/shard_map/ppermute | solution.py:308
  17.3 7.8 %collective-permute-start.4 = (bf16[384,128]{1,0:T(8,128)(2,1)S(1)}, bf16[384,128]{1,0:T(8,128)(2,1)S(1)}, u32[]{:S(2)}, u32[]{:S(2)}) collective-permute-start(bf16[384,128]{1,0:T(8,128)(2,1)S(1)} %get-tuple-element.32.refs_0_), channel_id=1, source_target_pairs={{3,0},{0,1},{1,2},{2,3},{7,4},{4,5},{5,6},{6,7},{11,8},{8,9},{9,10... | collective-permute-start | bytes 294920 | tf_op jit(solution)/shard_map/ppermute | solution.py:308
  25.9 1.4 %collective-permute-start.7 = (f32[256,128]{1,0:T(8,128)S(1)}, f32[256,128]{1,0:T(8,128)S(1)}, u32[]{:S(2)}, u32[]{:S(2)}) collective-permute-start(f32[256,128]{1,0:T(8,128)S(1)} %get-tuple-element.38), channel_id=1, source_target_pairs={{0,4},{4,0},{8,12},{12,8},{16,20},{20,16},{24,28},{28,24},{1,5},{5... | collective-permute-start | bytes 393224 | tf_op jit(solution)/shard_map/ppermute | solution.py:242
  27.5 5.9 %collective-permute-start.10 = (f16[272,128]{1,0:T(8,128)(2,1)S(1)}, f16[272,128]{1,0:T(8,128)(2,1)S(1)}, u32[]{:S(2)}, u32[]{:S(2)}) collective-permute-start(f16[272,128]{1,0:T(8,128)(2,1)S(1)} %convert_element_type.21), channel_id=1, source_target_pairs={{0,24},{4,28},{8,16},{12,20},{16,8},{20,12},{24,0},{28,4},{1,25},{... | collective-permute-start | bytes 208904 | tf_op jit(solution)/shard_map/ppermute | solution.py:257
  27.7 5.7 %collective-permute-start.9 = (f16[272,128]{1,0:T(8,128)(2,1)S(1)}, f16[272,128]{1,0:T(8,128)(2,1)S(1)}, u32[]{:S(2)}, u32[]{:S(2)}) collective-permute-start(f16[272,128]{1,0:T(8,128)(2,1)S(1)} %convert_element_type.21), channel_id=1, source_target_pairs={{0,16},{4,20},{8,24},{12,28},{16,0},{20,4},{24,8},{28,12},{1,17},{... | collective-permute-start | bytes 208904 | tf_op jit(solution)/shard_map/ppermute | solution.py:257
  29.4 4.4 %collective-permute-start.8 = (f16[272,128]{1,0:T(8,128)(2,1)S(1)}, f16[272,128]{1,0:T(8,128)(2,1)S(1)}, u32[]{:S(2)}, u32[]{:S(2)}) collective-permute-start(f16[272,128]{1,0:T(8,128)(2,1)S(1)} %convert_element_type.21), channel_id=1, source_target_pairs={{0,8},{4,12},{8,0},{12,4},{16,24},{20,28},{24,16},{28,20},{1,9},{5... | collective-permute-start | bytes 208904 | tf_op jit(solution)/shard_map/ppermute | solution.py:257
  33.9 1.4 %collective-permute-start.11 = (f32[256,128]{1,0:T(8,128)S(1)}, f32[256,128]{1,0:T(8,128)S(1)}, u32[]{:S(2)}, u32[]{:S(2)}) collective-permute-start(f32[256,128]{1,0:T(8,128)S(1)} %multiply_add_fusion.refs_1_), channel_id=1, source_target_pairs={{0,4},{4,0},{8,12},{12,8},{16,20},{20,16},{24,28},{28,24},{1,5},{5... | collective-permute-start | bytes 393224 | tf_op jit(solution)/shard_map/ppermute | solution.py:242
